TPU v7x, 32 devices: a whole 2x2x4 slice. The times are simulated.
32 devices in a mesh: gx: 2 (over y), gy: 4 (over z), lev: 4 (over x, core).
Axes of the slice: x: 2, y: 2, z: 4, core: 2. Of those that a mesh axis runs over, the one named last changes fastest.
Arguments:
- wind_x: float32 [128, 64, 512], P('lev', 'gx', 'gy'), may hold values from -6 to 6
- wind_y: float32 [128, 64, 512], P('lev', 'gx', 'gy'), may hold values from -6 to 6
- wind_z: float32 [128, 64, 512], P('lev', 'gx', 'gy'), may hold values from -6 to 6
- pressure: float32 [128, 64, 512], P('lev', 'gx', 'gy'), may hold values from -6 to 6
- jacobian: float32 [64, 512], P('gx', 'gy'), may hold values from 0.5 to 2
- slope_x: float32 [64, 512], P('gx', 'gy'), may hold values from -3 to 3
- slope_y: float32 [64, 512], P('gx', 'gy'), may hold values from -3 to 3
- stiffness: float32 [128, 64, 512], P('lev', 'gx', 'gy'), may hold values from 10 to 1000
Outputs:
- wind_x_out: float32 [128, 64, 512], P('lev', 'gx', 'gy')
- wind_y_out: float32 [128, 64, 512], P('lev', 'gx', 'gy')
- wind_z_out: float32 [128, 64, 512], P('lev', 'gx', 'gy')
- pressure_out: float32 [128, 64, 512], P('lev', 'gx', 'gy')
All inputs are finite; a program needn't handle non-finite values.
Results may differ from a plain program's by a relative error of at most 0.000096.
Values sent between devices are 32-bit elements; how exact they have to be, the bound alone decides.
No kernel may reach another device: no remote copies, remote signals or barrier semaphores. Data moves between devices by JAX's collectives and lax.ppermute only.
A program may use at most 64 MiB of HBM per device.

v0:
```python
import functools

import jax
import jax.numpy as jnp
from jax import lax
from jax.experimental import pallas as pl
from jax.experimental.pallas import tpu as pltpu
from jax.sharding import PartitionSpec as P

SUBSTEPS = 2

grad_coef = 0.35
div_coef = 0.35
vert_coef = 0.25

CG = grad_coef / 12.0
CD = div_coef / 12.0
ROWS = 8
SLOT = 4


def lane_index():
    return lax.broadcasted_iota(jnp.int32, (ROWS, 128), 1)


def row_index():
    return lax.broadcasted_iota(jnp.int32, (ROWS, 128), 0)


def only(mask, value):
    return jnp.where(mask, jnp.float32(value), jnp.float32(0.0))


def tiles_of(ref, level, count):
    return [ref[level, ROWS * t : ROWS * (t + 1), :] for t in range(count)]


def planes_of(ref, count):
    return [ref[ROWS * t : ROWS * (t + 1), :] for t in range(count)]


def put_tiles(ref, level, tiles):
    for t, tile in enumerate(tiles):
        ref[level, ROWS * t : ROWS * (t + 1), :] = tile


def put_planes(ref, tiles):
    for t, tile in enumerate(tiles):
        ref[ROWS * t : ROWS * (t + 1), :] = tile


class Stencil:
    def __init__(self, scale):
        lane, row = lane_index(), row_index()
        self.lane, self.row = lane, row
        self.scale = scale
        self.back2 = only(lane >= 2, scale)
        self.back1 = only(lane >= 1, -8.0 * scale)
        self.ahead1 = only(lane < 127, 8.0 * scale)
        self.ahead2 = only(lane < 126, -scale)

    def along_y(self, tile):
        return (
            self.back2 * pltpu.roll(tile, 2, 1)
            + self.back1 * pltpu.roll(tile, 1, 1)
            + self.ahead1 * pltpu.roll(tile, 127, 1)
            + self.ahead2 * pltpu.roll(tile, 126, 1)
        )

    def moved(self, tiles, by):
        count = len(tiles)
        rolled = [pltpu.roll(tile, by % ROWS, 0) for tile in tiles]
        zero = jnp.zeros_like(tiles[0])
        out = []
        for t in range(count):
            if by > 0:
                other = rolled[t - 1] if t > 0 else zero
                out.append(jnp.where(self.row < by, other, rolled[t]))
            else:
                other = rolled[t + 1] if t < count - 1 else zero
                out.append(jnp.where(self.row >= ROWS + by, other, rolled[t]))
        return out

    def along_x(self, tiles):
        back2, back1 = self.moved(tiles, 2), self.moved(tiles, 1)
        ahead1, ahead2 = self.moved(tiles, -1), self.moved(tiles, -2)
        return [
            self.scale * (b2 - a2) + (8.0 * self.scale) * (a1 - b1)
            for b2, b1, a1, a2 in zip(back2, back1, ahead1, ahead2)
        ]


def edge_of(tile, axis, place, near, cross, sign):
    size = 128 if axis == 1 else ROWS
    low = pltpu.roll(tile, 1, axis)
    high = pltpu.roll(tile, size - 1, axis)
    alpha = only(place < 2, sign * near) + only(place >= size - 2, near)
    beta = only(place == 1, cross)
    gamma = only(place == size - 2, sign * cross)
    return alpha * tile + beta * low + gamma * high


class Packer:
    def __init__(self):
        self.lane, self.row = lane_index(), row_index()

    def lanes(self, first, second):
        lane = self.lane
        far = jnp.where(lane < 64, pltpu.roll(second, 2, 1), pltpu.roll(second, 126, 1))
        return jnp.where((lane < 2) | (lane >= 126), first, far)

    def rows(self, first_low, first_high, second_low, second_high):
        row = self.row
        second = pltpu.roll(jnp.where(row < 4, second_low, second_high), 4, 0)
        first = jnp.where(row < 4, pltpu.roll(first_high, 2, 0), pltpu.roll(first_low, 6, 0))
        return jnp.where((row >= 2) & (row < 6), second, first)


def near_value(tile, axis, place, scale):
    size = 128 if axis == 1 else ROWS
    low = pltpu.roll(tile, 1, axis)
    high = pltpu.roll(tile, size - 1, axis)
    picked = jnp.where(place == 1, low, jnp.where(place == size - 2, high, tile))
    return scale * picked


def start_level(stencil, packer, level, pres, wind_x, wind_y, jac, low, high):
    lane, row = stencil.lane, stencil.row
    count = len(pres)
    new_y = [w - stencil.along_y(p) for w, p in zip(wind_y, pres)]
    new_x = [w - d for w, d in zip(wind_x, stencil.along_x(pres))]
    slot = lax.shift_right_logical(lane, 2)
    before = lax.rem(level + 31, 32)
    low_out, high_out = [], []
    for t in range(count):
        first = edge_of(pres[t], 1, lane, CG, 8.0 * CG, -1.0)
        second = edge_of(jac[t] * new_y[t], 1, lane, CD, 8.0 * CD, -1.0)
        packed = pltpu.roll(packer.lanes(first, second), SLOT * level, 1)
        low_out.append(jnp.where(slot == level, packed, low[t]))
        high_out.append(jnp.where(slot == before, packed, high[t]))
    last = count - 1
    rows = packer.rows(
        edge_of(pres[0], 0, row, CG, 8.0 * CG, -1.0),
        edge_of(pres[last], 0, row, CG, 8.0 * CG, -1.0),
        edge_of(jac[0] * new_x[0], 0, row, CD, 8.0 * CD, -1.0),
        edge_of(jac[last] * new_x[last], 0, row, CD, 8.0 * CD, -1.0),
    )
    return new_x, new_y, rows, low_out, high_out


def kernel_a(p_ref, wx_ref, wy_ref, jac_ref, nx_ref, ny_ref, rows_ref, low_ref, high_ref):
    levels, rows, _ = p_ref.shape
    count = rows // ROWS
    stencil, packer = Stencil(CG), Packer()
    lane, row = stencil.lane, stencil.row
    jac = planes_of(jac_ref, count)

    def step(level, carry):
        new_x, new_y, edge, low, high = start_level(
            stencil,
            packer,
            level,
            tiles_of(p_ref, level, count),
            tiles_of(wx_ref, level, count),
            tiles_of(wy_ref, level, count),
            jac,
            *carry,
        )
        put_tiles(nx_ref, level, new_x)
        put_tiles(ny_ref, level, new_y)
        rows_ref[level] = edge
        return low, high

    zeros = [jnp.zeros((ROWS, 128), jnp.float32)] * count
    low, high = lax.fori_loop(0, levels, step, (zeros, zeros))
    both = CG * CD
    static = [
        packer.lanes(
            edge_of(j, 1, lane, both, 64.0 * both, 1.0), near_value(j, 1, lane, -8.0 * both)
        )
        for j in jac
    ]
    put_tiles(low_ref, 0, low)
    put_tiles(high_ref, 0, high)
    put_tiles(low_ref, 1, static)
    put_tiles(high_ref, 1, static)
    rows_ref[levels] = packer.rows(
        edge_of(jac[0], 0, row, both, 64.0 * both, 1.0),
        edge_of(jac[-1], 0, row, both, 64.0 * both, 1.0),
        near_value(jac[0], 0, row, -8.0 * both),
        near_value(jac[-1], 0, row, -8.0 * both),
    )


def kernel_f(s_ref, r_ref, i_ref, q_ref, v_ref, stat_ref):
    levels, rows, _ = s_ref.shape

    def down(level, carry):
        excess, prod = carry
        rate = 1.0 / s_ref[level]
        excess = rate + excess
        inv = 1.0 / (1.0 + excess)
        prod = prod * inv
        r_ref[level] = rate
        i_ref[level] = inv
        q_ref[level] = prod
        return excess * inv, prod

    ones = jnp.ones((rows, 128), jnp.float32)
    lax.fori_loop(0, levels, down, (ones, ones))

    def up(step, value):
        level = levels - 1 - step
        value = q_ref[level] + i_ref[level] * value
        v_ref[level] = value
        return value

    first = lax.fori_loop(0, levels, up, jnp.zeros((rows, 128), jnp.float32))
    stat_ref[0] = first
    stat_ref[1] = q_ref[levels - 1]
    stat_ref[2] = i_ref[levels - 1]
    stat_ref[3] = r_ref[0]
    stat_ref[4] = r_ref[levels - 1]


def unpack_lanes(lane, low, high, level):
    turn = 128 - SLOT * level

    def placed(from_low, from_high):
        above = pltpu.roll(low, lax.rem(turn + from_low, 128), 1)
        below = pltpu.roll(high, lax.rem(turn + from_high, 128), 1)
        return jnp.where(lane < 2, below, jnp.where(lane >= 126, above, 0.0))

    return placed(126, 2), placed(124, 4)


def unpack_rows(row, tile):
    zero = jnp.zeros_like(tile)
    first = jnp.where(row < 2, tile, zero), jnp.where(row >= 6, tile, zero)
    near, far = pltpu.roll(tile, 6, 0), pltpu.roll(tile, 2, 0)
    second = jnp.where(row < 2, near, zero), jnp.where(row >= 6, far, zero)
    return first, second


def kernel_b(
    p_ref,
    nxz_ref,
    nyz_ref,
    wz_ref,
    jac_ref,
    sx_ref,
    sy_ref,
    r_ref,
    i_ref,
    v_ref,
    rows_ref,
    low_ref,
    high_ref,
    srows_ref,
    slow_ref,
    shigh_ref,
    nx_ref,
    ny_ref,
    ps_ref,
    y_ref,
    face_ref,
):
    levels, rows, _ = p_ref.shape
    count = rows // ROWS
    last = count - 1
    stencil = Stencil(CD)
    lane, row = stencil.lane, stencil.row
    jac = planes_of(jac_ref, count)
    inv_jac = [1.0 / j for j in jac]
    low = [low_ref[0, ROWS * t : ROWS * (t + 1), :] for t in range(count)]
    high = [high_ref[0, ROWS * t : ROWS * (t + 1), :] for t in range(count)]
    lane_stat = [
        unpack_lanes(
            lane,
            slow_ref[1, ROWS * t : ROWS * (t + 1), :],
            shigh_ref[1, ROWS * t : ROWS * (t + 1), :],
            0,
        )
        for t in range(count)
    ]
    row_self, row_cross = unpack_rows(row, srows_ref[levels])
    even_lane = (lane & 1) == 0
    even_row = (row & 1) == 0

    def cross(tile, axis, even, size):
        return jnp.where(even, pltpu.roll(tile, size - 1, axis), pltpu.roll(tile, 1, axis))

    def star(level):
        pres = tiles_of(p_ref, level, count)
        new_x = tiles_of(nxz_ref, level, count)
        new_y = tiles_of(nyz_ref, level, count)
        edge, flux = unpack_rows(row, rows_ref[level])
        new_x[0] = new_x[0] - edge[0]
        new_x[last] = new_x[last] - edge[1]
        lanes = [unpack_lanes(lane, low[t], high[t], level) for t in range(count)]
        new_y = [n - e[0] for n, e in zip(new_y, lanes)]
        put_tiles(nx_ref, level, new_x)
        put_tiles(ny_ref, level, new_y)
        total = stencil.along_x([j * n for j, n in zip(jac, new_x)])
        for side, t in ((0, 0), (1, last)):
            total[t] = (
                total[t]
                + flux[side]
                + row_self[side] * pres[t]
                + row_cross[side] * cross(pres[t], 0, even_row, ROWS)
            )
        stars, forces = [], []
        for t in range(count):
            spread = (
                total[t]
                + stencil.along_y(jac[t] * new_y[t])
                + lanes[t][1]
                + lane_stat[t][0] * pres[t]
                + lane_stat[t][1] * cross(pres[t], 1, even_lane, 128)
            )
            stars.append(pres[t] - inv_jac[t] * spread)
            part = slice(ROWS * t, ROWS * (t + 1))
            forces.append(
                wz_ref[level, part, :]
                + sx_ref[part, :] * new_x[t]
                + sy_ref[part, :] * new_y[t]
            )
        put_tiles(ps_ref, level, stars)
        return stars, forces

    def sweep(level, below, above, force, value, first):
        rate = tiles_of(r_ref, level, count)
        inv = tiles_of(i_ref, level, count)
        gain = tiles_of(v_ref, level, count)
        values, firsts = [], []
        for t in range(count):
            rhs = rate[t] * (force[t] - vert_coef * (above[t] - below[t]))
            firsts.append(first[t] + gain[t] * rhs)
            values.append((rhs + value[t]) * inv[t])
        put_tiles(y_ref, level, values)
        return values, firsts

    zeros = [jnp.zeros((ROWS, 128), jnp.float32)] * count
    here, force = star(0)
    put_tiles(face_ref, 2, here)

    def step(level, carry):
        below, here, force, value, first = carry
        above, force_next = star(level)
        value, first = sweep(level - 1, below, above, force, value, first)
        return here, above, force_next, value, first

    below, here, force, value, first = lax.fori_loop(
        1, levels, step, (zeros, here, force, zeros, zeros)
    )
    value, first = sweep(levels - 1, below, zeros, force, value, first)
    put_tiles(face_ref, 0, first)
    put_tiles(face_ref, 1, value)
    put_tiles(face_ref, 3, here)


def reduced(blocks, mine, face, stat):
    faces = [face(j) for j in range(blocks)]
    stats = [stat(j) for j in range(blocks)]
    up = [
        faces[j][1] + vert_coef * stats[j + 1][3] * faces[j][3] if j < blocks - 1 else None
        for j in range(blocks)
    ]
    down = [
        faces[j][0] - vert_coef * stats[j - 1][4] * faces[j][2] if j > 0 else None
        for j in range(blocks)
    ]
    base, slope = [up[0]], [stats[0][2]]
    scale, known = [None], [None]
    for j in range(1, blocks):
        near, link, far = stats[j][0], stats[j][1], stats[j][2]
        scale.append(1.0 / (1.0 - near * slope[j - 1]))
        known.append(scale[j] * (down[j] + near * base[j - 1]))
        if j < blocks - 1:
            base.append(up[j] + link * (base[j - 1] + slope[j - 1] * known[j]))
            slope.append(far + link * link * slope[j - 1] * scale[j])
    zero = jnp.zeros_like(faces[0][0])
    above = [None] * blocks + [zero]
    below = [zero] + [None] * blocks
    for j in range(blocks - 1, 0, -1):
        above[j] = known[j] + scale[j] * stats[j][1] * above[j + 1]
        below[j] = base[j - 1] + slope[j - 1] * above[j]
    lower, upper, under, over = zero, zero, zero, zero
    for j in range(blocks):
        here = mine == j
        if j > 0:
            lower = jnp.where(here, below[j], lower)
            under = jnp.where(
                here, below[j] - vert_coef * stats[j][3] * faces[j - 1][3], under
            )
        if j < blocks - 1:
            upper = jnp.where(here, above[j + 1], upper)
            over = jnp.where(
                here, above[j + 1] + vert_coef * stats[j][4] * faces[j + 1][2], over
            )
    return lower, upper, under, over


def boundary(blocks, mine, count, face_refs, stat_refs):
    def solve(t):
        part = slice(ROWS * t, ROWS * (t + 1))

        def read(refs, planes):
            own = [
                [ref[k, part, :] for k in range(planes)] for ref in refs
            ]

            def block(j):
                out = []
                for k in range(planes):
                    value = own[0][k]
                    for shift in range(1, blocks):
                        value = jnp.where(mine == (j ^ shift), own[shift][k], value)
                    out.append(value)
                return out

            return block

        return reduced(blocks, mine, read(face_refs, 4), read(stat_refs, 5))

    parts = [solve(t) for t in range(count)]
    return [[part[k] for part in parts] for k in range(4)]


def finish(blocks, count, levels, y_ref, q_ref, i_ref, ps_ref, x_ref, p_ref, face_refs, stat_refs, use):
    mine = lax.axis_index("lev")
    lower, upper, under, over = boundary(blocks, mine, count, face_refs, stat_refs)

    def solved(level, above):
        value = tiles_of(y_ref, level, count)
        prod = tiles_of(q_ref, level, count)
        inv = tiles_of(i_ref, level, count)
        out = [y + q * u + i * a for y, q, u, i, a in zip(value, prod, lower, inv, above)]
        put_tiles(x_ref, level, out)
        return out

    def pressed(level, above, below, state):
        star = tiles_of(ps_ref, level, count)
        pres = [s - vert_coef * (a - b) for s, a, b in zip(star, above, below)]
        put_tiles(p_ref, level, pres)
        return use(level, pres, state)

    def step(index, carry):
        above, here, state = carry
        level = levels - 2 - index
        below = solved(level, here)
        state = pressed(level + 1, above, below, state)
        return here, below, state

    top = solved(levels - 1, upper)
    zeros = [jnp.zeros((ROWS, 128), jnp.float32)] * count
    above, here, state = lax.fori_loop(0, levels - 1, step, (over, top, (zeros, zeros)))
    return pressed(0, above, under, state)


def kernel_c(blocks, y_ref, q_ref, i_ref, ps_ref, wx_ref, wy_ref, jac_ref, *refs):
    face_refs, stat_refs = refs[:blocks], refs[blocks : 2 * blocks]
    x_ref, p_ref, nx_ref, ny_ref, rows_ref, low_ref, high_ref = refs[2 * blocks :]
    levels, rows, _ = y_ref.shape
    count = rows // ROWS
    stencil, packer = Stencil(CG), Packer()

    def use(level, pres, state):
        new_x, new_y, edge, low, high = start_level(
            stencil,
            packer,
            level,
            pres,
            tiles_of(wx_ref, level, count),
            tiles_of(wy_ref, level, count),
            planes_of(jac_ref, count),
            *state,
        )
        put_tiles(nx_ref, level, new_x)
        put_tiles(ny_ref, level, new_y)
        rows_ref[level] = edge
        return low, high

    low, high = finish(
        blocks, count, levels, y_ref, q_ref, i_ref, ps_ref, x_ref, p_ref, face_refs, stat_refs, use
    )
    put_tiles(low_ref, 0, low)
    put_tiles(high_ref, 0, high)


def kernel_d(blocks, y_ref, q_ref, i_ref, ps_ref, *refs):
    face_refs, stat_refs = refs[:blocks], refs[blocks : 2 * blocks]
    x_ref, p_ref = refs[2 * blocks :]
    levels, rows, _ = y_ref.shape
    finish(
        blocks,
        rows // ROWS,
        levels,
        y_ref,
        q_ref,
        i_ref,
        ps_ref,
        x_ref,
        p_ref,
        face_refs,
        stat_refs,
        lambda level, pres, state: state,
    )


def call(kernel, name, shapes, *args):
    space = pl.BlockSpec(memory_space=pltpu.VMEM)
    size = sum(a.size for a in args) + sum(functools.reduce(lambda a, b: a * b, s) for s in shapes)
    return pl.pallas_call(
        kernel,
        out_shape=[jax.ShapeDtypeStruct(s, jnp.float32) for s in shapes],
        in_specs=[space] * len(args),
        out_specs=[space] * len(shapes),
        compiler_params=pltpu.CompilerParams(vmem_limit_bytes=32 * 1024 * 1024),
        cost_estimate=pl.CostEstimate(
            flops=8 * size, bytes_accessed=4 * size, transcendentals=0
        ),
        name=name,
    )(*args)


def swap(value, axis, partner):
    count = lax.axis_size(axis)
    return lax.ppermute(value, axis, [(i, partner(i)) for i in range(count)])


def exchange_rows(rows):
    count = lax.axis_size("gx")
    if count == 2:
        return swap(rows, "gx", lambda i: 1 - i)
    up = swap(rows[:, : ROWS // 2], "gx", lambda i: (i + 1) % count)
    down = swap(rows[:, ROWS // 2 :], "gx", lambda i: (i - 1) % count)
    return jnp.concatenate([up, down], axis=1)


def exchange_lanes(low, high):
    count = lax.axis_size("gy")
    from_above = swap(low, "gy", lambda i: (i - 1) % count)
    from_below = swap(high, "gy", lambda i: (i + 1) % count)
    return from_above, from_below


def gather_levels(planes):
    count = lax.axis_size("lev")
    return [planes] + [
        swap(planes, "lev", lambda i, shift=shift: i ^ shift) for shift in range(1, count)
    ]


def local(wind_x, wind_y, wind_z, pressure, jacobian, slope_x, slope_y, stiffness):
    field = wind_x.shape
    levels, rows, lanes = field
    blocks = lax.axis_size("lev")
    plane = (rows, lanes)
    assert lanes == 128 and levels * SLOT == 128 and rows % ROWS == 0
    assert blocks & (blocks - 1) == 0

    nxz, nyz, edge, low, high = call(
        kernel_a,
        "start",
        [field, field, (levels + 1, ROWS, lanes), (2,) + plane, (2,) + plane],
        pressure,
        wind_x,
        wind_y,
        jacobian,
    )
    edge = exchange_rows(edge)
    low, high = exchange_lanes(low, high)
    static_edges = (edge, low, high)
    rate, inv, prod, gain, stat = call(
        kernel_f, "factor", [field, field, field, field, (5,) + plane], stiffness
    )
    stats = gather_levels(stat)
    for substep in range(SUBSTEPS):
        new_x, new_y, star, value, face = call(
            kernel_b,
            "sweep",
            [field, field, field, field, (4,) + plane],
            pressure,
            nxz,
            nyz,
            wind_z,
            jacobian,
            slope_x,
            slope_y,
            rate,
            inv,
            gain,
            edge,
            low,
            high,
            *static_edges,
        )
        faces = gather_levels(face)
        if substep < SUBSTEPS - 1:
            wind_z, pressure, nxz, nyz, edge, low, high = call(
                functools.partial(kernel_c, blocks),
                "finish",
                [field, field, field, field, (levels, ROWS, lanes), (1,) + plane, (1,) + plane],
                value,
                prod,
                inv,
                star,
                new_x,
                new_y,
                jacobian,
                *faces,
                *stats,
            )
            edge = exchange_rows(edge)
            low, high = exchange_lanes(low, high)
        else:
            wind_z, pressure = call(
                functools.partial(kernel_d, blocks),
                "last",
                [field, field],
                value,
                prod,
                inv,
                star,
                *faces,
                *stats,
            )
    return new_x, new_y, wind_z, pressure


def solution(mesh):
    field = P("lev", "gx", "gy")
    column = P("gx", "gy")
    return jax.shard_map(
        local,
        mesh=mesh,
        in_specs=(field,) * 4 + (column,) * 3 + (field,),
        out_specs=(field,) * 4,
        check_vma=False,
    )
```

profile of v0, /device:TPU:0, one launch (start us, length us, event | category | flops | bytes accessed | tf_op | source)
XLA Modules:
  0.0 69.4 jit_solution(18214938061603758886)
XLA Ops:
  0.6 1.0 %copy-done = f32[32,32,128]{2,1,0:T(8,128)S(1)} copy-done((f32[32,32,128]{2,1,0:T(8,128)S(1)}, f32[32,32,128]{2,1,0:T(8,128)}, u32[]{:S(2)}) %copy-start) | copy-done | bytes 524312
  1.7 1.0 %copy-done.2 = f32[32,32,128]{2,1,0:T(8,128)S(1)} copy-done((f32[32,32,128]{2,1,0:T(8,128)S(1)}, f32[32,32,128]{2,1,0:T(8,128)}, u32[]{:S(2)}) %copy-start.2) | copy-done | bytes 524312
  2.7 1.0 %copy-done.3 = f32[32,32,128]{2,1,0:T(8,128)S(1)} copy-done((f32[32,32,128]{2,1,0:T(8,128)S(1)}, f32[32,32,128]{2,1,0:T(8,128)}, u32[]{:S(2)}) %copy-start.3) | copy-done | bytes 524312
  4.5 9.8 %start.1 = (f32[32,32,128]{2,1,0:T(8,128)S(1)}, f32[32,32,128]{2,1,0:T(8,128)S(1)}, f32[33,8,128]{2,1,0:T(8,128)S(1)}, f32[2,32,128]{2,1,0:T(8,128)S(1)}, f32[2,32,128]{2,1,0:T(8,128)S(1)}) custom-call(f32[32,32,128]{2,1,0:T(8,128)S(1)} %copy-done, f32[32,32,128]{2,1,0:T(8,128)S(1)} %copy-done.2, f32[32,32,128]{2,1,0:T(8,128)S(1)} %copy-done.3, ...), custom_call_target="tpu_custom_call" | custom-call | flops 5677056 | bytes 2838528 | tf_op jit(solution)/shard_map/start/pallas_call | solution.py:514
  14.3 3.0 %collective-permute-start = (f32[33,8,128]{2,1,0:T(8,128)S(1)}, f32[33,8,128]{2,1,0:T(8,128)S(1)}, u32[]{:S(2)}, u32[]{:S(2)}) collective-permute-start(f32[33,8,128]{2,1,0:T(8,128)S(1)} %get-tuple-element.38), channel_id=1, source_target_pairs={{0,16},{16,0},{1,17},{17,1},{2,18},{18,2},{3,19},{19,3},{4,20},{20... | collective-permute-start | bytes 405512 | tf_op jit(solution)/shard_map/ppermute | solution.py:529
  17.3 0.7 %factor.1 = (f32[32,32,128]{2,1,0:T(8,128)S(1)}, f32[32,32,128]{2,1,0:T(8,128)S(1)}, f32[32,32,128]{2,1,0:T(8,128)S(1)}, f32[32,32,128]{2,1,0:T(8,128)S(1)}, f32[5,32,128]{2,1,0:T(8,128)S(1)}) custom-call(f32[32,32,128]{2,1,0:T(8,128)S(1)} %copy-done.4), custom_call_target="tpu_custom_call" | custom-call | flops 5406720 | bytes 2703360 | tf_op jit(solution)/shard_map/factor/pallas_call | solution.py:514
  18.8 3.6 %collective-permute-start.1 = (f32[2,32,128]{2,1,0:T(8,128)S(1)}, f32[2,32,128]{2,1,0:T(8,128)S(1)}, u32[]{:S(2)}, u32[]{:S(2)}) collective-permute-start(f32[2,32,128]{2,1,0:T(8,128)S(1)} %get-tuple-element.39), channel_id=1, source_target_pairs={{0,12},{4,0},{8,4},{12,8},{1,13},{5,1},{9,5},{13,9},{2,14},{6,2},{... | collective-permute-start | bytes 98312 | tf_op jit(solution)/shard_map/ppermute | solution.py:529
  22.4 0.9 %collective-permute-start.7 = (f32[5,32,128]{2,1,0:T(8,128)S(1)}, f32[5,32,128]{2,1,0:T(8,128)S(1)}, u32[]{:S(2)}, u32[]{:S(2)}) collective-permute-start(f32[5,32,128]{2,1,0:T(8,128)S(1)} %get-tuple-element.47.refs_4_), channel_id=1, source_target_pairs={{0,2},{1,3},{2,0},{3,1},{4,6},{5,7},{6,4},{7,5},{8,10},{9,11},{10,... | collective-permute-start | bytes 245768 | tf_op jit(solution)/shard_map/ppermute | solution.py:529
  23.3 0.9 %collective-permute-done.1.low_ref.slow_ref = f32[2,32,128]{2,1,0:T(8,128)S(1)} collective-permute-done((f32[2,32,128]{2,1,0:T(8,128)S(1)}, f32[2,32,128]{2,1,0:T(8,128)S(1)}, u32[]{:S(2)}, u32[]{:S(2)}) %collective-permute-start.1) | collective-permute-done | bytes 32800 | tf_op jit(solution)/shard_map/ppermute | solution.py:529
  24.2 3.9 %collective-permute-done.2.high_ref.shigh_ref = f32[2,32,128]{2,1,0:T(8,128)S(1)} collective-permute-done((f32[2,32,128]{2,1,0:T(8,128)S(1)}, f32[2,32,128]{2,1,0:T(8,128)S(1)}, u32[]{:S(2)}, u32[]{:S(2)}) %collective-permute-start.2) | collective-permute-done | bytes 32800 | tf_op jit(solution)/shard_map/ppermute | solution.py:529
  28.2 5.7 %sweep.2 = (f32[32,32,128]{2,1,0:T(8,128)S(1)}, f32[32,32,128]{2,1,0:T(8,128)S(1)}, f32[32,32,128]{2,1,0:T(8,128)S(1)}, f32[32,32,128]{2,1,0:T(8,128)S(1)}, f32[4,32,128]{2,1,0:T(8,128)S(1)}) custom-call(f32[32,32,128]{2,1,0:T(8,128)S(1)} %copy-done.1, f32[32,32,128]{2,1,0:T(8,128)S(1)} %get-tuple-element.33.nxz_ref, ...), custom_call_target="tpu_custom_call" | custom-call | flops 12566528 | bytes 6283264 | tf_op jit(solution)/shard_map/sweep/pallas_call | solution.py:514
  34.0 1.4 %collective-permute-start.4 = (f32[4,32,128]{2,1,0:T(8,128)S(1)}, f32[4,32,128]{2,1,0:T(8,128)S(1)}, u32[]{:S(2)}, u32[]{:S(2)}) collective-permute-start(f32[4,32,128]{2,1,0:T(8,128)S(1)} %get-tuple-element.46.refs_0_), channel_id=1, source_target_pairs={{0,2},{1,3},{2,0},{3,1},{4,6},{5,7},{6,4},{7,5},{8,10},{9,11},{10,... | collective-permute-start | bytes 196616 | tf_op jit(solution)/shard_map/ppermute | solution.py:529
  35.9 2.5 %collective-permute-done.5.refs_3_ = f32[4,32,128]{2,1,0:T(8,128)S(1)} collective-permute-done((f32[4,32,128]{2,1,0:T(8,128)S(1)}, f32[4,32,128]{2,1,0:T(8,128)S(1)}, u32[]{:S(2)}, u32[]{:S(2)}) %collective-permute-start.5) | collective-permute-done | bytes 65568 | tf_op jit(solution)/shard_map/ppermute | solution.py:529
  38.4 1.4 %collective-permute-done.4.refs_2_ = f32[4,32,128]{2,1,0:T(8,128)S(1)} collective-permute-done((f32[4,32,128]{2,1,0:T(8,128)S(1)}, f32[4,32,128]{2,1,0:T(8,128)S(1)}, u32[]{:S(2)}, u32[]{:S(2)}) %collective-permute-start.4) | collective-permute-done | bytes 65568 | tf_op jit(solution)/shard_map/ppermute | solution.py:529
  39.8 10.0 %finish.1 = (f32[32,32,128]{2,1,0:T(8,128)S(1)}, f32[32,32,128]{2,1,0:T(8,128)S(1)}, f32[32,32,128]{2,1,0:T(8,128)S(1)}, f32[32,32,128]{2,1,0:T(8,128)S(1)}, f32...) custom-call(f32[32,32,128]{2,1,0:T(8,128)S(1)} %get-tuple-element.41.y_ref, ...), custom_call_target="tpu_custom_call" | custom-call | flops 12025856 | bytes 6012928 | tf_op jit(solution)/shard_map/finish/pallas_call | solution.py:514
  50.7 1.6 %collective-permute-start.11 = (f32[1,32,128]{2,1,0:T(8,128)S(1)}, f32[1,32,128]{2,1,0:T(8,128)S(1)}, u32[]{:S(2)}, u32[]{:S(2)}) collective-permute-start(f32[1,32,128]{2,1,0:T(8,128)S(1)} %get-tuple-element.54), channel_id=1, source_target_pairs={{0,4},{4,8},{8,12},{12,0},{1,5},{5,9},{9,13},{13,1},{2,6},{6,10},{... | collective-permute-start | bytes 49160 | tf_op jit(solution)/shard_map/ppermute | solution.py:529
  52.3 1.7 %collective-permute-done.10.low_ref = f32[1,32,128]{2,1,0:T(8,128)S(1)} collective-permute-done((f32[1,32,128]{2,1,0:T(8,128)S(1)}, f32[1,32,128]{2,1,0:T(8,128)S(1)}, u32[]{:S(2)}, u32[]{:S(2)}) %collective-permute-start.10) | collective-permute-done | bytes 16416 | tf_op jit(solution)/shard_map/ppermute | solution.py:529
  54.1 2.2 %collective-permute-done.11.high_ref = f32[1,32,128]{2,1,0:T(8,128)S(1)} collective-permute-done((f32[1,32,128]{2,1,0:T(8,128)S(1)}, f32[1,32,128]{2,1,0:T(8,128)S(1)}, u32[]{:S(2)}, u32[]{:S(2)}) %collective-permute-start.11) | collective-permute-done | bytes 16416 | tf_op jit(solution)/shard_map/ppermute | solution.py:529
  56.3 6.7 %sweep.3 = (f32[32,32,128]{2,1,0:T(8,128)}, f32[32,32,128]{2,1,0:T(8,128)}, f32[32,32,128]{2,1,0:T(8,128)S(1)}, f32[32,32,128]{2,1,0:T(8,128)S(1)}, f32[4,32,128]{2,1,0:T(8,128)S(1)}) custom-call(f32[32,32,128]{2,1,0:T(8,128)S(1)} %get-tuple-element.48.p_ref, f32[32,32,128]{2,1,0:T(8,128)S(1)} %get-tuple-element.49.nxz_ref, ...), custom_call_target="tpu_custom_call" | custom-call | flops 12492800 | bytes 6246400 | tf_op jit(solution)/shard_map/sweep/pallas_call | solution.py:514
  63.0 0.8 %collective-permute-start.13 = (f32[4,32,128]{2,1,0:T(8,128)S(1)}, f32[4,32,128]{2,1,0:T(8,128)S(1)}, u32[]{:S(2)}, u32[]{:S(2)}) collective-permute-start(f32[4,32,128]{2,1,0:T(8,128)S(1)} %get-tuple-element.59.refs_0_), channel_id=1, source_target_pairs={{0,2},{1,3},{2,0},{3,1},{4,6},{5,7},{6,4},{7,5},{8,10},{9,11},{10,... | collective-permute-start | bytes 196616 | tf_op jit(solution)/shard_map/ppermute | solution.py:529
  63.7 1.1 %collective-permute-start.12 = (f32[4,32,128]{2,1,0:T(8,128)S(1)}, f32[4,32,128]{2,1,0:T(8,128)S(1)}, u32[]{:S(2)}, u32[]{:S(2)}) collective-permute-start(f32[4,32,128]{2,1,0:T(8,128)S(1)} %get-tuple-element.59.refs_0_), channel_id=1, source_target_pairs={{0,1},{1,0},{2,3},{3,2},{4,5},{5,4},{6,7},{7,6},{8,9},{9,8},{10,11... | collective-permute-start | bytes 196616 | tf_op jit(solution)/shard_map/ppermute | solution.py:529
  64.8 2.0 %collective-permute-done.14.refs_3_ = f32[4,32,128]{2,1,0:T(8,128)S(1)} collective-permute-done((f32[4,32,128]{2,1,0:T(8,128)S(1)}, f32[4,32,128]{2,1,0:T(8,128)S(1)}, u32[]{:S(2)}, u32[]{:S(2)}) %collective-permute-start.14) | collective-permute-done | bytes 65568 | tf_op jit(solution)/shard_map/ppermute | solution.py:529
  66.8 1.1 %collective-permute-done.13.refs_2_ = f32[4,32,128]{2,1,0:T(8,128)S(1)} collective-permute-done((f32[4,32,128]{2,1,0:T(8,128)S(1)}, f32[4,32,128]{2,1,0:T(8,128)S(1)}, u32[]{:S(2)}, u32[]{:S(2)}) %collective-permute-start.13) | collective-permute-done | bytes 65568 | tf_op jit(solution)/shard_map/ppermute | solution.py:529
  67.9 1.5 %last.1 = (f32[32,32,128]{2,1,0:T(8,128)}, f32[32,32,128]{2,1,0:T(8,128)}) custom-call(f32[32,32,128]{2,1,0:T(8,128)S(1)} %get-tuple-element.57.y_ref, f32[32,32,128]{2,1,0:T(8,128)S(1)} %get-tuple-element.42.q_ref, f32[32,32,128]{2,1,0:T(8,128)S(1)} %get-tuple-element.36.i_ref, f32[32,32,128]{2,1,0:T(8,128)S(1)} %get-tuple-element.58.ps_ref, ...), custom_call_target="tpu_custom_call" | custom-call | flops 7471104 | bytes 3735552 | tf_op jit(solution)/shard_map/last/pallas_call | solution.py:514
  (30 shorter events, 3.0 us)
Async XLA Ops:
  0.6 1.0 %copy-start = (f32[32,32,128]{2,1,0:T(8,128)S(1)}, f32[32,32,128]{2,1,0:T(8,128)}, u32[]{:S(2)}) copy-start(f32[32,32,128]{2,1,0:T(8,128)} %p_ref.3) | copy-start | bytes 1572868
  1.7 1.0 %copy-start.2 = (f32[32,32,128]{2,1,0:T(8,128)S(1)}, f32[32,32,128]{2,1,0:T(8,128)}, u32[]{:S(2)}) copy-start(f32[32,32,128]{2,1,0:T(8,128)} %wx_ref.1) | copy-start | bytes 1572868
  2.7 1.0 %copy-start.3 = (f32[32,32,128]{2,1,0:T(8,128)S(1)}, f32[32,32,128]{2,1,0:T(8,128)}, u32[]{:S(2)}) copy-start(f32[32,32,128]{2,1,0:T(8,128)} %wy_ref.1) | copy-start | bytes 1572868
  3.8 0.7 %copy-start.6 = (f32[32,128]{1,0:T(8,128)S(1)}, f32[32,128]{1,0:T(8,128)}, u32[]{:S(2)}) copy-start(f32[32,128]{1,0:T(8,128)} %jac_ref.7) | copy-start | bytes 49156
  4.5 12.8 %copy-start.4 = (f32[32,32,128]{2,1,0:T(8,128)S(1)}, f32[32,32,128]{2,1,0:T(8,128)}, u32[]{:S(2)}) copy-start(f32[32,32,128]{2,1,0:T(8,128)} %s_ref.1) | copy-start | bytes 1572868
  4.5 23.7 %copy-start.5 = (f32[32,32,128]{2,1,0:T(8,128)S(1)}, f32[32,32,128]{2,1,0:T(8,128)}, u32[]{:S(2)}) copy-start(f32[32,32,128]{2,1,0:T(8,128)} %wz_ref.1) | copy-start | bytes 1572868
  4.5 23.7 %copy-start.8 = (f32[32,128]{1,0:T(8,128)S(1)}, f32[32,128]{1,0:T(8,128)}, u32[]{:S(2)}) copy-start(f32[32,128]{1,0:T(8,128)} %sy_ref.3) | copy-start | bytes 49156
  14.3 13.9 %copy-start.1 = (f32[32,32,128]{2,1,0:T(8,128)S(1)}, f32[32,32,128]{2,1,0:T(8,128)}, u32[]{:S(2)}) copy-start(f32[32,32,128]{2,1,0:T(8,128)} %p_ref.3) | copy-start | bytes 1572868
  14.3 13.9 %collective-permute-start = (f32[33,8,128]{2,1,0:T(8,128)S(1)}, f32[33,8,128]{2,1,0:T(8,128)S(1)}, u32[]{:S(2)}, u32[]{:S(2)}) collective-permute-start(f32[33,8,128]{2,1,0:T(8,128)S(1)} %get-tuple-element.38), channel_id=1, source_target_pairs={{0,16},{16,0},{1,17},{17,1},{2,18},{18,2},{3,19},{19,3},{4,20},{20... | collective-permute-start | bytes 405512 | tf_op jit(solution)/shard_map/ppermute | solution.py:529
  17.3 10.9 %copy-start.7 = (f32[32,128]{1,0:T(8,128)S(1)}, f32[32,128]{1,0:T(8,128)}, u32[]{:S(2)}) copy-start(f32[32,128]{1,0:T(8,128)} %sx_ref.3) | copy-start | bytes 49156
  18.1 17.4 %collective-permute-start.8 = (f32[5,32,128]{2,1,0:T(8,128)S(1)}, f32[5,32,128]{2,1,0:T(8,128)S(1)}, u32[]{:S(2)}, u32[]{:S(2)}) collective-permute-start(f32[5,32,128]{2,1,0:T(8,128)S(1)} %get-tuple-element.47.refs_4_), channel_id=1, source_target_pairs={{0,3},{1,2},{2,1},{3,0},{4,7},{5,6},{6,5},{7,4},{8,11},{9,10},{10,... | collective-permute-start | bytes 245768 | tf_op jit(solution)/shard_map/ppermute | solution.py:529
  18.8 5.4 %collective-permute-start.1 = (f32[2,32,128]{2,1,0:T(8,128)S(1)}, f32[2,32,128]{2,1,0:T(8,128)S(1)}, u32[]{:S(2)}, u32[]{:S(2)}) collective-permute-start(f32[2,32,128]{2,1,0:T(8,128)S(1)} %get-tuple-element.39), channel_id=1, source_target_pairs={{0,12},{4,0},{8,4},{12,8},{1,13},{5,1},{9,5},{13,9},{2,14},{6,2},{... | collective-permute-start | bytes 98312 | tf_op jit(solution)/shard_map/ppermute | solution.py:529
  22.4 5.8 %collective-permute-start.2 = (f32[2,32,128]{2,1,0:T(8,128)S(1)}, f32[2,32,128]{2,1,0:T(8,128)S(1)}, u32[]{:S(2)}, u32[]{:S(2)}) collective-permute-start(f32[2,32,128]{2,1,0:T(8,128)S(1)} %get-tuple-element.40), channel_id=1, source_target_pairs={{0,4},{4,8},{8,12},{12,0},{1,5},{5,9},{9,13},{13,1},{2,6},{6,10},{... | collective-permute-start | bytes 98312 | tf_op jit(solution)/shard_map/ppermute | solution.py:529
  22.4 13.5 %collective-permute-start.7 = (f32[5,32,128]{2,1,0:T(8,128)S(1)}, f32[5,32,128]{2,1,0:T(8,128)S(1)}, u32[]{:S(2)}, u32[]{:S(2)}) collective-permute-start(f32[5,32,128]{2,1,0:T(8,128)S(1)} %get-tuple-element.47.refs_4_), channel_id=1, source_target_pairs={{0,2},{1,3},{2,0},{3,1},{4,6},{5,7},{6,4},{7,5},{8,10},{9,11},{10,... | collective-permute-start | bytes 245768 | tf_op jit(solution)/shard_map/ppermute | solution.py:529
  24.2 11.7 %collective-permute-start.6 = (f32[5,32,128]{2,1,0:T(8,128)S(1)}, f32[5,32,128]{2,1,0:T(8,128)S(1)}, u32[]{:S(2)}, u32[]{:S(2)}) collective-permute-start(f32[5,32,128]{2,1,0:T(8,128)S(1)} %get-tuple-element.47.refs_4_), channel_id=1, source_target_pairs={{0,1},{1,0},{2,3},{3,2},{4,5},{5,4},{6,7},{7,6},{8,9},{9,8},{10,11... | collective-permute-start | bytes 245768 | tf_op jit(solution)/shard_map/ppermute | solution.py:529
  33.9 4.5 %collective-permute-start.5 = (f32[4,32,128]{2,1,0:T(8,128)S(1)}, f32[4,32,128]{2,1,0:T(8,128)S(1)}, u32[]{:S(2)}, u32[]{:S(2)}) collective-permute-start(f32[4,32,128]{2,1,0:T(8,128)S(1)} %get-tuple-element.46.refs_0_), channel_id=1, source_target_pairs={{0,3},{1,2},{2,1},{3,0},{4,7},{5,6},{6,5},{7,4},{8,11},{9,10},{10,... | collective-permute-start | bytes 196616 | tf_op jit(solution)/shard_map/ppermute | solution.py:529
  34.0 5.8 %collective-permute-start.4 = (f32[4,32,128]{2,1,0:T(8,128)S(1)}, f32[4,32,128]{2,1,0:T(8,128)S(1)}, u32[]{:S(2)}, u32[]{:S(2)}) collective-permute-start(f32[4,32,128]{2,1,0:T(8,128)S(1)} %get-tuple-element.46.refs_0_), channel_id=1, source_target_pairs={{0,2},{1,3},{2,0},{3,1},{4,6},{5,7},{6,4},{7,5},{8,10},{9,11},{10,... | collective-permute-start | bytes 196616 | tf_op jit(solution)/shard_map/ppermute | solution.py:529
  35.5 4.3 %collective-permute-start.3 = (f32[4,32,128]{2,1,0:T(8,128)S(1)}, f32[4,32,128]{2,1,0:T(8,128)S(1)}, u32[]{:S(2)}, u32[]{:S(2)}) collective-permute-start(f32[4,32,128]{2,1,0:T(8,128)S(1)} %get-tuple-element.46.refs_0_), channel_id=1, source_target_pairs={{0,1},{1,0},{2,3},{3,2},{4,5},{5,4},{6,7},{7,6},{8,9},{9,8},{10,11... | collective-permute-start | bytes 196616 | tf_op jit(solution)/shard_map/ppermute | solution.py:529
  49.8 6.5 %collective-permute-start.9 = (f32[32,8,128]{2,1,0:T(8,128)S(1)}, f32[32,8,128]{2,1,0:T(8,128)S(1)}, u32[]{:S(2)}, u32[]{:S(2)}) collective-permute-start(f32[32,8,128]{2,1,0:T(8,128)S(1)} %get-tuple-element.52), channel_id=1, source_target_pairs={{0,16},{16,0},{1,17},{17,1},{2,18},{18,2},{3,19},{19,3},{4,20},{20... | collective-permute-start | bytes 393224 | tf_op jit(solution)/shard_map/ppermute | solution.py:529
  50.3 3.7 %collective-permute-start.10 = (f32[1,32,128]{2,1,0:T(8,128)S(1)}, f32[1,32,128]{2,1,0:T(8,128)S(1)}, u32[]{:S(2)}, u32[]{:S(2)}) collective-permute-start(f32[1,32,128]{2,1,0:T(8,128)S(1)} %get-tuple-element.53), channel_id=1, source_target_pairs={{0,12},{4,0},{8,4},{12,8},{1,13},{5,1},{9,5},{13,9},{2,14},{6,2},{... | collective-permute-start | bytes 49160 | tf_op jit(solution)/shard_map/ppermute | solution.py:529
  50.7 5.5 %collective-permute-start.11 = (f32[1,32,128]{2,1,0:T(8,128)S(1)}, f32[1,32,128]{2,1,0:T(8,128)S(1)}, u32[]{:S(2)}, u32[]{:S(2)}) collective-permute-start(f32[1,32,128]{2,1,0:T(8,128)S(1)} %get-tuple-element.54), channel_id=1, source_target_pairs={{0,4},{4,8},{8,12},{12,0},{1,5},{5,9},{9,13},{13,1},{2,6},{6,10},{... | collective-permute-start | bytes 49160 | tf_op jit(solution)/shard_map/ppermute | solution.py:529
  63.0 3.8 %collective-permute-start.14 = (f32[4,32,128]{2,1,0:T(8,128)S(1)}, f32[4,32,128]{2,1,0:T(8,128)S(1)}, u32[]{:S(2)}, u32[]{:S(2)}) collective-permute-start(f32[4,32,128]{2,1,0:T(8,128)S(1)} %get-tuple-element.59.refs_0_), channel_id=1, source_target_pairs={{0,3},{1,2},{2,1},{3,0},{4,7},{5,6},{6,5},{7,4},{8,11},{9,10},{10,... | collective-permute-start | bytes 196616 | tf_op jit(solution)/shard_map/ppermute | solution.py:529
  63.0 4.9 %collective-permute-start.13 = (f32[4,32,128]{2,1,0:T(8,128)S(1)}, f32[4,32,128]{2,1,0:T(8,128)S(1)}, u32[]{:S(2)}, u32[]{:S(2)}) collective-permute-start(f32[4,32,128]{2,1,0:T(8,128)S(1)} %get-tuple-element.59.refs_0_), channel_id=1, source_target_pairs={{0,2},{1,3},{2,0},{3,1},{4,6},{5,7},{6,4},{7,5},{8,10},{9,11},{10,... | collective-permute-start | bytes 196616 | tf_op jit(solution)/shard_map/ppermute | solution.py:529
  63.7 4.2 %collective-permute-start.12 = (f32[4,32,128]{2,1,0:T(8,128)S(1)}, f32[4,32,128]{2,1,0:T(8,128)S(1)}, u32[]{:S(2)}, u32[]{:S(2)}) collective-permute-start(f32[4,32,128]{2,1,0:T(8,128)S(1)} %get-tuple-element.59.refs_0_), channel_id=1, source_target_pairs={{0,1},{1,0},{2,3},{3,2},{4,5},{5,4},{6,7},{7,6},{8,9},{9,8},{10,11... | collective-permute-start | bytes 196616 | tf_op jit(solution)/shard_map/ppermute | solution.py:529
where the time goes:
time: 69.7 us; the launch traced here: 69.4 us
  Pallas kernels  34.4 us (49%)
  waiting for transfers between devices  15.7 us (23%)
  starting transfers between devices  14.7 us (21%)
  local copies, waits for them, and re-layouts  3.86 us (6%)
  between operations  0.71 us (1%)
    pallas_call x6, Pallas kernels, call(): pl.pallas_call(kernel, out_shape=[jax.ShapeDtypeStruct(s, jnp.float32) fo...  34.4 us
    ppermute x15, waiting for transfers between devices, swap(): return lax.ppermute(value, axis, [(i, partner(i)) for i in range(count)])  15.7 us
    ppermute x15, starting transfers between devices, swap(): return lax.ppermute(value, axis, [(i, partner(i)) for i in range(count)])  14.7 us
    unnamed x18, local copies, waits for them, and re-layouts  3.86 us
  transfers between devices with their start and end apart: 15, of which 8 were waited for; matrix products, arithmetic and copies ran while one was open for 0% of the time, Pallas kernels for 9%

commit v1 on v0

v1 whole, which is shorter than its diff:
```python
import functools

import jax
import jax.numpy as jnp
from jax import lax
from jax.experimental import pallas as pl
from jax.experimental.pallas import tpu as pltpu
from jax.sharding import PartitionSpec as P

SUBSTEPS = 2

grad_coef = 0.35
div_coef = 0.35
vert_coef = 0.25

CG = grad_coef / 12.0
CD = div_coef / 12.0
ROWS = 8
SLOT = 4
UNROLL = 4


def lane_index():
    return lax.broadcasted_iota(jnp.int32, (ROWS, 128), 1)


def row_index():
    return lax.broadcasted_iota(jnp.int32, (ROWS, 128), 0)


def only(mask, value):
    return jnp.where(mask, jnp.float32(value), jnp.float32(0.0))


def tiles_of(ref, level, count):
    return [ref[level, ROWS * t : ROWS * (t + 1), :] for t in range(count)]


def planes_of(ref, count):
    return [ref[ROWS * t : ROWS * (t + 1), :] for t in range(count)]


def put_tiles(ref, level, tiles):
    for t, tile in enumerate(tiles):
        ref[level, ROWS * t : ROWS * (t + 1), :] = tile


def put_planes(ref, tiles):
    for t, tile in enumerate(tiles):
        ref[ROWS * t : ROWS * (t + 1), :] = tile


class Edge:
    def __init__(self, place, axis, held):
        self.place, self.axis, self.held = place, axis, held
        self.size = place.shape[axis]

    def at(self, places):
        total = None
        for position, value in places.items():
            if position in self.held:
                term = only(self.place == position, value)
                total = term if total is None else total + term
        return total

    def shifted(self, field, by):
        return field if by == 0 else pltpu.roll(field, (-by) % self.size, self.axis)

    def mix(self, field, table):
        total = None
        for by, places in table.items():
            weight = self.at(places)
            if weight is not None:
                term = weight * self.shifted(field, by)
                total = term if total is None else total + term
        return total

    def payload(self, pres, wind, jac):
        partial = self.mix(
            pres,
            {
                1: {0: 8.0, 1: 8.0, 6: 8.0},
                2: {0: -1.0, 1: -1.0},
                -1: {1: -8.0, 6: -8.0, 7: -8.0},
                -2: {6: 1.0, 7: 1.0},
            },
        )
        flux = jac * (wind - CG * partial)
        outer = self.mix(pres, {0: {0: 1.0, 1: 1.0, 6: 1.0, 7: 1.0}})
        return outer + self.mix(flux, {-2: {2: 1.0, 3: 1.0}, 2: {4: 1.0, 5: 1.0}})

    def correct(self, delta, pres, jac, delta_jac):
        grad = self.mix(
            delta, {2: {0: 1.0, 1: 1.0}, 3: {0: -8.0}, -2: {6: -1.0, 7: -1.0}, -3: {7: 8.0}}
        )
        wind = CG * grad
        own = -(jac * wind)
        far = self.mix(delta, {0: {0: 1.0, 1: 1.0, 6: 1.0, 7: 1.0}}) + CG * delta_jac * self.mix(
            pres, {0: {0: 1.0, 1: 1.0, 6: -1.0, 7: -1.0}, -1: {1: -8.0}, 1: {6: 8.0}}
        )
        spread = (
            self.mix(far, {0: {0: 1.0, 1: 1.0, 6: -1.0, 7: -1.0}})
            + self.mix(far - own, {1: {0: -8.0}, -1: {7: 8.0}})
            + self.mix(
                own,
                {
                    -1: {1: -8.0, 2: -8.0},
                    -2: {2: 1.0, 3: 1.0},
                    1: {5: 8.0, 6: 8.0},
                    2: {4: -1.0, 5: -1.0},
                },
            )
        )
        return wind, CD * spread / jac


LOW, HIGH = (0, 1, 2, 3), (4, 5, 6, 7)


def row_edge():
    return Edge(row_index(), 0, LOW + HIGH)


def lane_edge(held):
    return Edge((lane_index() & 3) + held[0], 1, held)


def both_ends(tiles):
    return jnp.where(row_index() < 4, tiles[0], tiles[-1])


def spread_slots(tile, low):
    lane = lane_index()
    if low:
        out = jnp.where(lane < SLOT, tile, 0.0)
    else:
        out = pltpu.roll(jnp.where(lane >= 128 - SLOT, tile, 0.0), SLOT, 1)
    by = SLOT
    while by < 128:
        out = out + pltpu.roll(out, by, 1)
        by *= 2
    return out


class Packer:
    def __init__(self, count):
        self.slot = lax.shift_right_logical(lane_index(), 2)
        self.start = [jnp.zeros((ROWS, 128), jnp.float32)] * (2 * count)
        self.count = count

    def add(self, level, tiles, state):
        before = lax.rem(level + 31, 32)
        rolled = [pltpu.roll(tile, SLOT * level, 1) for tile in tiles]
        low = [jnp.where(self.slot == level, r, s) for r, s in zip(rolled, state)]
        high = [jnp.where(self.slot == before, r, s) for r, s in zip(rolled, state[self.count :])]
        return low + high

    def done(self, state):
        return state[: self.count], [pltpu.roll(s, SLOT, 1) for s in state[self.count :]]


class Closed:
    def __init__(self):
        self.row = row_index()

    def along_y(self, tile):
        pair = tile - pltpu.roll(tile, 126, 1)
        return (pltpu.roll(pair, 2, 1) + pair) - 8.0 * pltpu.roll(pair, 1, 1)

    def moved(self, tiles, by):
        count = len(tiles)
        rolled = [pltpu.roll(tile, by % ROWS, 0) for tile in tiles]
        if by > 0:
            return [jnp.where(self.row < by, rolled[t - 1], rolled[t]) for t in range(count)]
        return [
            jnp.where(self.row >= ROWS + by, rolled[(t + 1) % count], rolled[t])
            for t in range(count)
        ]

    def along_x(self, tiles):
        pair = [f - m for f, m in zip(tiles, self.moved(tiles, -2))]
        return [
            (two + here) - 8.0 * one
            for two, here, one in zip(self.moved(pair, 2), pair, self.moved(pair, 1))
        ]


def lane_payload(pres, wind, jac):
    low, high = lane_edge(LOW), lane_edge(HIGH)
    down = [
        low.payload(p, w, spread_slots(j, True)) for p, w, j in zip(pres[0], wind[0], jac)
    ]
    up = [
        high.payload(p, w, spread_slots(j, False)) for p, w, j in zip(pres[1], wind[1], jac)
    ]
    return down, up


def pack_levels(ref, count, levels):
    packer = Packer(count)

    def step(level, state):
        return packer.add(level, tiles_of(ref, level, count), state)

    return packer.done(lax.fori_loop(0, levels, step, packer.start, unroll=UNROLL))


def kernel_a(p_ref, wx_ref, wy_ref, jac_ref, rows_ref, down_ref, up_ref, pp_ref):
    levels, rows, _ = p_ref.shape
    count = rows // ROWS
    jac = planes_of(jac_ref, count)
    ends = both_ends(jac)
    edge = row_edge()

    def step(level, state):
        rows_ref[level] = edge.payload(
            both_ends(tiles_of(p_ref, level, count)),
            both_ends(tiles_of(wx_ref, level, count)),
            ends,
        )
        return state

    lax.fori_loop(0, levels, step, 0, unroll=UNROLL)
    rows_ref[levels] = ends
    pres = pack_levels(p_ref, count, levels)
    wind = pack_levels(wy_ref, count, levels)
    down, up = lane_payload(pres, wind, jac)
    put_tiles(down_ref, 0, down)
    put_tiles(up_ref, 0, up)
    put_tiles(down_ref, 1, [spread_slots(j, True) for j in jac])
    put_tiles(up_ref, 1, [spread_slots(j, False) for j in jac])
    put_tiles(pp_ref, 0, pres[0])
    put_tiles(pp_ref, 1, pres[1])


def kernel_n(wy_ref, pw_ref):
    levels, rows, _ = wy_ref.shape
    count = rows // ROWS
    wind = pack_levels(wy_ref, count, levels)
    put_tiles(pw_ref, 0, wind[0])
    put_tiles(pw_ref, 1, wind[1])


def kernel_m(p_ref, wx_ref, wy_ref, jac_ref, nx_ref, ny_ref, ps_ref):
    levels, rows, _ = p_ref.shape
    count = rows // ROWS
    jac = planes_of(jac_ref, count)
    inv_jac = [CD / j for j in jac]
    closed = Closed()

    def step(level, state):
        pres = tiles_of(p_ref, level, count)
        wind_x = tiles_of(wx_ref, level, count)
        wind_y = tiles_of(wy_ref, level, count)
        new_x = [w - CG * d for w, d in zip(wind_x, closed.along_x(pres))]
        new_y = [w - CG * closed.along_y(p) for w, p in zip(wind_y, pres)]
        put_tiles(nx_ref, level, new_x)
        put_tiles(ny_ref, level, new_y)
        spread_x = closed.along_x([j * n for j, n in zip(jac, new_x)])
        spread_y = [closed.along_y(j * n) for j, n in zip(jac, new_y)]
        put_tiles(
            ps_ref,
            level,
            [p - i * (x + y) for p, i, x, y in zip(pres, inv_jac, spread_x, spread_y)],
        )
        return state

    lax.fori_loop(0, levels, step, 0, unroll=UNROLL)


def kernel_b(
    p_ref,
    nxc_ref,
    nyc_ref,
    psc_ref,
    wz_ref,
    jac_ref,
    sx_ref,
    sy_ref,
    r_ref,
    i_ref,
    v_ref,
    pp_ref,
    rows_ref,
    down_ref,
    up_ref,
    got_rows_ref,
    got_down_ref,
    got_up_ref,
    srows_ref,
    sdown_ref,
    sup_ref,
    got_srows_ref,
    got_sdown_ref,
    got_sup_ref,
    nx_ref,
    ny_ref,
    ps_ref,
    y_ref,
    face_ref,
):
    levels, rows, _ = p_ref.shape
    count = rows // ROWS
    last = count - 1
    lane, row = lane_index(), row_index()
    low_edge, high_edge, edge = lane_edge(LOW), lane_edge(HIGH), row_edge()
    wind_fix, low_fix, high_fix = [], [], []
    for t in range(count):
        part = slice(ROWS * t, ROWS * (t + 1))
        jac_low, jac_high = sdown_ref[1, part, :], sup_ref[1, part, :]
        low_wind, low_star = low_edge.correct(
            got_up_ref[0, part, :] - up_ref[0, part, :],
            pp_ref[0, part, :],
            jac_low,
            low_edge.shifted(got_sup_ref[1, part, :] - jac_high, 2),
        )
        high_wind, high_star = high_edge.correct(
            got_down_ref[0, part, :] - down_ref[0, part, :],
            pp_ref[1, part, :],
            jac_high,
            high_edge.shifted(got_sdown_ref[1, part, :] - jac_low, -2),
        )
        wind_fix.append(low_wind + pltpu.roll(high_wind, 128 - SLOT, 1))
        low_fix.append(low_star)
        high_fix.append(pltpu.roll(high_star, 128 - SLOT, 1))
    ends = srows_ref[levels]
    change = got_srows_ref[levels] - ends
    ends_change = jnp.where(row < 4, edge.shifted(change, -2), edge.shifted(change, 2))
    outer = (lane < 2) | (lane >= 126)
    low_lanes, high_lanes = lane < SLOT, lane >= 128 - SLOT
    first_rows = row < 4

    def star(level):
        new_x = tiles_of(nxc_ref, level, count)
        new_y = tiles_of(nyc_ref, level, count)
        stars = tiles_of(psc_ref, level, count)
        wind, press = edge.correct(
            pltpu.roll(got_rows_ref[level] - rows_ref[level], 4, 0),
            jnp.where(first_rows, p_ref[level, :ROWS, :], p_ref[level, ROWS * last :, :]),
            ends,
            ends_change,
        )
        new_x[0] = new_x[0] - jnp.where(first_rows, wind, 0.0)
        new_x[last] = new_x[last] - jnp.where(first_rows, 0.0, wind)
        stars[0] = stars[0] - jnp.where(first_rows, press, 0.0)
        stars[last] = stars[last] - jnp.where(first_rows, 0.0, press)
        back = lax.rem(128 - SLOT * level, 128)
        forces = []
        for t in range(count):
            part = slice(ROWS * t, ROWS * (t + 1))
            new_y[t] = new_y[t] - jnp.where(outer, pltpu.roll(wind_fix[t], back, 1), 0.0)
            fix = jnp.where(
                low_lanes,
                pltpu.roll(low_fix[t], back, 1),
                jnp.where(high_lanes, pltpu.roll(high_fix[t], back, 1), 0.0),
            )
            stars[t] = stars[t] - fix
            forces.append(
                wz_ref[level, part, :]
                + sx_ref[part, :] * new_x[t]
                + sy_ref[part, :] * new_y[t]
            )
        put_tiles(nx_ref, level, new_x)
        put_tiles(ny_ref, level, new_y)
        put_tiles(ps_ref, level, stars)
        return stars, forces

    def sweep(level, below, above, force, value, first):
        rate = tiles_of(r_ref, level, count)
        inv = tiles_of(i_ref, level, count)
        gain = tiles_of(v_ref, level, count)
        values, firsts = [], []
        for t in range(count):
            rhs = rate[t] * (force[t] - vert_coef * (above[t] - below[t]))
            firsts.append(first[t] + gain[t] * rhs)
            values.append((rhs + value[t]) * inv[t])
        put_tiles(y_ref, level, values)
        return values, firsts

    zeros = [jnp.zeros((ROWS, 128), jnp.float32)] * count
    here, force = star(0)
    put_tiles(face_ref, 2, here)

    def step(level, carry):
        below, here, force, value, first = carry
        above, force_next = star(level)
        value, first = sweep(level - 1, below, above, force, value, first)
        return here, above, force_next, value, first

    below, here, force, value, first = lax.fori_loop(
        1, levels, step, (zeros, here, force, zeros, zeros), unroll=UNROLL
    )
    value, first = sweep(levels - 1, below, zeros, force, value, first)
    put_tiles(face_ref, 0, first)
    put_tiles(face_ref, 1, value)
    put_tiles(face_ref, 3, here)


def kernel_f(s_ref, r_ref, i_ref, q_ref, v_ref, stat_ref):
    levels, rows, _ = s_ref.shape

    def down(level, carry):
        excess, prod = carry
        rate = 1.0 / s_ref[level]
        excess = rate + excess
        inv = 1.0 / (1.0 + excess)
        prod = prod * inv
        r_ref[level] = rate
        i_ref[level] = inv
        q_ref[level] = prod
        return excess * inv, prod

    ones = jnp.ones((rows, 128), jnp.float32)
    lax.fori_loop(0, levels, down, (ones, ones))

    def up(step, value):
        level = levels - 1 - step
        value = q_ref[level] + i_ref[level] * value
        v_ref[level] = value
        return value

    first = lax.fori_loop(0, levels, up, jnp.zeros((rows, 128), jnp.float32))
    stat_ref[0] = first
    stat_ref[1] = q_ref[levels - 1]
    stat_ref[2] = i_ref[levels - 1]
    stat_ref[3] = r_ref[0]
    stat_ref[4] = r_ref[levels - 1]


def reduced(blocks, mine, face, stat):
    faces = [face(j) for j in range(blocks)]
    stats = [stat(j) for j in range(blocks)]
    up = [
        faces[j][1] + vert_coef * stats[j + 1][3] * faces[j][3] if j < blocks - 1 else None
        for j in range(blocks)
    ]
    down = [
        faces[j][0] - vert_coef * stats[j - 1][4] * faces[j][2] if j > 0 else None
        for j in range(blocks)
    ]
    base, slope = [up[0]], [stats[0][2]]
    scale, known = [None], [None]
    for j in range(1, blocks):
        near, link, far = stats[j][0], stats[j][1], stats[j][2]
        scale.append(1.0 / (1.0 - near * slope[j - 1]))
        known.append(scale[j] * (down[j] + near * base[j - 1]))
        if j < blocks - 1:
            base.append(up[j] + link * (base[j - 1] + slope[j - 1] * known[j]))
            slope.append(far + link * link * slope[j - 1] * scale[j])
    zero = jnp.zeros_like(faces[0][0])
    above = [None] * blocks + [zero]
    below = [zero] + [None] * blocks
    for j in range(blocks - 1, 0, -1):
        above[j] = known[j] + scale[j] * stats[j][1] * above[j + 1]
        below[j] = base[j - 1] + slope[j - 1] * above[j]
    lower, upper, under, over = zero, zero, zero, zero
    for j in range(blocks):
        here = mine == j
        if j > 0:
            lower = jnp.where(here, below[j], lower)
            under = jnp.where(
                here, below[j] - vert_coef * stats[j][3] * faces[j - 1][3], under
            )
        if j < blocks - 1:
            upper = jnp.where(here, above[j + 1], upper)
            over = jnp.where(
                here, above[j + 1] + vert_coef * stats[j][4] * faces[j + 1][2], over
            )
    return lower, upper, under, over


def boundary(blocks, mine, count, face_refs, stat_refs):
    def solve(t):
        part = slice(ROWS * t, ROWS * (t + 1))

        def read(refs, planes):
            own = [
                [ref[k, part, :] for k in range(planes)] for ref in refs
            ]

            def block(j):
                out = []
                for k in range(planes):
                    value = own[0][k]
                    for shift in range(1, blocks):
                        value = jnp.where(mine == (j ^ shift), own[shift][k], value)
                    out.append(value)
                return out

            return block

        return reduced(blocks, mine, read(face_refs, 4), read(stat_refs, 5))

    parts = [solve(t) for t in range(count)]
    return [[part[k] for part in parts] for k in range(4)]


def finish(blocks, count, levels, y_ref, q_ref, i_ref, ps_ref, x_ref, p_ref, face_refs, stat_refs, use):
    mine = lax.axis_index("lev")
    lower, upper, under, over = boundary(blocks, mine, count, face_refs, stat_refs)

    def solved(level, above):
        value = tiles_of(y_ref, level, count)
        prod = tiles_of(q_ref, level, count)
        inv = tiles_of(i_ref, level, count)
        out = [y + q * u + i * a for y, q, u, i, a in zip(value, prod, lower, inv, above)]
        put_tiles(x_ref, level, out)
        return out

    def pressed(level, above, below, state):
        star = tiles_of(ps_ref, level, count)
        pres = [s - vert_coef * (a - b) for s, a, b in zip(star, above, below)]
        put_tiles(p_ref, level, pres)
        return use(level, pres, state)

    def step(index, carry):
        above, here, state = carry
        level = levels - 2 - index
        below = solved(level, here)
        state = pressed(level + 1, above, below, state)
        return here, below, state

    top = solved(levels - 1, upper)
    zeros = [jnp.zeros((ROWS, 128), jnp.float32)] * count
    above, here, state = lax.fori_loop(0, levels - 1, step, (over, top, (zeros, zeros)))
    return pressed(0, above, under, state)


def finish(blocks, count, levels, y_ref, q_ref, i_ref, ps_ref, x_ref, p_ref, face_refs, stat_refs, use, state):
    mine = lax.axis_index("lev")
    lower, upper, under, over = boundary(blocks, mine, count, face_refs, stat_refs)

    def solved(level, above):
        value = tiles_of(y_ref, level, count)
        prod = tiles_of(q_ref, level, count)
        inv = tiles_of(i_ref, level, count)
        out = [(y + q * u) + i * a for y, q, u, i, a in zip(value, prod, lower, inv, above)]
        put_tiles(x_ref, level, out)
        return out

    def pressed(level, above, below, state):
        star = tiles_of(ps_ref, level, count)
        pres = [s - vert_coef * (a - b) for s, a, b in zip(star, above, below)]
        put_tiles(p_ref, level, pres)
        return use(level, pres, state)

    def step(index, carry):
        above, here, state = carry
        level = levels - 2 - index
        below = solved(level, here)
        state = pressed(level + 1, above, below, state)
        return here, below, state

    top = solved(levels - 1, upper)
    above, here, state = lax.fori_loop(0, levels - 1, step, (over, top, state), unroll=UNROLL)
    return pressed(0, above, under, state)


def kernel_c(blocks, y_ref, q_ref, i_ref, ps_ref, wx_ref, pw_ref, jac_ref, *refs):
    face_refs, stat_refs = refs[:blocks], refs[blocks : 2 * blocks]
    x_ref, p_ref, rows_ref, down_ref, up_ref, pp_ref = refs[2 * blocks :]
    levels, rows, _ = y_ref.shape
    count = rows // ROWS
    packer = Packer(count)
    edge = row_edge()
    ends = both_ends(planes_of(jac_ref, count))

    def use(level, pres, state):
        rows_ref[level] = edge.payload(
            both_ends(pres), both_ends(tiles_of(wx_ref, level, count)), ends
        )
        return packer.add(level, pres, state)

    state = finish(
        blocks,
        count,
        levels,
        y_ref,
        q_ref,
        i_ref,
        ps_ref,
        x_ref,
        p_ref,
        face_refs,
        stat_refs,
        use,
        packer.start,
    )
    pres = packer.done(state)
    wind = tiles_of(pw_ref, 0, count), tiles_of(pw_ref, 1, count)
    down, up = lane_payload(pres, wind, planes_of(jac_ref, count))
    put_tiles(down_ref, 0, down)
    put_tiles(up_ref, 0, up)
    put_tiles(pp_ref, 0, pres[0])
    put_tiles(pp_ref, 1, pres[1])


def kernel_d(blocks, y_ref, q_ref, i_ref, ps_ref, *refs):
    face_refs, stat_refs = refs[:blocks], refs[blocks : 2 * blocks]
    x_ref, p_ref = refs[2 * blocks :]
    levels, rows, _ = y_ref.shape
    finish(
        blocks,
        rows // ROWS,
        levels,
        y_ref,
        q_ref,
        i_ref,
        ps_ref,
        x_ref,
        p_ref,
        face_refs,
        stat_refs,
        lambda level, pres, state: state,
        0,
    )


def call(kernel, name, shapes, *args):
    space = pl.BlockSpec(memory_space=pltpu.VMEM)
    size = sum(a.size for a in args) + sum(functools.reduce(lambda a, b: a * b, s) for s in shapes)
    return pl.pallas_call(
        kernel,
        out_shape=[jax.ShapeDtypeStruct(s, jnp.float32) for s in shapes],
        in_specs=[space] * len(args),
        out_specs=[space] * len(shapes),
        compiler_params=pltpu.CompilerParams(vmem_limit_bytes=32 * 1024 * 1024),
        cost_estimate=pl.CostEstimate(
            flops=8 * size, bytes_accessed=4 * size, transcendentals=0
        ),
        name=name,
    )(*args)


def swap(value, axis, partner):
    count = lax.axis_size(axis)
    return lax.ppermute(value, axis, [(i, partner(i)) for i in range(count)])


def exchange_rows(rows):
    count = lax.axis_size("gx")
    if count == 2:
        return swap(rows, "gx", lambda i: 1 - i)
    down = swap(rows[:, : ROWS // 2], "gx", lambda i: (i - 1) % count)
    up = swap(rows[:, ROWS // 2 :], "gx", lambda i: (i + 1) % count)
    return jnp.concatenate([down, up], axis=1)


def exchange_lanes(down, up):
    count = lax.axis_size("gy")
    from_above = swap(down, "gy", lambda i: (i - 1) % count)
    from_below = swap(up, "gy", lambda i: (i + 1) % count)
    return from_above, from_below


def gather_levels(planes):
    count = lax.axis_size("lev")
    return [planes] + [
        swap(planes, "lev", lambda i, shift=shift: i ^ shift) for shift in range(1, count)
    ]


def local(wind_x, wind_y, wind_z, pressure, jacobian, slope_x, slope_y, stiffness):
    field = wind_x.shape
    levels, rows, lanes = field
    blocks = lax.axis_size("lev")
    plane = (rows, lanes)
    pair = (2,) + plane
    assert lanes == 128 and levels * SLOT == 128 and rows % ROWS == 0
    assert blocks & (blocks - 1) == 0

    edge, down, up, ends = call(
        kernel_a,
        "start",
        [(levels + 1, ROWS, lanes), pair, pair, pair],
        pressure,
        wind_x,
        wind_y,
        jacobian,
    )
    sent = (edge, down, up)
    got = (exchange_rows(edge),) + exchange_lanes(down, up)
    static_edges = sent + got
    rate, inv, prod, gain, stat = call(
        kernel_f, "factor", [field, field, field, field, (5,) + plane], stiffness
    )
    stats = gather_levels(stat)
    for substep in range(SUBSTEPS):
        closed = call(
            kernel_m, "interior", [field, field, field], pressure, wind_x, wind_y, jacobian
        )
        wind_x, wind_y, star, value, face = call(
            kernel_b,
            "sweep",
            [field, field, field, field, (4,) + plane],
            pressure,
            *closed,
            wind_z,
            jacobian,
            slope_x,
            slope_y,
            rate,
            inv,
            gain,
            ends,
            *sent,
            *got,
            *static_edges,
        )
        faces = gather_levels(face)
        if substep < SUBSTEPS - 1:
            (packed,) = call(kernel_n, "pack", [pair], wind_y)
            wind_z, pressure, edge, down, up, ends = call(
                functools.partial(kernel_c, blocks),
                "finish",
                [field, field, (levels, ROWS, lanes), (1,) + plane, (1,) + plane, pair],
                value,
                prod,
                inv,
                star,
                wind_x,
                packed,
                jacobian,
                *faces,
                *stats,
            )
            sent = (edge, down, up)
            got = (exchange_rows(edge),) + exchange_lanes(down, up)
        else:
            wind_z, pressure = call(
                functools.partial(kernel_d, blocks),
                "last",
                [field, field],
                value,
                prod,
                inv,
                star,
                *faces,
                *stats,
            )
    return wind_x, wind_y, wind_z, pressure


def solution(mesh):
    field = P("lev", "gx", "gy")
    column = P("gx", "gy")
    return jax.shard_map(
        local,
        mesh=mesh,
        in_specs=(field,) * 4 + (column,) * 3 + (field,),
        out_specs=(field,) * 4,
        check_vma=False,
    )
```

time: 69.7 us -> 47.3 us (0.68)
  Pallas kernels: 34.4 us -> 15.2 us
  waiting for transfers between devices: 15.7 us -> 11.5 us
  starting transfers between devices: 14.7 us -> 15.7 us
    pallas_call x6 -> x9, Pallas kernels: 34.4 us -> 15.2 us  [call(): pl.pallas_call(kernel, out_shape=[jax.ShapeDtypeStruct(s, jnp.float32) fo...]
    ppermute x15, waiting for transfers between devices: 15.7 us -> 11.5 us  [swap(): return lax.ppermute(value, axis, [(i, partner(i)) for i in range(count)])]
    ppermute x15, starting transfers between devices: 14.7 us -> 15.7 us  [swap(): return lax.ppermute(value, axis, [(i, partner(i)) for i in range(count)])]
    unnamed x18 -> x22, local copies, waits for them, and re-layouts: 3.86 us -> 3.86 us
  transfers between devices with their start and end apart: 15 -> 15, of which waited for: 8 -> 7; matrix products, arithmetic and copies ran while one was open for 0% -> 0% of each run, Pallas kernels for 9% -> 17%
where the time goes in v1:
time: 47.3 us; the launch traced here: 47 us
  starting transfers between devices  15.7 us (33%)
  Pallas kernels  15.2 us (32%)
  waiting for transfers between devices  11.5 us (24%)
  local copies, waits for them, and re-layouts  3.86 us (8%)
  between operations  0.74 us (2%)
    ppermute x15, starting transfers between devices, swap(): return lax.ppermute(value, axis, [(i, partner(i)) for i in range(count)])  15.7 us
    pallas_call x9, Pallas kernels, call(): pl.pallas_call(kernel, out_shape=[jax.ShapeDtypeStruct(s, jnp.float32) fo...  15.2 us
    ppermute x15, waiting for transfers between devices, swap(): return lax.ppermute(value, axis, [(i, partner(i)) for i in range(count)])  11.5 us
    unnamed x22, local copies, waits for them, and re-layouts  3.86 us
  transfers between devices with their start and end apart: 15, of which 7 were waited for; matrix products, arithmetic and copies ran while one was open for 0% of the time, Pallas kernels for 17%

profile of v1, /device:TPU:0, one launch (start us, length us, event | category | flops | bytes accessed | tf_op | source)
XLA Modules:
  0.0 47.0 jit_solution(12560177560001535768)
XLA Ops:
  0.6 1.0 %copy-done = f32[32,32,128]{2,1,0:T(8,128)S(1)} copy-done((f32[32,32,128]{2,1,0:T(8,128)S(1)}, f32[32,32,128]{2,1,0:T(8,128)}, u32[]{:S(2)}) %copy-start) | copy-done | bytes 524312
  1.7 1.0 %copy-done.2 = f32[32,32,128]{2,1,0:T(8,128)S(1)} copy-done((f32[32,32,128]{2,1,0:T(8,128)S(1)}, f32[32,32,128]{2,1,0:T(8,128)}, u32[]{:S(2)}) %copy-start.2) | copy-done | bytes 524312
  2.7 1.0 %copy-done.4 = f32[32,32,128]{2,1,0:T(8,128)S(1)} copy-done((f32[32,32,128]{2,1,0:T(8,128)S(1)}, f32[32,32,128]{2,1,0:T(8,128)}, u32[]{:S(2)}) %copy-start.4) | copy-done | bytes 524312
  4.5 2.1 %start.1 = (f32[33,8,128]{2,1,0:T(8,128)S(1)}, f32[2,32,128]{2,1,0:T(8,128)S(1)}, f32[2,32,128]{2,1,0:T(8,128)S(1)}, f32[2,32,128]{2,1,0:T(8,128)S(1)}) custom-call(f32[32,32,128]{2,1,0:T(8,128)S(1)} %copy-done, f32[32,32,128]{2,1,0:T(8,128)S(1)} %copy-done.2, f32[32,32,128]{2,1,0:T(8,128)S(1)} %copy-done.4, f32[32,128]{1,0:T(8,128)S(1)} %copy-done.5), custom_call_target="tpu_custom_call" | custom-call | flops 3645440 | bytes 1822720 | tf_op jit(solution)/shard_map/start/pallas_call | solution.py:622
  6.6 3.0 %collective-permute-start = (f32[33,8,128]{2,1,0:T(8,128)S(1)}, f32[33,8,128]{2,1,0:T(8,128)S(1)}, u32[]{:S(2)}, u32[]{:S(2)}) collective-permute-start(f32[33,8,128]{2,1,0:T(8,128)S(1)} %get-tuple-element.44.rows_ref.srows_ref), channel_id=1, source_target_pairs={{0,16},{16,0},{1,17},{17,1},{2,18},{18,2},{3,19},{19,3},{4,20},{20... | collective-permute-start | bytes 405512 | tf_op jit(solution)/shard_map/ppermute | solution.py:637
  11.0 3.6 %collective-permute-start.1 = (f32[2,32,128]{2,1,0:T(8,128)S(1)}, f32[2,32,128]{2,1,0:T(8,128)S(1)}, u32[]{:S(2)}, u32[]{:S(2)}) collective-permute-start(f32[2,32,128]{2,1,0:T(8,128)S(1)} %get-tuple-element.45.down_ref.sdown_ref), channel_id=1, source_target_pairs={{0,12},{4,0},{8,4},{12,8},{1,13},{5,1},{9,5},{13,9},{2,14},{6,2},{... | collective-permute-start | bytes 98312 | tf_op jit(solution)/shard_map/ppermute | solution.py:637
  14.7 0.9 %collective-permute-start.7 = (f32[5,32,128]{2,1,0:T(8,128)S(1)}, f32[5,32,128]{2,1,0:T(8,128)S(1)}, u32[]{:S(2)}, u32[]{:S(2)}) collective-permute-start(f32[5,32,128]{2,1,0:T(8,128)S(1)} %get-tuple-element.53.refs_4_), channel_id=1, source_target_pairs={{0,2},{1,3},{2,0},{3,1},{4,6},{5,7},{6,4},{7,5},{8,10},{9,11},{10,... | collective-permute-start | bytes 245768 | tf_op jit(solution)/shard_map/ppermute | solution.py:637
  15.6 0.9 %collective-permute-done.1.got_down_ref.got_sdown_ref = f32[2,32,128]{2,1,0:T(8,128)S(1)} collective-permute-done((f32[2,32,128]{2,1,0:T(8,128)S(1)}, f32[2,32,128]{2,1,0:T(8,128)S(1)}, u32[]{:S(2)}, u32[]{:S(2)}) %collective-permute-start.1) | collective-permute-done | bytes 32800 | tf_op jit(solution)/shard_map/ppermute | solution.py:637
  16.5 2.5 %interior.2 = (f32[32,32,128]{2,1,0:T(8,128)S(1)}, f32[32,32,128]{2,1,0:T(8,128)S(1)}, f32[32,32,128]{2,1,0:T(8,128)S(1)}) custom-call(f32[32,32,128]{2,1,0:T(8,128)S(1)} %copy-done.1, f32[32,32,128]{2,1,0:T(8,128)S(1)} %copy-done.3, f32[32,32,128]{2,1,0:T(8,128)S(1)} %copy-done.4, f32[32,128]{1,0:T(8,128)S(1)} %copy-done.5), custom_call_target="tpu_custom_call" | custom-call | flops 6324224 | bytes 3162112 | tf_op jit(solution)/shard_map/interior/pallas_call | solution.py:622
  19.1 1.3 %collective-permute-done.2.got_up_ref.got_sup_ref = f32[2,32,128]{2,1,0:T(8,128)S(1)} collective-permute-done((f32[2,32,128]{2,1,0:T(8,128)S(1)}, f32[2,32,128]{2,1,0:T(8,128)S(1)}, u32[]{:S(2)}, u32[]{:S(2)}) %collective-permute-start.2) | collective-permute-done | bytes 32800 | tf_op jit(solution)/shard_map/ppermute | solution.py:637
  20.5 1.4 %sweep.2 = (f32[32,32,128]{2,1,0:T(8,128)S(1)}, f32[32,32,128]{2,1,0:T(8,128)S(1)}, f32[32,32,128]{2,1,0:T(8,128)S(1)}, f32[32,32,128]{2,1,0:T(8,128)S(1)}, f32[4,32,128]{2,1,0:T(8,128)S(1)}) custom-call(f32[32,32,128]{2,1,0:T(8,128)S(1)} %copy-done.1, f32[32,32,128]{2,1,0:T(8,128)S(1)} %get-tuple-element.37.nxc_ref, ...), custom_call_target="tpu_custom_call" | custom-call | flops 14483456 | bytes 7241728 | tf_op jit(solution)/shard_map/sweep/pallas_call | solution.py:622
  22.0 1.4 %collective-permute-start.4 = (f32[4,32,128]{2,1,0:T(8,128)S(1)}, f32[4,32,128]{2,1,0:T(8,128)S(1)}, u32[]{:S(2)}, u32[]{:S(2)}) collective-permute-start(f32[4,32,128]{2,1,0:T(8,128)S(1)} %get-tuple-element.52.refs_0_), channel_id=1, source_target_pairs={{0,2},{1,3},{2,0},{3,1},{4,6},{5,7},{6,4},{7,5},{8,10},{9,11},{10,... | collective-permute-start | bytes 196616 | tf_op jit(solution)/shard_map/ppermute | solution.py:637
  24.6 1.8 %collective-permute-done.5.refs_3_ = f32[4,32,128]{2,1,0:T(8,128)S(1)} collective-permute-done((f32[4,32,128]{2,1,0:T(8,128)S(1)}, f32[4,32,128]{2,1,0:T(8,128)S(1)}, u32[]{:S(2)}, u32[]{:S(2)}) %collective-permute-start.5) | collective-permute-done | bytes 65568 | tf_op jit(solution)/shard_map/ppermute | solution.py:637
  26.4 1.4 %collective-permute-done.4.refs_2_ = f32[4,32,128]{2,1,0:T(8,128)S(1)} collective-permute-done((f32[4,32,128]{2,1,0:T(8,128)S(1)}, f32[4,32,128]{2,1,0:T(8,128)S(1)}, u32[]{:S(2)}, u32[]{:S(2)}) %collective-permute-start.4) | collective-permute-done | bytes 65568 | tf_op jit(solution)/shard_map/ppermute | solution.py:637
  27.8 1.5 %finish.1 = (f32[32,32,128]{2,1,0:T(8,128)S(1)}, f32[32,32,128]{2,1,0:T(8,128)S(1)}, f32[32,8,128]{2,1,0:T(8,128)S(1)}, f32[1,32,128]{2,1,0:T(8,128)S(1)}, f32[1...) custom-call(f32[32,32,128]{2,1,0:T(8,128)S(1)} %get-tuple-element.47.y_ref, f32[32,32,128]{2,1,0:T(8,128)S(1)} %get-tuple-element.48.q_ref, ...), custom_call_target="tpu_custom_call" | custom-call | flops 9011200 | bytes 4505600 | tf_op jit(solution)/shard_map/finish/pallas_call | solution.py:622
  29.8 3.0 %collective-permute-start.10 = (f32[1,32,128]{2,1,0:T(8,128)S(1)}, f32[1,32,128]{2,1,0:T(8,128)S(1)}, u32[]{:S(2)}, u32[]{:S(2)}) collective-permute-start(f32[1,32,128]{2,1,0:T(8,128)S(1)} %get-tuple-element.61.down_ref), channel_id=1, source_target_pairs={{0,12},{4,0},{8,4},{12,8},{1,13},{5,1},{9,5},{13,9},{2,14},{6,2},{... | collective-permute-start | bytes 49160 | tf_op jit(solution)/shard_map/ppermute | solution.py:637
  32.8 2.5 %interior.3 = (f32[32,32,128]{2,1,0:T(8,128)S(1)}, f32[32,32,128]{2,1,0:T(8,128)S(1)}, f32[32,32,128]{2,1,0:T(8,128)S(1)}) custom-call(f32[32,32,128]{2,1,0:T(8,128)S(1)} %get-tuple-element.54.p_ref, f32[32,32,128]{2,1,0:T(8,128)S(1)} %get-tuple-element.50.wx_ref, f32[32,32,128]{2,1,0:T(8,128)S(1)} %get-tuple-element.51.wy_ref, f32[32,128]{1,0:T(8,128)S(1)} %copy-done.6), custom_call_target="tpu_custom_call" | custom-call | flops 6324224 | bytes 3162112 | tf_op jit(solution)/shard_map/interior/pallas_call | solution.py:622
  35.4 3.0 %collective-permute-done.11.got_up_ref = f32[1,32,128]{2,1,0:T(8,128)S(1)} collective-permute-done((f32[1,32,128]{2,1,0:T(8,128)S(1)}, f32[1,32,128]{2,1,0:T(8,128)S(1)}, u32[]{:S(2)}, u32[]{:S(2)}) %collective-permute-start.11) | collective-permute-done | bytes 16416 | tf_op jit(solution)/shard_map/ppermute | solution.py:637
  38.3 2.4 %sweep.3 = (f32[32,32,128]{2,1,0:T(8,128)}, f32[32,32,128]{2,1,0:T(8,128)}, f32[32,32,128]{2,1,0:T(8,128)S(1)}, f32[32,32,128]{2,1,0:T(8,128)S(1)}, f32[4,32,128]{2,1,0:T(8,128)S(1)}) custom-call(f32[32,32,128]{2,1,0:T(8,128)S(1)} %get-tuple-element.54.p_ref, f32[32,32,128]{2,1,0:T(8,128)S(1)} %get-tuple-element.55.nxc_ref, ...), custom_call_target="tpu_custom_call" | custom-call | flops 14336000 | bytes 7168000 | tf_op jit(solution)/shard_map/sweep/pallas_call | solution.py:622
  40.7 0.8 %collective-permute-start.13 = (f32[4,32,128]{2,1,0:T(8,128)S(1)}, f32[4,32,128]{2,1,0:T(8,128)S(1)}, u32[]{:S(2)}, u32[]{:S(2)}) collective-permute-start(f32[4,32,128]{2,1,0:T(8,128)S(1)} %get-tuple-element.67.refs_0_), channel_id=1, source_target_pairs={{0,2},{1,3},{2,0},{3,1},{4,6},{5,7},{6,4},{7,5},{8,10},{9,11},{10,... | collective-permute-start | bytes 196616 | tf_op jit(solution)/shard_map/ppermute | solution.py:637
  41.5 1.1 %collective-permute-start.12 = (f32[4,32,128]{2,1,0:T(8,128)S(1)}, f32[4,32,128]{2,1,0:T(8,128)S(1)}, u32[]{:S(2)}, u32[]{:S(2)}) collective-permute-start(f32[4,32,128]{2,1,0:T(8,128)S(1)} %get-tuple-element.67.refs_0_), channel_id=1, source_target_pairs={{0,1},{1,0},{2,3},{3,2},{4,5},{5,4},{6,7},{7,6},{8,9},{9,8},{10,11... | collective-permute-start | bytes 196616 | tf_op jit(solution)/shard_map/ppermute | solution.py:637
  42.6 2.0 %collective-permute-done.14.refs_3_ = f32[4,32,128]{2,1,0:T(8,128)S(1)} collective-permute-done((f32[4,32,128]{2,1,0:T(8,128)S(1)}, f32[4,32,128]{2,1,0:T(8,128)S(1)}, u32[]{:S(2)}, u32[]{:S(2)}) %collective-permute-start.14) | collective-permute-done | bytes 65568 | tf_op jit(solution)/shard_map/ppermute | solution.py:637
  44.6 1.1 %collective-permute-done.13.refs_2_ = f32[4,32,128]{2,1,0:T(8,128)S(1)} collective-permute-done((f32[4,32,128]{2,1,0:T(8,128)S(1)}, f32[4,32,128]{2,1,0:T(8,128)S(1)}, u32[]{:S(2)}, u32[]{:S(2)}) %collective-permute-start.13) | collective-permute-done | bytes 65568 | tf_op jit(solution)/shard_map/ppermute | solution.py:637
  45.7 1.3 %last.1 = (f32[32,32,128]{2,1,0:T(8,128)}, f32[32,32,128]{2,1,0:T(8,128)}) custom-call(f32[32,32,128]{2,1,0:T(8,128)S(1)} %get-tuple-element.65.y_ref, f32[32,32,128]{2,1,0:T(8,128)S(1)} %get-tuple-element.48.q_ref, f32[32,32,128]{2,1,0:T(8,128)S(1)} %get-tuple-element.41.i_ref, f32[32,32,128]{2,1,0:T(8,128)S(1)} %get-tuple-element.66.ps_ref, ...), custom_call_target="tpu_custom_call" | custom-call | flops 7471104 | bytes 3735552 | tf_op jit(solution)/shard_map/last/pallas_call | solution.py:622
  (37 shorter events, 4.1 us)
Async XLA Ops:
  0.6 1.0 %copy-start = (f32[32,32,128]{2,1,0:T(8,128)S(1)}, f32[32,32,128]{2,1,0:T(8,128)}, u32[]{:S(2)}) copy-start(f32[32,32,128]{2,1,0:T(8,128)} %p_ref.5) | copy-start | bytes 1572868
  1.7 1.0 %copy-start.2 = (f32[32,32,128]{2,1,0:T(8,128)S(1)}, f32[32,32,128]{2,1,0:T(8,128)}, u32[]{:S(2)}) copy-start(f32[32,32,128]{2,1,0:T(8,128)} %wx_ref.3) | copy-start | bytes 1572868
  4.5 5.1 %copy-start.8 = (f32[32,32,128]{2,1,0:T(8,128)S(1)}, f32[32,32,128]{2,1,0:T(8,128)}, u32[]{:S(2)}) copy-start(f32[32,32,128]{2,1,0:T(8,128)} %s_ref.1) | copy-start | bytes 1572868
  4.5 12.0 %copy-start.3 = (f32[32,32,128]{2,1,0:T(8,128)S(1)}, f32[32,32,128]{2,1,0:T(8,128)}, u32[]{:S(2)}) copy-start(f32[32,32,128]{2,1,0:T(8,128)} %wx_ref.3) | copy-start | bytes 1572868
  6.6 10.0 %copy-start.1 = (f32[32,32,128]{2,1,0:T(8,128)S(1)}, f32[32,32,128]{2,1,0:T(8,128)}, u32[]{:S(2)}) copy-start(f32[32,32,128]{2,1,0:T(8,128)} %p_ref.5) | copy-start | bytes 1572868
  6.6 13.9 %collective-permute-start = (f32[33,8,128]{2,1,0:T(8,128)S(1)}, f32[33,8,128]{2,1,0:T(8,128)S(1)}, u32[]{:S(2)}, u32[]{:S(2)}) collective-permute-start(f32[33,8,128]{2,1,0:T(8,128)S(1)} %get-tuple-element.44.rows_ref.srows_ref), channel_id=1, source_target_pairs={{0,16},{16,0},{1,17},{17,1},{2,18},{18,2},{3,19},{19,3},{4,20},{20... | collective-permute-start | bytes 405512 | tf_op jit(solution)/shard_map/ppermute | solution.py:637
  10.3 13.1 %collective-permute-start.8 = (f32[5,32,128]{2,1,0:T(8,128)S(1)}, f32[5,32,128]{2,1,0:T(8,128)S(1)}, u32[]{:S(2)}, u32[]{:S(2)}) collective-permute-start(f32[5,32,128]{2,1,0:T(8,128)S(1)} %get-tuple-element.53.refs_4_), channel_id=1, source_target_pairs={{0,3},{1,2},{2,1},{3,0},{4,7},{5,6},{6,5},{7,4},{8,11},{9,10},{10,... | collective-permute-start | bytes 245768 | tf_op jit(solution)/shard_map/ppermute | solution.py:637
  11.0 5.4 %collective-permute-start.1 = (f32[2,32,128]{2,1,0:T(8,128)S(1)}, f32[2,32,128]{2,1,0:T(8,128)S(1)}, u32[]{:S(2)}, u32[]{:S(2)}) collective-permute-start(f32[2,32,128]{2,1,0:T(8,128)S(1)} %get-tuple-element.45.down_ref.sdown_ref), channel_id=1, source_target_pairs={{0,12},{4,0},{8,4},{12,8},{1,13},{5,1},{9,5},{13,9},{2,14},{6,2},{... | collective-permute-start | bytes 98312 | tf_op jit(solution)/shard_map/ppermute | solution.py:637
  14.6 5.8 %copy-start.7 = (f32[32,32,128]{2,1,0:T(8,128)S(1)}, f32[32,32,128]{2,1,0:T(8,128)}, u32[]{:S(2)}) copy-start(f32[32,32,128]{2,1,0:T(8,128)} %wz_ref.1) | copy-start | bytes 1572868
  14.7 5.8 %collective-permute-start.2 = (f32[2,32,128]{2,1,0:T(8,128)S(1)}, f32[2,32,128]{2,1,0:T(8,128)S(1)}, u32[]{:S(2)}, u32[]{:S(2)}) collective-permute-start(f32[2,32,128]{2,1,0:T(8,128)S(1)} %get-tuple-element.46.up_ref.sup_ref), channel_id=1, source_target_pairs={{0,4},{4,8},{8,12},{12,0},{1,5},{5,9},{9,13},{13,1},{2,6},{6,10},{... | collective-permute-start | bytes 98312 | tf_op jit(solution)/shard_map/ppermute | solution.py:637
  14.7 9.9 %collective-permute-start.7 = (f32[5,32,128]{2,1,0:T(8,128)S(1)}, f32[5,32,128]{2,1,0:T(8,128)S(1)}, u32[]{:S(2)}, u32[]{:S(2)}) collective-permute-start(f32[5,32,128]{2,1,0:T(8,128)S(1)} %get-tuple-element.53.refs_4_), channel_id=1, source_target_pairs={{0,2},{1,3},{2,0},{3,1},{4,6},{5,7},{6,4},{7,5},{8,10},{9,11},{10,... | collective-permute-start | bytes 245768 | tf_op jit(solution)/shard_map/ppermute | solution.py:637
  16.4 8.1 %collective-permute-start.6 = (f32[5,32,128]{2,1,0:T(8,128)S(1)}, f32[5,32,128]{2,1,0:T(8,128)S(1)}, u32[]{:S(2)}, u32[]{:S(2)}) collective-permute-start(f32[5,32,128]{2,1,0:T(8,128)S(1)} %get-tuple-element.53.refs_4_), channel_id=1, source_target_pairs={{0,1},{1,0},{2,3},{3,2},{4,5},{5,4},{6,7},{7,6},{8,9},{9,8},{10,11... | collective-permute-start | bytes 245768 | tf_op jit(solution)/shard_map/ppermute | solution.py:637
  16.5 3.9 %copy-start.6 = (f32[32,128]{1,0:T(8,128)S(1)}, f32[32,128]{1,0:T(8,128)}, u32[]{:S(2)}) copy-start(f32[32,128]{1,0:T(8,128)} %jac_ref.11) | copy-start | bytes 49156
  16.5 3.9 %copy-start.9 = (f32[32,128]{1,0:T(8,128)S(1)}, f32[32,128]{1,0:T(8,128)}, u32[]{:S(2)}) copy-start(f32[32,128]{1,0:T(8,128)} %sx_ref.3) | copy-start | bytes 49156
  16.5 3.9 %copy-start.10 = (f32[32,128]{1,0:T(8,128)S(1)}, f32[32,128]{1,0:T(8,128)}, u32[]{:S(2)}) copy-start(f32[32,128]{1,0:T(8,128)} %sy_ref.3) | copy-start | bytes 49156
  21.9 4.5 %collective-permute-start.5 = (f32[4,32,128]{2,1,0:T(8,128)S(1)}, f32[4,32,128]{2,1,0:T(8,128)S(1)}, u32[]{:S(2)}, u32[]{:S(2)}) collective-permute-start(f32[4,32,128]{2,1,0:T(8,128)S(1)} %get-tuple-element.52.refs_0_), channel_id=1, source_target_pairs={{0,3},{1,2},{2,1},{3,0},{4,7},{5,6},{6,5},{7,4},{8,11},{9,10},{10,... | collective-permute-start | bytes 196616 | tf_op jit(solution)/shard_map/ppermute | solution.py:637
  22.0 5.8 %collective-permute-start.4 = (f32[4,32,128]{2,1,0:T(8,128)S(1)}, f32[4,32,128]{2,1,0:T(8,128)S(1)}, u32[]{:S(2)}, u32[]{:S(2)}) collective-permute-start(f32[4,32,128]{2,1,0:T(8,128)S(1)} %get-tuple-element.52.refs_0_), channel_id=1, source_target_pairs={{0,2},{1,3},{2,0},{3,1},{4,6},{5,7},{6,4},{7,5},{8,10},{9,11},{10,... | collective-permute-start | bytes 196616 | tf_op jit(solution)/shard_map/ppermute | solution.py:637
  23.4 4.3 %collective-permute-start.3 = (f32[4,32,128]{2,1,0:T(8,128)S(1)}, f32[4,32,128]{2,1,0:T(8,128)S(1)}, u32[]{:S(2)}, u32[]{:S(2)}) collective-permute-start(f32[4,32,128]{2,1,0:T(8,128)S(1)} %get-tuple-element.52.refs_0_), channel_id=1, source_target_pairs={{0,1},{1,0},{2,3},{3,2},{4,5},{5,4},{6,7},{7,6},{8,9},{9,8},{10,11... | collective-permute-start | bytes 196616 | tf_op jit(solution)/shard_map/ppermute | solution.py:637
  29.2 9.1 %collective-permute-start.9 = (f32[32,8,128]{2,1,0:T(8,128)S(1)}, f32[32,8,128]{2,1,0:T(8,128)S(1)}, u32[]{:S(2)}, u32[]{:S(2)}) collective-permute-start(f32[32,8,128]{2,1,0:T(8,128)S(1)} %get-tuple-element.60.rows_ref), channel_id=1, source_target_pairs={{0,16},{16,0},{1,17},{17,1},{2,18},{18,2},{3,19},{19,3},{4,20},{20... | collective-permute-start | bytes 393224 | tf_op jit(solution)/shard_map/ppermute | solution.py:637
  29.8 5.5 %collective-permute-start.10 = (f32[1,32,128]{2,1,0:T(8,128)S(1)}, f32[1,32,128]{2,1,0:T(8,128)S(1)}, u32[]{:S(2)}, u32[]{:S(2)}) collective-permute-start(f32[1,32,128]{2,1,0:T(8,128)S(1)} %get-tuple-element.61.down_ref), channel_id=1, source_target_pairs={{0,12},{4,0},{8,4},{12,8},{1,13},{5,1},{9,5},{13,9},{2,14},{6,2},{... | collective-permute-start | bytes 49160 | tf_op jit(solution)/shard_map/ppermute | solution.py:637
  32.8 5.5 %collective-permute-start.11 = (f32[1,32,128]{2,1,0:T(8,128)S(1)}, f32[1,32,128]{2,1,0:T(8,128)S(1)}, u32[]{:S(2)}, u32[]{:S(2)}) collective-permute-start(f32[1,32,128]{2,1,0:T(8,128)S(1)} %get-tuple-element.62.up_ref), channel_id=1, source_target_pairs={{0,4},{4,8},{8,12},{12,0},{1,5},{5,9},{9,13},{13,1},{2,6},{6,10},{... | collective-permute-start | bytes 49160 | tf_op jit(solution)/shard_map/ppermute | solution.py:637
  40.7 3.9 %collective-permute-start.14 = (f32[4,32,128]{2,1,0:T(8,128)S(1)}, f32[4,32,128]{2,1,0:T(8,128)S(1)}, u32[]{:S(2)}, u32[]{:S(2)}) collective-permute-start(f32[4,32,128]{2,1,0:T(8,128)S(1)} %get-tuple-element.67.refs_0_), channel_id=1, source_target_pairs={{0,3},{1,2},{2,1},{3,0},{4,7},{5,6},{6,5},{7,4},{8,11},{9,10},{10,... | collective-permute-start | bytes 196616 | tf_op jit(solution)/shard_map/ppermute | solution.py:637
  40.7 4.9 %collective-permute-start.13 = (f32[4,32,128]{2,1,0:T(8,128)S(1)}, f32[4,32,128]{2,1,0:T(8,128)S(1)}, u32[]{:S(2)}, u32[]{:S(2)}) collective-permute-start(f32[4,32,128]{2,1,0:T(8,128)S(1)} %get-tuple-element.67.refs_0_), channel_id=1, source_target_pairs={{0,2},{1,3},{2,0},{3,1},{4,6},{5,7},{6,4},{7,5},{8,10},{9,11},{10,... | collective-permute-start | bytes 196616 | tf_op jit(solution)/shard_map/ppermute | solution.py:637
  41.5 4.2 %collective-permute-start.12 = (f32[4,32,128]{2,1,0:T(8,128)S(1)}, f32[4,32,128]{2,1,0:T(8,128)S(1)}, u32[]{:S(2)}, u32[]{:S(2)}) collective-permute-start(f32[4,32,128]{2,1,0:T(8,128)S(1)} %get-tuple-element.67.refs_0_), channel_id=1, source_target_pairs={{0,1},{1,0},{2,3},{3,2},{4,5},{5,4},{6,7},{7,6},{8,9},{9,8},{10,11... | collective-permute-start | bytes 196616 | tf_op jit(solution)/shard_map/ppermute | solution.py:637
  (2 other events, 1.8 us)

commit v2 on v1

--- a/solution.py
+++ b/solution.py
@@ -18,6 +18,7 @@
 ROWS = 8
 SLOT = 4
 UNROLL = 4
+CHUNKS = 4
 
 
 def lane_index():
@@ -185,6 +186,22 @@
         ]
 
 
+def even_place():
+    return lax.rem(lax.axis_index("gy"), 2) == 0
+
+
+def put_pair(inner_ref, outer_ref, index, down, up):
+    even = even_place()
+    put_tiles(inner_ref, index, [jnp.where(even, u, d) for u, d in zip(up, down)])
+    put_tiles(outer_ref, index, [jnp.where(even, d, u) for u, d in zip(up, down)])
+
+
+def get_pair(inner_ref, outer_ref, index, part):
+    even = even_place()
+    inner, outer = inner_ref[index, part, :], outer_ref[index, part, :]
+    return jnp.where(even, outer, inner), jnp.where(even, inner, outer)
+
+
 def lane_payload(pres, wind, jac):
     low, high = lane_edge(LOW), lane_edge(HIGH)
     down = [
@@ -205,30 +222,67 @@
     return packer.done(lax.fori_loop(0, levels, step, packer.start, unroll=UNROLL))
 
 
-def kernel_a(p_ref, wx_ref, wy_ref, jac_ref, rows_ref, down_ref, up_ref, pp_ref):
-    levels, rows, _ = p_ref.shape
+def kernel_a(
+    p_hbm, wx_hbm, wy_hbm, jac_hbm, rows_ref, inner_ref, outer_ref, pp_ref, p_ref, wx_ref, wy_ref, jac_ref, sems
+):
+    levels, rows, _ = p_hbm.shape
     count = rows // ROWS
+    share = levels // CHUNKS
+
+    def fetch(source, target, sem):
+        copy = pltpu.make_async_copy(source, target, sem)
+        copy.start()
+        return copy
+
+    tail = pl.ds(rows - ROWS, ROWS)
+    parts = [pl.ds(c * share, share) for c in range(CHUNKS)]
+    pres_in = [fetch(p_hbm.at[s], p_ref.at[s], sems.at[0, c]) for c, s in enumerate(parts)]
+    wind_in = [fetch(wy_hbm.at[s], wy_ref.at[s], sems.at[1, c]) for c, s in enumerate(parts)]
+    ends_in = [
+        fetch(jac_hbm, jac_ref, sems.at[2, 0]),
+        fetch(wx_hbm.at[:, pl.ds(0, ROWS)], wx_ref.at[:, pl.ds(0, ROWS)], sems.at[2, 1]),
+        fetch(wx_hbm.at[:, tail], wx_ref.at[:, pl.ds(ROWS, ROWS)], sems.at[2, 2]),
+    ]
+
+    def pack(ref, copies):
+        packer = Packer(count)
+        state = packer.start
+        for c, copy in enumerate(copies):
+            copy.wait()
+            state = lax.fori_loop(
+                c * share,
+                (c + 1) * share,
+                lambda level, state: packer.add(level, tiles_of(ref, level, count), state),
+                state,
+                unroll=UNROLL,
+            )
+        return packer.done(state)
+
+    pres = pack(p_ref, pres_in)
+    wind = pack(wy_ref, wind_in)
+    for copy in ends_in:
+        copy.wait()
     jac = planes_of(jac_ref, count)
     ends = both_ends(jac)
     edge = row_edge()
 
     def step(level, state):
         rows_ref[level] = edge.payload(
-            both_ends(tiles_of(p_ref, level, count)),
-            both_ends(tiles_of(wx_ref, level, count)),
-            ends,
+            both_ends(tiles_of(p_ref, level, count)), both_ends(tiles_of(wx_ref, level, 2)), ends
         )
         return state
 
     lax.fori_loop(0, levels, step, 0, unroll=UNROLL)
     rows_ref[levels] = ends
-    pres = pack_levels(p_ref, count, levels)
-    wind = pack_levels(wy_ref, count, levels)
     down, up = lane_payload(pres, wind, jac)
-    put_tiles(down_ref, 0, down)
-    put_tiles(up_ref, 0, up)
-    put_tiles(down_ref, 1, [spread_slots(j, True) for j in jac])
-    put_tiles(up_ref, 1, [spread_slots(j, False) for j in jac])
+    put_pair(inner_ref, outer_ref, 0, down, up)
+    put_pair(
+        inner_ref,
+        outer_ref,
+        1,
+        [spread_slots(j, True) for j in jac],
+        [spread_slots(j, False) for j in jac],
+    )
     put_tiles(pp_ref, 0, pres[0])
     put_tiles(pp_ref, 1, pres[1])
 
@@ -282,17 +336,17 @@
     v_ref,
     pp_ref,
     rows_ref,
-    down_ref,
-    up_ref,
+    inner_ref,
+    outer_ref,
     got_rows_ref,
-    got_down_ref,
-    got_up_ref,
+    got_inner_ref,
+    got_outer_ref,
     srows_ref,
-    sdown_ref,
-    sup_ref,
+    sinner_ref,
+    souter_ref,
     got_srows_ref,
-    got_sdown_ref,
-    got_sup_ref,
+    got_sinner_ref,
+    got_souter_ref,
     nx_ref,
     ny_ref,
     ps_ref,
@@ -307,18 +361,15 @@
     wind_fix, low_fix, high_fix = [], [], []
     for t in range(count):
         part = slice(ROWS * t, ROWS * (t + 1))
-        jac_low, jac_high = sdown_ref[1, part, :], sup_ref[1, part, :]
+        jac_low, jac_high = get_pair(sinner_ref, souter_ref, 1, part)
+        jac_below, jac_above = get_pair(got_sinner_ref, got_souter_ref, 1, part)
+        down, up = get_pair(inner_ref, outer_ref, 0, part)
+        below, above = get_pair(got_inner_ref, got_outer_ref, 0, part)
         low_wind, low_star = low_edge.correct(
-            got_up_ref[0, part, :] - up_ref[0, part, :],
-            pp_ref[0, part, :],
-            jac_low,
-            low_edge.shifted(got_sup_ref[1, part, :] - jac_high, 2),
+            below - up, pp_ref[0, part, :], jac_low, low_edge.shifted(jac_below - jac_high, 2)
         )
         high_wind, high_star = high_edge.correct(
-            got_down_ref[0, part, :] - down_ref[0, part, :],
-            pp_ref[1, part, :],
-            jac_high,
-            high_edge.shifted(got_sdown_ref[1, part, :] - jac_low, -2),
+            above - down, pp_ref[1, part, :], jac_high, high_edge.shifted(jac_above - jac_low, -2)
         )
         wind_fix.append(low_wind + pltpu.roll(high_wind, 128 - SLOT, 1))
         low_fix.append(low_star)
@@ -526,7 +577,7 @@
     return pressed(0, above, under, state)
 
 
-def finish(blocks, count, levels, y_ref, q_ref, i_ref, ps_ref, x_ref, p_ref, face_refs, stat_refs, use, state):
+def finish(blocks, count, levels, y_ref, q_ref, i_ref, ps_ref, x_ref, p_ref, face_refs, stat_refs, use, state, ready=None):
     mine = lax.axis_index("lev")
     lower, upper, under, over = boundary(blocks, mine, count, face_refs, stat_refs)
 
@@ -552,13 +603,23 @@
         return here, below, state
 
     top = solved(levels - 1, upper)
-    above, here, state = lax.fori_loop(0, levels - 1, step, (over, top, state), unroll=UNROLL)
+    carry = (over, top, state)
+    if ready is None:
+        carry = lax.fori_loop(0, levels - 1, step, carry, unroll=UNROLL)
+    else:
+        done, share = 0, levels // CHUNKS
+        for c in range(CHUNKS - 1, -1, -1):
+            goal = levels - 1 - c * share
+            carry = lax.fori_loop(done, goal, step, carry, unroll=UNROLL)
+            done = goal
+            ready(c)
+    above, here, state = carry
     return pressed(0, above, under, state)
 
 
 def kernel_c(blocks, y_ref, q_ref, i_ref, ps_ref, wx_ref, pw_ref, jac_ref, *refs):
     face_refs, stat_refs = refs[:blocks], refs[blocks : 2 * blocks]
-    x_ref, p_ref, rows_ref, down_ref, up_ref, pp_ref = refs[2 * blocks :]
+    x_ref, p_ref, rows_ref, inner_ref, outer_ref, pp_ref = refs[2 * blocks :]
     levels, rows, _ = y_ref.shape
     count = rows // ROWS
     packer = Packer(count)
@@ -589,16 +650,29 @@
     pres = packer.done(state)
     wind = tiles_of(pw_ref, 0, count), tiles_of(pw_ref, 1, count)
     down, up = lane_payload(pres, wind, planes_of(jac_ref, count))
-    put_tiles(down_ref, 0, down)
-    put_tiles(up_ref, 0, up)
+    put_pair(inner_ref, outer_ref, 0, down, up)
     put_tiles(pp_ref, 0, pres[0])
     put_tiles(pp_ref, 1, pres[1])
 
 
 def kernel_d(blocks, y_ref, q_ref, i_ref, ps_ref, *refs):
     face_refs, stat_refs = refs[:blocks], refs[blocks : 2 * blocks]
-    x_ref, p_ref = refs[2 * blocks :]
+    x_hbm, p_hbm, x_ref, p_ref, sems = refs[2 * blocks :]
     levels, rows, _ = y_ref.shape
+    share = levels // CHUNKS
+    copies = []
+
+    def send(index, source, target, c):
+        part = pl.ds(c * share, share)
+        copy = pltpu.make_async_copy(source.at[part], target.at[part], sems.at[index, c])
+        copy.start()
+        copies.append(copy)
+
+    def ready(c):
+        send(0, x_ref, x_hbm, c)
+        if c < CHUNKS - 1:
+            send(1, p_ref, p_hbm, c + 1)
+
     finish(
         blocks,
         rows // ROWS,
@@ -613,17 +687,27 @@
         stat_refs,
         lambda level, pres, state: state,
         0,
+        ready,
     )
-
-
-def call(kernel, name, shapes, *args):
-    space = pl.BlockSpec(memory_space=pltpu.VMEM)
+    send(1, p_ref, p_hbm, 0)
+    for copy in copies:
+        copy.wait()
+
+
+def call(kernel, name, shapes, *args, far_in=False, far_out=False, scratch=(), keep=()):
+    near, far = pl.BlockSpec(memory_space=pltpu.VMEM), pl.BlockSpec(memory_space=pl.ANY)
     size = sum(a.size for a in args) + sum(functools.reduce(lambda a, b: a * b, s) for s in shapes)
+    if far_in:
+        args = [pltpu.with_memory_space_constraint(a, pltpu.HBM) for a in args]
     return pl.pallas_call(
         kernel,
-        out_shape=[jax.ShapeDtypeStruct(s, jnp.float32) for s in shapes],
-        in_specs=[space] * len(args),
-        out_specs=[space] * len(shapes),
+        out_shape=[
+            pltpu.VMEM(s, jnp.float32) if k in keep else jax.ShapeDtypeStruct(s, jnp.float32)
+            for k, s in enumerate(shapes)
+        ],
+        in_specs=[far if far_in else near] * len(args),
+        out_specs=[far if far_out else near] * len(shapes),
+        scratch_shapes=list(scratch),
         compiler_params=pltpu.CompilerParams(vmem_limit_bytes=32 * 1024 * 1024),
         cost_estimate=pl.CostEstimate(
             flops=8 * size, bytes_accessed=4 * size, transcendentals=0
@@ -646,11 +730,11 @@
     return jnp.concatenate([down, up], axis=1)
 
 
-def exchange_lanes(down, up):
+def exchange_lanes(inner, outer):
     count = lax.axis_size("gy")
-    from_above = swap(down, "gy", lambda i: (i - 1) % count)
-    from_below = swap(up, "gy", lambda i: (i + 1) % count)
-    return from_above, from_below
+    got_outer = swap(outer, "gy", lambda i: (i + 1 if i % 2 else i - 1) % count)
+    got_inner = swap(inner, "gy", lambda i: i ^ 1)
+    return got_inner, got_outer
 
 
 def gather_levels(planes):
@@ -667,9 +751,9 @@
     plane = (rows, lanes)
     pair = (2,) + plane
     assert lanes == 128 and levels * SLOT == 128 and rows % ROWS == 0
-    assert blocks & (blocks - 1) == 0
-
-    edge, down, up, ends = call(
+    assert blocks & (blocks - 1) == 0 and lax.axis_size("gy") % 2 == 0
+
+    edge, inner, outer, ends = call(
         kernel_a,
         "start",
         [(levels + 1, ROWS, lanes), pair, pair, pair],
@@ -677,9 +761,17 @@
         wind_x,
         wind_y,
         jacobian,
+        far_in=True,
+        scratch=[
+            pltpu.VMEM(field, jnp.float32),
+            pltpu.VMEM((levels, 2 * ROWS, lanes), jnp.float32),
+            pltpu.VMEM(field, jnp.float32),
+            pltpu.VMEM(plane, jnp.float32),
+            pltpu.SemaphoreType.DMA((3, CHUNKS)),
+        ],
     )
-    sent = (edge, down, up)
-    got = (exchange_rows(edge),) + exchange_lanes(down, up)
+    sent = (edge, inner, outer)
+    got = (exchange_rows(edge),) + exchange_lanes(inner, outer)
     static_edges = sent + got
     rate, inv, prod, gain, stat = call(
         kernel_f, "factor", [field, field, field, field, (5,) + plane], stiffness
@@ -706,11 +798,12 @@
             *sent,
             *got,
             *static_edges,
+            keep=(0, 1, 2, 3, 4),
         )
         faces = gather_levels(face)
         if substep < SUBSTEPS - 1:
             (packed,) = call(kernel_n, "pack", [pair], wind_y)
-            wind_z, pressure, edge, down, up, ends = call(
+            wind_z, pressure, edge, inner, outer, ends = call(
                 functools.partial(kernel_c, blocks),
                 "finish",
                 [field, field, (levels, ROWS, lanes), (1,) + plane, (1,) + plane, pair],
@@ -724,8 +817,8 @@
                 *faces,
                 *stats,
             )
-            sent = (edge, down, up)
-            got = (exchange_rows(edge),) + exchange_lanes(down, up)
+            sent = (edge, inner, outer)
+            got = (exchange_rows(edge),) + exchange_lanes(inner, outer)
         else:
             wind_z, pressure = call(
                 functools.partial(kernel_d, blocks),
@@ -737,6 +830,12 @@
                 star,
                 *faces,
                 *stats,
+                far_out=True,
+                scratch=[
+                    pltpu.VMEM(field, jnp.float32),
+                    pltpu.VMEM(field, jnp.float32),
+                    pltpu.SemaphoreType.DMA((2, CHUNKS)),
+                ],
             )
     return wind_x, wind_y, wind_z, pressure
 

time: 47.3 us -> 39.8 us (0.84)
  waiting for transfers between devices: 11.5 us -> 5.01 us
  local copies, waits for them, and re-layouts: 3.86 us -> 1.62 us
  starting transfers between devices: 15.7 us -> 16.8 us
    ppermute x15, waiting for transfers between devices: 11.5 us -> 5.01 us  [swap(): return lax.ppermute(value, axis, [(i, partner(i)) for i in range(count)])]
    unnamed x22 -> x18, local copies, waits for them, and re-layouts: 3.86 us -> 1.62 us
    ppermute x15, starting transfers between devices: 15.7 us -> 16.8 us  [swap(): return lax.ppermute(value, axis, [(i, partner(i)) for i in range(count)])]
  transfers between devices with their start and end apart: 15 -> 15, of which waited for: 7 -> 5; matrix products, arithmetic and copies ran while one was open for 0% -> 4% of each run, Pallas kernels for 17% -> 20%
where the time goes in v2:
time: 39.8 us; the launch traced here: 39.7 us
  starting transfers between devices  16.8 us (42%)
  Pallas kernels  15.4 us (39%)
  waiting for transfers between devices  5.01 us (13%)
  local copies, waits for them, and re-layouts  1.62 us (4%)
  between operations  0.84 us (2%)
    ppermute x15, starting transfers between devices, swap(): return lax.ppermute(value, axis, [(i, partner(i)) for i in range(count)])  16.8 us
    pallas_call x9, Pallas kernels, call(): pl.pallas_call(kernel, out_shape=[pltpu.VMEM(s, jnp.float32) if k in keep...  15.4 us
    ppermute x15, waiting for transfers between devices, swap(): return lax.ppermute(value, axis, [(i, partner(i)) for i in range(count)])  5.01 us
    unnamed x18, local copies, waits for them, and re-layouts  1.62 us
  transfers between devices with their start and end apart: 15, of which 5 were waited for; matrix products, arithmetic and copies ran while one was open for 4% of the time, Pallas kernels for 20%

profile of v2, /device:TPU:0, one launch (start us, length us, event | category | flops | bytes accessed | tf_op | source)
XLA Modules:
  0.0 39.7 jit_solution(14846985068874862046)
XLA Ops:
  0.7 3.3 %start.1 = (f32[33,8,128]{2,1,0:T(8,128)S(1)}, f32[2,32,128]{2,1,0:T(8,128)S(1)}, f32[2,32,128]{2,1,0:T(8,128)S(1)}, f32[2,32,128]{2,1,0:T(8,128)S(1)}) custom-call(f32[32,32,128]{2,1,0:T(8,128)} %p_ref.3, f32[32,32,128]{2,1,0:T(8,128)} %wx_hbm.1, f32[32,32,128]{2,1,0:T(8,128)} %wy_hbm.1, f32[32,128]{1,0:T(8,128)} %jac_ref.9), custom_call_target="tpu_custom_call" | custom-call | flops 3645440 | bytes 1822720 | tf_op jit(solution)/shard_map/start/pallas_call | solution.py:702
  4.0 3.0 %collective-permute-start = (f32[33,8,128]{2,1,0:T(8,128)S(1)}, f32[33,8,128]{2,1,0:T(8,128)S(1)}, u32[]{:S(2)}, u32[]{:S(2)}) collective-permute-start(f32[33,8,128]{2,1,0:T(8,128)S(1)} %get-tuple-element.44.rows_ref.srows_ref), channel_id=1, source_target_pairs={{0,16},{16,0},{1,17},{17,1},{2,18},{18,2},{3,19},{19,3},{4,20},{20... | collective-permute-start | bytes 405512 | tf_op jit(solution)/shard_map/ppermute | solution.py:721
  7.0 0.7 %factor.1 = (f32[32,32,128]{2,1,0:T(8,128)S(1)}, f32[32,32,128]{2,1,0:T(8,128)S(1)}, f32[32,32,128]{2,1,0:T(8,128)S(1)}, f32[32,32,128]{2,1,0:T(8,128)S(1)}, f32[5,32,128]{2,1,0:T(8,128)S(1)}) custom-call(f32[32,32,128]{2,1,0:T(8,128)S(1)} %copy-done.5), custom_call_target="tpu_custom_call" | custom-call | flops 5406720 | bytes 2703360 | tf_op jit(solution)/shard_map/factor/pallas_call | solution.py:702
  8.5 1.6 %collective-permute-start.1 = (f32[2,32,128]{2,1,0:T(8,128)S(1)}, f32[2,32,128]{2,1,0:T(8,128)S(1)}, u32[]{:S(2)}, u32[]{:S(2)}) collective-permute-start(f32[2,32,128]{2,1,0:T(8,128)S(1)} %get-tuple-element.45.inner_ref.sinner_ref), channel_id=1, source_target_pairs={{0,4},{4,0},{8,12},{12,8},{1,5},{5,1},{9,13},{13,9},{2,6},{6,2},{1... | collective-permute-start | bytes 98312 | tf_op jit(solution)/shard_map/ppermute | solution.py:721
  10.1 2.5 %collective-permute-start.2 = (f32[2,32,128]{2,1,0:T(8,128)S(1)}, f32[2,32,128]{2,1,0:T(8,128)S(1)}, u32[]{:S(2)}, u32[]{:S(2)}) collective-permute-start(f32[2,32,128]{2,1,0:T(8,128)S(1)} %get-tuple-element.46.outer_ref.souter_ref), channel_id=1, source_target_pairs={{0,12},{4,8},{8,4},{12,0},{1,13},{5,9},{9,5},{13,1},{2,14},{6,10},... | collective-permute-start | bytes 98312 | tf_op jit(solution)/shard_map/ppermute | solution.py:721
  12.5 0.9 %collective-permute-start.7 = (f32[5,32,128]{2,1,0:T(8,128)S(1)}, f32[5,32,128]{2,1,0:T(8,128)S(1)}, u32[]{:S(2)}, u32[]{:S(2)}) collective-permute-start(f32[5,32,128]{2,1,0:T(8,128)S(1)} %get-tuple-element.53.refs_4_), channel_id=1, source_target_pairs={{0,2},{1,3},{2,0},{3,1},{4,6},{5,7},{6,4},{7,5},{8,10},{9,11},{10,... | collective-permute-start | bytes 245768 | tf_op jit(solution)/shard_map/ppermute | solution.py:721
  13.5 2.5 %interior.2 = (f32[32,32,128]{2,1,0:T(8,128)S(1)}, f32[32,32,128]{2,1,0:T(8,128)S(1)}, f32[32,32,128]{2,1,0:T(8,128)S(1)}) custom-call(f32[32,32,128]{2,1,0:T(8,128)S(1)} %copy-done, f32[32,32,128]{2,1,0:T(8,128)S(1)} %copy-done.1, f32[32,32,128]{2,1,0:T(8,128)S(1)} %copy-done.2, f32[32,128]{1,0:T(8,128)S(1)} %copy-done.3), custom_call_target="tpu_custom_call" | custom-call | flops 6324224 | bytes 3162112 | tf_op jit(solution)/shard_map/interior/pallas_call | solution.py:702
  16.1 1.4 %sweep.2 = (f32[32,32,128]{2,1,0:T(8,128)S(1)}, f32[32,32,128]{2,1,0:T(8,128)S(1)}, f32[32,32,128]{2,1,0:T(8,128)S(1)}, f32[32,32,128]{2,1,0:T(8,128)S(1)}, f32[4,32,128]{2,1,0:T(8,128)S(1)}) custom-call(f32[32,32,128]{2,1,0:T(8,128)S(1)} %copy-done, f32[32,32,128]{2,1,0:T(8,128)S(1)} %get-tuple-element.37.nxc_ref, ...), custom_call_target="tpu_custom_call" | custom-call | flops 14483456 | bytes 7241728 | tf_op jit(solution)/shard_map/sweep/pallas_call | solution.py:702
  17.6 1.3 %collective-permute-start.5 = (f32[4,32,128]{2,1,0:T(8,128)S(1)}, f32[4,32,128]{2,1,0:T(8,128)S(1)}, u32[]{:S(2)}, u32[]{:S(2)}) collective-permute-start(f32[4,32,128]{2,1,0:T(8,128)S(1)} %get-tuple-element.52.refs_0_), channel_id=1, source_target_pairs={{0,3},{1,2},{2,1},{3,0},{4,7},{5,6},{6,5},{7,4},{8,11},{9,10},{10,... | collective-permute-start | bytes 196616 | tf_op jit(solution)/shard_map/ppermute | solution.py:721
  18.8 0.9 %collective-permute-start.4 = (f32[4,32,128]{2,1,0:T(8,128)S(1)}, f32[4,32,128]{2,1,0:T(8,128)S(1)}, u32[]{:S(2)}, u32[]{:S(2)}) collective-permute-start(f32[4,32,128]{2,1,0:T(8,128)S(1)} %get-tuple-element.52.refs_0_), channel_id=1, source_target_pairs={{0,2},{1,3},{2,0},{3,1},{4,6},{5,7},{6,4},{7,5},{8,10},{9,11},{10,... | collective-permute-start | bytes 196616 | tf_op jit(solution)/shard_map/ppermute | solution.py:721
  19.8 0.7 %pack.1.pw_ref = f32[2,32,128]{2,1,0:T(8,128)S(1)} custom-call(f32[32,32,128]{2,1,0:T(8,128)S(1)} %get-tuple-element.51.wy_ref), custom_call_target="tpu_custom_call" | custom-call | flops 1114112 | bytes 557056 | tf_op jit(solution)/shard_map/pack/pallas_call | solution.py:702
  20.5 0.9 %collective-permute-done.5.refs_3_ = f32[4,32,128]{2,1,0:T(8,128)S(1)} collective-permute-done((f32[4,32,128]{2,1,0:T(8,128)S(1)}, f32[4,32,128]{2,1,0:T(8,128)S(1)}, u32[]{:S(2)}, u32[]{:S(2)}) %collective-permute-start.5) | collective-permute-done | bytes 65568 | tf_op jit(solution)/shard_map/ppermute | solution.py:721
  21.4 2.0 %collective-permute-done.4.refs_2_ = f32[4,32,128]{2,1,0:T(8,128)S(1)} collective-permute-done((f32[4,32,128]{2,1,0:T(8,128)S(1)}, f32[4,32,128]{2,1,0:T(8,128)S(1)}, u32[]{:S(2)}, u32[]{:S(2)}) %collective-permute-start.4) | collective-permute-done | bytes 65568 | tf_op jit(solution)/shard_map/ppermute | solution.py:721
  23.4 1.5 %finish.1 = (f32[32,32,128]{2,1,0:T(8,128)S(1)}, f32[32,32,128]{2,1,0:T(8,128)S(1)}, f32[32,8,128]{2,1,0:T(8,128)S(1)}, f32[1,32,128]{2,1,0:T(8,128)S(1)}, f32[1...) custom-call(f32[32,32,128]{2,1,0:T(8,128)S(1)} %get-tuple-element.47.y_ref, f32[32,32,128]{2,1,0:T(8,128)S(1)} %get-tuple-element.48.q_ref, ...), custom_call_target="tpu_custom_call" | custom-call | flops 9011200 | bytes 4505600 | tf_op jit(solution)/shard_map/finish/pallas_call | solution.py:702
  25.5 0.9 %collective-permute-start.10 = (f32[1,32,128]{2,1,0:T(8,128)S(1)}, f32[1,32,128]{2,1,0:T(8,128)S(1)}, u32[]{:S(2)}, u32[]{:S(2)}) collective-permute-start(f32[1,32,128]{2,1,0:T(8,128)S(1)} %get-tuple-element.61.inner_ref), channel_id=1, source_target_pairs={{0,4},{4,0},{8,12},{12,8},{1,5},{5,1},{9,13},{13,9},{2,6},{6,2},{1... | collective-permute-start | bytes 49160 | tf_op jit(solution)/shard_map/ppermute | solution.py:721
  26.4 2.5 %collective-permute-start.11 = (f32[1,32,128]{2,1,0:T(8,128)S(1)}, f32[1,32,128]{2,1,0:T(8,128)S(1)}, u32[]{:S(2)}, u32[]{:S(2)}) collective-permute-start(f32[1,32,128]{2,1,0:T(8,128)S(1)} %get-tuple-element.62.outer_ref), channel_id=1, source_target_pairs={{0,12},{4,8},{8,4},{12,0},{1,13},{5,9},{9,5},{13,1},{2,14},{6,10},... | collective-permute-start | bytes 49160 | tf_op jit(solution)/shard_map/ppermute | solution.py:721
  28.9 2.5 %interior.3 = (f32[32,32,128]{2,1,0:T(8,128)S(1)}, f32[32,32,128]{2,1,0:T(8,128)S(1)}, f32[32,32,128]{2,1,0:T(8,128)S(1)}) custom-call(f32[32,32,128]{2,1,0:T(8,128)S(1)} %get-tuple-element.54.p_ref, f32[32,32,128]{2,1,0:T(8,128)S(1)} %get-tuple-element.50.wx_ref, f32[32,32,128]{2,1,0:T(8,128)S(1)} %get-tuple-element.51.wy_ref, f32[32,128]{1,0:T(8,128)S(1)} %copy-done.3), custom_call_target="tpu_custom_call" | custom-call | flops 6324224 | bytes 3162112 | tf_op jit(solution)/shard_map/interior/pallas_call | solution.py:702
  32.0 1.4 %sweep.3 = (f32[32,32,128]{2,1,0:T(8,128)S(1)}, f32[32,32,128]{2,1,0:T(8,128)S(1)}, f32[32,32,128]{2,1,0:T(8,128)S(1)}, f32[32,32,128]{2,1,0:T(8,128)S(1)}, f32[4,32,128]{2,1,0:T(8,128)S(1)}) custom-call(f32[32,32,128]{2,1,0:T(8,128)S(1)} %get-tuple-element.54.p_ref, f32[32,32,128]{2,1,0:T(8,128)S(1)} %get-tuple-element.55.nxc_ref, ...), custom_call_target="tpu_custom_call" | custom-call | flops 14336000 | bytes 7168000 | tf_op jit(solution)/shard_map/sweep/pallas_call | solution.py:702
  33.5 1.1 %collective-permute-start.13 = (f32[4,32,128]{2,1,0:T(8,128)S(1)}, f32[4,32,128]{2,1,0:T(8,128)S(1)}, u32[]{:S(2)}, u32[]{:S(2)}) collective-permute-start(f32[4,32,128]{2,1,0:T(8,128)S(1)} %get-tuple-element.67.refs_0_), channel_id=1, source_target_pairs={{0,2},{1,3},{2,0},{3,1},{4,6},{5,7},{6,4},{7,5},{8,10},{9,11},{10,... | collective-permute-start | bytes 196616 | tf_op jit(solution)/shard_map/ppermute | solution.py:721
  34.6 0.8 %collective-permute-start.12 = (f32[4,32,128]{2,1,0:T(8,128)S(1)}, f32[4,32,128]{2,1,0:T(8,128)S(1)}, u32[]{:S(2)}, u32[]{:S(2)}) collective-permute-start(f32[4,32,128]{2,1,0:T(8,128)S(1)} %get-tuple-element.67.refs_0_), channel_id=1, source_target_pairs={{0,1},{1,0},{2,3},{3,2},{4,5},{5,4},{6,7},{7,6},{8,9},{9,8},{10,11... | collective-permute-start | bytes 196616 | tf_op jit(solution)/shard_map/ppermute | solution.py:721
  35.3 0.8 %copy.12 = f32[32,32,128]{2,1,0:T(8,128)} copy(f32[32,32,128]{2,1,0:T(8,128)S(1)} %get-tuple-element.70) | data formatting | bytes 1048576
  36.1 0.8 %copy.13 = f32[32,32,128]{2,1,0:T(8,128)} copy(f32[32,32,128]{2,1,0:T(8,128)S(1)} %get-tuple-element.71) | data formatting | bytes 1048576
  36.9 0.8 %collective-permute-done.14.refs_3_ = f32[4,32,128]{2,1,0:T(8,128)S(1)} collective-permute-done((f32[4,32,128]{2,1,0:T(8,128)S(1)}, f32[4,32,128]{2,1,0:T(8,128)S(1)}, u32[]{:S(2)}, u32[]{:S(2)}) %collective-permute-start.14) | collective-permute-done | bytes 65568 | tf_op jit(solution)/shard_map/ppermute | solution.py:721
  38.5 1.2 %last.1 = (f32[32,32,128]{2,1,0:T(8,128)}, f32[32,32,128]{2,1,0:T(8,128)}) custom-call(f32[32,32,128]{2,1,0:T(8,128)S(1)} %get-tuple-element.65.y_ref, f32[32,32,128]{2,1,0:T(8,128)S(1)} %get-tuple-element.48.q_ref, f32[32,32,128]{2,1,0:T(8,128)S(1)} %get-tuple-element.41.i_ref, f32[32,32,128]{2,1,0:T(8,128)S(1)} %get-tuple-element.66.ps_ref, ...), custom_call_target="tpu_custom_call" | custom-call | flops 7471104 | bytes 3735552 | tf_op jit(solution)/shard_map/last/pallas_call | solution.py:702
  (33 shorter events, 2.6 us)
Async XLA Ops:
  0.6 6.4 %copy-start.5 = (f32[32,32,128]{2,1,0:T(8,128)S(1)}, f32[32,32,128]{2,1,0:T(8,128)}, u32[]{:S(2)}) copy-start(f32[32,32,128]{2,1,0:T(8,128)} %s_ref.1) | copy-start | bytes 1572868
  0.6 12.8 %copy-start.1 = (f32[32,32,128]{2,1,0:T(8,128)S(1)}, f32[32,32,128]{2,1,0:T(8,128)}, u32[]{:S(2)}) copy-start(f32[32,32,128]{2,1,0:T(8,128)} %wx_hbm.1) | copy-start | bytes 1572868
  0.7 12.8 %copy-start.2 = (f32[32,32,128]{2,1,0:T(8,128)S(1)}, f32[32,32,128]{2,1,0:T(8,128)}, u32[]{:S(2)}) copy-start(f32[32,32,128]{2,1,0:T(8,128)} %wy_hbm.1) | copy-start | bytes 1572868
  0.7 12.8 %copy-start.3 = (f32[32,128]{1,0:T(8,128)S(1)}, f32[32,128]{1,0:T(8,128)}, u32[]{:S(2)}) copy-start(f32[32,128]{1,0:T(8,128)} %jac_ref.9) | copy-start | bytes 49156
  4.0 9.5 %copy-start = (f32[32,32,128]{2,1,0:T(8,128)S(1)}, f32[32,32,128]{2,1,0:T(8,128)}, u32[]{:S(2)}) copy-start(f32[32,32,128]{2,1,0:T(8,128)} %p_ref.3) | copy-start | bytes 1572868
  4.0 12.1 %collective-permute-start = (f32[33,8,128]{2,1,0:T(8,128)S(1)}, f32[33,8,128]{2,1,0:T(8,128)S(1)}, u32[]{:S(2)}, u32[]{:S(2)}) collective-permute-start(f32[33,8,128]{2,1,0:T(8,128)S(1)} %get-tuple-element.44.rows_ref.srows_ref), channel_id=1, source_target_pairs={{0,16},{16,0},{1,17},{17,1},{2,18},{18,2},{3,19},{19,3},{4,20},{20... | collective-permute-start | bytes 405512 | tf_op jit(solution)/shard_map/ppermute | solution.py:721
  7.8 12.0 %collective-permute-start.8 = (f32[5,32,128]{2,1,0:T(8,128)S(1)}, f32[5,32,128]{2,1,0:T(8,128)S(1)}, u32[]{:S(2)}, u32[]{:S(2)}) collective-permute-start(f32[5,32,128]{2,1,0:T(8,128)S(1)} %get-tuple-element.53.refs_4_), channel_id=1, source_target_pairs={{0,3},{1,2},{2,1},{3,0},{4,7},{5,6},{6,5},{7,4},{8,11},{9,10},{10,... | collective-permute-start | bytes 245768 | tf_op jit(solution)/shard_map/ppermute | solution.py:721
  8.5 5.0 %collective-permute-start.1 = (f32[2,32,128]{2,1,0:T(8,128)S(1)}, f32[2,32,128]{2,1,0:T(8,128)S(1)}, u32[]{:S(2)}, u32[]{:S(2)}) collective-permute-start(f32[2,32,128]{2,1,0:T(8,128)S(1)} %get-tuple-element.45.inner_ref.sinner_ref), channel_id=1, source_target_pairs={{0,4},{4,0},{8,12},{12,8},{1,5},{5,1},{9,13},{13,9},{2,6},{6,2},{1... | collective-permute-start | bytes 98312 | tf_op jit(solution)/shard_map/ppermute | solution.py:721
  10.1 6.0 %copy-start.4 = (f32[32,32,128]{2,1,0:T(8,128)S(1)}, f32[32,32,128]{2,1,0:T(8,128)}, u32[]{:S(2)}) copy-start(f32[32,32,128]{2,1,0:T(8,128)} %wz_ref.1) | copy-start | bytes 1572868
  10.1 6.0 %collective-permute-start.2 = (f32[2,32,128]{2,1,0:T(8,128)S(1)}, f32[2,32,128]{2,1,0:T(8,128)S(1)}, u32[]{:S(2)}, u32[]{:S(2)}) collective-permute-start(f32[2,32,128]{2,1,0:T(8,128)S(1)} %get-tuple-element.46.outer_ref.souter_ref), channel_id=1, source_target_pairs={{0,12},{4,8},{8,4},{12,0},{1,13},{5,9},{9,5},{13,1},{2,14},{6,10},... | collective-permute-start | bytes 98312 | tf_op jit(solution)/shard_map/ppermute | solution.py:721
  12.5 8.0 %collective-permute-start.7 = (f32[5,32,128]{2,1,0:T(8,128)S(1)}, f32[5,32,128]{2,1,0:T(8,128)S(1)}, u32[]{:S(2)}, u32[]{:S(2)}) collective-permute-start(f32[5,32,128]{2,1,0:T(8,128)S(1)} %get-tuple-element.53.refs_4_), channel_id=1, source_target_pairs={{0,2},{1,3},{2,0},{3,1},{4,6},{5,7},{6,4},{7,5},{8,10},{9,11},{10,... | collective-permute-start | bytes 245768 | tf_op jit(solution)/shard_map/ppermute | solution.py:721
  13.5 7.1 %collective-permute-start.6 = (f32[5,32,128]{2,1,0:T(8,128)S(1)}, f32[5,32,128]{2,1,0:T(8,128)S(1)}, u32[]{:S(2)}, u32[]{:S(2)}) collective-permute-start(f32[5,32,128]{2,1,0:T(8,128)S(1)} %get-tuple-element.53.refs_4_), channel_id=1, source_target_pairs={{0,1},{1,0},{2,3},{3,2},{4,5},{5,4},{6,7},{7,6},{8,9},{9,8},{10,11... | collective-permute-start | bytes 245768 | tf_op jit(solution)/shard_map/ppermute | solution.py:721
  13.5 2.6 %copy-start.6 = (f32[32,128]{1,0:T(8,128)S(1)}, f32[32,128]{1,0:T(8,128)}, u32[]{:S(2)}) copy-start(f32[32,128]{1,0:T(8,128)} %sx_ref.3) | copy-start | bytes 49156
  13.5 2.6 %copy-start.7 = (f32[32,128]{1,0:T(8,128)S(1)}, f32[32,128]{1,0:T(8,128)}, u32[]{:S(2)}) copy-start(f32[32,128]{1,0:T(8,128)} %sy_ref.3) | copy-start | bytes 49156
  17.6 3.8 %collective-permute-start.5 = (f32[4,32,128]{2,1,0:T(8,128)S(1)}, f32[4,32,128]{2,1,0:T(8,128)S(1)}, u32[]{:S(2)}, u32[]{:S(2)}) collective-permute-start(f32[4,32,128]{2,1,0:T(8,128)S(1)} %get-tuple-element.52.refs_0_), channel_id=1, source_target_pairs={{0,3},{1,2},{2,1},{3,0},{4,7},{5,6},{6,5},{7,4},{8,11},{9,10},{10,... | collective-permute-start | bytes 196616 | tf_op jit(solution)/shard_map/ppermute | solution.py:721
  18.8 4.6 %collective-permute-start.4 = (f32[4,32,128]{2,1,0:T(8,128)S(1)}, f32[4,32,128]{2,1,0:T(8,128)S(1)}, u32[]{:S(2)}, u32[]{:S(2)}) collective-permute-start(f32[4,32,128]{2,1,0:T(8,128)S(1)} %get-tuple-element.52.refs_0_), channel_id=1, source_target_pairs={{0,2},{1,3},{2,0},{3,1},{4,6},{5,7},{6,4},{7,5},{8,10},{9,11},{10,... | collective-permute-start | bytes 196616 | tf_op jit(solution)/shard_map/ppermute | solution.py:721
  19.8 3.7 %collective-permute-start.3 = (f32[4,32,128]{2,1,0:T(8,128)S(1)}, f32[4,32,128]{2,1,0:T(8,128)S(1)}, u32[]{:S(2)}, u32[]{:S(2)}) collective-permute-start(f32[4,32,128]{2,1,0:T(8,128)S(1)} %get-tuple-element.52.refs_0_), channel_id=1, source_target_pairs={{0,1},{1,0},{2,3},{3,2},{4,5},{5,4},{6,7},{7,6},{8,9},{9,8},{10,11... | collective-permute-start | bytes 196616 | tf_op jit(solution)/shard_map/ppermute | solution.py:721
  24.9 7.0 %collective-permute-start.9 = (f32[32,8,128]{2,1,0:T(8,128)S(1)}, f32[32,8,128]{2,1,0:T(8,128)S(1)}, u32[]{:S(2)}, u32[]{:S(2)}) collective-permute-start(f32[32,8,128]{2,1,0:T(8,128)S(1)} %get-tuple-element.60.rows_ref), channel_id=1, source_target_pairs={{0,16},{16,0},{1,17},{17,1},{2,18},{18,2},{3,19},{19,3},{4,20},{20... | collective-permute-start | bytes 393224 | tf_op jit(solution)/shard_map/ppermute | solution.py:721
  25.5 5.9 %collective-permute-start.10 = (f32[1,32,128]{2,1,0:T(8,128)S(1)}, f32[1,32,128]{2,1,0:T(8,128)S(1)}, u32[]{:S(2)}, u32[]{:S(2)}) collective-permute-start(f32[1,32,128]{2,1,0:T(8,128)S(1)} %get-tuple-element.61.inner_ref), channel_id=1, source_target_pairs={{0,4},{4,0},{8,12},{12,8},{1,5},{5,1},{9,13},{13,9},{2,6},{6,2},{1... | collective-permute-start | bytes 49160 | tf_op jit(solution)/shard_map/ppermute | solution.py:721
  26.4 5.5 %collective-permute-start.11 = (f32[1,32,128]{2,1,0:T(8,128)S(1)}, f32[1,32,128]{2,1,0:T(8,128)S(1)}, u32[]{:S(2)}, u32[]{:S(2)}) collective-permute-start(f32[1,32,128]{2,1,0:T(8,128)S(1)} %get-tuple-element.62.outer_ref), channel_id=1, source_target_pairs={{0,12},{4,8},{8,4},{12,0},{1,13},{5,9},{9,5},{13,1},{2,14},{6,10},... | collective-permute-start | bytes 49160 | tf_op jit(solution)/shard_map/ppermute | solution.py:721
  33.4 4.4 %collective-permute-start.14 = (f32[4,32,128]{2,1,0:T(8,128)S(1)}, f32[4,32,128]{2,1,0:T(8,128)S(1)}, u32[]{:S(2)}, u32[]{:S(2)}) collective-permute-start(f32[4,32,128]{2,1,0:T(8,128)S(1)} %get-tuple-element.67.refs_0_), channel_id=1, source_target_pairs={{0,3},{1,2},{2,1},{3,0},{4,7},{5,6},{6,5},{7,4},{8,11},{9,10},{10,... | collective-permute-start | bytes 196616 | tf_op jit(solution)/shard_map/ppermute | solution.py:721
  33.5 5.0 %collective-permute-start.13 = (f32[4,32,128]{2,1,0:T(8,128)S(1)}, f32[4,32,128]{2,1,0:T(8,128)S(1)}, u32[]{:S(2)}, u32[]{:S(2)}) collective-permute-start(f32[4,32,128]{2,1,0:T(8,128)S(1)} %get-tuple-element.67.refs_0_), channel_id=1, source_target_pairs={{0,2},{1,3},{2,0},{3,1},{4,6},{5,7},{6,4},{7,5},{8,10},{9,11},{10,... | collective-permute-start | bytes 196616 | tf_op jit(solution)/shard_map/ppermute | solution.py:721
  34.6 3.9 %collective-permute-start.12 = (f32[4,32,128]{2,1,0:T(8,128)S(1)}, f32[4,32,128]{2,1,0:T(8,128)S(1)}, u32[]{:S(2)}, u32[]{:S(2)}) collective-permute-start(f32[4,32,128]{2,1,0:T(8,128)S(1)} %get-tuple-element.67.refs_0_), channel_id=1, source_target_pairs={{0,1},{1,0},{2,3},{3,2},{4,5},{5,4},{6,7},{7,6},{8,9},{9,8},{10,11... | collective-permute-start | bytes 196616 | tf_op jit(solution)/shard_map/ppermute | solution.py:721

commit v3 on v2

--- a/solution.py
+++ b/solution.py
@@ -17,7 +17,7 @@
 CD = div_coef / 12.0
 ROWS = 8
 SLOT = 4
-UNROLL = 4
+UNROLL = 8
 CHUNKS = 4
 
 
@@ -272,7 +272,7 @@
         )
         return state
 
-    lax.fori_loop(0, levels, step, 0, unroll=UNROLL)
+    lax.fori_loop(0, levels, step, 0, unroll=2 * UNROLL)
     rows_ref[levels] = ends
     down, up = lane_payload(pres, wind, jac)
     put_pair(inner_ref, outer_ref, 0, down, up)

time: 39.8 us -> 38.2 us (0.960)
  Pallas kernels: 15.4 us -> 12.4 us
  waiting for transfers between devices: 5.01 us -> 7.53 us
  starting transfers between devices: 16.8 us -> 15.7 us
    pallas_call x9, Pallas kernels: 15.4 us -> 12.4 us  [call(): pl.pallas_call(kernel, out_shape=[pltpu.VMEM(s, jnp.float32) if k in keep...]
    ppermute x15, waiting for transfers between devices: 5.01 us -> 7.53 us  [swap(): return lax.ppermute(value, axis, [(i, partner(i)) for i in range(count)])]
    ppermute x15, starting transfers between devices: 16.8 us -> 15.7 us  [swap(): return lax.ppermute(value, axis, [(i, partner(i)) for i in range(count)])]
  transfers between devices with their start and end apart: 15 -> 15, of which waited for: 5 -> 6; matrix products, arithmetic and copies ran while one was open for 4% -> 4% of each run, Pallas kernels for 20% -> 14%
where the time goes in v3:
time: 38.2 us; the launch traced here: 38.1 us
  starting transfers between devices  15.7 us (41%)
  Pallas kernels  12.4 us (32%)
  waiting for transfers between devices  7.53 us (20%)
  local copies, waits for them, and re-layouts  1.62 us (4%)
  between operations  0.82 us (2%)
    ppermute x15, starting transfers between devices, swap(): return lax.ppermute(value, axis, [(i, partner(i)) for i in range(count)])  15.7 us
    pallas_call x9, Pallas kernels, call(): pl.pallas_call(kernel, out_shape=[pltpu.VMEM(s, jnp.float32) if k in keep...  12.4 us
    ppermute x15, waiting for transfers between devices, swap(): return lax.ppermute(value, axis, [(i, partner(i)) for i in range(count)])  7.53 us
    unnamed x18, local copies, waits for them, and re-layouts  1.62 us
  transfers between devices with their start and end apart: 15, of which 6 were waited for; matrix products, arithmetic and copies ran while one was open for 4% of the time, Pallas kernels for 14%

profile of v3, /device:TPU:0, one launch (start us, length us, event | category | flops | bytes accessed | tf_op | source)
XLA Modules:
  0.0 38.1 jit_solution(5409727559119949742)
XLA Ops:
  0.7 2.7 %start.1 = (f32[33,8,128]{2,1,0:T(8,128)S(1)}, f32[2,32,128]{2,1,0:T(8,128)S(1)}, f32[2,32,128]{2,1,0:T(8,128)S(1)}, f32[2,32,128]{2,1,0:T(8,128)S(1)}) custom-call(f32[32,32,128]{2,1,0:T(8,128)} %p_ref.3, f32[32,32,128]{2,1,0:T(8,128)} %wx_hbm.1, f32[32,32,128]{2,1,0:T(8,128)} %wy_hbm.1, f32[32,128]{1,0:T(8,128)} %jac_ref.9), custom_call_target="tpu_custom_call" | custom-call | flops 3645440 | bytes 1822720 | tf_op jit(solution)/shard_map/start/pallas_call | solution.py:702
  3.4 3.0 %collective-permute-start = (f32[33,8,128]{2,1,0:T(8,128)S(1)}, f32[33,8,128]{2,1,0:T(8,128)S(1)}, u32[]{:S(2)}, u32[]{:S(2)}) collective-permute-start(f32[33,8,128]{2,1,0:T(8,128)S(1)} %get-tuple-element.44.rows_ref.srows_ref), channel_id=1, source_target_pairs={{0,16},{16,0},{1,17},{17,1},{2,18},{18,2},{3,19},{19,3},{4,20},{20... | collective-permute-start | bytes 405512 | tf_op jit(solution)/shard_map/ppermute | solution.py:721
  6.4 0.7 %factor.1 = (f32[32,32,128]{2,1,0:T(8,128)S(1)}, f32[32,32,128]{2,1,0:T(8,128)S(1)}, f32[32,32,128]{2,1,0:T(8,128)S(1)}, f32[32,32,128]{2,1,0:T(8,128)S(1)}, f32[5,32,128]{2,1,0:T(8,128)S(1)}) custom-call(f32[32,32,128]{2,1,0:T(8,128)S(1)} %copy-done.5), custom_call_target="tpu_custom_call" | custom-call | flops 5406720 | bytes 2703360 | tf_op jit(solution)/shard_map/factor/pallas_call | solution.py:702
  7.1 0.7 %collective-permute-start.8 = (f32[5,32,128]{2,1,0:T(8,128)S(1)}, f32[5,32,128]{2,1,0:T(8,128)S(1)}, u32[]{:S(2)}, u32[]{:S(2)}) collective-permute-start(f32[5,32,128]{2,1,0:T(8,128)S(1)} %get-tuple-element.53.refs_4_), channel_id=1, source_target_pairs={{0,3},{1,2},{2,1},{3,0},{4,7},{5,6},{6,5},{7,4},{8,11},{9,10},{10,... | collective-permute-start | bytes 245768 | tf_op jit(solution)/shard_map/ppermute | solution.py:721
  7.9 1.6 %collective-permute-start.1 = (f32[2,32,128]{2,1,0:T(8,128)S(1)}, f32[2,32,128]{2,1,0:T(8,128)S(1)}, u32[]{:S(2)}, u32[]{:S(2)}) collective-permute-start(f32[2,32,128]{2,1,0:T(8,128)S(1)} %get-tuple-element.45.inner_ref.sinner_ref), channel_id=1, source_target_pairs={{0,4},{4,0},{8,12},{12,8},{1,5},{5,1},{9,13},{13,9},{2,6},{6,2},{1... | collective-permute-start | bytes 98312 | tf_op jit(solution)/shard_map/ppermute | solution.py:721
  9.4 2.5 %collective-permute-start.2 = (f32[2,32,128]{2,1,0:T(8,128)S(1)}, f32[2,32,128]{2,1,0:T(8,128)S(1)}, u32[]{:S(2)}, u32[]{:S(2)}) collective-permute-start(f32[2,32,128]{2,1,0:T(8,128)S(1)} %get-tuple-element.46.outer_ref.souter_ref), channel_id=1, source_target_pairs={{0,12},{4,8},{8,4},{12,0},{1,13},{5,9},{9,5},{13,1},{2,14},{6,10},... | collective-permute-start | bytes 98312 | tf_op jit(solution)/shard_map/ppermute | solution.py:721
  11.9 0.9 %collective-permute-start.7 = (f32[5,32,128]{2,1,0:T(8,128)S(1)}, f32[5,32,128]{2,1,0:T(8,128)S(1)}, u32[]{:S(2)}, u32[]{:S(2)}) collective-permute-start(f32[5,32,128]{2,1,0:T(8,128)S(1)} %get-tuple-element.53.refs_4_), channel_id=1, source_target_pairs={{0,2},{1,3},{2,0},{3,1},{4,6},{5,7},{6,4},{7,5},{8,10},{9,11},{10,... | collective-permute-start | bytes 245768 | tf_op jit(solution)/shard_map/ppermute | solution.py:721
  12.9 1.4 %interior.2 = (f32[32,32,128]{2,1,0:T(8,128)S(1)}, f32[32,32,128]{2,1,0:T(8,128)S(1)}, f32[32,32,128]{2,1,0:T(8,128)S(1)}) custom-call(f32[32,32,128]{2,1,0:T(8,128)S(1)} %copy-done, f32[32,32,128]{2,1,0:T(8,128)S(1)} %copy-done.1, f32[32,32,128]{2,1,0:T(8,128)S(1)} %copy-done.2, f32[32,128]{1,0:T(8,128)S(1)} %copy-done.3), custom_call_target="tpu_custom_call" | custom-call | flops 6324224 | bytes 3162112 | tf_op jit(solution)/shard_map/interior/pallas_call | solution.py:702
  14.3 0.9 %collective-permute-done.2.got_outer_ref.got_souter_ref = f32[2,32,128]{2,1,0:T(8,128)S(1)} collective-permute-done((f32[2,32,128]{2,1,0:T(8,128)S(1)}, f32[2,32,128]{2,1,0:T(8,128)S(1)}, u32[]{:S(2)}, u32[]{:S(2)}) %collective-permute-start.2) | collective-permute-done | bytes 32800 | tf_op jit(solution)/shard_map/ppermute | solution.py:721
  15.2 1.5 %sweep.2 = (f32[32,32,128]{2,1,0:T(8,128)S(1)}, f32[32,32,128]{2,1,0:T(8,128)S(1)}, f32[32,32,128]{2,1,0:T(8,128)S(1)}, f32[32,32,128]{2,1,0:T(8,128)S(1)}, f32[4,32,128]{2,1,0:T(8,128)S(1)}) custom-call(f32[32,32,128]{2,1,0:T(8,128)S(1)} %copy-done, f32[32,32,128]{2,1,0:T(8,128)S(1)} %get-tuple-element.37.nxc_ref, ...), custom_call_target="tpu_custom_call" | custom-call | flops 14483456 | bytes 7241728 | tf_op jit(solution)/shard_map/sweep/pallas_call | solution.py:702
  17.1 1.1 %collective-permute-start.4 = (f32[4,32,128]{2,1,0:T(8,128)S(1)}, f32[4,32,128]{2,1,0:T(8,128)S(1)}, u32[]{:S(2)}, u32[]{:S(2)}) collective-permute-start(f32[4,32,128]{2,1,0:T(8,128)S(1)} %get-tuple-element.52.refs_0_), channel_id=1, source_target_pairs={{0,2},{1,3},{2,0},{3,1},{4,6},{5,7},{6,4},{7,5},{8,10},{9,11},{10,... | collective-permute-start | bytes 196616 | tf_op jit(solution)/shard_map/ppermute | solution.py:721
  19.1 2.0 %collective-permute-done.5.refs_3_ = f32[4,32,128]{2,1,0:T(8,128)S(1)} collective-permute-done((f32[4,32,128]{2,1,0:T(8,128)S(1)}, f32[4,32,128]{2,1,0:T(8,128)S(1)}, u32[]{:S(2)}, u32[]{:S(2)}) %collective-permute-start.5) | collective-permute-done | bytes 65568 | tf_op jit(solution)/shard_map/ppermute | solution.py:721
  21.2 1.4 %collective-permute-done.4.refs_2_ = f32[4,32,128]{2,1,0:T(8,128)S(1)} collective-permute-done((f32[4,32,128]{2,1,0:T(8,128)S(1)}, f32[4,32,128]{2,1,0:T(8,128)S(1)}, u32[]{:S(2)}, u32[]{:S(2)}) %collective-permute-start.4) | collective-permute-done | bytes 65568 | tf_op jit(solution)/shard_map/ppermute | solution.py:721
  22.6 1.5 %finish.1 = (f32[32,32,128]{2,1,0:T(8,128)S(1)}, f32[32,32,128]{2,1,0:T(8,128)S(1)}, f32[32,8,128]{2,1,0:T(8,128)S(1)}, f32[1,32,128]{2,1,0:T(8,128)S(1)}, f32[1...) custom-call(f32[32,32,128]{2,1,0:T(8,128)S(1)} %get-tuple-element.47.y_ref, f32[32,32,128]{2,1,0:T(8,128)S(1)} %get-tuple-element.48.q_ref, ...), custom_call_target="tpu_custom_call" | custom-call | flops 9011200 | bytes 4505600 | tf_op jit(solution)/shard_map/finish/pallas_call | solution.py:702
  24.7 2.5 %collective-permute-start.11 = (f32[1,32,128]{2,1,0:T(8,128)S(1)}, f32[1,32,128]{2,1,0:T(8,128)S(1)}, u32[]{:S(2)}, u32[]{:S(2)}) collective-permute-start(f32[1,32,128]{2,1,0:T(8,128)S(1)} %get-tuple-element.62.outer_ref), channel_id=1, source_target_pairs={{0,12},{4,8},{8,4},{12,0},{1,13},{5,9},{9,5},{13,1},{2,14},{6,10},... | collective-permute-start | bytes 49160 | tf_op jit(solution)/shard_map/ppermute | solution.py:721
  27.2 1.4 %interior.3 = (f32[32,32,128]{2,1,0:T(8,128)S(1)}, f32[32,32,128]{2,1,0:T(8,128)S(1)}, f32[32,32,128]{2,1,0:T(8,128)S(1)}) custom-call(f32[32,32,128]{2,1,0:T(8,128)S(1)} %get-tuple-element.54.p_ref, f32[32,32,128]{2,1,0:T(8,128)S(1)} %get-tuple-element.50.wx_ref, f32[32,32,128]{2,1,0:T(8,128)S(1)} %get-tuple-element.51.wy_ref, f32[32,128]{1,0:T(8,128)S(1)} %copy-done.3), custom_call_target="tpu_custom_call" | custom-call | flops 6324224 | bytes 3162112 | tf_op jit(solution)/shard_map/interior/pallas_call | solution.py:702
  28.7 1.6 %collective-permute-done.11.got_outer_ref = f32[1,32,128]{2,1,0:T(8,128)S(1)} collective-permute-done((f32[1,32,128]{2,1,0:T(8,128)S(1)}, f32[1,32,128]{2,1,0:T(8,128)S(1)}, u32[]{:S(2)}, u32[]{:S(2)}) %collective-permute-start.11) | collective-permute-done | bytes 16416 | tf_op jit(solution)/shard_map/ppermute | solution.py:721
  30.3 1.5 %sweep.3 = (f32[32,32,128]{2,1,0:T(8,128)S(1)}, f32[32,32,128]{2,1,0:T(8,128)S(1)}, f32[32,32,128]{2,1,0:T(8,128)S(1)}, f32[32,32,128]{2,1,0:T(8,128)S(1)}, f32[4,32,128]{2,1,0:T(8,128)S(1)}) custom-call(f32[32,32,128]{2,1,0:T(8,128)S(1)} %get-tuple-element.54.p_ref, f32[32,32,128]{2,1,0:T(8,128)S(1)} %get-tuple-element.55.nxc_ref, ...), custom_call_target="tpu_custom_call" | custom-call | flops 14336000 | bytes 7168000 | tf_op jit(solution)/shard_map/sweep/pallas_call | solution.py:702
  31.8 1.1 %collective-permute-start.13 = (f32[4,32,128]{2,1,0:T(8,128)S(1)}, f32[4,32,128]{2,1,0:T(8,128)S(1)}, u32[]{:S(2)}, u32[]{:S(2)}) collective-permute-start(f32[4,32,128]{2,1,0:T(8,128)S(1)} %get-tuple-element.67.refs_0_), channel_id=1, source_target_pairs={{0,2},{1,3},{2,0},{3,1},{4,6},{5,7},{6,4},{7,5},{8,10},{9,11},{10,... | collective-permute-start | bytes 196616 | tf_op jit(solution)/shard_map/ppermute | solution.py:721
  32.9 0.8 %collective-permute-start.12 = (f32[4,32,128]{2,1,0:T(8,128)S(1)}, f32[4,32,128]{2,1,0:T(8,128)S(1)}, u32[]{:S(2)}, u32[]{:S(2)}) collective-permute-start(f32[4,32,128]{2,1,0:T(8,128)S(1)} %get-tuple-element.67.refs_0_), channel_id=1, source_target_pairs={{0,1},{1,0},{2,3},{3,2},{4,5},{5,4},{6,7},{7,6},{8,9},{9,8},{10,11... | collective-permute-start | bytes 196616 | tf_op jit(solution)/shard_map/ppermute | solution.py:721
  33.7 0.8 %copy.12 = f32[32,32,128]{2,1,0:T(8,128)} copy(f32[32,32,128]{2,1,0:T(8,128)S(1)} %get-tuple-element.70) | data formatting | bytes 1048576
  34.5 0.8 %copy.13 = f32[32,32,128]{2,1,0:T(8,128)} copy(f32[32,32,128]{2,1,0:T(8,128)S(1)} %get-tuple-element.71) | data formatting | bytes 1048576
  35.3 0.8 %collective-permute-done.14.refs_3_ = f32[4,32,128]{2,1,0:T(8,128)S(1)} collective-permute-done((f32[4,32,128]{2,1,0:T(8,128)S(1)}, f32[4,32,128]{2,1,0:T(8,128)S(1)}, u32[]{:S(2)}, u32[]{:S(2)}) %collective-permute-start.14) | collective-permute-done | bytes 65568 | tf_op jit(solution)/shard_map/ppermute | solution.py:721
  36.8 1.2 %last.1 = (f32[32,32,128]{2,1,0:T(8,128)}, f32[32,32,128]{2,1,0:T(8,128)}) custom-call(f32[32,32,128]{2,1,0:T(8,128)S(1)} %get-tuple-element.65.y_ref, f32[32,32,128]{2,1,0:T(8,128)S(1)} %get-tuple-element.48.q_ref, f32[32,32,128]{2,1,0:T(8,128)S(1)} %get-tuple-element.41.i_ref, f32[32,32,128]{2,1,0:T(8,128)S(1)} %get-tuple-element.66.ps_ref, ...), custom_call_target="tpu_custom_call" | custom-call | flops 7471104 | bytes 3735552 | tf_op jit(solution)/shard_map/last/pallas_call | solution.py:702
  (33 shorter events, 2.8 us)
Async XLA Ops:
  0.6 5.8 %copy-start.5 = (f32[32,32,128]{2,1,0:T(8,128)S(1)}, f32[32,32,128]{2,1,0:T(8,128)}, u32[]{:S(2)}) copy-start(f32[32,32,128]{2,1,0:T(8,128)} %s_ref.1) | copy-start | bytes 1572868
  0.6 12.2 %copy-start.1 = (f32[32,32,128]{2,1,0:T(8,128)S(1)}, f32[32,32,128]{2,1,0:T(8,128)}, u32[]{:S(2)}) copy-start(f32[32,32,128]{2,1,0:T(8,128)} %wx_hbm.1) | copy-start | bytes 1572868
  0.7 12.2 %copy-start.2 = (f32[32,32,128]{2,1,0:T(8,128)S(1)}, f32[32,32,128]{2,1,0:T(8,128)}, u32[]{:S(2)}) copy-start(f32[32,32,128]{2,1,0:T(8,128)} %wy_hbm.1) | copy-start | bytes 1572868
  0.7 12.2 %copy-start.3 = (f32[32,128]{1,0:T(8,128)S(1)}, f32[32,128]{1,0:T(8,128)}, u32[]{:S(2)}) copy-start(f32[32,128]{1,0:T(8,128)} %jac_ref.9) | copy-start | bytes 49156
  3.3 9.5 %copy-start = (f32[32,32,128]{2,1,0:T(8,128)S(1)}, f32[32,32,128]{2,1,0:T(8,128)}, u32[]{:S(2)}) copy-start(f32[32,32,128]{2,1,0:T(8,128)} %p_ref.3) | copy-start | bytes 1572868
  3.4 11.8 %collective-permute-start = (f32[33,8,128]{2,1,0:T(8,128)S(1)}, f32[33,8,128]{2,1,0:T(8,128)S(1)}, u32[]{:S(2)}, u32[]{:S(2)}) collective-permute-start(f32[33,8,128]{2,1,0:T(8,128)S(1)} %get-tuple-element.44.rows_ref.srows_ref), channel_id=1, source_target_pairs={{0,16},{16,0},{1,17},{17,1},{2,18},{18,2},{3,19},{19,3},{4,20},{20... | collective-permute-start | bytes 405512 | tf_op jit(solution)/shard_map/ppermute | solution.py:721
  7.1 11.1 %collective-permute-start.8 = (f32[5,32,128]{2,1,0:T(8,128)S(1)}, f32[5,32,128]{2,1,0:T(8,128)S(1)}, u32[]{:S(2)}, u32[]{:S(2)}) collective-permute-start(f32[5,32,128]{2,1,0:T(8,128)S(1)} %get-tuple-element.53.refs_4_), channel_id=1, source_target_pairs={{0,3},{1,2},{2,1},{3,0},{4,7},{5,6},{6,5},{7,4},{8,11},{9,10},{10,... | collective-permute-start | bytes 245768 | tf_op jit(solution)/shard_map/ppermute | solution.py:721
  7.9 5.0 %collective-permute-start.1 = (f32[2,32,128]{2,1,0:T(8,128)S(1)}, f32[2,32,128]{2,1,0:T(8,128)S(1)}, u32[]{:S(2)}, u32[]{:S(2)}) collective-permute-start(f32[2,32,128]{2,1,0:T(8,128)S(1)} %get-tuple-element.45.inner_ref.sinner_ref), channel_id=1, source_target_pairs={{0,4},{4,0},{8,12},{12,8},{1,5},{5,1},{9,13},{13,9},{2,6},{6,2},{1... | collective-permute-start | bytes 98312 | tf_op jit(solution)/shard_map/ppermute | solution.py:721
  9.4 5.8 %copy-start.4 = (f32[32,32,128]{2,1,0:T(8,128)S(1)}, f32[32,32,128]{2,1,0:T(8,128)}, u32[]{:S(2)}) copy-start(f32[32,32,128]{2,1,0:T(8,128)} %wz_ref.1) | copy-start | bytes 1572868
  9.4 5.8 %collective-permute-start.2 = (f32[2,32,128]{2,1,0:T(8,128)S(1)}, f32[2,32,128]{2,1,0:T(8,128)S(1)}, u32[]{:S(2)}, u32[]{:S(2)}) collective-permute-start(f32[2,32,128]{2,1,0:T(8,128)S(1)} %get-tuple-element.46.outer_ref.souter_ref), channel_id=1, source_target_pairs={{0,12},{4,8},{8,4},{12,0},{1,13},{5,9},{9,5},{13,1},{2,14},{6,10},... | collective-permute-start | bytes 98312 | tf_op jit(solution)/shard_map/ppermute | solution.py:721
  11.9 7.2 %collective-permute-start.7 = (f32[5,32,128]{2,1,0:T(8,128)S(1)}, f32[5,32,128]{2,1,0:T(8,128)S(1)}, u32[]{:S(2)}, u32[]{:S(2)}) collective-permute-start(f32[5,32,128]{2,1,0:T(8,128)S(1)} %get-tuple-element.53.refs_4_), channel_id=1, source_target_pairs={{0,2},{1,3},{2,0},{3,1},{4,6},{5,7},{6,4},{7,5},{8,10},{9,11},{10,... | collective-permute-start | bytes 245768 | tf_op jit(solution)/shard_map/ppermute | solution.py:721
  12.8 6.3 %collective-permute-start.6 = (f32[5,32,128]{2,1,0:T(8,128)S(1)}, f32[5,32,128]{2,1,0:T(8,128)S(1)}, u32[]{:S(2)}, u32[]{:S(2)}) collective-permute-start(f32[5,32,128]{2,1,0:T(8,128)S(1)} %get-tuple-element.53.refs_4_), channel_id=1, source_target_pairs={{0,1},{1,0},{2,3},{3,2},{4,5},{5,4},{6,7},{7,6},{8,9},{9,8},{10,11... | collective-permute-start | bytes 245768 | tf_op jit(solution)/shard_map/ppermute | solution.py:721
  12.9 2.3 %copy-start.6 = (f32[32,128]{1,0:T(8,128)S(1)}, f32[32,128]{1,0:T(8,128)}, u32[]{:S(2)}) copy-start(f32[32,128]{1,0:T(8,128)} %sx_ref.3) | copy-start | bytes 49156
  12.9 2.3 %copy-start.7 = (f32[32,128]{1,0:T(8,128)S(1)}, f32[32,128]{1,0:T(8,128)}, u32[]{:S(2)}) copy-start(f32[32,128]{1,0:T(8,128)} %sy_ref.3) | copy-start | bytes 49156
  16.7 4.5 %collective-permute-start.5 = (f32[4,32,128]{2,1,0:T(8,128)S(1)}, f32[4,32,128]{2,1,0:T(8,128)S(1)}, u32[]{:S(2)}, u32[]{:S(2)}) collective-permute-start(f32[4,32,128]{2,1,0:T(8,128)S(1)} %get-tuple-element.52.refs_0_), channel_id=1, source_target_pairs={{0,3},{1,2},{2,1},{3,0},{4,7},{5,6},{6,5},{7,4},{8,11},{9,10},{10,... | collective-permute-start | bytes 196616 | tf_op jit(solution)/shard_map/ppermute | solution.py:721
  17.1 5.4 %collective-permute-start.4 = (f32[4,32,128]{2,1,0:T(8,128)S(1)}, f32[4,32,128]{2,1,0:T(8,128)S(1)}, u32[]{:S(2)}, u32[]{:S(2)}) collective-permute-start(f32[4,32,128]{2,1,0:T(8,128)S(1)} %get-tuple-element.52.refs_0_), channel_id=1, source_target_pairs={{0,2},{1,3},{2,0},{3,1},{4,6},{5,7},{6,4},{7,5},{8,10},{9,11},{10,... | collective-permute-start | bytes 196616 | tf_op jit(solution)/shard_map/ppermute | solution.py:721
  18.2 4.3 %collective-permute-start.3 = (f32[4,32,128]{2,1,0:T(8,128)S(1)}, f32[4,32,128]{2,1,0:T(8,128)S(1)}, u32[]{:S(2)}, u32[]{:S(2)}) collective-permute-start(f32[4,32,128]{2,1,0:T(8,128)S(1)} %get-tuple-element.52.refs_0_), channel_id=1, source_target_pairs={{0,1},{1,0},{2,3},{3,2},{4,5},{5,4},{6,7},{7,6},{8,9},{9,8},{10,11... | collective-permute-start | bytes 196616 | tf_op jit(solution)/shard_map/ppermute | solution.py:721
  24.1 6.2 %collective-permute-start.9 = (f32[32,8,128]{2,1,0:T(8,128)S(1)}, f32[32,8,128]{2,1,0:T(8,128)S(1)}, u32[]{:S(2)}, u32[]{:S(2)}) collective-permute-start(f32[32,8,128]{2,1,0:T(8,128)S(1)} %get-tuple-element.60.rows_ref), channel_id=1, source_target_pairs={{0,16},{16,0},{1,17},{17,1},{2,18},{18,2},{3,19},{19,3},{4,20},{20... | collective-permute-start | bytes 393224 | tf_op jit(solution)/shard_map/ppermute | solution.py:721
  24.7 4.0 %collective-permute-start.10 = (f32[1,32,128]{2,1,0:T(8,128)S(1)}, f32[1,32,128]{2,1,0:T(8,128)S(1)}, u32[]{:S(2)}, u32[]{:S(2)}) collective-permute-start(f32[1,32,128]{2,1,0:T(8,128)S(1)} %get-tuple-element.61.inner_ref), channel_id=1, source_target_pairs={{0,4},{4,0},{8,12},{12,8},{1,5},{5,1},{9,13},{13,9},{2,6},{6,2},{1... | collective-permute-start | bytes 49160 | tf_op jit(solution)/shard_map/ppermute | solution.py:721
  24.7 5.5 %collective-permute-start.11 = (f32[1,32,128]{2,1,0:T(8,128)S(1)}, f32[1,32,128]{2,1,0:T(8,128)S(1)}, u32[]{:S(2)}, u32[]{:S(2)}) collective-permute-start(f32[1,32,128]{2,1,0:T(8,128)S(1)} %get-tuple-element.62.outer_ref), channel_id=1, source_target_pairs={{0,12},{4,8},{8,4},{12,0},{1,13},{5,9},{9,5},{13,1},{2,14},{6,10},... | collective-permute-start | bytes 49160 | tf_op jit(solution)/shard_map/ppermute | solution.py:721
  31.8 4.4 %collective-permute-start.14 = (f32[4,32,128]{2,1,0:T(8,128)S(1)}, f32[4,32,128]{2,1,0:T(8,128)S(1)}, u32[]{:S(2)}, u32[]{:S(2)}) collective-permute-start(f32[4,32,128]{2,1,0:T(8,128)S(1)} %get-tuple-element.67.refs_0_), channel_id=1, source_target_pairs={{0,3},{1,2},{2,1},{3,0},{4,7},{5,6},{6,5},{7,4},{8,11},{9,10},{10,... | collective-permute-start | bytes 196616 | tf_op jit(solution)/shard_map/ppermute | solution.py:721
  31.8 5.0 %collective-permute-start.13 = (f32[4,32,128]{2,1,0:T(8,128)S(1)}, f32[4,32,128]{2,1,0:T(8,128)S(1)}, u32[]{:S(2)}, u32[]{:S(2)}) collective-permute-start(f32[4,32,128]{2,1,0:T(8,128)S(1)} %get-tuple-element.67.refs_0_), channel_id=1, source_target_pairs={{0,2},{1,3},{2,0},{3,1},{4,6},{5,7},{6,4},{7,5},{8,10},{9,11},{10,... | collective-permute-start | bytes 196616 | tf_op jit(solution)/shard_map/ppermute | solution.py:721
  32.9 3.9 %collective-permute-start.12 = (f32[4,32,128]{2,1,0:T(8,128)S(1)}, f32[4,32,128]{2,1,0:T(8,128)S(1)}, u32[]{:S(2)}, u32[]{:S(2)}) collective-permute-start(f32[4,32,128]{2,1,0:T(8,128)S(1)} %get-tuple-element.67.refs_0_), channel_id=1, source_target_pairs={{0,1},{1,0},{2,3},{3,2},{4,5},{5,4},{6,7},{7,6},{8,9},{9,8},{10,11... | collective-permute-start | bytes 196616 | tf_op jit(solution)/shard_map/ppermute | solution.py:721

commit v4 on v3

--- a/solution.py
+++ b/solution.py
@@ -19,6 +19,7 @@
 SLOT = 4
 UNROLL = 8
 CHUNKS = 4
+COLUMN = 7
 
 
 def lane_index():
@@ -347,11 +348,15 @@
     got_srows_ref,
     got_sinner_ref,
     got_souter_ref,
+    coef_ref,
+    far_ref,
     nx_ref,
     ny_ref,
     ps_ref,
     y_ref,
-    face_ref,
+    near_ref,
+    cross_ref,
+    next_ref,
 ):
     levels, rows, _ = p_ref.shape
     count = rows // ROWS
@@ -430,7 +435,7 @@
 
     zeros = [jnp.zeros((ROWS, 128), jnp.float32)] * count
     here, force = star(0)
-    put_tiles(face_ref, 2, here)
+    bottom = here
 
     def step(level, carry):
         below, here, force, value, first = carry
@@ -442,9 +447,7 @@
         1, levels, step, (zeros, here, force, zeros, zeros), unroll=UNROLL
     )
     value, first = sweep(levels - 1, below, zeros, force, value, first)
-    put_tiles(face_ref, 0, first)
-    put_tiles(face_ref, 1, value)
-    put_tiles(face_ref, 3, here)
+    interface(first, value, bottom, here, coef_ref, far_ref, near_ref, cross_ref, next_ref)
 
 
 def kernel_f(s_ref, r_ref, i_ref, q_ref, v_ref, stat_ref):
@@ -478,108 +481,100 @@
     stat_ref[4] = r_ref[levels - 1]
 
 
-def reduced(blocks, mine, face, stat):
-    faces = [face(j) for j in range(blocks)]
-    stats = [stat(j) for j in range(blocks)]
-    up = [
-        faces[j][1] + vert_coef * stats[j + 1][3] * faces[j][3] if j < blocks - 1 else None
-        for j in range(blocks)
-    ]
-    down = [
-        faces[j][0] - vert_coef * stats[j - 1][4] * faces[j][2] if j > 0 else None
-        for j in range(blocks)
-    ]
-    base, slope = [up[0]], [stats[0][2]]
-    scale, known = [None], [None]
-    for j in range(1, blocks):
-        near, link, far = stats[j][0], stats[j][1], stats[j][2]
-        scale.append(1.0 / (1.0 - near * slope[j - 1]))
-        known.append(scale[j] * (down[j] + near * base[j - 1]))
-        if j < blocks - 1:
-            base.append(up[j] + link * (base[j - 1] + slope[j - 1] * known[j]))
-            slope.append(far + link * link * slope[j - 1] * scale[j])
-    zero = jnp.zeros_like(faces[0][0])
-    above = [None] * blocks + [zero]
-    below = [zero] + [None] * blocks
-    for j in range(blocks - 1, 0, -1):
-        above[j] = known[j] + scale[j] * stats[j][1] * above[j + 1]
-        below[j] = base[j - 1] + slope[j - 1] * above[j]
-    lower, upper, under, over = zero, zero, zero, zero
-    for j in range(blocks):
-        here = mine == j
-        if j > 0:
-            lower = jnp.where(here, below[j], lower)
-            under = jnp.where(
-                here, below[j] - vert_coef * stats[j][3] * faces[j - 1][3], under
-            )
-        if j < blocks - 1:
-            upper = jnp.where(here, above[j + 1], upper)
-            over = jnp.where(
-                here, above[j + 1] + vert_coef * stats[j][4] * faces[j + 1][2], over
-            )
-    return lower, upper, under, over
-
-
-def boundary(blocks, mine, count, face_refs, stat_refs):
-    def solve(t):
+PAIR_COEFS = ("own", "other", "den", "den_end", "den_link", "outer", "total", "facing")
+
+
+def place_in_column():
+    mine = lax.axis_index("lev")
+    return (mine == 0) | (mine == 3), mine < 2, lax.rem(mine, 2) == 0
+
+
+def kernel_s(stat_ref, mate_ref, coef_ref, send_ref):
+    outermost, lower, even = place_in_column()
+    count = stat_ref.shape[1] // ROWS
+    for t in range(count):
         part = slice(ROWS * t, ROWS * (t + 1))
-
-        def read(refs, planes):
-            own = [
-                [ref[k, part, :] for k in range(planes)] for ref in refs
-            ]
-
-            def block(j):
-                out = []
-                for k in range(planes):
-                    value = own[0][k]
-                    for shift in range(1, blocks):
-                        value = jnp.where(mine == (j ^ shift), own[shift][k], value)
-                    out.append(value)
-                return out
-
-            return block
-
-        return reduced(blocks, mine, read(face_refs, 4), read(stat_refs, 5))
-
-    parts = [solve(t) for t in range(count)]
+        mine = [stat_ref[k, part, :] for k in range(5)]
+        mate = [mate_ref[k, part, :] for k in range(5)]
+        outer = [jnp.where(outermost, a, b) for a, b in zip(mine, mate)]
+        inner = [jnp.where(outermost, b, a) for a, b in zip(mine, mate)]
+        outer_end = jnp.where(lower, outer[2], outer[0])
+        end = jnp.where(lower, inner[0], inner[2])
+        centre = jnp.where(lower, inner[2], inner[0])
+        link = inner[1]
+        den = 1.0 / (1.0 - end * outer_end)
+        den_link = den * link
+        weight = outer_end * den_link
+        one, zero = jnp.ones_like(den), jnp.zeros_like(den)
+        coefs = dict(
+            own=jnp.where(outermost, den_link, one),
+            other=jnp.where(outermost, zero, weight),
+            den=den,
+            den_end=den * end,
+            den_link=den_link,
+            outer=outer_end,
+            total=centre + weight * link,
+            facing=vert_coef * jnp.where(even, mate[3], mate[4]),
+        )
+        for k, name in enumerate(PAIR_COEFS):
+            coef_ref[k, part, :] = coefs[name]
+        send_ref[0, part, :] = coefs["total"]
+        send_ref[1, part, :] = vert_coef * jnp.where(lower, inner[4], inner[3])
+
+
+def interface(first, value, star_first, star_last, coef_ref, far_ref, near_ref, cross_ref, next_ref):
+    outermost, lower, even = place_in_column()
+    for t in range(len(first)):
+        part = slice(ROWS * t, ROWS * (t + 1))
+        coef = {name: coef_ref[k, part, :] for k, name in enumerate(PAIR_COEFS)}
+        sign = jnp.where(lower, 1.0, -1.0)
+        star_centre = jnp.where(lower, star_last[t], star_first[t])
+        star_outer = jnp.where(lower, star_first[t], star_last[t])
+        facing = jnp.where(outermost, coef["facing"], far_ref[1, part, :])
+        centre = jnp.where(lower, value[t], first[t]) + sign * facing * star_centre
+        outer = jnp.where(lower, first[t], value[t]) - sign * coef["facing"] * star_outer
+        total = coef["own"] * centre + coef["other"] * outer
+        near_ref[0, part, :] = jnp.where(outermost, centre, outer)
+        near_ref[1, part, :] = jnp.where(even, star_last[t], star_first[t])
+        near_ref[2, part, :] = total
+        cross_ref[0, part, :] = total
+        next_ref[0, part, :] = total
+        next_ref[1, part, :] = star_centre
+
+
+def boundary(count, coef_ref, far_ref, stat_ref, near_ref, got_near_ref, got_cross_ref, got_next_ref):
+    outermost, lower, _ = place_in_column()
+    parts = []
+    for t in range(count):
+        part = slice(ROWS * t, ROWS * (t + 1))
+        coef = {name: coef_ref[k, part, :] for k, name in enumerate(PAIR_COEFS)}
+        far_total = far_ref[0, part, :]
+        own, got = near_ref[0, part, :], got_near_ref[0, part, :]
+        this = near_ref[2, part, :] + got_near_ref[2, part, :]
+        that = got_cross_ref[0, part, :] + got_next_ref[0, part, :]
+        middle = (that + far_total * this) / (1.0 - coef["total"] * far_total)
+        from_outer = jnp.where(outermost, own, got)
+        from_inner = jnp.where(outermost, got, own)
+        between = (
+            coef["den"] * from_inner + coef["den_end"] * from_outer + coef["den_link"] * middle
+        )
+        zero = jnp.zeros_like(own)
+        centre = jnp.where(outermost, between, middle)
+        outer = jnp.where(outermost, zero, from_outer + coef["outer"] * between)
+        mate_star, next_star = got_near_ref[1, part, :], got_next_ref[1, part, :]
+        star_centre = jnp.where(outermost, mate_star, next_star)
+        star_outer = jnp.where(outermost, zero, mate_star)
+        below, above = jnp.where(lower, outer, centre), jnp.where(lower, centre, outer)
+        star_below = jnp.where(lower, star_outer, star_centre)
+        star_above = jnp.where(lower, star_centre, star_outer)
+        under = below - vert_coef * stat_ref[3, part, :] * star_below
+        over = above + vert_coef * stat_ref[4, part, :] * star_above
+        parts.append((below, above, under, over))
     return [[part[k] for part in parts] for k in range(4)]
 
 
-def finish(blocks, count, levels, y_ref, q_ref, i_ref, ps_ref, x_ref, p_ref, face_refs, stat_refs, use):
-    mine = lax.axis_index("lev")
-    lower, upper, under, over = boundary(blocks, mine, count, face_refs, stat_refs)
-
-    def solved(level, above):
-        value = tiles_of(y_ref, level, count)
-        prod = tiles_of(q_ref, level, count)
-        inv = tiles_of(i_ref, level, count)
-        out = [y + q * u + i * a for y, q, u, i, a in zip(value, prod, lower, inv, above)]
-        put_tiles(x_ref, level, out)
-        return out
-
-    def pressed(level, above, below, state):
-        star = tiles_of(ps_ref, level, count)
-        pres = [s - vert_coef * (a - b) for s, a, b in zip(star, above, below)]
-        put_tiles(p_ref, level, pres)
-        return use(level, pres, state)
-
-    def step(index, carry):
-        above, here, state = carry
-        level = levels - 2 - index
-        below = solved(level, here)
-        state = pressed(level + 1, above, below, state)
-        return here, below, state
-
-    top = solved(levels - 1, upper)
-    zeros = [jnp.zeros((ROWS, 128), jnp.float32)] * count
-    above, here, state = lax.fori_loop(0, levels - 1, step, (over, top, (zeros, zeros)))
-    return pressed(0, above, under, state)
-
-
-def finish(blocks, count, levels, y_ref, q_ref, i_ref, ps_ref, x_ref, p_ref, face_refs, stat_refs, use, state, ready=None):
-    mine = lax.axis_index("lev")
-    lower, upper, under, over = boundary(blocks, mine, count, face_refs, stat_refs)
+def finish(count, levels, y_ref, q_ref, i_ref, ps_ref, x_ref, p_ref, column_refs, use, state, ready=None):
+    lower, upper, under, over = boundary(count, *column_refs)
 
     def solved(level, above):
         value = tiles_of(y_ref, level, count)
@@ -617,9 +612,9 @@
     return pressed(0, above, under, state)
 
 
-def kernel_c(blocks, y_ref, q_ref, i_ref, ps_ref, wx_ref, pw_ref, jac_ref, *refs):
-    face_refs, stat_refs = refs[:blocks], refs[blocks : 2 * blocks]
-    x_ref, p_ref, rows_ref, inner_ref, outer_ref, pp_ref = refs[2 * blocks :]
+def kernel_c(y_ref, q_ref, i_ref, ps_ref, wx_ref, pw_ref, jac_ref, *refs):
+    column_refs = refs[:COLUMN]
+    x_ref, p_ref, rows_ref, inner_ref, outer_ref, pp_ref = refs[COLUMN:]
     levels, rows, _ = y_ref.shape
     count = rows // ROWS
     packer = Packer(count)
@@ -633,7 +628,6 @@
         return packer.add(level, pres, state)
 
     state = finish(
-        blocks,
         count,
         levels,
         y_ref,
@@ -642,8 +636,7 @@
         ps_ref,
         x_ref,
         p_ref,
-        face_refs,
-        stat_refs,
+        column_refs,
         use,
         packer.start,
     )
@@ -655,9 +648,9 @@
     put_tiles(pp_ref, 1, pres[1])
 
 
-def kernel_d(blocks, y_ref, q_ref, i_ref, ps_ref, *refs):
-    face_refs, stat_refs = refs[:blocks], refs[blocks : 2 * blocks]
-    x_hbm, p_hbm, x_ref, p_ref, sems = refs[2 * blocks :]
+def kernel_d(y_ref, q_ref, i_ref, ps_ref, *refs):
+    column_refs = refs[:COLUMN]
+    x_hbm, p_hbm, x_ref, p_ref, sems = refs[COLUMN:]
     levels, rows, _ = y_ref.shape
     share = levels // CHUNKS
     copies = []
@@ -674,7 +667,6 @@
             send(1, p_ref, p_hbm, c + 1)
 
     finish(
-        blocks,
         rows // ROWS,
         levels,
         y_ref,
@@ -683,8 +675,7 @@
         ps_ref,
         x_ref,
         p_ref,
-        face_refs,
-        stat_refs,
+        column_refs,
         lambda level, pres, state: state,
         0,
         ready,
@@ -737,21 +728,20 @@
     return got_inner, got_outer
 
 
-def gather_levels(planes):
-    count = lax.axis_size("lev")
-    return [planes] + [
-        swap(planes, "lev", lambda i, shift=shift: i ^ shift) for shift in range(1, count)
-    ]
+def exchange_column(near, cross, following):
+    got_next = swap(following, "lev", lambda i: i ^ 3)
+    got_cross = swap(cross, "lev", lambda i: i ^ 2)
+    got_near = swap(near, "lev", lambda i: i ^ 1)
+    return near, got_near, got_cross, got_next
 
 
 def local(wind_x, wind_y, wind_z, pressure, jacobian, slope_x, slope_y, stiffness):
     field = wind_x.shape
     levels, rows, lanes = field
-    blocks = lax.axis_size("lev")
     plane = (rows, lanes)
     pair = (2,) + plane
     assert lanes == 128 and levels * SLOT == 128 and rows % ROWS == 0
-    assert blocks & (blocks - 1) == 0 and lax.axis_size("gy") % 2 == 0
+    assert lax.axis_size("lev") == 4 and lax.axis_size("gy") % 2 == 0
 
     edge, inner, outer, ends = call(
         kernel_a,
@@ -776,15 +766,17 @@
     rate, inv, prod, gain, stat = call(
         kernel_f, "factor", [field, field, field, field, (5,) + plane], stiffness
     )
-    stats = gather_levels(stat)
+    mate = swap(stat, "lev", lambda i: i ^ 1)
+    coef, send = call(kernel_s, "pairs", [(len(PAIR_COEFS),) + plane, pair], stat, mate)
+    far = swap(send, "lev", lambda i: i ^ 2)
     for substep in range(SUBSTEPS):
         closed = call(
             kernel_m, "interior", [field, field, field], pressure, wind_x, wind_y, jacobian
         )
-        wind_x, wind_y, star, value, face = call(
+        wind_x, wind_y, star, value, *faces = call(
             kernel_b,
             "sweep",
-            [field, field, field, field, (4,) + plane],
+            [field, field, field, field, (3,) + plane, (1,) + plane, pair],
             pressure,
             *closed,
             wind_z,
@@ -798,13 +790,15 @@
             *sent,
             *got,
             *static_edges,
-            keep=(0, 1, 2, 3, 4),
-        )
-        faces = gather_levels(face)
+            coef,
+            far,
+            keep=tuple(range(7)),
+        )
+        column = (coef, far, stat) + exchange_column(*faces)
         if substep < SUBSTEPS - 1:
             (packed,) = call(kernel_n, "pack", [pair], wind_y)
             wind_z, pressure, edge, inner, outer, ends = call(
-                functools.partial(kernel_c, blocks),
+                kernel_c,
                 "finish",
                 [field, field, (levels, ROWS, lanes), (1,) + plane, (1,) + plane, pair],
                 value,
@@ -814,22 +808,20 @@
                 wind_x,
                 packed,
                 jacobian,
-                *faces,
-                *stats,
+                *column,
             )
             sent = (edge, inner, outer)
             got = (exchange_rows(edge),) + exchange_lanes(inner, outer)
         else:
             wind_z, pressure = call(
-                functools.partial(kernel_d, blocks),
+                kernel_d,
                 "last",
                 [field, field],
                 value,
                 prod,
                 inv,
                 star,
-                *faces,
-                *stats,
+                *column,
                 far_out=True,
                 scratch=[
                     pltpu.VMEM(field, jnp.float32),

time: 38.2 us -> 37.8 us (0.990)
    ppermute x15 -> x14, waiting for transfers between devices: 7.53 us -> 7.35 us  [swap(): return lax.ppermute(value, axis, [(i, partner(i)) for i in range(count)])]
    ppermute x15 -> x14, starting transfers between devices: 15.7 us -> 15.5 us  [swap(): return lax.ppermute(value, axis, [(i, partner(i)) for i in range(count)])]
    pallas_call x9 -> x10, Pallas kernels: 12.4 us -> 12.3 us  [call(): pl.pallas_call(kernel, out_shape=[pltpu.VMEM(s, jnp.float32) if k in keep...]
  transfers between devices with their start and end apart: 15 -> 14, of which waited for: 6 -> 6; matrix products, arithmetic and copies ran while one was open for 4% -> 4% of each run, Pallas kernels for 14% -> 11%
where the time goes in v4:
time: 37.8 us; the launch traced here: 37.6 us
  starting transfers between devices  15.5 us (41%)
  Pallas kernels  12.3 us (33%)
  waiting for transfers between devices  7.35 us (19%)
  local copies, waits for them, and re-layouts  1.63 us (4%)
  between operations  0.8 us (2%)
    ppermute x14, starting transfers between devices, swap(): return lax.ppermute(value, axis, [(i, partner(i)) for i in range(count)])  15.5 us
    pallas_call x10, Pallas kernels, call(): pl.pallas_call(kernel, out_shape=[pltpu.VMEM(s, jnp.float32) if k in keep...  12.3 us
    ppermute x14, waiting for transfers between devices, swap(): return lax.ppermute(value, axis, [(i, partner(i)) for i in range(count)])  7.35 us
    unnamed x18, local copies, waits for them, and re-layouts  1.63 us
  transfers between devices with their start and end apart: 14, of which 6 were waited for; matrix products, arithmetic and copies ran while one was open for 4% of the time, Pallas kernels for 11%

profile of v4, /device:TPU:0, one launch (start us, length us, event | category | flops | bytes accessed | tf_op | source)
XLA Modules:
  0.0 37.6 jit_solution(14342808012322735161)
XLA Ops:
  0.7 2.7 %start.1 = (f32[33,8,128]{2,1,0:T(8,128)S(1)}, f32[2,32,128]{2,1,0:T(8,128)S(1)}, f32[2,32,128]{2,1,0:T(8,128)S(1)}, f32[2,32,128]{2,1,0:T(8,128)S(1)}) custom-call(f32[32,32,128]{2,1,0:T(8,128)} %p_ref.3, f32[32,32,128]{2,1,0:T(8,128)} %wx_hbm.1, f32[32,32,128]{2,1,0:T(8,128)} %wy_hbm.1, f32[32,128]{1,0:T(8,128)} %jac_ref.9), custom_call_target="tpu_custom_call" | custom-call | flops 3645440 | bytes 1822720 | tf_op jit(solution)/shard_map/start/pallas_call | solution.py:693
  3.4 3.0 %collective-permute-start = (f32[33,8,128]{2,1,0:T(8,128)S(1)}, f32[33,8,128]{2,1,0:T(8,128)S(1)}, u32[]{:S(2)}, u32[]{:S(2)}) collective-permute-start(f32[33,8,128]{2,1,0:T(8,128)S(1)} %get-tuple-element.50.rows_ref.srows_ref), channel_id=1, source_target_pairs={{0,16},{16,0},{1,17},{17,1},{2,18},{18,2},{3,19},{19,3},{4,20},{20... | collective-permute-start | bytes 405512 | tf_op jit(solution)/shard_map/ppermute | solution.py:712
  6.4 0.7 %factor.1 = (f32[32,32,128]{2,1,0:T(8,128)S(1)}, f32[32,32,128]{2,1,0:T(8,128)S(1)}, f32[32,32,128]{2,1,0:T(8,128)S(1)}, f32[32,32,128]{2,1,0:T(8,128)S(1)}, f32[5,32,128]{2,1,0:T(8,128)S(1)}) custom-call(f32[32,32,128]{2,1,0:T(8,128)S(1)} %copy-done.5), custom_call_target="tpu_custom_call" | custom-call | flops 5406720 | bytes 2703360 | tf_op jit(solution)/shard_map/factor/pallas_call | solution.py:693
  7.2 1.6 %collective-permute-start.1 = (f32[2,32,128]{2,1,0:T(8,128)S(1)}, f32[2,32,128]{2,1,0:T(8,128)S(1)}, u32[]{:S(2)}, u32[]{:S(2)}) collective-permute-start(f32[2,32,128]{2,1,0:T(8,128)S(1)} %get-tuple-element.51.inner_ref.sinner_ref), channel_id=1, source_target_pairs={{0,4},{4,0},{8,12},{12,8},{1,5},{5,1},{9,13},{13,9},{2,6},{6,2},{1... | collective-permute-start | bytes 98312 | tf_op jit(solution)/shard_map/ppermute | solution.py:712
  8.9 2.5 %collective-permute-start.2 = (f32[2,32,128]{2,1,0:T(8,128)S(1)}, f32[2,32,128]{2,1,0:T(8,128)S(1)}, u32[]{:S(2)}, u32[]{:S(2)}) collective-permute-start(f32[2,32,128]{2,1,0:T(8,128)S(1)} %get-tuple-element.52.outer_ref.souter_ref), channel_id=1, source_target_pairs={{0,12},{4,8},{8,4},{12,0},{1,13},{5,9},{9,5},{13,1},{2,14},{6,10},... | collective-permute-start | bytes 98312 | tf_op jit(solution)/shard_map/ppermute | solution.py:712
  11.4 1.6 %collective-permute-start.4 = (f32[2,32,128]{2,1,0:T(8,128)S(1)}, f32[2,32,128]{2,1,0:T(8,128)S(1)}, u32[]{:S(2)}, u32[]{:S(2)}) collective-permute-start(f32[2,32,128]{2,1,0:T(8,128)S(1)} %get-tuple-element.55), channel_id=1, source_target_pairs={{0,2},{1,3},{2,0},{3,1},{4,6},{5,7},{6,4},{7,5},{8,10},{9,11},{10,... | collective-permute-start | bytes 98312 | tf_op jit(solution)/shard_map/ppermute | solution.py:712
  13.0 1.4 %interior.2 = (f32[32,32,128]{2,1,0:T(8,128)S(1)}, f32[32,32,128]{2,1,0:T(8,128)S(1)}, f32[32,32,128]{2,1,0:T(8,128)S(1)}) custom-call(f32[32,32,128]{2,1,0:T(8,128)S(1)} %copy-done, f32[32,32,128]{2,1,0:T(8,128)S(1)} %copy-done.1, f32[32,32,128]{2,1,0:T(8,128)S(1)} %copy-done.2, f32[32,128]{1,0:T(8,128)S(1)} %copy-done.3), custom_call_target="tpu_custom_call" | custom-call | flops 6324224 | bytes 3162112 | tf_op jit(solution)/shard_map/interior/pallas_call | solution.py:693
  14.6 0.8 %collective-permute-done.4.far_ref.refs_1_ = f32[2,32,128]{2,1,0:T(8,128)S(1)} collective-permute-done((f32[2,32,128]{2,1,0:T(8,128)S(1)}, f32[2,32,128]{2,1,0:T(8,128)S(1)}, u32[]{:S(2)}, u32[]{:S(2)}) %collective-permute-start.4) | collective-permute-done | bytes 32800 | tf_op jit(solution)/shard_map/ppermute | solution.py:712
  15.4 1.5 %sweep.2 = (f32[32,32,128]{2,1,0:T(8,128)S(1)}, f32[32,32,128]{2,1,0:T(8,128)S(1)}, f32[32,32,128]{2,1,0:T(8,128)S(1)}, f32[32,32,128]{2,1,0:T(8,128)S(1)}, f32[...) custom-call(f32[32,32,128]{2,1,0:T(8,128)S(1)} %copy-done, ...), custom_call_target="tpu_custom_call" | custom-call | flops 14876672 | bytes 7438336 | tf_op jit(solution)/shard_map/sweep/pallas_call | solution.py:693
  17.0 1.6 %collective-permute-start.7 = (f32[2,32,128]{2,1,0:T(8,128)S(1)}, f32[2,32,128]{2,1,0:T(8,128)S(1)}, u32[]{:S(2)}, u32[]{:S(2)}) collective-permute-start(f32[2,32,128]{2,1,0:T(8,128)S(1)} %get-tuple-element.63), channel_id=1, source_target_pairs={{0,3},{1,2},{2,1},{3,0},{4,7},{5,6},{6,5},{7,4},{8,11},{9,10},{10,... | collective-permute-start | bytes 98312 | tf_op jit(solution)/shard_map/ppermute | solution.py:712
  19.6 2.7 %collective-permute-done.6.refs_5_ = f32[1,32,128]{2,1,0:T(8,128)S(1)} collective-permute-done((f32[1,32,128]{2,1,0:T(8,128)S(1)}, f32[1,32,128]{2,1,0:T(8,128)S(1)}, u32[]{:S(2)}, u32[]{:S(2)}) %collective-permute-start.6) | collective-permute-done | bytes 16416 | tf_op jit(solution)/shard_map/ppermute | solution.py:712
  22.3 1.5 %finish.1 = (f32[32,32,128]{2,1,0:T(8,128)S(1)}, f32[32,32,128]{2,1,0:T(8,128)S(1)}, f32[32,8,128]{2,1,0:T(8,128)S(1)}, f32[1,32,128]{2,1,0:T(8,128)S(1)}, f32[1...) custom-call(f32[32,32,128]{2,1,0:T(8,128)S(1)} %get-tuple-element.56.y_ref, f32[32,32,128]{2,1,0:T(8,128)S(1)} %get-tuple-element.57.q_ref, ...), custom_call_target="tpu_custom_call" | custom-call | flops 8617984 | bytes 4308992 | tf_op jit(solution)/shard_map/finish/pallas_call | solution.py:693
  24.3 0.7 %collective-permute-start.9 = (f32[1,32,128]{2,1,0:T(8,128)S(1)}, f32[1,32,128]{2,1,0:T(8,128)S(1)}, u32[]{:S(2)}, u32[]{:S(2)}) collective-permute-start(f32[1,32,128]{2,1,0:T(8,128)S(1)} %get-tuple-element.71.inner_ref), channel_id=1, source_target_pairs={{0,4},{4,0},{8,12},{12,8},{1,5},{5,1},{9,13},{13,9},{2,6},{6,2},{1... | collective-permute-start | bytes 49160 | tf_op jit(solution)/shard_map/ppermute | solution.py:712
  25.0 1.1 %collective-permute-start.10 = (f32[1,32,128]{2,1,0:T(8,128)S(1)}, f32[1,32,128]{2,1,0:T(8,128)S(1)}, u32[]{:S(2)}, u32[]{:S(2)}) collective-permute-start(f32[1,32,128]{2,1,0:T(8,128)S(1)} %get-tuple-element.72.outer_ref), channel_id=1, source_target_pairs={{0,12},{4,8},{8,4},{12,0},{1,13},{5,9},{9,5},{13,1},{2,14},{6,10},... | collective-permute-start | bytes 49160 | tf_op jit(solution)/shard_map/ppermute | solution.py:712
  26.1 1.4 %interior.3 = (f32[32,32,128]{2,1,0:T(8,128)S(1)}, f32[32,32,128]{2,1,0:T(8,128)S(1)}, f32[32,32,128]{2,1,0:T(8,128)S(1)}) custom-call(f32[32,32,128]{2,1,0:T(8,128)S(1)} %get-tuple-element.64.p_ref, f32[32,32,128]{2,1,0:T(8,128)S(1)} %get-tuple-element.59.wx_ref, f32[32,32,128]{2,1,0:T(8,128)S(1)} %get-tuple-element.60.wy_ref, f32[32,128]{1,0:T(8,128)S(1)} %copy-done.3), custom_call_target="tpu_custom_call" | custom-call | flops 6324224 | bytes 3162112 | tf_op jit(solution)/shard_map/interior/pallas_call | solution.py:693
  27.6 0.6 %collective-permute-done.9.got_inner_ref = f32[1,32,128]{2,1,0:T(8,128)S(1)} collective-permute-done((f32[1,32,128]{2,1,0:T(8,128)S(1)}, f32[1,32,128]{2,1,0:T(8,128)S(1)}, u32[]{:S(2)}, u32[]{:S(2)}) %collective-permute-start.9) | collective-permute-done | bytes 16416 | tf_op jit(solution)/shard_map/ppermute | solution.py:712
  28.2 2.4 %collective-permute-done.10.got_outer_ref = f32[1,32,128]{2,1,0:T(8,128)S(1)} collective-permute-done((f32[1,32,128]{2,1,0:T(8,128)S(1)}, f32[1,32,128]{2,1,0:T(8,128)S(1)}, u32[]{:S(2)}, u32[]{:S(2)}) %collective-permute-start.10) | collective-permute-done | bytes 16416 | tf_op jit(solution)/shard_map/ppermute | solution.py:712
  30.6 1.5 %sweep.3 = (f32[32,32,128]{2,1,0:T(8,128)S(1)}, f32[32,32,128]{2,1,0:T(8,128)S(1)}, f32[32,32,128]{2,1,0:T(8,128)S(1)}, f32[32,32,128]{2,1,0:T(8,128)S(1)}, f32[...) custom-call(f32[32,32,128]{2,1,0:T(8,128)S(1)} %get-tuple-element.64.p_ref, ...), custom_call_target="tpu_custom_call" | custom-call | flops 14729216 | bytes 7364608 | tf_op jit(solution)/shard_map/sweep/pallas_call | solution.py:693
  32.1 0.7 %collective-permute-start.13 = (f32[2,32,128]{2,1,0:T(8,128)S(1)}, f32[2,32,128]{2,1,0:T(8,128)S(1)}, u32[]{:S(2)}, u32[]{:S(2)}) collective-permute-start(f32[2,32,128]{2,1,0:T(8,128)S(1)} %get-tuple-element.79), channel_id=1, source_target_pairs={{0,3},{1,2},{2,1},{3,0},{4,7},{5,6},{6,5},{7,4},{8,11},{9,10},{10,... | collective-permute-start | bytes 98312 | tf_op jit(solution)/shard_map/ppermute | solution.py:712
  32.8 1.5 %collective-permute-start.12 = (f32[1,32,128]{2,1,0:T(8,128)S(1)}, f32[1,32,128]{2,1,0:T(8,128)S(1)}, u32[]{:S(2)}, u32[]{:S(2)}) collective-permute-start(f32[1,32,128]{2,1,0:T(8,128)S(1)} %get-tuple-element.78), channel_id=1, source_target_pairs={{0,2},{1,3},{2,0},{3,1},{4,6},{5,7},{6,4},{7,5},{8,10},{9,11},{10,... | collective-permute-start | bytes 49160 | tf_op jit(solution)/shard_map/ppermute | solution.py:712
  34.2 0.8 %copy.12 = f32[32,32,128]{2,1,0:T(8,128)} copy(f32[32,32,128]{2,1,0:T(8,128)S(1)} %get-tuple-element.82) | data formatting | bytes 1048576
  35.0 0.8 %copy.13 = f32[32,32,128]{2,1,0:T(8,128)} copy(f32[32,32,128]{2,1,0:T(8,128)S(1)} %get-tuple-element.83) | data formatting | bytes 1048576
  35.8 0.7 %collective-permute-done.12.refs_5_ = f32[1,32,128]{2,1,0:T(8,128)S(1)} collective-permute-done((f32[1,32,128]{2,1,0:T(8,128)S(1)}, f32[1,32,128]{2,1,0:T(8,128)S(1)}, u32[]{:S(2)}, u32[]{:S(2)}) %collective-permute-start.12) | collective-permute-done | bytes 16416 | tf_op jit(solution)/shard_map/ppermute | solution.py:712
  36.5 1.1 %last.1 = (f32[32,32,128]{2,1,0:T(8,128)}, f32[32,32,128]{2,1,0:T(8,128)}) custom-call(f32[32,32,128]{2,1,0:T(8,128)S(1)} %get-tuple-element.75.y_ref, f32[32,32,128]{2,1,0:T(8,128)S(1)} %get-tuple-element.57.q_ref, f32[32,32,128]{2,1,0:T(8,128)S(1)} %get-tuple-element.47.i_ref, f32[32,32,128]{2,1,0:T(8,128)S(1)} %get-tuple-element.76.ps_ref, ...), custom_call_target="tpu_custom_call" | custom-call | flops 7077888 | bytes 3538944 | tf_op jit(solution)/shard_map/last/pallas_call | solution.py:693
  (32 shorter events, 2.0 us)
Async XLA Ops:
  0.6 5.8 %copy-start.5 = (f32[32,32,128]{2,1,0:T(8,128)S(1)}, f32[32,32,128]{2,1,0:T(8,128)}, u32[]{:S(2)}) copy-start(f32[32,32,128]{2,1,0:T(8,128)} %s_ref.1) | copy-start | bytes 1572868
  0.6 12.3 %copy-start.1 = (f32[32,32,128]{2,1,0:T(8,128)S(1)}, f32[32,32,128]{2,1,0:T(8,128)}, u32[]{:S(2)}) copy-start(f32[32,32,128]{2,1,0:T(8,128)} %wx_hbm.1) | copy-start | bytes 1572868
  0.7 12.3 %copy-start.2 = (f32[32,32,128]{2,1,0:T(8,128)S(1)}, f32[32,32,128]{2,1,0:T(8,128)}, u32[]{:S(2)}) copy-start(f32[32,32,128]{2,1,0:T(8,128)} %wy_hbm.1) | copy-start | bytes 1572868
  3.3 9.6 %copy-start = (f32[32,32,128]{2,1,0:T(8,128)S(1)}, f32[32,32,128]{2,1,0:T(8,128)}, u32[]{:S(2)}) copy-start(f32[32,32,128]{2,1,0:T(8,128)} %p_ref.3) | copy-start | bytes 1572868
  3.4 12.0 %collective-permute-start = (f32[33,8,128]{2,1,0:T(8,128)S(1)}, f32[33,8,128]{2,1,0:T(8,128)S(1)}, u32[]{:S(2)}, u32[]{:S(2)}) collective-permute-start(f32[33,8,128]{2,1,0:T(8,128)S(1)} %get-tuple-element.50.rows_ref.srows_ref), channel_id=1, source_target_pairs={{0,16},{16,0},{1,17},{17,1},{2,18},{18,2},{3,19},{19,3},{4,20},{20... | collective-permute-start | bytes 405512 | tf_op jit(solution)/shard_map/ppermute | solution.py:712
  7.1 4.2 %collective-permute-start.3 = (f32[5,32,128]{2,1,0:T(8,128)S(1)}, f32[5,32,128]{2,1,0:T(8,128)S(1)}, u32[]{:S(2)}, u32[]{:S(2)}) collective-permute-start(f32[5,32,128]{2,1,0:T(8,128)S(1)} %get-tuple-element.53.stat_ref.refs_2_), channel_id=1, source_target_pairs={{0,1},{1,0},{2,3},{3,2},{4,5},{5,4},{6,7},{7,6},{8,9},{9,8},{10,11... | collective-permute-start | bytes 245768 | tf_op jit(solution)/shard_map/ppermute | solution.py:712
  7.2 7.2 %collective-permute-start.1 = (f32[2,32,128]{2,1,0:T(8,128)S(1)}, f32[2,32,128]{2,1,0:T(8,128)S(1)}, u32[]{:S(2)}, u32[]{:S(2)}) collective-permute-start(f32[2,32,128]{2,1,0:T(8,128)S(1)} %get-tuple-element.51.inner_ref.sinner_ref), channel_id=1, source_target_pairs={{0,4},{4,0},{8,12},{12,8},{1,5},{5,1},{9,13},{13,9},{2,6},{6,2},{1... | collective-permute-start | bytes 98312 | tf_op jit(solution)/shard_map/ppermute | solution.py:712
  8.9 4.1 %copy-start.3 = (f32[32,128]{1,0:T(8,128)S(1)}, f32[32,128]{1,0:T(8,128)}, u32[]{:S(2)}) copy-start(f32[32,128]{1,0:T(8,128)} %jac_ref.9) | copy-start | bytes 49156
  8.9 5.7 %collective-permute-start.2 = (f32[2,32,128]{2,1,0:T(8,128)S(1)}, f32[2,32,128]{2,1,0:T(8,128)S(1)}, u32[]{:S(2)}, u32[]{:S(2)}) collective-permute-start(f32[2,32,128]{2,1,0:T(8,128)S(1)} %get-tuple-element.52.outer_ref.souter_ref), channel_id=1, source_target_pairs={{0,12},{4,8},{8,4},{12,0},{1,13},{5,9},{9,5},{13,1},{2,14},{6,10},... | collective-permute-start | bytes 98312 | tf_op jit(solution)/shard_map/ppermute | solution.py:712
  11.4 4.0 %copy-start.4 = (f32[32,32,128]{2,1,0:T(8,128)S(1)}, f32[32,32,128]{2,1,0:T(8,128)}, u32[]{:S(2)}) copy-start(f32[32,32,128]{2,1,0:T(8,128)} %wz_ref.1) | copy-start | bytes 1572868
  11.4 4.0 %collective-permute-start.4 = (f32[2,32,128]{2,1,0:T(8,128)S(1)}, f32[2,32,128]{2,1,0:T(8,128)S(1)}, u32[]{:S(2)}, u32[]{:S(2)}) collective-permute-start(f32[2,32,128]{2,1,0:T(8,128)S(1)} %get-tuple-element.55), channel_id=1, source_target_pairs={{0,2},{1,3},{2,0},{3,1},{4,6},{5,7},{6,4},{7,5},{8,10},{9,11},{10,... | collective-permute-start | bytes 98312 | tf_op jit(solution)/shard_map/ppermute | solution.py:712
  13.0 2.4 %copy-start.6 = (f32[32,128]{1,0:T(8,128)S(1)}, f32[32,128]{1,0:T(8,128)}, u32[]{:S(2)}) copy-start(f32[32,128]{1,0:T(8,128)} %sx_ref.3) | copy-start | bytes 49156
  13.0 2.4 %copy-start.7 = (f32[32,128]{1,0:T(8,128)S(1)}, f32[32,128]{1,0:T(8,128)}, u32[]{:S(2)}) copy-start(f32[32,128]{1,0:T(8,128)} %sy_ref.3) | copy-start | bytes 49156
  16.9 5.4 %collective-permute-start.5 = (f32[3,32,128]{2,1,0:T(8,128)S(1)}, f32[3,32,128]{2,1,0:T(8,128)S(1)}, u32[]{:S(2)}, u32[]{:S(2)}) collective-permute-start(f32[3,32,128]{2,1,0:T(8,128)S(1)} %get-tuple-element.61.refs_3_), channel_id=1, source_target_pairs={{0,1},{1,0},{2,3},{3,2},{4,5},{5,4},{6,7},{7,6},{8,9},{9,8},{10,11... | collective-permute-start | bytes 147464 | tf_op jit(solution)/shard_map/ppermute | solution.py:712
  17.0 5.3 %collective-permute-start.7 = (f32[2,32,128]{2,1,0:T(8,128)S(1)}, f32[2,32,128]{2,1,0:T(8,128)S(1)}, u32[]{:S(2)}, u32[]{:S(2)}) collective-permute-start(f32[2,32,128]{2,1,0:T(8,128)S(1)} %get-tuple-element.63), channel_id=1, source_target_pairs={{0,3},{1,2},{2,1},{3,0},{4,7},{5,6},{6,5},{7,4},{8,11},{9,10},{10,... | collective-permute-start | bytes 98312 | tf_op jit(solution)/shard_map/ppermute | solution.py:712
  18.6 3.7 %collective-permute-start.6 = (f32[1,32,128]{2,1,0:T(8,128)S(1)}, f32[1,32,128]{2,1,0:T(8,128)S(1)}, u32[]{:S(2)}, u32[]{:S(2)}) collective-permute-start(f32[1,32,128]{2,1,0:T(8,128)S(1)} %get-tuple-element.62), channel_id=1, source_target_pairs={{0,2},{1,3},{2,0},{3,1},{4,6},{5,7},{6,4},{7,5},{8,10},{9,11},{10,... | collective-permute-start | bytes 49160 | tf_op jit(solution)/shard_map/ppermute | solution.py:712
  23.8 6.8 %collective-permute-start.8 = (f32[32,8,128]{2,1,0:T(8,128)S(1)}, f32[32,8,128]{2,1,0:T(8,128)S(1)}, u32[]{:S(2)}, u32[]{:S(2)}) collective-permute-start(f32[32,8,128]{2,1,0:T(8,128)S(1)} %get-tuple-element.70.rows_ref), channel_id=1, source_target_pairs={{0,16},{16,0},{1,17},{17,1},{2,18},{18,2},{3,19},{19,3},{4,20},{20... | collective-permute-start | bytes 393224 | tf_op jit(solution)/shard_map/ppermute | solution.py:712
  24.3 3.8 %collective-permute-start.9 = (f32[1,32,128]{2,1,0:T(8,128)S(1)}, f32[1,32,128]{2,1,0:T(8,128)S(1)}, u32[]{:S(2)}, u32[]{:S(2)}) collective-permute-start(f32[1,32,128]{2,1,0:T(8,128)S(1)} %get-tuple-element.71.inner_ref), channel_id=1, source_target_pairs={{0,4},{4,0},{8,12},{12,8},{1,5},{5,1},{9,13},{13,9},{2,6},{6,2},{1... | collective-permute-start | bytes 49160 | tf_op jit(solution)/shard_map/ppermute | solution.py:712
  25.0 5.5 %collective-permute-start.10 = (f32[1,32,128]{2,1,0:T(8,128)S(1)}, f32[1,32,128]{2,1,0:T(8,128)S(1)}, u32[]{:S(2)}, u32[]{:S(2)}) collective-permute-start(f32[1,32,128]{2,1,0:T(8,128)S(1)} %get-tuple-element.72.outer_ref), channel_id=1, source_target_pairs={{0,12},{4,8},{8,4},{12,0},{1,13},{5,9},{9,5},{13,1},{2,14},{6,10},... | collective-permute-start | bytes 49160 | tf_op jit(solution)/shard_map/ppermute | solution.py:712
  32.0 4.5 %collective-permute-start.11 = (f32[3,32,128]{2,1,0:T(8,128)S(1)}, f32[3,32,128]{2,1,0:T(8,128)S(1)}, u32[]{:S(2)}, u32[]{:S(2)}) collective-permute-start(f32[3,32,128]{2,1,0:T(8,128)S(1)} %get-tuple-element.77.refs_3_), channel_id=1, source_target_pairs={{0,1},{1,0},{2,3},{3,2},{4,5},{5,4},{6,7},{7,6},{8,9},{9,8},{10,11... | collective-permute-start | bytes 147464 | tf_op jit(solution)/shard_map/ppermute | solution.py:712
  32.1 4.4 %collective-permute-start.13 = (f32[2,32,128]{2,1,0:T(8,128)S(1)}, f32[2,32,128]{2,1,0:T(8,128)S(1)}, u32[]{:S(2)}, u32[]{:S(2)}) collective-permute-start(f32[2,32,128]{2,1,0:T(8,128)S(1)} %get-tuple-element.79), channel_id=1, source_target_pairs={{0,3},{1,2},{2,1},{3,0},{4,7},{5,6},{6,5},{7,4},{8,11},{9,10},{10,... | collective-permute-start | bytes 98312 | tf_op jit(solution)/shard_map/ppermute | solution.py:712
  32.8 3.7 %collective-permute-start.12 = (f32[1,32,128]{2,1,0:T(8,128)S(1)}, f32[1,32,128]{2,1,0:T(8,128)S(1)}, u32[]{:S(2)}, u32[]{:S(2)}) collective-permute-start(f32[1,32,128]{2,1,0:T(8,128)S(1)} %get-tuple-element.78), channel_id=1, source_target_pairs={{0,2},{1,3},{2,0},{3,1},{4,6},{5,7},{6,4},{7,5},{8,10},{9,11},{10,... | collective-permute-start | bytes 49160 | tf_op jit(solution)/shard_map/ppermute | solution.py:712

commit v5 on v4

--- a/solution.py
+++ b/solution.py
@@ -19,7 +19,7 @@
 SLOT = 4
 UNROLL = 8
 CHUNKS = 4
-COLUMN = 7
+COLUMN = 6
 
 
 def lane_index():
@@ -355,8 +355,8 @@
     ps_ref,
     y_ref,
     near_ref,
-    cross_ref,
-    next_ref,
+    wind_ref,
+    press_ref,
 ):
     levels, rows, _ = p_ref.shape
     count = rows // ROWS
@@ -386,16 +386,22 @@
     low_lanes, high_lanes = lane < SLOT, lane >= 128 - SLOT
     first_rows = row < 4
 
+    def correct_rows(level, state):
+        wind_ref[level], press_ref[level] = edge.correct(
+            pltpu.roll(got_rows_ref[level] - rows_ref[level], 4, 0),
+            jnp.where(first_rows, p_ref[level, :ROWS, :], p_ref[level, ROWS * last :, :]),
+            ends,
+            ends_change,
+        )
+        return state
+
+    lax.fori_loop(0, levels, correct_rows, 0, unroll=2 * UNROLL)
+
     def star(level):
         new_x = tiles_of(nxc_ref, level, count)
         new_y = tiles_of(nyc_ref, level, count)
         stars = tiles_of(psc_ref, level, count)
-        wind, press = edge.correct(
-            pltpu.roll(got_rows_ref[level] - rows_ref[level], 4, 0),
-            jnp.where(first_rows, p_ref[level, :ROWS, :], p_ref[level, ROWS * last :, :]),
-            ends,
-            ends_change,
-        )
+        wind, press = wind_ref[level], press_ref[level]
         new_x[0] = new_x[0] - jnp.where(first_rows, wind, 0.0)
         new_x[last] = new_x[last] - jnp.where(first_rows, 0.0, wind)
         stars[0] = stars[0] - jnp.where(first_rows, press, 0.0)
@@ -447,7 +453,7 @@
         1, levels, step, (zeros, here, force, zeros, zeros), unroll=UNROLL
     )
     value, first = sweep(levels - 1, below, zeros, force, value, first)
-    interface(first, value, bottom, here, coef_ref, far_ref, near_ref, cross_ref, next_ref)
+    interface(first, value, bottom, here, coef_ref, far_ref, near_ref)
 
 
 def kernel_f(s_ref, r_ref, i_ref, q_ref, v_ref, stat_ref):
@@ -522,7 +528,7 @@
         send_ref[1, part, :] = vert_coef * jnp.where(lower, inner[4], inner[3])
 
 
-def interface(first, value, star_first, star_last, coef_ref, far_ref, near_ref, cross_ref, next_ref):
+def interface(first, value, star_first, star_last, coef_ref, far_ref, near_ref):
     outermost, lower, even = place_in_column()
     for t in range(len(first)):
         part = slice(ROWS * t, ROWS * (t + 1))
@@ -537,12 +543,16 @@
         near_ref[0, part, :] = jnp.where(outermost, centre, outer)
         near_ref[1, part, :] = jnp.where(even, star_last[t], star_first[t])
         near_ref[2, part, :] = total
-        cross_ref[0, part, :] = total
-        next_ref[0, part, :] = total
-        next_ref[1, part, :] = star_centre
-
-
-def boundary(count, coef_ref, far_ref, stat_ref, near_ref, got_near_ref, got_cross_ref, got_next_ref):
+        near_ref[3, part, :] = star_centre
+
+
+def kernel_u(near_ref, got_ref, send_ref):
+    outermost, _, _ = place_in_column()
+    send_ref[0] = near_ref[2] + got_ref[2]
+    send_ref[1] = jnp.where(outermost, got_ref[3], near_ref[3])
+
+
+def boundary(count, coef_ref, far_ref, stat_ref, near_ref, got_near_ref, got_far_ref):
     outermost, lower, _ = place_in_column()
     parts = []
     for t in range(count):
@@ -551,7 +561,7 @@
         far_total = far_ref[0, part, :]
         own, got = near_ref[0, part, :], got_near_ref[0, part, :]
         this = near_ref[2, part, :] + got_near_ref[2, part, :]
-        that = got_cross_ref[0, part, :] + got_next_ref[0, part, :]
+        that = got_far_ref[0, part, :]
         middle = (that + far_total * this) / (1.0 - coef["total"] * far_total)
         from_outer = jnp.where(outermost, own, got)
         from_inner = jnp.where(outermost, got, own)
@@ -561,7 +571,7 @@
         zero = jnp.zeros_like(own)
         centre = jnp.where(outermost, between, middle)
         outer = jnp.where(outermost, zero, from_outer + coef["outer"] * between)
-        mate_star, next_star = got_near_ref[1, part, :], got_next_ref[1, part, :]
+        mate_star, next_star = got_near_ref[1, part, :], got_far_ref[1, part, :]
         star_centre = jnp.where(outermost, mate_star, next_star)
         star_outer = jnp.where(outermost, zero, mate_star)
         below, above = jnp.where(lower, outer, centre), jnp.where(lower, centre, outer)
@@ -573,7 +583,7 @@
     return [[part[k] for part in parts] for k in range(4)]
 
 
-def finish(count, levels, y_ref, q_ref, i_ref, ps_ref, x_ref, p_ref, column_refs, use, state, ready=None):
+def finish(count, levels, y_ref, q_ref, i_ref, ps_ref, x_ref, p_ref, column_refs, ready=None):
     lower, upper, under, over = boundary(count, *column_refs)
 
     def solved(level, above):
@@ -584,21 +594,18 @@
         put_tiles(x_ref, level, out)
         return out
 
-    def pressed(level, above, below, state):
+    def pressed(level, above, below):
         star = tiles_of(ps_ref, level, count)
-        pres = [s - vert_coef * (a - b) for s, a, b in zip(star, above, below)]
-        put_tiles(p_ref, level, pres)
-        return use(level, pres, state)
+        put_tiles(p_ref, level, [s - vert_coef * (a - b) for s, a, b in zip(star, above, below)])
 
     def step(index, carry):
-        above, here, state = carry
+        above, here = carry
         level = levels - 2 - index
         below = solved(level, here)
-        state = pressed(level + 1, above, below, state)
-        return here, below, state
-
-    top = solved(levels - 1, upper)
-    carry = (over, top, state)
+        pressed(level + 1, above, below)
+        return here, below
+
+    carry = over, solved(levels - 1, upper)
     if ready is None:
         carry = lax.fori_loop(0, levels - 1, step, carry, unroll=UNROLL)
     else:
@@ -608,8 +615,8 @@
             carry = lax.fori_loop(done, goal, step, carry, unroll=UNROLL)
             done = goal
             ready(c)
-    above, here, state = carry
-    return pressed(0, above, under, state)
+    above, here = carry
+    pressed(0, above, under)
 
 
 def kernel_c(y_ref, q_ref, i_ref, ps_ref, wx_ref, pw_ref, jac_ref, *refs):
@@ -617,30 +624,20 @@
     x_ref, p_ref, rows_ref, inner_ref, outer_ref, pp_ref = refs[COLUMN:]
     levels, rows, _ = y_ref.shape
     count = rows // ROWS
-    packer = Packer(count)
     edge = row_edge()
     ends = both_ends(planes_of(jac_ref, count))
-
-    def use(level, pres, state):
+    finish(count, levels, y_ref, q_ref, i_ref, ps_ref, x_ref, p_ref, column_refs)
+
+    def step(level, state):
         rows_ref[level] = edge.payload(
-            both_ends(pres), both_ends(tiles_of(wx_ref, level, count)), ends
-        )
-        return packer.add(level, pres, state)
-
-    state = finish(
-        count,
-        levels,
-        y_ref,
-        q_ref,
-        i_ref,
-        ps_ref,
-        x_ref,
-        p_ref,
-        column_refs,
-        use,
-        packer.start,
-    )
-    pres = packer.done(state)
+            both_ends(tiles_of(p_ref, level, count)),
+            both_ends(tiles_of(wx_ref, level, count)),
+            ends,
+        )
+        return state
+
+    lax.fori_loop(0, levels, step, 0, unroll=2 * UNROLL)
+    pres = pack_levels(p_ref, count, levels)
     wind = tiles_of(pw_ref, 0, count), tiles_of(pw_ref, 1, count)
     down, up = lane_payload(pres, wind, planes_of(jac_ref, count))
     put_pair(inner_ref, outer_ref, 0, down, up)
@@ -676,8 +673,6 @@
         x_ref,
         p_ref,
         column_refs,
-        lambda level, pres, state: state,
-        0,
         ready,
     )
     send(1, p_ref, p_hbm, 0)
@@ -685,7 +680,7 @@
         copy.wait()
 
 
-def call(kernel, name, shapes, *args, far_in=False, far_out=False, scratch=(), keep=()):
+def call(kernel, name, shapes, *args, weight=1, far_in=False, far_out=False, scratch=(), keep=()):
     near, far = pl.BlockSpec(memory_space=pltpu.VMEM), pl.BlockSpec(memory_space=pl.ANY)
     size = sum(a.size for a in args) + sum(functools.reduce(lambda a, b: a * b, s) for s in shapes)
     if far_in:
@@ -701,7 +696,7 @@
         scratch_shapes=list(scratch),
         compiler_params=pltpu.CompilerParams(vmem_limit_bytes=32 * 1024 * 1024),
         cost_estimate=pl.CostEstimate(
-            flops=8 * size, bytes_accessed=4 * size, transcendentals=0
+            flops=weight * size, bytes_accessed=4 * weight * size, transcendentals=0
         ),
         name=name,
     )(*args)
@@ -728,11 +723,11 @@
     return got_inner, got_outer
 
 
-def exchange_column(near, cross, following):
-    got_next = swap(following, "lev", lambda i: i ^ 3)
-    got_cross = swap(cross, "lev", lambda i: i ^ 2)
+def exchange_column(near):
+    plane = near.shape[1:]
     got_near = swap(near, "lev", lambda i: i ^ 1)
-    return near, got_near, got_cross, got_next
+    (send,) = call(kernel_u, "meet", [(2,) + plane], near, got_near)
+    return near, got_near, swap(send, "lev", lambda i: i ^ 2)
 
 
 def local(wind_x, wind_y, wind_z, pressure, jacobian, slope_x, slope_y, stiffness):
@@ -773,10 +768,10 @@
         closed = call(
             kernel_m, "interior", [field, field, field], pressure, wind_x, wind_y, jacobian
         )
-        wind_x, wind_y, star, value, *faces = call(
+        wind_x, wind_y, star, value, near = call(
             kernel_b,
             "sweep",
-            [field, field, field, field, (3,) + plane, (1,) + plane, pair],
+            [field, field, field, field, (4,) + plane],
             pressure,
             *closed,
             wind_z,
@@ -792,9 +787,10 @@
             *static_edges,
             coef,
             far,
-            keep=tuple(range(7)),
-        )
-        column = (coef, far, stat) + exchange_column(*faces)
+            keep=tuple(range(5)),
+            scratch=[pltpu.VMEM((levels, ROWS, lanes), jnp.float32)] * 2,
+        )
+        column = (coef, far, stat) + exchange_column(near)
         if substep < SUBSTEPS - 1:
             (packed,) = call(kernel_n, "pack", [pair], wind_y)
             wind_z, pressure, edge, inner, outer, ends = call(

time: 37.8 us -> 38.8 us (1.026)
  waiting for transfers between devices: 7.35 us -> 9.22 us
  starting transfers between devices: 15.5 us -> 14.4 us
    ppermute x14 -> x12, waiting for transfers between devices: 7.35 us -> 9.22 us  [swap(): return lax.ppermute(value, axis, [(i, partner(i)) for i in range(count)])]
    ppermute x14 -> x12, starting transfers between devices: 15.5 us -> 14.4 us  [swap(): return lax.ppermute(value, axis, [(i, partner(i)) for i in range(count)])]
    pallas_call x10 -> x12, Pallas kernels: 12.3 us -> 12.6 us  [call(): pl.pallas_call(kernel, out_shape=[pltpu.VMEM(s, jnp.float32) if k in keep...]
  transfers between devices with their start and end apart: 14 -> 12, of which waited for: 6 -> 8; matrix products, arithmetic and copies ran while one was open for 4% -> 4% of each run, Pallas kernels for 11% -> 11%
where the time goes in v5:
time: 38.8 us; the launch traced here: 38.6 us
  starting transfers between devices  14.4 us (37%)
  Pallas kernels  12.6 us (32%)
  waiting for transfers between devices  9.22 us (24%)
  local copies, waits for them, and re-layouts  1.63 us (4%)
  between operations  0.8 us (2%)
    ppermute x12, starting transfers between devices, swap(): return lax.ppermute(value, axis, [(i, partner(i)) for i in range(count)])  14.4 us
    pallas_call x12, Pallas kernels, call(): pl.pallas_call(kernel, out_shape=[pltpu.VMEM(s, jnp.float32) if k in keep...  12.6 us
    ppermute x12, waiting for transfers between devices, swap(): return lax.ppermute(value, axis, [(i, partner(i)) for i in range(count)])  9.22 us
    unnamed x18, local copies, waits for them, and re-layouts  1.63 us
  transfers between devices with their start and end apart: 12, of which 8 were waited for; matrix products, arithmetic and copies ran while one was open for 4% of the time, Pallas kernels for 11%

profile of v5, /device:TPU:0, one launch (start us, length us, event | category | flops | bytes accessed | tf_op | source)
XLA Modules:
  0.0 38.6 jit_solution(6434388666497150473)
XLA Ops:
  0.7 2.7 %start.1 = (f32[33,8,128]{2,1,0:T(8,128)S(1)}, f32[2,32,128]{2,1,0:T(8,128)S(1)}, f32[2,32,128]{2,1,0:T(8,128)S(1)}, f32[2,32,128]{2,1,0:T(8,128)S(1)}) custom-call(f32[32,32,128]{2,1,0:T(8,128)} %p_ref.3, f32[32,32,128]{2,1,0:T(8,128)} %wx_hbm.1, f32[32,32,128]{2,1,0:T(8,128)} %wy_hbm.1, f32[32,128]{1,0:T(8,128)} %jac_ref.9), custom_call_target="tpu_custom_call" | custom-call | flops 455680 | bytes 1822720 | tf_op jit(solution)/shard_map/start/pallas_call | solution.py:688
  3.4 3.0 %collective-permute-start = (f32[33,8,128]{2,1,0:T(8,128)S(1)}, f32[33,8,128]{2,1,0:T(8,128)S(1)}, u32[]{:S(2)}, u32[]{:S(2)}) collective-permute-start(f32[33,8,128]{2,1,0:T(8,128)S(1)} %get-tuple-element.46.rows_ref.srows_ref), channel_id=1, source_target_pairs={{0,16},{16,0},{1,17},{17,1},{2,18},{18,2},{3,19},{19,3},{4,20},{20... | collective-permute-start | bytes 405512 | tf_op jit(solution)/shard_map/ppermute | solution.py:707
  6.4 0.7 %factor.1 = (f32[32,32,128]{2,1,0:T(8,128)S(1)}, f32[32,32,128]{2,1,0:T(8,128)S(1)}, f32[32,32,128]{2,1,0:T(8,128)S(1)}, f32[32,32,128]{2,1,0:T(8,128)S(1)}, f32[5,32,128]{2,1,0:T(8,128)S(1)}) custom-call(f32[32,32,128]{2,1,0:T(8,128)S(1)} %copy-done.5), custom_call_target="tpu_custom_call" | custom-call | flops 675840 | bytes 2703360 | tf_op jit(solution)/shard_map/factor/pallas_call | solution.py:688
  7.2 1.6 %collective-permute-start.1 = (f32[2,32,128]{2,1,0:T(8,128)S(1)}, f32[2,32,128]{2,1,0:T(8,128)S(1)}, u32[]{:S(2)}, u32[]{:S(2)}) collective-permute-start(f32[2,32,128]{2,1,0:T(8,128)S(1)} %get-tuple-element.47.inner_ref.sinner_ref), channel_id=1, source_target_pairs={{0,4},{4,0},{8,12},{12,8},{1,5},{5,1},{9,13},{13,9},{2,6},{6,2},{1... | collective-permute-start | bytes 98312 | tf_op jit(solution)/shard_map/ppermute | solution.py:707
  8.9 2.5 %collective-permute-start.2 = (f32[2,32,128]{2,1,0:T(8,128)S(1)}, f32[2,32,128]{2,1,0:T(8,128)S(1)}, u32[]{:S(2)}, u32[]{:S(2)}) collective-permute-start(f32[2,32,128]{2,1,0:T(8,128)S(1)} %get-tuple-element.48.outer_ref.souter_ref), channel_id=1, source_target_pairs={{0,12},{4,8},{8,4},{12,0},{1,13},{5,9},{9,5},{13,1},{2,14},{6,10},... | collective-permute-start | bytes 98312 | tf_op jit(solution)/shard_map/ppermute | solution.py:707
  11.4 1.6 %collective-permute-start.4 = (f32[2,32,128]{2,1,0:T(8,128)S(1)}, f32[2,32,128]{2,1,0:T(8,128)S(1)}, u32[]{:S(2)}, u32[]{:S(2)}) collective-permute-start(f32[2,32,128]{2,1,0:T(8,128)S(1)} %get-tuple-element.51), channel_id=1, source_target_pairs={{0,2},{1,3},{2,0},{3,1},{4,6},{5,7},{6,4},{7,5},{8,10},{9,11},{10,... | collective-permute-start | bytes 98312 | tf_op jit(solution)/shard_map/ppermute | solution.py:707
  13.0 1.4 %interior.2 = (f32[32,32,128]{2,1,0:T(8,128)S(1)}, f32[32,32,128]{2,1,0:T(8,128)S(1)}, f32[32,32,128]{2,1,0:T(8,128)S(1)}) custom-call(f32[32,32,128]{2,1,0:T(8,128)S(1)} %copy-done, f32[32,32,128]{2,1,0:T(8,128)S(1)} %copy-done.1, f32[32,32,128]{2,1,0:T(8,128)S(1)} %copy-done.2, f32[32,128]{1,0:T(8,128)S(1)} %copy-done.3), custom_call_target="tpu_custom_call" | custom-call | flops 790528 | bytes 3162112 | tf_op jit(solution)/shard_map/interior/pallas_call | solution.py:688
  14.6 0.8 %collective-permute-done.4.far_ref.refs_1_ = f32[2,32,128]{2,1,0:T(8,128)S(1)} collective-permute-done((f32[2,32,128]{2,1,0:T(8,128)S(1)}, f32[2,32,128]{2,1,0:T(8,128)S(1)}, u32[]{:S(2)}, u32[]{:S(2)}) %collective-permute-start.4) | collective-permute-done | bytes 32800 | tf_op jit(solution)/shard_map/ppermute | solution.py:707
  15.4 1.7 %sweep.2 = (f32[32,32,128]{2,1,0:T(8,128)S(1)}, f32[32,32,128]{2,1,0:T(8,128)S(1)}, f32[32,32,128]{2,1,0:T(8,128)S(1)}, f32[32,32,128]{2,1,0:T(8,128)S(1)}, f32[4,32,128]{2,1,0:T(8,128)S(1)}) custom-call(f32[32,32,128]{2,1,0:T(8,128)S(1)} %copy-done, f32[32,32,128]{2,1,0:T(8,128)S(1)} %get-tuple-element.39.nxc_ref, ...), custom_call_target="tpu_custom_call" | custom-call | flops 1851392 | bytes 7405568 | tf_op jit(solution)/shard_map/sweep/pallas_call | solution.py:688
  17.2 1.2 %collective-permute-done.5.got_ref.refs_4_ = f32[4,32,128]{2,1,0:T(8,128)S(1)} collective-permute-done((f32[4,32,128]{2,1,0:T(8,128)S(1)}, f32[4,32,128]{2,1,0:T(8,128)S(1)}, u32[]{:S(2)}, u32[]{:S(2)}) %collective-permute-start.5) | collective-permute-done | bytes 65568 | tf_op jit(solution)/shard_map/ppermute | solution.py:707
  18.5 1.6 %collective-permute-start.6 = (f32[2,32,128]{2,1,0:T(8,128)S(1)}, f32[2,32,128]{2,1,0:T(8,128)S(1)}, u32[]{:S(2)}, u32[]{:S(2)}) collective-permute-start(f32[2,32,128]{2,1,0:T(8,128)S(1)} %meet.2), channel_id=1, source_target_pairs={{0,2},{1,3},{2,0},{3,1},{4,6},{5,7},{6,4},{7,5},{8,10},{9,11},{10,... | collective-permute-start | bytes 98312 | tf_op jit(solution)/shard_map/ppermute | solution.py:707
  20.5 2.0 %collective-permute-done.6.refs_5_ = f32[2,32,128]{2,1,0:T(8,128)S(1)} collective-permute-done((f32[2,32,128]{2,1,0:T(8,128)S(1)}, f32[2,32,128]{2,1,0:T(8,128)S(1)}, u32[]{:S(2)}, u32[]{:S(2)}) %collective-permute-start.6) | collective-permute-done | bytes 32800 | tf_op jit(solution)/shard_map/ppermute | solution.py:707
  22.4 1.3 %finish.1 = (f32[32,32,128]{2,1,0:T(8,128)S(1)}, f32[32,32,128]{2,1,0:T(8,128)S(1)}, f32[32,8,128]{2,1,0:T(8,128)S(1)}, f32[1,32,128]{2,1,0:T(8,128)S(1)}, f32[1...) custom-call(f32[32,32,128]{2,1,0:T(8,128)S(1)} %get-tuple-element.52.y_ref, f32[32,32,128]{2,1,0:T(8,128)S(1)} %get-tuple-element.53.q_ref, ...), custom_call_target="tpu_custom_call" | custom-call | flops 1081344 | bytes 4325376 | tf_op jit(solution)/shard_map/finish/pallas_call | solution.py:688
  24.3 0.7 %collective-permute-start.8 = (f32[1,32,128]{2,1,0:T(8,128)S(1)}, f32[1,32,128]{2,1,0:T(8,128)S(1)}, u32[]{:S(2)}, u32[]{:S(2)}) collective-permute-start(f32[1,32,128]{2,1,0:T(8,128)S(1)} %get-tuple-element.65.inner_ref), channel_id=1, source_target_pairs={{0,4},{4,0},{8,12},{12,8},{1,5},{5,1},{9,13},{13,9},{2,6},{6,2},{1... | collective-permute-start | bytes 49160 | tf_op jit(solution)/shard_map/ppermute | solution.py:707
  24.9 1.1 %collective-permute-start.9 = (f32[1,32,128]{2,1,0:T(8,128)S(1)}, f32[1,32,128]{2,1,0:T(8,128)S(1)}, u32[]{:S(2)}, u32[]{:S(2)}) collective-permute-start(f32[1,32,128]{2,1,0:T(8,128)S(1)} %get-tuple-element.66.outer_ref), channel_id=1, source_target_pairs={{0,12},{4,8},{8,4},{12,0},{1,13},{5,9},{9,5},{13,1},{2,14},{6,10},... | collective-permute-start | bytes 49160 | tf_op jit(solution)/shard_map/ppermute | solution.py:707
  26.1 1.4 %interior.3 = (f32[32,32,128]{2,1,0:T(8,128)S(1)}, f32[32,32,128]{2,1,0:T(8,128)S(1)}, f32[32,32,128]{2,1,0:T(8,128)S(1)}) custom-call(f32[32,32,128]{2,1,0:T(8,128)S(1)} %get-tuple-element.58.p_ref, f32[32,32,128]{2,1,0:T(8,128)S(1)} %get-tuple-element.55.wx_ref, f32[32,32,128]{2,1,0:T(8,128)S(1)} %get-tuple-element.56.wy_ref, f32[32,128]{1,0:T(8,128)S(1)} %copy-done.3), custom_call_target="tpu_custom_call" | custom-call | flops 790528 | bytes 3162112 | tf_op jit(solution)/shard_map/interior/pallas_call | solution.py:688
  28.1 2.4 %collective-permute-done.9.got_outer_ref = f32[1,32,128]{2,1,0:T(8,128)S(1)} collective-permute-done((f32[1,32,128]{2,1,0:T(8,128)S(1)}, f32[1,32,128]{2,1,0:T(8,128)S(1)}, u32[]{:S(2)}, u32[]{:S(2)}) %collective-permute-start.9) | collective-permute-done | bytes 16416 | tf_op jit(solution)/shard_map/ppermute | solution.py:707
  30.5 1.7 %sweep.3 = (f32[32,32,128]{2,1,0:T(8,128)S(1)}, f32[32,32,128]{2,1,0:T(8,128)S(1)}, f32[32,32,128]{2,1,0:T(8,128)S(1)}, f32[32,32,128]{2,1,0:T(8,128)S(1)}, f32[4,32,128]{2,1,0:T(8,128)S(1)}) custom-call(f32[32,32,128]{2,1,0:T(8,128)S(1)} %get-tuple-element.58.p_ref, f32[32,32,128]{2,1,0:T(8,128)S(1)} %get-tuple-element.59.nxc_ref, ...), custom_call_target="tpu_custom_call" | custom-call | flops 1832960 | bytes 7331840 | tf_op jit(solution)/shard_map/sweep/pallas_call | solution.py:688
  32.3 1.2 %collective-permute-done.10.got_ref.refs_4_ = f32[4,32,128]{2,1,0:T(8,128)S(1)} collective-permute-done((f32[4,32,128]{2,1,0:T(8,128)S(1)}, f32[4,32,128]{2,1,0:T(8,128)S(1)}, u32[]{:S(2)}, u32[]{:S(2)}) %collective-permute-start.10) | collective-permute-done | bytes 65568 | tf_op jit(solution)/shard_map/ppermute | solution.py:707
  33.5 1.6 %collective-permute-start.11 = (f32[2,32,128]{2,1,0:T(8,128)S(1)}, f32[2,32,128]{2,1,0:T(8,128)S(1)}, u32[]{:S(2)}, u32[]{:S(2)}) collective-permute-start(f32[2,32,128]{2,1,0:T(8,128)S(1)} %meet.3), channel_id=1, source_target_pairs={{0,2},{1,3},{2,0},{3,1},{4,6},{5,7},{6,4},{7,5},{8,10},{9,11},{10,... | collective-permute-start | bytes 98312 | tf_op jit(solution)/shard_map/ppermute | solution.py:707
  35.1 0.8 %copy.12 = f32[32,32,128]{2,1,0:T(8,128)} copy(f32[32,32,128]{2,1,0:T(8,128)S(1)} %get-tuple-element.74) | data formatting | bytes 1048576
  35.9 0.8 %copy.13 = f32[32,32,128]{2,1,0:T(8,128)} copy(f32[32,32,128]{2,1,0:T(8,128)S(1)} %get-tuple-element.75) | data formatting | bytes 1048576
  36.7 0.8 %collective-permute-done.11.refs_5_ = f32[2,32,128]{2,1,0:T(8,128)S(1)} collective-permute-done((f32[2,32,128]{2,1,0:T(8,128)S(1)}, f32[2,32,128]{2,1,0:T(8,128)S(1)}, u32[]{:S(2)}, u32[]{:S(2)}) %collective-permute-start.11) | collective-permute-done | bytes 32800 | tf_op jit(solution)/shard_map/ppermute | solution.py:707
  37.5 1.1 %last.1 = (f32[32,32,128]{2,1,0:T(8,128)}, f32[32,32,128]{2,1,0:T(8,128)}) custom-call(f32[32,32,128]{2,1,0:T(8,128)S(1)} %get-tuple-element.69.y_ref, f32[32,32,128]{2,1,0:T(8,128)S(1)} %get-tuple-element.53.q_ref, f32[32,32,128]{2,1,0:T(8,128)S(1)} %get-tuple-element.43.i_ref, f32[32,32,128]{2,1,0:T(8,128)S(1)} %get-tuple-element.70.ps_ref, ...), custom_call_target="tpu_custom_call" | custom-call | flops 888832 | bytes 3555328 | tf_op jit(solution)/shard_map/last/pallas_call | solution.py:688
  (30 shorter events, 2.1 us)
Async XLA Ops:
  0.6 5.8 %copy-start.5 = (f32[32,32,128]{2,1,0:T(8,128)S(1)}, f32[32,32,128]{2,1,0:T(8,128)}, u32[]{:S(2)}) copy-start(f32[32,32,128]{2,1,0:T(8,128)} %s_ref.1) | copy-start | bytes 1572868
  0.6 12.3 %copy-start.1 = (f32[32,32,128]{2,1,0:T(8,128)S(1)}, f32[32,32,128]{2,1,0:T(8,128)}, u32[]{:S(2)}) copy-start(f32[32,32,128]{2,1,0:T(8,128)} %wx_hbm.1) | copy-start | bytes 1572868
  0.7 12.3 %copy-start.2 = (f32[32,32,128]{2,1,0:T(8,128)S(1)}, f32[32,32,128]{2,1,0:T(8,128)}, u32[]{:S(2)}) copy-start(f32[32,32,128]{2,1,0:T(8,128)} %wy_hbm.1) | copy-start | bytes 1572868
  3.3 9.6 %copy-start = (f32[32,32,128]{2,1,0:T(8,128)S(1)}, f32[32,32,128]{2,1,0:T(8,128)}, u32[]{:S(2)}) copy-start(f32[32,32,128]{2,1,0:T(8,128)} %p_ref.3) | copy-start | bytes 1572868
  3.4 12.0 %collective-permute-start = (f32[33,8,128]{2,1,0:T(8,128)S(1)}, f32[33,8,128]{2,1,0:T(8,128)S(1)}, u32[]{:S(2)}, u32[]{:S(2)}) collective-permute-start(f32[33,8,128]{2,1,0:T(8,128)S(1)} %get-tuple-element.46.rows_ref.srows_ref), channel_id=1, source_target_pairs={{0,16},{16,0},{1,17},{17,1},{2,18},{18,2},{3,19},{19,3},{4,20},{20... | collective-permute-start | bytes 405512 | tf_op jit(solution)/shard_map/ppermute | solution.py:707
  7.1 4.2 %collective-permute-start.3 = (f32[5,32,128]{2,1,0:T(8,128)S(1)}, f32[5,32,128]{2,1,0:T(8,128)S(1)}, u32[]{:S(2)}, u32[]{:S(2)}) collective-permute-start(f32[5,32,128]{2,1,0:T(8,128)S(1)} %get-tuple-element.49.stat_ref.refs_2_), channel_id=1, source_target_pairs={{0,1},{1,0},{2,3},{3,2},{4,5},{5,4},{6,7},{7,6},{8,9},{9,8},{10,11... | collective-permute-start | bytes 245768 | tf_op jit(solution)/shard_map/ppermute | solution.py:707
  7.2 7.2 %collective-permute-start.1 = (f32[2,32,128]{2,1,0:T(8,128)S(1)}, f32[2,32,128]{2,1,0:T(8,128)S(1)}, u32[]{:S(2)}, u32[]{:S(2)}) collective-permute-start(f32[2,32,128]{2,1,0:T(8,128)S(1)} %get-tuple-element.47.inner_ref.sinner_ref), channel_id=1, source_target_pairs={{0,4},{4,0},{8,12},{12,8},{1,5},{5,1},{9,13},{13,9},{2,6},{6,2},{1... | collective-permute-start | bytes 98312 | tf_op jit(solution)/shard_map/ppermute | solution.py:707
  8.9 4.1 %copy-start.3 = (f32[32,128]{1,0:T(8,128)S(1)}, f32[32,128]{1,0:T(8,128)}, u32[]{:S(2)}) copy-start(f32[32,128]{1,0:T(8,128)} %jac_ref.9) | copy-start | bytes 49156
  8.9 5.7 %collective-permute-start.2 = (f32[2,32,128]{2,1,0:T(8,128)S(1)}, f32[2,32,128]{2,1,0:T(8,128)S(1)}, u32[]{:S(2)}, u32[]{:S(2)}) collective-permute-start(f32[2,32,128]{2,1,0:T(8,128)S(1)} %get-tuple-element.48.outer_ref.souter_ref), channel_id=1, source_target_pairs={{0,12},{4,8},{8,4},{12,0},{1,13},{5,9},{9,5},{13,1},{2,14},{6,10},... | collective-permute-start | bytes 98312 | tf_op jit(solution)/shard_map/ppermute | solution.py:707
  11.4 4.0 %copy-start.4 = (f32[32,32,128]{2,1,0:T(8,128)S(1)}, f32[32,32,128]{2,1,0:T(8,128)}, u32[]{:S(2)}) copy-start(f32[32,32,128]{2,1,0:T(8,128)} %wz_ref.1) | copy-start | bytes 1572868
  11.4 4.0 %collective-permute-start.4 = (f32[2,32,128]{2,1,0:T(8,128)S(1)}, f32[2,32,128]{2,1,0:T(8,128)S(1)}, u32[]{:S(2)}, u32[]{:S(2)}) collective-permute-start(f32[2,32,128]{2,1,0:T(8,128)S(1)} %get-tuple-element.51), channel_id=1, source_target_pairs={{0,2},{1,3},{2,0},{3,1},{4,6},{5,7},{6,4},{7,5},{8,10},{9,11},{10,... | collective-permute-start | bytes 98312 | tf_op jit(solution)/shard_map/ppermute | solution.py:707
  13.0 2.4 %copy-start.6 = (f32[32,128]{1,0:T(8,128)S(1)}, f32[32,128]{1,0:T(8,128)}, u32[]{:S(2)}) copy-start(f32[32,128]{1,0:T(8,128)} %sx_ref.3) | copy-start | bytes 49156
  13.0 2.4 %copy-start.7 = (f32[32,128]{1,0:T(8,128)S(1)}, f32[32,128]{1,0:T(8,128)}, u32[]{:S(2)}) copy-start(f32[32,128]{1,0:T(8,128)} %sy_ref.3) | copy-start | bytes 49156
  17.1 1.3 %collective-permute-start.5 = (f32[4,32,128]{2,1,0:T(8,128)S(1)}, f32[4,32,128]{2,1,0:T(8,128)S(1)}, u32[]{:S(2)}, u32[]{:S(2)}) collective-permute-start(f32[4,32,128]{2,1,0:T(8,128)S(1)} %get-tuple-element.57.near_ref.refs_3_), channel_id=1, source_target_pairs={{0,1},{1,0},{2,3},{3,2},{4,5},{5,4},{6,7},{7,6},{8,9},{9,8},{10,11... | collective-permute-start | bytes 196616 | tf_op jit(solution)/shard_map/ppermute | solution.py:707
  18.5 4.0 %collective-permute-start.6 = (f32[2,32,128]{2,1,0:T(8,128)S(1)}, f32[2,32,128]{2,1,0:T(8,128)S(1)}, u32[]{:S(2)}, u32[]{:S(2)}) collective-permute-start(f32[2,32,128]{2,1,0:T(8,128)S(1)} %meet.2), channel_id=1, source_target_pairs={{0,2},{1,3},{2,0},{3,1},{4,6},{5,7},{6,4},{7,5},{8,10},{9,11},{10,... | collective-permute-start | bytes 98312 | tf_op jit(solution)/shard_map/ppermute | solution.py:707
  23.7 6.8 %collective-permute-start.7 = (f32[32,8,128]{2,1,0:T(8,128)S(1)}, f32[32,8,128]{2,1,0:T(8,128)S(1)}, u32[]{:S(2)}, u32[]{:S(2)}) collective-permute-start(f32[32,8,128]{2,1,0:T(8,128)S(1)} %get-tuple-element.64.rows_ref), channel_id=1, source_target_pairs={{0,16},{16,0},{1,17},{17,1},{2,18},{18,2},{3,19},{19,3},{4,20},{20... | collective-permute-start | bytes 393224 | tf_op jit(solution)/shard_map/ppermute | solution.py:707
  24.3 3.9 %collective-permute-start.8 = (f32[1,32,128]{2,1,0:T(8,128)S(1)}, f32[1,32,128]{2,1,0:T(8,128)S(1)}, u32[]{:S(2)}, u32[]{:S(2)}) collective-permute-start(f32[1,32,128]{2,1,0:T(8,128)S(1)} %get-tuple-element.65.inner_ref), channel_id=1, source_target_pairs={{0,4},{4,0},{8,12},{12,8},{1,5},{5,1},{9,13},{13,9},{2,6},{6,2},{1... | collective-permute-start | bytes 49160 | tf_op jit(solution)/shard_map/ppermute | solution.py:707
  24.9 5.5 %collective-permute-start.9 = (f32[1,32,128]{2,1,0:T(8,128)S(1)}, f32[1,32,128]{2,1,0:T(8,128)S(1)}, u32[]{:S(2)}, u32[]{:S(2)}) collective-permute-start(f32[1,32,128]{2,1,0:T(8,128)S(1)} %get-tuple-element.66.outer_ref), channel_id=1, source_target_pairs={{0,12},{4,8},{8,4},{12,0},{1,13},{5,9},{9,5},{13,1},{2,14},{6,10},... | collective-permute-start | bytes 49160 | tf_op jit(solution)/shard_map/ppermute | solution.py:707
  32.2 1.3 %collective-permute-start.10 = (f32[4,32,128]{2,1,0:T(8,128)S(1)}, f32[4,32,128]{2,1,0:T(8,128)S(1)}, u32[]{:S(2)}, u32[]{:S(2)}) collective-permute-start(f32[4,32,128]{2,1,0:T(8,128)S(1)} %get-tuple-element.71.near_ref.refs_3_), channel_id=1, source_target_pairs={{0,1},{1,0},{2,3},{3,2},{4,5},{5,4},{6,7},{7,6},{8,9},{9,8},{10,11... | collective-permute-start | bytes 196616 | tf_op jit(solution)/shard_map/ppermute | solution.py:707
  33.5 4.0 %collective-permute-start.11 = (f32[2,32,128]{2,1,0:T(8,128)S(1)}, f32[2,32,128]{2,1,0:T(8,128)S(1)}, u32[]{:S(2)}, u32[]{:S(2)}) collective-permute-start(f32[2,32,128]{2,1,0:T(8,128)S(1)} %meet.3), channel_id=1, source_target_pairs={{0,2},{1,3},{2,0},{3,1},{4,6},{5,7},{6,4},{7,5},{8,10},{9,11},{10,... | collective-permute-start | bytes 98312 | tf_op jit(solution)/shard_map/ppermute | solution.py:707

commit v6 on v5

--- a/solution.py
+++ b/solution.py
@@ -19,7 +19,7 @@
 SLOT = 4
 UNROLL = 8
 CHUNKS = 4
-COLUMN = 6
+COLUMN = 10
 
 
 def lane_index():
@@ -349,14 +349,14 @@
     got_sinner_ref,
     got_souter_ref,
     coef_ref,
-    far_ref,
     nx_ref,
     ny_ref,
     ps_ref,
     y_ref,
-    near_ref,
-    wind_ref,
-    press_ref,
+    next_ref,
+    cross_ref,
+    mate_ref,
+    share_ref,
 ):
     levels, rows, _ = p_ref.shape
     count = rows // ROWS
@@ -386,22 +386,16 @@
     low_lanes, high_lanes = lane < SLOT, lane >= 128 - SLOT
     first_rows = row < 4
 
-    def correct_rows(level, state):
-        wind_ref[level], press_ref[level] = edge.correct(
+    def star(level):
+        new_x = tiles_of(nxc_ref, level, count)
+        new_y = tiles_of(nyc_ref, level, count)
+        stars = tiles_of(psc_ref, level, count)
+        wind, press = edge.correct(
             pltpu.roll(got_rows_ref[level] - rows_ref[level], 4, 0),
             jnp.where(first_rows, p_ref[level, :ROWS, :], p_ref[level, ROWS * last :, :]),
             ends,
             ends_change,
         )
-        return state
-
-    lax.fori_loop(0, levels, correct_rows, 0, unroll=2 * UNROLL)
-
-    def star(level):
-        new_x = tiles_of(nxc_ref, level, count)
-        new_y = tiles_of(nyc_ref, level, count)
-        stars = tiles_of(psc_ref, level, count)
-        wind, press = wind_ref[level], press_ref[level]
         new_x[0] = new_x[0] - jnp.where(first_rows, wind, 0.0)
         new_x[last] = new_x[last] - jnp.where(first_rows, 0.0, wind)
         stars[0] = stars[0] - jnp.where(first_rows, press, 0.0)
@@ -453,7 +447,7 @@
         1, levels, step, (zeros, here, force, zeros, zeros), unroll=UNROLL
     )
     value, first = sweep(levels - 1, below, zeros, force, value, first)
-    interface(first, value, bottom, here, coef_ref, far_ref, near_ref)
+    interface(first, value, bottom, here, coef_ref, next_ref, cross_ref, mate_ref, share_ref)
 
 
 def kernel_f(s_ref, r_ref, i_ref, q_ref, v_ref, stat_ref):
@@ -487,7 +481,7 @@
     stat_ref[4] = r_ref[levels - 1]
 
 
-PAIR_COEFS = ("own", "other", "den", "den_end", "den_link", "outer", "total", "facing")
+PAIR_COEFS = ("own", "other", "den", "den_end", "den_link", "outer", "total", "facing", "centre")
 
 
 def place_in_column():
@@ -495,7 +489,7 @@
     return (mine == 0) | (mine == 3), mine < 2, lax.rem(mine, 2) == 0
 
 
-def kernel_s(stat_ref, mate_ref, coef_ref, send_ref):
+def kernel_s(stat_ref, mate_ref, coef_ref):
     outermost, lower, even = place_in_column()
     count = stat_ref.shape[1] // ROWS
     for t in range(count):
@@ -521,14 +515,15 @@
             outer=outer_end,
             total=centre + weight * link,
             facing=vert_coef * jnp.where(even, mate[3], mate[4]),
+            centre=vert_coef * jnp.where(lower, inner[4], inner[3]),
         )
         for k, name in enumerate(PAIR_COEFS):
             coef_ref[k, part, :] = coefs[name]
-        send_ref[0, part, :] = coefs["total"]
-        send_ref[1, part, :] = vert_coef * jnp.where(lower, inner[4], inner[3])
-
-
-def interface(first, value, star_first, star_last, coef_ref, far_ref, near_ref):
+
+
+def interface(
+    first, value, star_first, star_last, coef_ref, next_ref, cross_ref, mate_ref, share_ref
+):
     outermost, lower, even = place_in_column()
     for t in range(len(first)):
         part = slice(ROWS * t, ROWS * (t + 1))
@@ -536,32 +531,48 @@
         sign = jnp.where(lower, 1.0, -1.0)
         star_centre = jnp.where(lower, star_last[t], star_first[t])
         star_outer = jnp.where(lower, star_first[t], star_last[t])
-        facing = jnp.where(outermost, coef["facing"], far_ref[1, part, :])
+        facing = jnp.where(outermost, coef["facing"], 0.0)
         centre = jnp.where(lower, value[t], first[t]) + sign * facing * star_centre
         outer = jnp.where(lower, first[t], value[t]) - sign * coef["facing"] * star_outer
         total = coef["own"] * centre + coef["other"] * outer
-        near_ref[0, part, :] = jnp.where(outermost, centre, outer)
-        near_ref[1, part, :] = jnp.where(even, star_last[t], star_first[t])
-        near_ref[2, part, :] = total
-        near_ref[3, part, :] = star_centre
-
-
-def kernel_u(near_ref, got_ref, send_ref):
-    outermost, _, _ = place_in_column()
-    send_ref[0] = near_ref[2] + got_ref[2]
-    send_ref[1] = jnp.where(outermost, got_ref[3], near_ref[3])
-
-
-def boundary(count, coef_ref, far_ref, stat_ref, near_ref, got_near_ref, got_far_ref):
+        for ref in (next_ref, cross_ref, share_ref):
+            ref[0, part, :] = total
+            ref[1, part, :] = star_centre
+        if next_ref.shape[0] > 3:
+            next_ref[2, part, :] = coef["total"]
+            next_ref[3, part, :] = coef["centre"]
+        mate_ref[0, part, :] = jnp.where(outermost, centre, outer)
+        mate_ref[1, part, :] = jnp.where(even, star_last[t], star_first[t])
+
+
+def boundary(
+    count,
+    got_next_ref,
+    got_cross_ref,
+    got_mate_ref,
+    got_share_ref,
+    mate_ref,
+    share_ref,
+    coef_ref,
+    far_ref,
+    stat_ref,
+    mate_stat_ref,
+):
     outermost, lower, _ = place_in_column()
+    sign = jnp.where(lower, 1.0, -1.0)
     parts = []
     for t in range(count):
         part = slice(ROWS * t, ROWS * (t + 1))
         coef = {name: coef_ref[k, part, :] for k, name in enumerate(PAIR_COEFS)}
-        far_total = far_ref[0, part, :]
-        own, got = near_ref[0, part, :], got_near_ref[0, part, :]
-        this = near_ref[2, part, :] + got_near_ref[2, part, :]
-        that = got_far_ref[0, part, :]
+        far_total, far_facing = far_ref[2, part, :], far_ref[3, part, :]
+        own, got = mate_ref[0, part, :], got_mate_ref[0, part, :]
+        this_star = jnp.where(outermost, got_share_ref[1, part, :], share_ref[1, part, :])
+        next_star = jnp.where(outermost, got_cross_ref[1, part, :], got_next_ref[1, part, :])
+        first_rate = jnp.where(outermost, mate_stat_ref[3, part, :], stat_ref[3, part, :])
+        last_rate = jnp.where(outermost, mate_stat_ref[4, part, :], stat_ref[4, part, :])
+        facing = vert_coef * jnp.where(lower, last_rate, first_rate)
+        this = share_ref[0, part, :] + got_share_ref[0, part, :] + sign * far_facing * this_star
+        that = got_cross_ref[0, part, :] + got_next_ref[0, part, :] - sign * facing * next_star
         middle = (that + far_total * this) / (1.0 - coef["total"] * far_total)
         from_outer = jnp.where(outermost, own, got)
         from_inner = jnp.where(outermost, got, own)
@@ -571,7 +582,7 @@
         zero = jnp.zeros_like(own)
         centre = jnp.where(outermost, between, middle)
         outer = jnp.where(outermost, zero, from_outer + coef["outer"] * between)
-        mate_star, next_star = got_near_ref[1, part, :], got_far_ref[1, part, :]
+        mate_star = got_mate_ref[1, part, :]
         star_centre = jnp.where(outermost, mate_star, next_star)
         star_outer = jnp.where(outermost, zero, mate_star)
         below, above = jnp.where(lower, outer, centre), jnp.where(lower, centre, outer)
@@ -619,9 +630,10 @@
     pressed(0, above, under)
 
 
-def kernel_c(y_ref, q_ref, i_ref, ps_ref, wx_ref, pw_ref, jac_ref, *refs):
+def kernel_c(*refs):
     column_refs = refs[:COLUMN]
-    x_ref, p_ref, rows_ref, inner_ref, outer_ref, pp_ref = refs[COLUMN:]
+    y_ref, q_ref, i_ref, ps_ref, wx_ref, pw_ref, jac_ref = refs[COLUMN : COLUMN + 7]
+    x_ref, p_ref, rows_ref, inner_ref, outer_ref, pp_ref = refs[COLUMN + 7 :]
     levels, rows, _ = y_ref.shape
     count = rows // ROWS
     edge = row_edge()
@@ -645,9 +657,10 @@
     put_tiles(pp_ref, 1, pres[1])
 
 
-def kernel_d(y_ref, q_ref, i_ref, ps_ref, *refs):
+def kernel_d(*refs):
     column_refs = refs[:COLUMN]
-    x_hbm, p_hbm, x_ref, p_ref, sems = refs[COLUMN:]
+    y_ref, q_ref, i_ref, ps_ref = refs[COLUMN : COLUMN + 4]
+    x_hbm, p_hbm, x_ref, p_ref, sems = refs[COLUMN + 4 :]
     levels, rows, _ = y_ref.shape
     share = levels // CHUNKS
     copies = []
@@ -718,16 +731,17 @@
 
 def exchange_lanes(inner, outer):
     count = lax.axis_size("gy")
+    got_inner = swap(inner, "gy", lambda i: i ^ 1)
     got_outer = swap(outer, "gy", lambda i: (i + 1 if i % 2 else i - 1) % count)
-    got_inner = swap(inner, "gy", lambda i: i ^ 1)
     return got_inner, got_outer
 
 
-def exchange_column(near):
-    plane = near.shape[1:]
-    got_near = swap(near, "lev", lambda i: i ^ 1)
-    (send,) = call(kernel_u, "meet", [(2,) + plane], near, got_near)
-    return near, got_near, swap(send, "lev", lambda i: i ^ 2)
+def exchange_column(following, cross, mate, share):
+    got_cross = swap(cross, "lev", lambda i: i ^ 2)
+    got_next = swap(following, "lev", lambda i: i ^ 3)
+    got_mate = swap(mate, "lev", lambda i: i ^ 1)
+    got_share = swap(share, "lev", lambda i: i ^ 1)
+    return got_next, got_cross, got_mate, got_share, mate, share
 
 
 def local(wind_x, wind_y, wind_z, pressure, jacobian, slope_x, slope_y, stiffness):
@@ -741,7 +755,7 @@
     edge, inner, outer, ends = call(
         kernel_a,
         "start",
-        [(levels + 1, ROWS, lanes), pair, pair, pair],
+        [(levels + 1, ROWS, lanes), pair, (3,) + plane, pair],
         pressure,
         wind_x,
         wind_y,
@@ -762,16 +776,15 @@
         kernel_f, "factor", [field, field, field, field, (5,) + plane], stiffness
     )
     mate = swap(stat, "lev", lambda i: i ^ 1)
-    coef, send = call(kernel_s, "pairs", [(len(PAIR_COEFS),) + plane, pair], stat, mate)
-    far = swap(send, "lev", lambda i: i ^ 2)
+    (coef,) = call(kernel_s, "pairs", [(len(PAIR_COEFS),) + plane], stat, mate)
     for substep in range(SUBSTEPS):
         closed = call(
             kernel_m, "interior", [field, field, field], pressure, wind_x, wind_y, jacobian
         )
-        wind_x, wind_y, star, value, near = call(
+        wind_x, wind_y, star, value, *faces = call(
             kernel_b,
             "sweep",
-            [field, field, field, field, (4,) + plane],
+            [field, field, field, field, (3 if substep else 4,) + plane, pair, pair, pair],
             pressure,
             *closed,
             wind_z,
@@ -786,17 +799,19 @@
             *got,
             *static_edges,
             coef,
-            far,
-            keep=tuple(range(5)),
-            scratch=[pltpu.VMEM((levels, ROWS, lanes), jnp.float32)] * 2,
-        )
-        column = (coef, far, stat) + exchange_column(near)
+            keep=tuple(range(8)),
+        )
+        column = exchange_column(*faces)
+        if not substep:
+            far = column[0]
+        column += (coef, far, stat, mate)
         if substep < SUBSTEPS - 1:
             (packed,) = call(kernel_n, "pack", [pair], wind_y)
             wind_z, pressure, edge, inner, outer, ends = call(
                 kernel_c,
                 "finish",
-                [field, field, (levels, ROWS, lanes), (1,) + plane, (1,) + plane, pair],
+                [field, field, (levels, ROWS, lanes), (1,) + plane, pair, pair],
+                *column,
                 value,
                 prod,
                 inv,
@@ -804,7 +819,6 @@
                 wind_x,
                 packed,
                 jacobian,
-                *column,
             )
             sent = (edge, inner, outer)
             got = (exchange_rows(edge),) + exchange_lanes(inner, outer)
@@ -813,11 +827,11 @@
                 kernel_d,
                 "last",
                 [field, field],
+                *column,
                 value,
                 prod,
                 inv,
                 star,
-                *column,
                 far_out=True,
                 scratch=[
                     pltpu.VMEM(field, jnp.float32),

time: 38.8 us -> 36.5 us (0.941)
  waiting for transfers between devices: 9.22 us -> 8.03 us
  starting transfers between devices: 14.4 us -> 13.7 us
  Pallas kernels: 12.6 us -> 12.1 us
    ppermute x12 -> x15, waiting for transfers between devices: 9.22 us -> 8.03 us  [swap(): return lax.ppermute(value, axis, [(i, partner(i)) for i in range(count)])]
    ppermute x12 -> x15, starting transfers between devices: 14.4 us -> 13.7 us  [swap(): return lax.ppermute(value, axis, [(i, partner(i)) for i in range(count)])]
    pallas_call x12 -> x10, Pallas kernels: 12.6 us -> 12.1 us  [call(): pl.pallas_call(kernel, out_shape=[pltpu.VMEM(s, jnp.float32) if k in keep...]
  transfers between devices with their start and end apart: 12 -> 15, of which waited for: 8 -> 4; matrix products, arithmetic and copies ran while one was open for 4% -> 4% of each run, Pallas kernels for 11% -> 11%
where the time goes in v6:
time: 36.5 us; the launch traced here: 36.3 us
  starting transfers between devices  13.7 us (38%)
  Pallas kernels  12.1 us (33%)
  waiting for transfers between devices  8.03 us (22%)
  local copies, waits for them, and re-layouts  1.63 us (4%)
  between operations  0.83 us (2%)
    ppermute x15, starting transfers between devices, swap(): return lax.ppermute(value, axis, [(i, partner(i)) for i in range(count)])  13.7 us
    pallas_call x10, Pallas kernels, call(): pl.pallas_call(kernel, out_shape=[pltpu.VMEM(s, jnp.float32) if k in keep...  12.1 us
    ppermute x15, waiting for transfers between devices, swap(): return lax.ppermute(value, axis, [(i, partner(i)) for i in range(count)])  8.03 us
    unnamed x18, local copies, waits for them, and re-layouts  1.63 us
  transfers between devices with their start and end apart: 15, of which 4 were waited for; matrix products, arithmetic and copies ran while one was open for 4% of the time, Pallas kernels for 11%

profile of v6, /device:TPU:0, one launch (start us, length us, event | category | flops | bytes accessed | tf_op | source)
XLA Modules:
  0.0 36.3 jit_solution(14035626842305552924)
XLA Ops:
  0.7 2.7 %start.1 = (f32[33,8,128]{2,1,0:T(8,128)S(1)}, f32[2,32,128]{2,1,0:T(8,128)S(1)}, f32[3,32,128]{2,1,0:T(8,128)S(1)}, f32[2,32,128]{2,1,0:T(8,128)S(1)}) custom-call(f32[32,32,128]{2,1,0:T(8,128)} %p_ref.3, f32[32,32,128]{2,1,0:T(8,128)} %wx_hbm.1, f32[32,32,128]{2,1,0:T(8,128)} %wy_hbm.1, f32[32,128]{1,0:T(8,128)} %jac_ref.7), custom_call_target="tpu_custom_call" | custom-call | flops 459776 | bytes 1839104 | tf_op jit(solution)/shard_map/start/pallas_call | solution.py:701
  3.4 3.0 %collective-permute-start = (f32[33,8,128]{2,1,0:T(8,128)S(1)}, f32[33,8,128]{2,1,0:T(8,128)S(1)}, u32[]{:S(2)}, u32[]{:S(2)}) collective-permute-start(f32[33,8,128]{2,1,0:T(8,128)S(1)} %get-tuple-element.50.rows_ref.srows_ref), channel_id=1, source_target_pairs={{0,16},{16,0},{1,17},{17,1},{2,18},{18,2},{3,19},{19,3},{4,20},{20... | collective-permute-start | bytes 405512 | tf_op jit(solution)/shard_map/ppermute | solution.py:720
  6.4 0.7 %factor.1 = (f32[32,32,128]{2,1,0:T(8,128)S(1)}, f32[32,32,128]{2,1,0:T(8,128)S(1)}, f32[32,32,128]{2,1,0:T(8,128)S(1)}, f32[32,32,128]{2,1,0:T(8,128)S(1)}, f32[5,32,128]{2,1,0:T(8,128)S(1)}) custom-call(f32[32,32,128]{2,1,0:T(8,128)S(1)} %copy-done.5), custom_call_target="tpu_custom_call" | custom-call | flops 675840 | bytes 2703360 | tf_op jit(solution)/shard_map/factor/pallas_call | solution.py:701
  7.2 3.7 %collective-permute-start.2 = (f32[3,32,128]{2,1,0:T(8,128)S(1)}, f32[3,32,128]{2,1,0:T(8,128)S(1)}, u32[]{:S(2)}, u32[]{:S(2)}) collective-permute-start(f32[3,32,128]{2,1,0:T(8,128)S(1)} %get-tuple-element.52.outer_ref.souter_ref), channel_id=1, source_target_pairs={{0,12},{4,8},{8,4},{12,0},{1,13},{5,9},{9,5},{13,1},{2,14},{6,10},... | collective-permute-start | bytes 147464 | tf_op jit(solution)/shard_map/ppermute | solution.py:720
  10.9 1.4 %interior.2 = (f32[32,32,128]{2,1,0:T(8,128)S(1)}, f32[32,32,128]{2,1,0:T(8,128)S(1)}, f32[32,32,128]{2,1,0:T(8,128)S(1)}) custom-call(f32[32,32,128]{2,1,0:T(8,128)S(1)} %copy-done, f32[32,32,128]{2,1,0:T(8,128)S(1)} %copy-done.1, f32[32,32,128]{2,1,0:T(8,128)S(1)} %copy-done.2, f32[32,128]{1,0:T(8,128)S(1)} %copy-done.3), custom_call_target="tpu_custom_call" | custom-call | flops 790528 | bytes 3162112 | tf_op jit(solution)/shard_map/interior/pallas_call | solution.py:701
  12.4 2.4 %collective-permute-done.1.got_inner_ref.got_sinner_ref = f32[2,32,128]{2,1,0:T(8,128)S(1)} collective-permute-done((f32[2,32,128]{2,1,0:T(8,128)S(1)}, f32[2,32,128]{2,1,0:T(8,128)S(1)}, u32[]{:S(2)}, u32[]{:S(2)}) %collective-permute-start.1) | collective-permute-done | bytes 32800 | tf_op jit(solution)/shard_map/ppermute | solution.py:720
  14.8 1.5 %sweep.2 = (f32[32,32,128]{2,1,0:T(8,128)S(1)}, f32[32,32,128]{2,1,0:T(8,128)S(1)}, f32[32,32,128]{2,1,0:T(8,128)S(1)}, f32[32,32,128]{2,1,0:T(8,128)S(1)}, f32[...) custom-call(f32[32,32,128]{2,1,0:T(8,128)S(1)} %copy-done, ...), custom_call_target="tpu_custom_call" | custom-call | flops 1888256 | bytes 7553024 | tf_op jit(solution)/shard_map/sweep/pallas_call | solution.py:701
  16.5 1.5 %collective-permute-start.5 = (f32[2,32,128]{2,1,0:T(8,128)S(1)}, f32[2,32,128]{2,1,0:T(8,128)S(1)}, u32[]{:S(2)}, u32[]{:S(2)}) collective-permute-start(f32[2,32,128]{2,1,0:T(8,128)S(1)} %get-tuple-element.55), channel_id=1, source_target_pairs={{0,2},{1,3},{2,0},{3,1},{4,6},{5,7},{6,4},{7,5},{8,10},{9,11},{10,... | collective-permute-start | bytes 98312 | tf_op jit(solution)/shard_map/ppermute | solution.py:720
  18.0 0.3 collective-permute-start.6
  18.3 0.2 collective-permute-start.7
  18.5 0.5 %pack.1.refs_15_ = f32[2,32,128]{2,1,0:T(8,128)S(1)} custom-call(f32[32,32,128]{2,1,0:T(8,128)S(1)} %get-tuple-element.62.wy_ref), custom_call_target="tpu_custom_call" | custom-call | flops 139264 | bytes 557056 | tf_op jit(solution)/shard_map/pack/pallas_call | solution.py:701
  19.0 2.5 %collective-permute-done.5.refs_1_ = f32[2,32,128]{2,1,0:T(8,128)S(1)} collective-permute-done((f32[2,32,128]{2,1,0:T(8,128)S(1)}, f32[2,32,128]{2,1,0:T(8,128)S(1)}, u32[]{:S(2)}, u32[]{:S(2)}) %collective-permute-start.5) | collective-permute-done | bytes 32800 | tf_op jit(solution)/shard_map/ppermute | solution.py:720
  21.5 1.3 %finish.1 = (f32[32,32,128]{2,1,0:T(8,128)S(1)}, f32[32,32,128]{2,1,0:T(8,128)S(1)}, f32[32,8,128]{2,1,0:T(8,128)S(1)}, f32[1,32,128]{2,1,0:T(8,128)S(1)}, f32[2...) custom-call(f32[4,32,128]{2,1,0:T(8,128)S(1)} %collective-permute-done.4.refs_0_.refs_7_, ...), custom_call_target="tpu_custom_call" | custom-call | flops 1134592 | bytes 4538368 | tf_op jit(solution)/shard_map/finish/pallas_call | solution.py:701
  22.8 0.6 %collective-permute-start.8 = (f32[32,8,128]{2,1,0:T(8,128)S(1)}, f32[32,8,128]{2,1,0:T(8,128)S(1)}, u32[]{:S(2)}, u32[]{:S(2)}) collective-permute-start(f32[32,8,128]{2,1,0:T(8,128)S(1)} %get-tuple-element.69.rows_ref), channel_id=1, source_target_pairs={{0,16},{16,0},{1,17},{17,1},{2,18},{18,2},{3,19},{19,3},{4,20},{20... | collective-permute-start | bytes 393224 | tf_op jit(solution)/shard_map/ppermute | solution.py:720
  23.4 2.3 %collective-permute-start.10 = (f32[2,32,128]{2,1,0:T(8,128)S(1)}, f32[2,32,128]{2,1,0:T(8,128)S(1)}, u32[]{:S(2)}, u32[]{:S(2)}) collective-permute-start(f32[2,32,128]{2,1,0:T(8,128)S(1)} %get-tuple-element.71.outer_ref), channel_id=1, source_target_pairs={{0,12},{4,8},{8,4},{12,0},{1,13},{5,9},{9,5},{13,1},{2,14},{6,10},... | collective-permute-start | bytes 98312 | tf_op jit(solution)/shard_map/ppermute | solution.py:720
  25.7 1.4 %interior.3 = (f32[32,32,128]{2,1,0:T(8,128)S(1)}, f32[32,32,128]{2,1,0:T(8,128)S(1)}, f32[32,32,128]{2,1,0:T(8,128)S(1)}) custom-call(f32[32,32,128]{2,1,0:T(8,128)S(1)} %get-tuple-element.63.p_ref, f32[32,32,128]{2,1,0:T(8,128)S(1)} %get-tuple-element.61.refs_14_.wx_ref, f32[32,32,128]{2,1,0:T(8,128)S(1)} %get-tuple-element.62.wy_ref, f32[32,128]{1,0:T(8,128)S(1)} %copy-done.3), custom_call_target="tpu_custom_call" | custom-call | flops 790528 | bytes 3162112 | tf_op jit(solution)/shard_map/interior/pallas_call | solution.py:701
  27.1 2.3 %collective-permute-done.9.got_inner_ref = f32[1,32,128]{2,1,0:T(8,128)S(1)} collective-permute-done((f32[1,32,128]{2,1,0:T(8,128)S(1)}, f32[1,32,128]{2,1,0:T(8,128)S(1)}, u32[]{:S(2)}, u32[]{:S(2)}) %collective-permute-start.9) | collective-permute-done | bytes 16416 | tf_op jit(solution)/shard_map/ppermute | solution.py:720
  29.4 1.5 %sweep.3 = (f32[32,32,128]{2,1,0:T(8,128)S(1)}, f32[32,32,128]{2,1,0:T(8,128)S(1)}, f32[32,32,128]{2,1,0:T(8,128)S(1)}, f32[32,32,128]{2,1,0:T(8,128)S(1)}, f32[...) custom-call(f32[32,32,128]{2,1,0:T(8,128)S(1)} %get-tuple-element.63.p, ...), custom_call_target="tpu_custom_call" | custom-call | flops 1865728 | bytes 7462912 | tf_op jit(solution)/shard_map/sweep/pallas_call | solution.py:701
  31.0 0.8 %collective-permute-start.12 = (f32[2,32,128]{2,1,0:T(8,128)S(1)}, f32[2,32,128]{2,1,0:T(8,128)S(1)}, u32[]{:S(2)}, u32[]{:S(2)}) collective-permute-start(f32[2,32,128]{2,1,0:T(8,128)S(1)} %get-tuple-element.75), channel_id=1, source_target_pairs={{0,2},{1,3},{2,0},{3,1},{4,6},{5,7},{6,4},{7,5},{8,10},{9,11},{10,... | collective-permute-start | bytes 98312 | tf_op jit(solution)/shard_map/ppermute | solution.py:720
  31.7 1.1 %collective-permute-start.13 = (f32[2,32,128]{2,1,0:T(8,128)S(1)}, f32[2,32,128]{2,1,0:T(8,128)S(1)}, u32[]{:S(2)}, u32[]{:S(2)}) collective-permute-start(f32[2,32,128]{2,1,0:T(8,128)S(1)} %get-tuple-element.76.refs_4_), channel_id=1, source_target_pairs={{0,1},{1,0},{2,3},{3,2},{4,5},{5,4},{6,7},{7,6},{8,9},{9,8},{10,11... | collective-permute-start | bytes 98312 | tf_op jit(solution)/shard_map/ppermute | solution.py:720
  32.8 0.8 %copy.12 = f32[32,32,128]{2,1,0:T(8,128)} copy(f32[32,32,128]{2,1,0:T(8,128)S(1)} %get-tuple-element.82) | data formatting | bytes 1048576
  33.6 0.8 %copy.13 = f32[32,32,128]{2,1,0:T(8,128)} copy(f32[32,32,128]{2,1,0:T(8,128)S(1)} %get-tuple-element.83) | data formatting | bytes 1048576
  34.4 0.8 %collective-permute-done.12.refs_1_ = f32[2,32,128]{2,1,0:T(8,128)S(1)} collective-permute-done((f32[2,32,128]{2,1,0:T(8,128)S(1)}, f32[2,32,128]{2,1,0:T(8,128)S(1)}, u32[]{:S(2)}, u32[]{:S(2)}) %collective-permute-start.12) | collective-permute-done | bytes 32800 | tf_op jit(solution)/shard_map/ppermute | solution.py:720
  35.2 1.2 %last.1 = (f32[32,32,128]{2,1,0:T(8,128)}, f32[32,32,128]{2,1,0:T(8,128)}) custom-call(f32[3,32,128]{2,1,0:T(8,128)S(1)} %collective-permute-done.11.refs_0_, f32[2,32,128]{2,1,0:T(8,128)S(1)} %collective-permute-done.12.refs_1_, f32[2,32,128]{2,1,0:T(8,128)S(1)} %collective-permute-done.13.refs_2_, f32[2,32,128]{2,1,0:T(8,128)S(1)} %collective-permute-done.14.refs_3_, ...), custom_call_target="tpu_custom_call" | custom-call | flops 933888 | bytes 3735552 | tf_op jit(solution)/shard_map/last/pallas_call | solution.py:701
  (34 shorter events, 0.4 us)
Async XLA Ops:
  0.6 5.8 %copy-start.5 = (f32[32,32,128]{2,1,0:T(8,128)S(1)}, f32[32,32,128]{2,1,0:T(8,128)}, u32[]{:S(2)}) copy-start(f32[32,32,128]{2,1,0:T(8,128)} %s_ref.1) | copy-start | bytes 1572868
  0.6 10.3 %copy-start.1 = (f32[32,32,128]{2,1,0:T(8,128)S(1)}, f32[32,32,128]{2,1,0:T(8,128)}, u32[]{:S(2)}) copy-start(f32[32,32,128]{2,1,0:T(8,128)} %wx_hbm.1) | copy-start | bytes 1572868
  0.7 10.2 %copy-start.2 = (f32[32,32,128]{2,1,0:T(8,128)S(1)}, f32[32,32,128]{2,1,0:T(8,128)}, u32[]{:S(2)}) copy-start(f32[32,32,128]{2,1,0:T(8,128)} %wy_hbm.1) | copy-start | bytes 1572868
  0.7 10.2 %copy-start.3 = (f32[32,128]{1,0:T(8,128)S(1)}, f32[32,128]{1,0:T(8,128)}, u32[]{:S(2)}) copy-start(f32[32,128]{1,0:T(8,128)} %jac_ref.7) | copy-start | bytes 49156
  3.3 7.6 %copy-start = (f32[32,32,128]{2,1,0:T(8,128)S(1)}, f32[32,32,128]{2,1,0:T(8,128)}, u32[]{:S(2)}) copy-start(f32[32,32,128]{2,1,0:T(8,128)} %p_ref.3) | copy-start | bytes 1572868
  3.4 11.4 %collective-permute-start = (f32[33,8,128]{2,1,0:T(8,128)S(1)}, f32[33,8,128]{2,1,0:T(8,128)S(1)}, u32[]{:S(2)}, u32[]{:S(2)}) collective-permute-start(f32[33,8,128]{2,1,0:T(8,128)S(1)} %get-tuple-element.50.rows_ref.srows_ref), channel_id=1, source_target_pairs={{0,16},{16,0},{1,17},{17,1},{2,18},{18,2},{3,19},{19,3},{4,20},{20... | collective-permute-start | bytes 405512 | tf_op jit(solution)/shard_map/ppermute | solution.py:720
  7.1 5.2 %collective-permute-start.3 = (f32[5,32,128]{2,1,0:T(8,128)S(1)}, f32[5,32,128]{2,1,0:T(8,128)S(1)}, u32[]{:S(2)}, u32[]{:S(2)}) collective-permute-start(f32[5,32,128]{2,1,0:T(8,128)S(1)} %get-tuple-element.53.stat_ref.refs_8_), channel_id=1, source_target_pairs={{0,1},{1,0},{2,3},{3,2},{4,5},{5,4},{6,7},{7,6},{8,9},{9,8},{10,11... | collective-permute-start | bytes 245768 | tf_op jit(solution)/shard_map/ppermute | solution.py:720
  7.2 7.6 %collective-permute-start.2 = (f32[3,32,128]{2,1,0:T(8,128)S(1)}, f32[3,32,128]{2,1,0:T(8,128)S(1)}, u32[]{:S(2)}, u32[]{:S(2)}) collective-permute-start(f32[3,32,128]{2,1,0:T(8,128)S(1)} %get-tuple-element.52.outer_ref.souter_ref), channel_id=1, source_target_pairs={{0,12},{4,8},{8,4},{12,0},{1,13},{5,9},{9,5},{13,1},{2,14},{6,10},... | collective-permute-start | bytes 147464 | tf_op jit(solution)/shard_map/ppermute | solution.py:720
  10.9 3.9 %collective-permute-start.1 = (f32[2,32,128]{2,1,0:T(8,128)S(1)}, f32[2,32,128]{2,1,0:T(8,128)S(1)}, u32[]{:S(2)}, u32[]{:S(2)}) collective-permute-start(f32[2,32,128]{2,1,0:T(8,128)S(1)} %get-tuple-element.51.inner_ref.sinner_ref), channel_id=1, source_target_pairs={{0,4},{4,0},{8,12},{12,8},{1,5},{5,1},{9,13},{13,9},{2,6},{6,2},{1... | collective-permute-start | bytes 98312 | tf_op jit(solution)/shard_map/ppermute | solution.py:720
  10.9 3.9 %copy-start.4 = (f32[32,32,128]{2,1,0:T(8,128)S(1)}, f32[32,32,128]{2,1,0:T(8,128)}, u32[]{:S(2)}) copy-start(f32[32,32,128]{2,1,0:T(8,128)} %wz_ref.1) | copy-start | bytes 1572868
  12.4 2.5 %copy-start.6 = (f32[32,128]{1,0:T(8,128)S(1)}, f32[32,128]{1,0:T(8,128)}, u32[]{:S(2)}) copy-start(f32[32,128]{1,0:T(8,128)} %sx_ref.3) | copy-start | bytes 49156
  12.4 2.5 %copy-start.7 = (f32[32,128]{1,0:T(8,128)S(1)}, f32[32,128]{1,0:T(8,128)}, u32[]{:S(2)}) copy-start(f32[32,128]{1,0:T(8,128)} %sy_ref.3) | copy-start | bytes 49156
  16.3 5.2 %collective-permute-start.4 = (f32[4,32,128]{2,1,0:T(8,128)S(1)}, f32[4,32,128]{2,1,0:T(8,128)S(1)}, u32[]{:S(2)}, u32[]{:S(2)}) collective-permute-start(f32[4,32,128]{2,1,0:T(8,128)S(1)} %get-tuple-element.54), channel_id=1, source_target_pairs={{0,3},{1,2},{2,1},{3,0},{4,7},{5,6},{6,5},{7,4},{8,11},{9,10},{10,... | collective-permute-start | bytes 196616 | tf_op jit(solution)/shard_map/ppermute | solution.py:720
  16.5 5.0 %collective-permute-start.5 = (f32[2,32,128]{2,1,0:T(8,128)S(1)}, f32[2,32,128]{2,1,0:T(8,128)S(1)}, u32[]{:S(2)}, u32[]{:S(2)}) collective-permute-start(f32[2,32,128]{2,1,0:T(8,128)S(1)} %get-tuple-element.55), channel_id=1, source_target_pairs={{0,2},{1,3},{2,0},{3,1},{4,6},{5,7},{6,4},{7,5},{8,10},{9,11},{10,... | collective-permute-start | bytes 98312 | tf_op jit(solution)/shard_map/ppermute | solution.py:720
  18.0 3.5 %collective-permute-start.6 = (f32[2,32,128]{2,1,0:T(8,128)S(1)}, f32[2,32,128]{2,1,0:T(8,128)S(1)}, u32[]{:S(2)}, u32[]{:S(2)}) collective-permute-start(f32[2,32,128]{2,1,0:T(8,128)S(1)} %get-tuple-element.56.refs_4_), channel_id=1, source_target_pairs={{0,1},{1,0},{2,3},{3,2},{4,5},{5,4},{6,7},{7,6},{8,9},{9,8},{10,11... | collective-permute-start | bytes 98312 | tf_op jit(solution)/shard_map/ppermute | solution.py:720
  18.3 3.2 %collective-permute-start.7 = (f32[2,32,128]{2,1,0:T(8,128)S(1)}, f32[2,32,128]{2,1,0:T(8,128)S(1)}, u32[]{:S(2)}, u32[]{:S(2)}) collective-permute-start(f32[2,32,128]{2,1,0:T(8,128)S(1)} %get-tuple-element.57.refs_5_), channel_id=1, source_target_pairs={{0,1},{1,0},{2,3},{3,2},{4,5},{5,4},{6,7},{7,6},{8,9},{9,8},{10,11... | collective-permute-start | bytes 98312 | tf_op jit(solution)/shard_map/ppermute | solution.py:720
  22.8 6.6 %collective-permute-start.8 = (f32[32,8,128]{2,1,0:T(8,128)S(1)}, f32[32,8,128]{2,1,0:T(8,128)S(1)}, u32[]{:S(2)}, u32[]{:S(2)}) collective-permute-start(f32[32,8,128]{2,1,0:T(8,128)S(1)} %get-tuple-element.69.rows_ref), channel_id=1, source_target_pairs={{0,16},{16,0},{1,17},{17,1},{2,18},{18,2},{3,19},{19,3},{4,20},{20... | collective-permute-start | bytes 393224 | tf_op jit(solution)/shard_map/ppermute | solution.py:720
  23.4 6.1 %collective-permute-start.10 = (f32[2,32,128]{2,1,0:T(8,128)S(1)}, f32[2,32,128]{2,1,0:T(8,128)S(1)}, u32[]{:S(2)}, u32[]{:S(2)}) collective-permute-start(f32[2,32,128]{2,1,0:T(8,128)S(1)} %get-tuple-element.71.outer_ref), channel_id=1, source_target_pairs={{0,12},{4,8},{8,4},{12,0},{1,13},{5,9},{9,5},{13,1},{2,14},{6,10},... | collective-permute-start | bytes 98312 | tf_op jit(solution)/shard_map/ppermute | solution.py:720
  25.7 3.7 %collective-permute-start.9 = (f32[1,32,128]{2,1,0:T(8,128)S(1)}, f32[1,32,128]{2,1,0:T(8,128)S(1)}, u32[]{:S(2)}, u32[]{:S(2)}) collective-permute-start(f32[1,32,128]{2,1,0:T(8,128)S(1)} %get-tuple-element.70.inner_ref), channel_id=1, source_target_pairs={{0,4},{4,0},{8,12},{12,8},{1,5},{5,1},{9,13},{13,9},{2,6},{6,2},{1... | collective-permute-start | bytes 49160 | tf_op jit(solution)/shard_map/ppermute | solution.py:720
  30.9 4.3 %collective-permute-start.11 = (f32[3,32,128]{2,1,0:T(8,128)S(1)}, f32[3,32,128]{2,1,0:T(8,128)S(1)}, u32[]{:S(2)}, u32[]{:S(2)}) collective-permute-start(f32[3,32,128]{2,1,0:T(8,128)S(1)} %get-tuple-element.74), channel_id=1, source_target_pairs={{0,3},{1,2},{2,1},{3,0},{4,7},{5,6},{6,5},{7,4},{8,11},{9,10},{10,... | collective-permute-start | bytes 147464 | tf_op jit(solution)/shard_map/ppermute | solution.py:720
  31.0 4.2 %collective-permute-start.12 = (f32[2,32,128]{2,1,0:T(8,128)S(1)}, f32[2,32,128]{2,1,0:T(8,128)S(1)}, u32[]{:S(2)}, u32[]{:S(2)}) collective-permute-start(f32[2,32,128]{2,1,0:T(8,128)S(1)} %get-tuple-element.75), channel_id=1, source_target_pairs={{0,2},{1,3},{2,0},{3,1},{4,6},{5,7},{6,4},{7,5},{8,10},{9,11},{10,... | collective-permute-start | bytes 98312 | tf_op jit(solution)/shard_map/ppermute | solution.py:720
  31.7 3.5 %collective-permute-start.13 = (f32[2,32,128]{2,1,0:T(8,128)S(1)}, f32[2,32,128]{2,1,0:T(8,128)S(1)}, u32[]{:S(2)}, u32[]{:S(2)}) collective-permute-start(f32[2,32,128]{2,1,0:T(8,128)S(1)} %get-tuple-element.76.refs_4_), channel_id=1, source_target_pairs={{0,1},{1,0},{2,3},{3,2},{4,5},{5,4},{6,7},{7,6},{8,9},{9,8},{10,11... | collective-permute-start | bytes 98312 | tf_op jit(solution)/shard_map/ppermute | solution.py:720
  32.8 2.4 %collective-permute-start.14 = (f32[2,32,128]{2,1,0:T(8,128)S(1)}, f32[2,32,128]{2,1,0:T(8,128)S(1)}, u32[]{:S(2)}, u32[]{:S(2)}) collective-permute-start(f32[2,32,128]{2,1,0:T(8,128)S(1)} %get-tuple-element.77.refs_5_), channel_id=1, source_target_pairs={{0,1},{1,0},{2,3},{3,2},{4,5},{5,4},{6,7},{7,6},{8,9},{9,8},{10,11... | collective-permute-start | bytes 98312 | tf_op jit(solution)/shard_map/ppermute | solution.py:720

commit v7 on v6

--- a/solution.py
+++ b/solution.py
@@ -19,7 +19,8 @@
 SLOT = 4
 UNROLL = 8
 CHUNKS = 4
-COLUMN = 10
+COLUMN = 8
+STATS = 5
 
 
 def lane_index():
@@ -224,7 +225,26 @@
 
 
 def kernel_a(
-    p_hbm, wx_hbm, wy_hbm, jac_hbm, rows_ref, inner_ref, outer_ref, pp_ref, p_ref, wx_ref, wy_ref, jac_ref, sems
+    p_hbm,
+    wx_hbm,
+    wy_hbm,
+    jac_hbm,
+    s_hbm,
+    rows_ref,
+    inner_ref,
+    outer_ref,
+    pp_ref,
+    r_ref,
+    i_ref,
+    q_ref,
+    v_ref,
+    stat_ref,
+    p_ref,
+    wx_ref,
+    wy_ref,
+    jac_ref,
+    s_ref,
+    sems,
 ):
     levels, rows, _ = p_hbm.shape
     count = rows // ROWS
@@ -238,29 +258,56 @@
     tail = pl.ds(rows - ROWS, ROWS)
     parts = [pl.ds(c * share, share) for c in range(CHUNKS)]
     pres_in = [fetch(p_hbm.at[s], p_ref.at[s], sems.at[0, c]) for c, s in enumerate(parts)]
-    wind_in = [fetch(wy_hbm.at[s], wy_ref.at[s], sems.at[1, c]) for c, s in enumerate(parts)]
+    stiff_in = [fetch(s_hbm.at[s], s_ref.at[s], sems.at[1, c]) for c, s in enumerate(parts)]
+    wind_in = [fetch(wy_hbm.at[s], wy_ref.at[s], sems.at[2, c]) for c, s in enumerate(parts)]
     ends_in = [
-        fetch(jac_hbm, jac_ref, sems.at[2, 0]),
-        fetch(wx_hbm.at[:, pl.ds(0, ROWS)], wx_ref.at[:, pl.ds(0, ROWS)], sems.at[2, 1]),
-        fetch(wx_hbm.at[:, tail], wx_ref.at[:, pl.ds(ROWS, ROWS)], sems.at[2, 2]),
+        fetch(jac_hbm, jac_ref, sems.at[3, 0]),
+        fetch(wx_hbm.at[:, pl.ds(0, ROWS)], wx_ref.at[:, pl.ds(0, ROWS)], sems.at[3, 1]),
+        fetch(wx_hbm.at[:, tail], wx_ref.at[:, pl.ds(ROWS, ROWS)], sems.at[3, 2]),
     ]
-
-    def pack(ref, copies):
-        packer = Packer(count)
-        state = packer.start
-        for c, copy in enumerate(copies):
-            copy.wait()
-            state = lax.fori_loop(
-                c * share,
-                (c + 1) * share,
-                lambda level, state: packer.add(level, tiles_of(ref, level, count), state),
-                state,
-                unroll=UNROLL,
-            )
-        return packer.done(state)
-
-    pres = pack(p_ref, pres_in)
-    wind = pack(wy_ref, wind_in)
+    packer = Packer(count)
+
+    def down(level, carry):
+        state, excess, prod = carry
+        for t in range(count):
+            part = slice(ROWS * t, ROWS * (t + 1))
+            rate = 1.0 / s_ref[level, part, :]
+            grown = rate + excess[t]
+            inv = 1.0 / (1.0 + grown)
+            excess[t] = grown * inv
+            prod[t] = prod[t] * inv
+            r_ref[level, part, :] = rate
+            i_ref[level, part, :] = inv
+            q_ref[level, part, :] = prod[t]
+        return packer.add(level, tiles_of(p_ref, level, count), state), excess, prod
+
+    def up(step, carry):
+        state, value = carry
+        level = levels - 1 - step
+        for t in range(count):
+            part = slice(ROWS * t, ROWS * (t + 1))
+            value[t] = q_ref[level, part, :] + i_ref[level, part, :] * value[t]
+            v_ref[level, part, :] = value[t]
+        return packer.add(step, tiles_of(wy_ref, step, count), state), value
+
+    ones = [jnp.ones((ROWS, 128), jnp.float32)] * count
+    carry = packer.start, list(ones), list(ones)
+    for c in range(CHUNKS):
+        pres_in[c].wait()
+        stiff_in[c].wait()
+        carry = lax.fori_loop(c * share, (c + 1) * share, down, carry, unroll=UNROLL)
+    pres = packer.done(carry[0])
+    carry = packer.start, [jnp.zeros_like(one) for one in ones]
+    for c in range(CHUNKS):
+        wind_in[c].wait()
+        carry = lax.fori_loop(c * share, (c + 1) * share, up, carry, unroll=UNROLL)
+    wind = packer.done(carry[0])
+    put_tiles(stat_ref, 0, carry[1])
+    stat_ref[1] = q_ref[levels - 1]
+    stat_ref[2] = i_ref[levels - 1]
+    stat_ref[3] = r_ref[0]
+    stat_ref[4] = r_ref[levels - 1]
+
     for copy in ends_in:
         copy.wait()
     jac = planes_of(jac_ref, count)
@@ -275,8 +322,8 @@
 
     lax.fori_loop(0, levels, step, 0, unroll=2 * UNROLL)
     rows_ref[levels] = ends
-    down, up = lane_payload(pres, wind, jac)
-    put_pair(inner_ref, outer_ref, 0, down, up)
+    down_out, up_out = lane_payload(pres, wind, jac)
+    put_pair(inner_ref, outer_ref, 0, down_out, up_out)
     put_pair(
         inner_ref,
         outer_ref,
@@ -386,25 +433,27 @@
     low_lanes, high_lanes = lane < SLOT, lane >= 128 - SLOT
     first_rows = row < 4
 
-    def star(level):
-        new_x = tiles_of(nxc_ref, level, count)
-        new_y = tiles_of(nyc_ref, level, count)
-        stars = tiles_of(psc_ref, level, count)
-        wind, press = edge.correct(
-            pltpu.roll(got_rows_ref[level] - rows_ref[level], 4, 0),
-            jnp.where(first_rows, p_ref[level, :ROWS, :], p_ref[level, ROWS * last :, :]),
-            ends,
-            ends_change,
-        )
-        new_x[0] = new_x[0] - jnp.where(first_rows, wind, 0.0)
-        new_x[last] = new_x[last] - jnp.where(first_rows, 0.0, wind)
-        stars[0] = stars[0] - jnp.where(first_rows, press, 0.0)
-        stars[last] = stars[last] - jnp.where(first_rows, 0.0, press)
+    def star(level, which):
+        new_x = {t: nxc_ref[level, ROWS * t : ROWS * (t + 1), :] for t in which}
+        stars = {t: psc_ref[level, ROWS * t : ROWS * (t + 1), :] for t in which}
+        if 0 in which:
+            wind, press = edge.correct(
+                pltpu.roll(got_rows_ref[level] - rows_ref[level], 4, 0),
+                jnp.where(first_rows, p_ref[level, :ROWS, :], p_ref[level, ROWS * last :, :]),
+                ends,
+                ends_change,
+            )
+            new_x[0] = new_x[0] - jnp.where(first_rows, wind, 0.0)
+            new_x[last] = new_x[last] - jnp.where(first_rows, 0.0, wind)
+            stars[0] = stars[0] - jnp.where(first_rows, press, 0.0)
+            stars[last] = stars[last] - jnp.where(first_rows, 0.0, press)
         back = lax.rem(128 - SLOT * level, 128)
         forces = []
-        for t in range(count):
+        for t in which:
             part = slice(ROWS * t, ROWS * (t + 1))
-            new_y[t] = new_y[t] - jnp.where(outer, pltpu.roll(wind_fix[t], back, 1), 0.0)
+            new_y = nyc_ref[level, part, :] - jnp.where(
+                outer, pltpu.roll(wind_fix[t], back, 1), 0.0
+            )
             fix = jnp.where(
                 low_lanes,
                 pltpu.roll(low_fix[t], back, 1),
@@ -412,76 +461,43 @@
             )
             stars[t] = stars[t] - fix
             forces.append(
-                wz_ref[level, part, :]
-                + sx_ref[part, :] * new_x[t]
-                + sy_ref[part, :] * new_y[t]
+                wz_ref[level, part, :] + sx_ref[part, :] * new_x[t] + sy_ref[part, :] * new_y
             )
-        put_tiles(nx_ref, level, new_x)
-        put_tiles(ny_ref, level, new_y)
-        put_tiles(ps_ref, level, stars)
-        return stars, forces
-
-    def sweep(level, below, above, force, value, first):
-        rate = tiles_of(r_ref, level, count)
-        inv = tiles_of(i_ref, level, count)
-        gain = tiles_of(v_ref, level, count)
+            nx_ref[level, part, :] = new_x[t]
+            ny_ref[level, part, :] = new_y
+            ps_ref[level, part, :] = stars[t]
+        return [stars[t] for t in which], forces
+
+    def sweep(level, which, below, above, force, value, first):
         values, firsts = [], []
-        for t in range(count):
-            rhs = rate[t] * (force[t] - vert_coef * (above[t] - below[t]))
-            firsts.append(first[t] + gain[t] * rhs)
-            values.append((rhs + value[t]) * inv[t])
-        put_tiles(y_ref, level, values)
+        for k, t in enumerate(which):
+            part = slice(ROWS * t, ROWS * (t + 1))
+            rhs = r_ref[level, part, :] * (force[k] - vert_coef * (above[k] - below[k]))
+            firsts.append(first[k] + v_ref[level, part, :] * rhs)
+            values.append((rhs + value[k]) * i_ref[level, part, :])
+            y_ref[level, part, :] = values[k]
         return values, firsts
 
-    zeros = [jnp.zeros((ROWS, 128), jnp.float32)] * count
-    here, force = star(0)
-    bottom = here
-
-    def step(level, carry):
-        below, here, force, value, first = carry
-        above, force_next = star(level)
-        value, first = sweep(level - 1, below, above, force, value, first)
-        return here, above, force_next, value, first
-
-    below, here, force, value, first = lax.fori_loop(
-        1, levels, step, (zeros, here, force, zeros, zeros), unroll=UNROLL
-    )
-    value, first = sweep(levels - 1, below, zeros, force, value, first)
-    interface(first, value, bottom, here, coef_ref, next_ref, cross_ref, mate_ref, share_ref)
-
-
-def kernel_f(s_ref, r_ref, i_ref, q_ref, v_ref, stat_ref):
-    levels, rows, _ = s_ref.shape
-
-    def down(level, carry):
-        excess, prod = carry
-        rate = 1.0 / s_ref[level]
-        excess = rate + excess
-        inv = 1.0 / (1.0 + excess)
-        prod = prod * inv
-        r_ref[level] = rate
-        i_ref[level] = inv
-        q_ref[level] = prod
-        return excess * inv, prod
-
-    ones = jnp.ones((rows, 128), jnp.float32)
-    lax.fori_loop(0, levels, down, (ones, ones))
-
-    def up(step, value):
-        level = levels - 1 - step
-        value = q_ref[level] + i_ref[level] * value
-        v_ref[level] = value
-        return value
-
-    first = lax.fori_loop(0, levels, up, jnp.zeros((rows, 128), jnp.float32))
-    stat_ref[0] = first
-    stat_ref[1] = q_ref[levels - 1]
-    stat_ref[2] = i_ref[levels - 1]
-    stat_ref[3] = r_ref[0]
-    stat_ref[4] = r_ref[levels - 1]
-
-
-PAIR_COEFS = ("own", "other", "den", "den_end", "den_link", "outer", "total", "facing", "centre")
+    for which in ((0, last), tuple(range(1, last))):
+        zeros = [jnp.zeros((ROWS, 128), jnp.float32)] * len(which)
+        bottom, force = star(0, which)
+
+        def step(level, carry, which=which):
+            below, here, force, value, first = carry
+            above, force_next = star(level, which)
+            value, first = sweep(level - 1, which, below, above, force, value, first)
+            return here, above, force_next, value, first
+
+        below, here, force, value, first = lax.fori_loop(
+            1, levels, step, (zeros, bottom, force, zeros, zeros), unroll=UNROLL
+        )
+        value, first = sweep(levels - 1, which, below, zeros, force, value, first)
+        interface(
+            which, first, value, bottom, here, coef_ref, next_ref, cross_ref, mate_ref, share_ref
+        )
+
+
+PAIR_COEFS = ("own", "other", "den", "den_end", "den_link", "outer", "total", "facing", "centre", "first", "last")
 
 
 def place_in_column():
@@ -491,11 +507,10 @@
 
 def kernel_s(stat_ref, mate_ref, coef_ref):
     outermost, lower, even = place_in_column()
-    count = stat_ref.shape[1] // ROWS
-    for t in range(count):
+    for t in range(coef_ref.shape[1] // ROWS):
         part = slice(ROWS * t, ROWS * (t + 1))
-        mine = [stat_ref[k, part, :] for k in range(5)]
-        mate = [mate_ref[k, part, :] for k in range(5)]
+        mine = [stat_ref[k, part, :] for k in range(STATS)]
+        mate = [mate_ref[k, part, :] for k in range(STATS)]
         outer = [jnp.where(outermost, a, b) for a, b in zip(mine, mate)]
         inner = [jnp.where(outermost, b, a) for a, b in zip(mine, mate)]
         outer_end = jnp.where(lower, outer[2], outer[0])
@@ -516,17 +531,19 @@
             total=centre + weight * link,
             facing=vert_coef * jnp.where(even, mate[3], mate[4]),
             centre=vert_coef * jnp.where(lower, inner[4], inner[3]),
+            first=vert_coef * mine[3],
+            last=vert_coef * mine[4],
         )
         for k, name in enumerate(PAIR_COEFS):
             coef_ref[k, part, :] = coefs[name]
 
 
 def interface(
-    first, value, star_first, star_last, coef_ref, next_ref, cross_ref, mate_ref, share_ref
+    which, first, value, star_first, star_last, coef_ref, next_ref, cross_ref, mate_ref, share_ref
 ):
     outermost, lower, even = place_in_column()
-    for t in range(len(first)):
-        part = slice(ROWS * t, ROWS * (t + 1))
+    for t, tile in enumerate(which):
+        part = slice(ROWS * tile, ROWS * (tile + 1))
         coef = {name: coef_ref[k, part, :] for k, name in enumerate(PAIR_COEFS)}
         sign = jnp.where(lower, 1.0, -1.0)
         star_centre = jnp.where(lower, star_last[t], star_first[t])
@@ -555,8 +572,6 @@
     share_ref,
     coef_ref,
     far_ref,
-    stat_ref,
-    mate_stat_ref,
 ):
     outermost, lower, _ = place_in_column()
     sign = jnp.where(lower, 1.0, -1.0)
@@ -568,11 +583,12 @@
         own, got = mate_ref[0, part, :], got_mate_ref[0, part, :]
         this_star = jnp.where(outermost, got_share_ref[1, part, :], share_ref[1, part, :])
         next_star = jnp.where(outermost, got_cross_ref[1, part, :], got_next_ref[1, part, :])
-        first_rate = jnp.where(outermost, mate_stat_ref[3, part, :], stat_ref[3, part, :])
-        last_rate = jnp.where(outermost, mate_stat_ref[4, part, :], stat_ref[4, part, :])
-        facing = vert_coef * jnp.where(lower, last_rate, first_rate)
         this = share_ref[0, part, :] + got_share_ref[0, part, :] + sign * far_facing * this_star
-        that = got_cross_ref[0, part, :] + got_next_ref[0, part, :] - sign * facing * next_star
+        that = (
+            got_cross_ref[0, part, :]
+            + got_next_ref[0, part, :]
+            - sign * coef["centre"] * next_star
+        )
         middle = (that + far_total * this) / (1.0 - coef["total"] * far_total)
         from_outer = jnp.where(outermost, own, got)
         from_inner = jnp.where(outermost, got, own)
@@ -588,8 +604,8 @@
         below, above = jnp.where(lower, outer, centre), jnp.where(lower, centre, outer)
         star_below = jnp.where(lower, star_outer, star_centre)
         star_above = jnp.where(lower, star_centre, star_outer)
-        under = below - vert_coef * stat_ref[3, part, :] * star_below
-        over = above + vert_coef * stat_ref[4, part, :] * star_above
+        under = below - coef["first"] * star_below
+        over = above + coef["last"] * star_above
         parts.append((below, above, under, over))
     return [[part[k] for part in parts] for k in range(4)]
 
@@ -693,10 +709,10 @@
         copy.wait()
 
 
-def call(kernel, name, shapes, *args, weight=1, far_in=False, far_out=False, scratch=(), keep=()):
+def call(kernel, name, shapes, *args, far_in=(), far_out=False, scratch=(), keep=()):
     near, far = pl.BlockSpec(memory_space=pltpu.VMEM), pl.BlockSpec(memory_space=pl.ANY)
     size = sum(a.size for a in args) + sum(functools.reduce(lambda a, b: a * b, s) for s in shapes)
-    if far_in:
+    if len(far_in) == len(args):
         args = [pltpu.with_memory_space_constraint(a, pltpu.HBM) for a in args]
     return pl.pallas_call(
         kernel,
@@ -704,12 +720,12 @@
             pltpu.VMEM(s, jnp.float32) if k in keep else jax.ShapeDtypeStruct(s, jnp.float32)
             for k, s in enumerate(shapes)
         ],
-        in_specs=[far if far_in else near] * len(args),
+        in_specs=[far if k in far_in else near for k in range(len(args))],
         out_specs=[far if far_out else near] * len(shapes),
         scratch_shapes=list(scratch),
         compiler_params=pltpu.CompilerParams(vmem_limit_bytes=32 * 1024 * 1024),
         cost_estimate=pl.CostEstimate(
-            flops=weight * size, bytes_accessed=4 * weight * size, transcendentals=0
+            flops=8 * size, bytes_accessed=4 * size, transcendentals=0
         ),
         name=name,
     )(*args)
@@ -752,31 +768,30 @@
     assert lanes == 128 and levels * SLOT == 128 and rows % ROWS == 0
     assert lax.axis_size("lev") == 4 and lax.axis_size("gy") % 2 == 0
 
-    edge, inner, outer, ends = call(
+    edge, inner, outer, ends, rate, inv, prod, gain, stat = call(
         kernel_a,
         "start",
-        [(levels + 1, ROWS, lanes), pair, (3,) + plane, pair],
+        [(levels + 1, ROWS, lanes), pair, (3,) + plane, pair] + [field] * 4 + [(STATS,) + plane],
         pressure,
         wind_x,
         wind_y,
         jacobian,
-        far_in=True,
+        stiffness,
+        far_in=(0, 1, 2, 3, 4),
         scratch=[
             pltpu.VMEM(field, jnp.float32),
             pltpu.VMEM((levels, 2 * ROWS, lanes), jnp.float32),
             pltpu.VMEM(field, jnp.float32),
             pltpu.VMEM(plane, jnp.float32),
-            pltpu.SemaphoreType.DMA((3, CHUNKS)),
+            pltpu.VMEM(field, jnp.float32),
+            pltpu.SemaphoreType.DMA((4, CHUNKS)),
         ],
     )
+    mate = swap(stat, "lev", lambda i: i ^ 1)
+    (coef,) = call(kernel_s, "pairs", [(len(PAIR_COEFS),) + plane], stat, mate)
     sent = (edge, inner, outer)
     got = (exchange_rows(edge),) + exchange_lanes(inner, outer)
     static_edges = sent + got
-    rate, inv, prod, gain, stat = call(
-        kernel_f, "factor", [field, field, field, field, (5,) + plane], stiffness
-    )
-    mate = swap(stat, "lev", lambda i: i ^ 1)
-    (coef,) = call(kernel_s, "pairs", [(len(PAIR_COEFS),) + plane], stat, mate)
     for substep in range(SUBSTEPS):
         closed = call(
             kernel_m, "interior", [field, field, field], pressure, wind_x, wind_y, jacobian
@@ -804,7 +819,7 @@
         column = exchange_column(*faces)
         if not substep:
             far = column[0]
-        column += (coef, far, stat, mate)
+        column += (coef, far)
         if substep < SUBSTEPS - 1:
             (packed,) = call(kernel_n, "pack", [pair], wind_y)
             wind_z, pressure, edge, inner, outer, ends = call(

time: 36.5 us -> 37.5 us (1.027)
  Pallas kernels: 12.1 us -> 13.3 us
    pallas_call x10 -> x9, Pallas kernels: 12.1 us -> 13.3 us  [call(): pl.pallas_call(kernel, out_shape=[pltpu.VMEM(s, jnp.float32) if k in keep...]
    unnamed x18 -> x16, local copies, waits for them, and re-layouts: 1.63 us -> 1.62 us
  transfers between devices with their start and end apart: 15 -> 15, of which waited for: 4 -> 4; matrix products, arithmetic and copies ran while one was open for 4% -> 4% of each run, Pallas kernels for 11% -> 9%
where the time goes in v7:
time: 37.5 us; the launch traced here: 37.3 us
  starting transfers between devices  13.6 us (36%)
  Pallas kernels  13.3 us (35%)
  waiting for transfers between devices  8.02 us (21%)
  local copies, waits for them, and re-layouts  1.62 us (4%)
  between operations  0.81 us (2%)
    ppermute x15, starting transfers between devices, swap(): return lax.ppermute(value, axis, [(i, partner(i)) for i in range(count)])  13.6 us
    pallas_call x9, Pallas kernels, call(): pl.pallas_call(kernel, out_shape=[pltpu.VMEM(s, jnp.float32) if k in keep...  13.3 us
    ppermute x15, waiting for transfers between devices, swap(): return lax.ppermute(value, axis, [(i, partner(i)) for i in range(count)])  8.02 us
    unnamed x16, local copies, waits for them, and re-layouts  1.62 us
  transfers between devices with their start and end apart: 15, of which 4 were waited for; matrix products, arithmetic and copies ran while one was open for 4% of the time, Pallas kernels for 9%

profile of v7, /device:TPU:0, one launch (start us, length us, event | category | flops | bytes accessed | tf_op | source)
XLA Modules:
  0.0 37.3 jit_solution(3390194235704851160)
XLA Ops:
  0.7 3.0 %start.1 = (f32[33,8,128]{2,1,0:T(8,128)S(1)}, f32[2,32,128]{2,1,0:T(8,128)S(1)}, f32[3,32,128]{2,1,0:T(8,128)S(1)}, f32[2,32,128]{2,1,0:T(8,128)S(1)}, f32[32,3...) custom-call(f32[32,32,128]{2,1,0:T(8,128)} %p_ref.3, ...), custom_call_target="tpu_custom_call" | custom-call | flops 9084928 | bytes 4542464 | tf_op jit(solution)/shard_map/start/pallas_call | solution.py:717
  3.7 3.0 %collective-permute-start = (f32[33,8,128]{2,1,0:T(8,128)S(1)}, f32[33,8,128]{2,1,0:T(8,128)S(1)}, u32[]{:S(2)}, u32[]{:S(2)}) collective-permute-start(f32[33,8,128]{2,1,0:T(8,128)S(1)} %get-tuple-element.50.rows_ref.srows_ref), channel_id=1, source_target_pairs={{0,16},{16,0},{1,17},{17,1},{2,18},{18,2},{3,19},{19,3},{4,20},{20... | collective-permute-start | bytes 405512 | tf_op jit(solution)/shard_map/ppermute | solution.py:736
  6.7 3.6 %collective-permute-start.2 = (f32[3,32,128]{2,1,0:T(8,128)S(1)}, f32[3,32,128]{2,1,0:T(8,128)S(1)}, u32[]{:S(2)}, u32[]{:S(2)}) collective-permute-start(f32[3,32,128]{2,1,0:T(8,128)S(1)} %get-tuple-element.52.outer_ref.souter_ref), channel_id=1, source_target_pairs={{0,12},{4,8},{8,4},{12,0},{1,13},{5,9},{9,5},{13,1},{2,14},{6,10},... | collective-permute-start | bytes 147464 | tf_op jit(solution)/shard_map/ppermute | solution.py:736
  10.4 1.4 %interior.2 = (f32[32,32,128]{2,1,0:T(8,128)S(1)}, f32[32,32,128]{2,1,0:T(8,128)S(1)}, f32[32,32,128]{2,1,0:T(8,128)S(1)}) custom-call(f32[32,32,128]{2,1,0:T(8,128)S(1)} %copy-done, f32[32,32,128]{2,1,0:T(8,128)S(1)} %copy-done.1, f32[32,32,128]{2,1,0:T(8,128)S(1)} %copy-done.2, f32[32,128]{1,0:T(8,128)S(1)} %copy-done.3), custom_call_target="tpu_custom_call" | custom-call | flops 6324224 | bytes 3162112 | tf_op jit(solution)/shard_map/interior/pallas_call | solution.py:717
  11.9 2.4 %collective-permute-done.1.got_inner_ref.got_sinner_ref = f32[2,32,128]{2,1,0:T(8,128)S(1)} collective-permute-done((f32[2,32,128]{2,1,0:T(8,128)S(1)}, f32[2,32,128]{2,1,0:T(8,128)S(1)}, u32[]{:S(2)}, u32[]{:S(2)}) %collective-permute-start.1) | collective-permute-done | bytes 32800 | tf_op jit(solution)/shard_map/ppermute | solution.py:736
  14.3 2.2 %sweep.2 = (f32[32,32,128]{2,1,0:T(8,128)S(1)}, f32[32,32,128]{2,1,0:T(8,128)S(1)}, f32[32,32,128]{2,1,0:T(8,128)S(1)}, f32[32,32,128]{2,1,0:T(8,128)S(1)}, f32[...) custom-call(f32[32,32,128]{2,1,0:T(8,128)S(1)} %copy-done, ...), custom_call_target="tpu_custom_call" | custom-call | flops 15171584 | bytes 7585792 | tf_op jit(solution)/shard_map/sweep/pallas_call | solution.py:717
  16.5 0.2 collective-permute-start.4
  16.8 1.4 %collective-permute-start.5 = (f32[2,32,128]{2,1,0:T(8,128)S(1)}, f32[2,32,128]{2,1,0:T(8,128)S(1)}, u32[]{:S(2)}, u32[]{:S(2)}) collective-permute-start(f32[2,32,128]{2,1,0:T(8,128)S(1)} %get-tuple-element.55), channel_id=1, source_target_pairs={{0,2},{1,3},{2,0},{3,1},{4,6},{5,7},{6,4},{7,5},{8,10},{9,11},{10,... | collective-permute-start | bytes 98312 | tf_op jit(solution)/shard_map/ppermute | solution.py:736
  18.2 0.3 collective-permute-start.6
  18.5 0.2 collective-permute-start.7
  18.7 0.5 %pack.1.refs_13_ = f32[2,32,128]{2,1,0:T(8,128)S(1)} custom-call(f32[32,32,128]{2,1,0:T(8,128)S(1)} %get-tuple-element.62.wy_ref), custom_call_target="tpu_custom_call" | custom-call | flops 1114112 | bytes 557056 | tf_op jit(solution)/shard_map/pack/pallas_call | solution.py:717
  19.2 2.5 %collective-permute-done.5.refs_1_ = f32[2,32,128]{2,1,0:T(8,128)S(1)} collective-permute-done((f32[2,32,128]{2,1,0:T(8,128)S(1)}, f32[2,32,128]{2,1,0:T(8,128)S(1)}, u32[]{:S(2)}, u32[]{:S(2)}) %collective-permute-start.5) | collective-permute-done | bytes 32800 | tf_op jit(solution)/shard_map/ppermute | solution.py:736
  21.7 1.3 %finish.1 = (f32[32,32,128]{2,1,0:T(8,128)S(1)}, f32[32,32,128]{2,1,0:T(8,128)S(1)}, f32[32,8,128]{2,1,0:T(8,128)S(1)}, f32[1,32,128]{2,1,0:T(8,128)S(1)}, f32[2...) custom-call(f32[4,32,128]{2,1,0:T(8,128)S(1)} %collective-permute-done.4.refs_0_.refs_7_, ...), custom_call_target="tpu_custom_call" | custom-call | flops 8814592 | bytes 4407296 | tf_op jit(solution)/shard_map/finish/pallas_call | solution.py:717
  23.0 0.6 %collective-permute-start.8 = (f32[32,8,128]{2,1,0:T(8,128)S(1)}, f32[32,8,128]{2,1,0:T(8,128)S(1)}, u32[]{:S(2)}, u32[]{:S(2)}) collective-permute-start(f32[32,8,128]{2,1,0:T(8,128)S(1)} %get-tuple-element.69.rows_ref), channel_id=1, source_target_pairs={{0,16},{16,0},{1,17},{17,1},{2,18},{18,2},{3,19},{19,3},{4,20},{20... | collective-permute-start | bytes 393224 | tf_op jit(solution)/shard_map/ppermute | solution.py:736
  23.6 2.4 %collective-permute-start.10 = (f32[2,32,128]{2,1,0:T(8,128)S(1)}, f32[2,32,128]{2,1,0:T(8,128)S(1)}, u32[]{:S(2)}, u32[]{:S(2)}) collective-permute-start(f32[2,32,128]{2,1,0:T(8,128)S(1)} %get-tuple-element.71.outer_ref), channel_id=1, source_target_pairs={{0,12},{4,8},{8,4},{12,0},{1,13},{5,9},{9,5},{13,1},{2,14},{6,10},... | collective-permute-start | bytes 98312 | tf_op jit(solution)/shard_map/ppermute | solution.py:736
  25.9 1.4 %interior.3 = (f32[32,32,128]{2,1,0:T(8,128)S(1)}, f32[32,32,128]{2,1,0:T(8,128)S(1)}, f32[32,32,128]{2,1,0:T(8,128)S(1)}) custom-call(f32[32,32,128]{2,1,0:T(8,128)S(1)} %get-tuple-element.63.p_ref, f32[32,32,128]{2,1,0:T(8,128)S(1)} %get-tuple-element.61.refs_12_.wx_ref, f32[32,32,128]{2,1,0:T(8,128)S(1)} %get-tuple-element.62.wy_ref, f32[32,128]{1,0:T(8,128)S(1)} %copy-done.3), custom_call_target="tpu_custom_call" | custom-call | flops 6324224 | bytes 3162112 | tf_op jit(solution)/shard_map/interior/pallas_call | solution.py:717
  27.4 2.3 %collective-permute-done.9.got_inner_ref = f32[1,32,128]{2,1,0:T(8,128)S(1)} collective-permute-done((f32[1,32,128]{2,1,0:T(8,128)S(1)}, f32[1,32,128]{2,1,0:T(8,128)S(1)}, u32[]{:S(2)}, u32[]{:S(2)}) %collective-permute-start.9) | collective-permute-done | bytes 16416 | tf_op jit(solution)/shard_map/ppermute | solution.py:736
  29.7 2.2 %sweep.3 = (f32[32,32,128]{2,1,0:T(8,128)S(1)}, f32[32,32,128]{2,1,0:T(8,128)S(1)}, f32[32,32,128]{2,1,0:T(8,128)S(1)}, f32[32,32,128]{2,1,0:T(8,128)S(1)}, f32[...) custom-call(f32[32,32,128]{2,1,0:T(8,128)S(1)} %get-tuple-element.63.p, ...), custom_call_target="tpu_custom_call" | custom-call | flops 14991360 | bytes 7495680 | tf_op jit(solution)/shard_map/sweep/pallas_call | solution.py:717
  32.0 0.8 %collective-permute-start.12 = (f32[2,32,128]{2,1,0:T(8,128)S(1)}, f32[2,32,128]{2,1,0:T(8,128)S(1)}, u32[]{:S(2)}, u32[]{:S(2)}) collective-permute-start(f32[2,32,128]{2,1,0:T(8,128)S(1)} %get-tuple-element.75), channel_id=1, source_target_pairs={{0,2},{1,3},{2,0},{3,1},{4,6},{5,7},{6,4},{7,5},{8,10},{9,11},{10,... | collective-permute-start | bytes 98312 | tf_op jit(solution)/shard_map/ppermute | solution.py:736
  32.7 1.1 %collective-permute-start.13 = (f32[2,32,128]{2,1,0:T(8,128)S(1)}, f32[2,32,128]{2,1,0:T(8,128)S(1)}, u32[]{:S(2)}, u32[]{:S(2)}) collective-permute-start(f32[2,32,128]{2,1,0:T(8,128)S(1)} %get-tuple-element.76.refs_4_), channel_id=1, source_target_pairs={{0,1},{1,0},{2,3},{3,2},{4,5},{5,4},{6,7},{7,6},{8,9},{9,8},{10,11... | collective-permute-start | bytes 98312 | tf_op jit(solution)/shard_map/ppermute | solution.py:736
  33.8 0.8 %copy.12 = f32[32,32,128]{2,1,0:T(8,128)} copy(f32[32,32,128]{2,1,0:T(8,128)S(1)} %get-tuple-element.82) | data formatting | bytes 1048576
  34.6 0.8 %copy.13 = f32[32,32,128]{2,1,0:T(8,128)} copy(f32[32,32,128]{2,1,0:T(8,128)S(1)} %get-tuple-element.83) | data formatting | bytes 1048576
  35.4 0.8 %collective-permute-done.12.refs_1_ = f32[2,32,128]{2,1,0:T(8,128)S(1)} collective-permute-done((f32[2,32,128]{2,1,0:T(8,128)S(1)}, f32[2,32,128]{2,1,0:T(8,128)S(1)}, u32[]{:S(2)}, u32[]{:S(2)}) %collective-permute-start.12) | collective-permute-done | bytes 32800 | tf_op jit(solution)/shard_map/ppermute | solution.py:736
  36.2 1.1 %last.1 = (f32[32,32,128]{2,1,0:T(8,128)}, f32[32,32,128]{2,1,0:T(8,128)}) custom-call(f32[3,32,128]{2,1,0:T(8,128)S(1)} %collective-permute-done.11.refs_0_, f32[2,32,128]{2,1,0:T(8,128)S(1)} %collective-permute-done.12.refs_1_, f32[2,32,128]{2,1,0:T(8,128)S(1)} %collective-permute-done.13.refs_2_, f32[2,32,128]{2,1,0:T(8,128)S(1)} %collective-permute-done.14.refs_3_, ...), custom_call_target="tpu_custom_call" | custom-call | flops 7208960 | bytes 3604480 | tf_op jit(solution)/shard_map/last/pallas_call | solution.py:717
  (31 shorter events, 0.2 us)
Async XLA Ops:
  0.6 9.7 %copy-start = (f32[32,32,128]{2,1,0:T(8,128)S(1)}, f32[32,32,128]{2,1,0:T(8,128)}, u32[]{:S(2)}) copy-start(f32[32,32,128]{2,1,0:T(8,128)} %p_ref.3) | copy-start | bytes 1572868
  0.6 9.7 %copy-start.2 = (f32[32,32,128]{2,1,0:T(8,128)S(1)}, f32[32,32,128]{2,1,0:T(8,128)}, u32[]{:S(2)}) copy-start(f32[32,32,128]{2,1,0:T(8,128)} %wy_hbm.1) | copy-start | bytes 1572868
  0.7 9.7 %copy-start.1 = (f32[32,32,128]{2,1,0:T(8,128)S(1)}, f32[32,32,128]{2,1,0:T(8,128)}, u32[]{:S(2)}) copy-start(f32[32,32,128]{2,1,0:T(8,128)} %wx_hbm.1) | copy-start | bytes 1572868
  0.7 9.7 %copy-start.3 = (f32[32,128]{1,0:T(8,128)S(1)}, f32[32,128]{1,0:T(8,128)}, u32[]{:S(2)}) copy-start(f32[32,128]{1,0:T(8,128)} %jac_ref.7) | copy-start | bytes 49156
  3.7 10.6 %collective-permute-start = (f32[33,8,128]{2,1,0:T(8,128)S(1)}, f32[33,8,128]{2,1,0:T(8,128)S(1)}, u32[]{:S(2)}, u32[]{:S(2)}) collective-permute-start(f32[33,8,128]{2,1,0:T(8,128)S(1)} %get-tuple-element.50.rows_ref.srows_ref), channel_id=1, source_target_pairs={{0,16},{16,0},{1,17},{17,1},{2,18},{18,2},{3,19},{19,3},{4,20},{20... | collective-permute-start | bytes 405512 | tf_op jit(solution)/shard_map/ppermute | solution.py:736
  6.7 5.1 %collective-permute-start.3 = (f32[5,32,128]{2,1,0:T(8,128)S(1)}, f32[5,32,128]{2,1,0:T(8,128)S(1)}, u32[]{:S(2)}, u32[]{:S(2)}) collective-permute-start(f32[5,32,128]{2,1,0:T(8,128)S(1)} %get-tuple-element.53.stat_ref), channel_id=1, source_target_pairs={{0,1},{1,0},{2,3},{3,2},{4,5},{5,4},{6,7},{7,6},{8,9},{9,8},{10,11... | collective-permute-start | bytes 245768 | tf_op jit(solution)/shard_map/ppermute | solution.py:736
  6.7 7.5 %collective-permute-start.2 = (f32[3,32,128]{2,1,0:T(8,128)S(1)}, f32[3,32,128]{2,1,0:T(8,128)S(1)}, u32[]{:S(2)}, u32[]{:S(2)}) collective-permute-start(f32[3,32,128]{2,1,0:T(8,128)S(1)} %get-tuple-element.52.outer_ref.souter_ref), channel_id=1, source_target_pairs={{0,12},{4,8},{8,4},{12,0},{1,13},{5,9},{9,5},{13,1},{2,14},{6,10},... | collective-permute-start | bytes 147464 | tf_op jit(solution)/shard_map/ppermute | solution.py:736
  10.3 3.9 %collective-permute-start.1 = (f32[2,32,128]{2,1,0:T(8,128)S(1)}, f32[2,32,128]{2,1,0:T(8,128)S(1)}, u32[]{:S(2)}, u32[]{:S(2)}) collective-permute-start(f32[2,32,128]{2,1,0:T(8,128)S(1)} %get-tuple-element.51.inner_ref.sinner_ref), channel_id=1, source_target_pairs={{0,4},{4,0},{8,12},{12,8},{1,5},{5,1},{9,13},{13,9},{2,6},{6,2},{1... | collective-permute-start | bytes 98312 | tf_op jit(solution)/shard_map/ppermute | solution.py:736
  10.4 3.9 %copy-start.4 = (f32[32,32,128]{2,1,0:T(8,128)S(1)}, f32[32,32,128]{2,1,0:T(8,128)}, u32[]{:S(2)}) copy-start(f32[32,32,128]{2,1,0:T(8,128)} %wz_ref.1) | copy-start | bytes 1572868
  11.8 2.5 %copy-start.5 = (f32[32,128]{1,0:T(8,128)S(1)}, f32[32,128]{1,0:T(8,128)}, u32[]{:S(2)}) copy-start(f32[32,128]{1,0:T(8,128)} %sx_ref.3) | copy-start | bytes 49156
  11.8 2.4 %copy-start.6 = (f32[32,128]{1,0:T(8,128)S(1)}, f32[32,128]{1,0:T(8,128)}, u32[]{:S(2)}) copy-start(f32[32,128]{1,0:T(8,128)} %sy_ref.3) | copy-start | bytes 49156
  16.5 5.2 %collective-permute-start.4 = (f32[4,32,128]{2,1,0:T(8,128)S(1)}, f32[4,32,128]{2,1,0:T(8,128)S(1)}, u32[]{:S(2)}, u32[]{:S(2)}) collective-permute-start(f32[4,32,128]{2,1,0:T(8,128)S(1)} %get-tuple-element.54), channel_id=1, source_target_pairs={{0,3},{1,2},{2,1},{3,0},{4,7},{5,6},{6,5},{7,4},{8,11},{9,10},{10,... | collective-permute-start | bytes 196616 | tf_op jit(solution)/shard_map/ppermute | solution.py:736
  16.8 4.9 %collective-permute-start.5 = (f32[2,32,128]{2,1,0:T(8,128)S(1)}, f32[2,32,128]{2,1,0:T(8,128)S(1)}, u32[]{:S(2)}, u32[]{:S(2)}) collective-permute-start(f32[2,32,128]{2,1,0:T(8,128)S(1)} %get-tuple-element.55), channel_id=1, source_target_pairs={{0,2},{1,3},{2,0},{3,1},{4,6},{5,7},{6,4},{7,5},{8,10},{9,11},{10,... | collective-permute-start | bytes 98312 | tf_op jit(solution)/shard_map/ppermute | solution.py:736
  18.2 3.5 %collective-permute-start.6 = (f32[2,32,128]{2,1,0:T(8,128)S(1)}, f32[2,32,128]{2,1,0:T(8,128)S(1)}, u32[]{:S(2)}, u32[]{:S(2)}) collective-permute-start(f32[2,32,128]{2,1,0:T(8,128)S(1)} %get-tuple-element.56.refs_4_), channel_id=1, source_target_pairs={{0,1},{1,0},{2,3},{3,2},{4,5},{5,4},{6,7},{7,6},{8,9},{9,8},{10,11... | collective-permute-start | bytes 98312 | tf_op jit(solution)/shard_map/ppermute | solution.py:736
  18.5 3.2 %collective-permute-start.7 = (f32[2,32,128]{2,1,0:T(8,128)S(1)}, f32[2,32,128]{2,1,0:T(8,128)S(1)}, u32[]{:S(2)}, u32[]{:S(2)}) collective-permute-start(f32[2,32,128]{2,1,0:T(8,128)S(1)} %get-tuple-element.57.refs_5_), channel_id=1, source_target_pairs={{0,1},{1,0},{2,3},{3,2},{4,5},{5,4},{6,7},{7,6},{8,9},{9,8},{10,11... | collective-permute-start | bytes 98312 | tf_op jit(solution)/shard_map/ppermute | solution.py:736
  23.0 6.7 %collective-permute-start.8 = (f32[32,8,128]{2,1,0:T(8,128)S(1)}, f32[32,8,128]{2,1,0:T(8,128)S(1)}, u32[]{:S(2)}, u32[]{:S(2)}) collective-permute-start(f32[32,8,128]{2,1,0:T(8,128)S(1)} %get-tuple-element.69.rows_ref), channel_id=1, source_target_pairs={{0,16},{16,0},{1,17},{17,1},{2,18},{18,2},{3,19},{19,3},{4,20},{20... | collective-permute-start | bytes 393224 | tf_op jit(solution)/shard_map/ppermute | solution.py:736
  23.6 6.1 %collective-permute-start.10 = (f32[2,32,128]{2,1,0:T(8,128)S(1)}, f32[2,32,128]{2,1,0:T(8,128)S(1)}, u32[]{:S(2)}, u32[]{:S(2)}) collective-permute-start(f32[2,32,128]{2,1,0:T(8,128)S(1)} %get-tuple-element.71.outer_ref), channel_id=1, source_target_pairs={{0,12},{4,8},{8,4},{12,0},{1,13},{5,9},{9,5},{13,1},{2,14},{6,10},... | collective-permute-start | bytes 98312 | tf_op jit(solution)/shard_map/ppermute | solution.py:736
  25.9 3.7 %collective-permute-start.9 = (f32[1,32,128]{2,1,0:T(8,128)S(1)}, f32[1,32,128]{2,1,0:T(8,128)S(1)}, u32[]{:S(2)}, u32[]{:S(2)}) collective-permute-start(f32[1,32,128]{2,1,0:T(8,128)S(1)} %get-tuple-element.70.inner_ref), channel_id=1, source_target_pairs={{0,4},{4,0},{8,12},{12,8},{1,5},{5,1},{9,13},{13,9},{2,6},{6,2},{1... | collective-permute-start | bytes 49160 | tf_op jit(solution)/shard_map/ppermute | solution.py:736
  31.9 4.3 %collective-permute-start.11 = (f32[3,32,128]{2,1,0:T(8,128)S(1)}, f32[3,32,128]{2,1,0:T(8,128)S(1)}, u32[]{:S(2)}, u32[]{:S(2)}) collective-permute-start(f32[3,32,128]{2,1,0:T(8,128)S(1)} %get-tuple-element.74), channel_id=1, source_target_pairs={{0,3},{1,2},{2,1},{3,0},{4,7},{5,6},{6,5},{7,4},{8,11},{9,10},{10,... | collective-permute-start | bytes 147464 | tf_op jit(solution)/shard_map/ppermute | solution.py:736
  32.0 4.2 %collective-permute-start.12 = (f32[2,32,128]{2,1,0:T(8,128)S(1)}, f32[2,32,128]{2,1,0:T(8,128)S(1)}, u32[]{:S(2)}, u32[]{:S(2)}) collective-permute-start(f32[2,32,128]{2,1,0:T(8,128)S(1)} %get-tuple-element.75), channel_id=1, source_target_pairs={{0,2},{1,3},{2,0},{3,1},{4,6},{5,7},{6,4},{7,5},{8,10},{9,11},{10,... | collective-permute-start | bytes 98312 | tf_op jit(solution)/shard_map/ppermute | solution.py:736
  32.7 3.5 %collective-permute-start.13 = (f32[2,32,128]{2,1,0:T(8,128)S(1)}, f32[2,32,128]{2,1,0:T(8,128)S(1)}, u32[]{:S(2)}, u32[]{:S(2)}) collective-permute-start(f32[2,32,128]{2,1,0:T(8,128)S(1)} %get-tuple-element.76.refs_4_), channel_id=1, source_target_pairs={{0,1},{1,0},{2,3},{3,2},{4,5},{5,4},{6,7},{7,6},{8,9},{9,8},{10,11... | collective-permute-start | bytes 98312 | tf_op jit(solution)/shard_map/ppermute | solution.py:736
  33.8 2.4 %collective-permute-start.14 = (f32[2,32,128]{2,1,0:T(8,128)S(1)}, f32[2,32,128]{2,1,0:T(8,128)S(1)}, u32[]{:S(2)}, u32[]{:S(2)}) collective-permute-start(f32[2,32,128]{2,1,0:T(8,128)S(1)} %get-tuple-element.77.refs_5_), channel_id=1, source_target_pairs={{0,1},{1,0},{2,3},{3,2},{4,5},{5,4},{6,7},{7,6},{8,9},{9,8},{10,11... | collective-permute-start | bytes 98312 | tf_op jit(solution)/shard_map/ppermute | solution.py:736

commit v8 on v7

--- a/solution.py
+++ b/solution.py
@@ -67,7 +67,7 @@
         return total
 
     def shifted(self, field, by):
-        return field if by == 0 else pltpu.roll(field, (-by) % self.size, self.axis)
+        return field if by % self.size == 0 else pltpu.roll(field, (-by) % self.size, self.axis)
 
     def mix(self, field, table):
         total = None
@@ -92,13 +92,19 @@
         outer = self.mix(pres, {0: {0: 1.0, 1: 1.0, 6: 1.0, 7: 1.0}})
         return outer + self.mix(flux, {-2: {2: 1.0, 3: 1.0}, 2: {4: 1.0, 5: 1.0}})
 
-    def correct(self, delta, pres, jac, delta_jac):
+    def correct(self, delta, pres, jac, delta_jac, base=0):
         grad = self.mix(
-            delta, {2: {0: 1.0, 1: 1.0}, 3: {0: -8.0}, -2: {6: -1.0, 7: -1.0}, -3: {7: 8.0}}
+            delta,
+            {
+                base + 2: {0: 1.0, 1: 1.0},
+                base + 3: {0: -8.0},
+                base - 2: {6: -1.0, 7: -1.0},
+                base - 3: {7: 8.0},
+            },
         )
         wind = CG * grad
         own = -(jac * wind)
-        far = self.mix(delta, {0: {0: 1.0, 1: 1.0, 6: 1.0, 7: 1.0}}) + CG * delta_jac * self.mix(
+        far = self.mix(delta, {base: {0: 1.0, 1: 1.0, 6: 1.0, 7: 1.0}}) + CG * delta_jac * self.mix(
             pres, {0: {0: 1.0, 1: 1.0, 6: -1.0, 7: -1.0}, -1: {1: -8.0}, 1: {6: 8.0}}
         )
         spread = (
@@ -438,10 +444,11 @@
         stars = {t: psc_ref[level, ROWS * t : ROWS * (t + 1), :] for t in which}
         if 0 in which:
             wind, press = edge.correct(
-                pltpu.roll(got_rows_ref[level] - rows_ref[level], 4, 0),
+                got_rows_ref[level] - rows_ref[level],
                 jnp.where(first_rows, p_ref[level, :ROWS, :], p_ref[level, ROWS * last :, :]),
                 ends,
                 ends_change,
+                base=4,
             )
             new_x[0] = new_x[0] - jnp.where(first_rows, wind, 0.0)
             new_x[last] = new_x[last] - jnp.where(first_rows, 0.0, wind)
@@ -478,7 +485,7 @@
             y_ref[level, part, :] = values[k]
         return values, firsts
 
-    for which in ((0, last), tuple(range(1, last))):
+    for which in (tuple(range(count)),):
         zeros = [jnp.zeros((ROWS, 128), jnp.float32)] * len(which)
         bottom, force = star(0, which)
 
@@ -489,7 +496,7 @@
             return here, above, force_next, value, first
 
         below, here, force, value, first = lax.fori_loop(
-            1, levels, step, (zeros, bottom, force, zeros, zeros), unroll=UNROLL
+            1, levels, step, (zeros, bottom, force, zeros, zeros), unroll=2 * UNROLL
         )
         value, first = sweep(levels - 1, which, below, zeros, force, value, first)
         interface(

time: 37.5 us -> 37 us (0.987)
  Pallas kernels: 13.3 us -> 12.7 us
    pallas_call x9, Pallas kernels: 13.3 us -> 12.7 us  [call(): pl.pallas_call(kernel, out_shape=[pltpu.VMEM(s, jnp.float32) if k in keep...]
where the time goes in v8:
time: 37 us; the launch traced here: 36.8 us
  starting transfers between devices  13.6 us (37%)
  Pallas kernels  12.7 us (34%)
  waiting for transfers between devices  8.02 us (22%)
  local copies, waits for them, and re-layouts  1.62 us (4%)
  between operations  0.81 us (2%)
    ppermute x15, starting transfers between devices, swap(): return lax.ppermute(value, axis, [(i, partner(i)) for i in range(count)])  13.6 us
    pallas_call x9, Pallas kernels, call(): pl.pallas_call(kernel, out_shape=[pltpu.VMEM(s, jnp.float32) if k in keep...  12.7 us
    ppermute x15, waiting for transfers between devices, swap(): return lax.ppermute(value, axis, [(i, partner(i)) for i in range(count)])  8.02 us
    unnamed x16, local copies, waits for them, and re-layouts  1.62 us
  transfers between devices with their start and end apart: 15, of which 4 were waited for; matrix products, arithmetic and copies ran while one was open for 4% of the time, Pallas kernels for 9%

profile of v8, /device:TPU:0, one launch (start us, length us, event | category | flops | bytes accessed | tf_op | source)
XLA Modules:
  0.0 36.8 jit_solution(17412284857268148899)
XLA Ops:
  0.7 3.0 %start.1 = (f32[33,8,128]{2,1,0:T(8,128)S(1)}, f32[2,32,128]{2,1,0:T(8,128)S(1)}, f32[3,32,128]{2,1,0:T(8,128)S(1)}, f32[2,32,128]{2,1,0:T(8,128)S(1)}, f32[32,3...) custom-call(f32[32,32,128]{2,1,0:T(8,128)} %p_ref.3, ...), custom_call_target="tpu_custom_call" | custom-call | flops 9084928 | bytes 4542464 | tf_op jit(solution)/shard_map/start/pallas_call | solution.py:724
  3.7 3.0 %collective-permute-start = (f32[33,8,128]{2,1,0:T(8,128)S(1)}, f32[33,8,128]{2,1,0:T(8,128)S(1)}, u32[]{:S(2)}, u32[]{:S(2)}) collective-permute-start(f32[33,8,128]{2,1,0:T(8,128)S(1)} %get-tuple-element.50.rows_ref.srows_ref), channel_id=1, source_target_pairs={{0,16},{16,0},{1,17},{17,1},{2,18},{18,2},{3,19},{19,3},{4,20},{20... | collective-permute-start | bytes 405512 | tf_op jit(solution)/shard_map/ppermute | solution.py:743
  6.7 3.6 %collective-permute-start.2 = (f32[3,32,128]{2,1,0:T(8,128)S(1)}, f32[3,32,128]{2,1,0:T(8,128)S(1)}, u32[]{:S(2)}, u32[]{:S(2)}) collective-permute-start(f32[3,32,128]{2,1,0:T(8,128)S(1)} %get-tuple-element.52.outer_ref.souter_ref), channel_id=1, source_target_pairs={{0,12},{4,8},{8,4},{12,0},{1,13},{5,9},{9,5},{13,1},{2,14},{6,10},... | collective-permute-start | bytes 147464 | tf_op jit(solution)/shard_map/ppermute | solution.py:743
  10.4 1.4 %interior.2 = (f32[32,32,128]{2,1,0:T(8,128)S(1)}, f32[32,32,128]{2,1,0:T(8,128)S(1)}, f32[32,32,128]{2,1,0:T(8,128)S(1)}) custom-call(f32[32,32,128]{2,1,0:T(8,128)S(1)} %copy-done, f32[32,32,128]{2,1,0:T(8,128)S(1)} %copy-done.1, f32[32,32,128]{2,1,0:T(8,128)S(1)} %copy-done.2, f32[32,128]{1,0:T(8,128)S(1)} %copy-done.3), custom_call_target="tpu_custom_call" | custom-call | flops 6324224 | bytes 3162112 | tf_op jit(solution)/shard_map/interior/pallas_call | solution.py:724
  11.9 2.4 %collective-permute-done.1.got_inner_ref.got_sinner_ref = f32[2,32,128]{2,1,0:T(8,128)S(1)} collective-permute-done((f32[2,32,128]{2,1,0:T(8,128)S(1)}, f32[2,32,128]{2,1,0:T(8,128)S(1)}, u32[]{:S(2)}, u32[]{:S(2)}) %collective-permute-start.1) | collective-permute-done | bytes 32800 | tf_op jit(solution)/shard_map/ppermute | solution.py:743
  14.3 2.0 %sweep.2 = (f32[32,32,128]{2,1,0:T(8,128)S(1)}, f32[32,32,128]{2,1,0:T(8,128)S(1)}, f32[32,32,128]{2,1,0:T(8,128)S(1)}, f32[32,32,128]{2,1,0:T(8,128)S(1)}, f32[...) custom-call(f32[32,32,128]{2,1,0:T(8,128)S(1)} %copy-done, ...), custom_call_target="tpu_custom_call" | custom-call | flops 15171584 | bytes 7585792 | tf_op jit(solution)/shard_map/sweep/pallas_call | solution.py:724
  16.3 0.2 collective-permute-start.4
  16.5 1.4 %collective-permute-start.5 = (f32[2,32,128]{2,1,0:T(8,128)S(1)}, f32[2,32,128]{2,1,0:T(8,128)S(1)}, u32[]{:S(2)}, u32[]{:S(2)}) collective-permute-start(f32[2,32,128]{2,1,0:T(8,128)S(1)} %get-tuple-element.55), channel_id=1, source_target_pairs={{0,2},{1,3},{2,0},{3,1},{4,6},{5,7},{6,4},{7,5},{8,10},{9,11},{10,... | collective-permute-start | bytes 98312 | tf_op jit(solution)/shard_map/ppermute | solution.py:743
  17.9 0.3 collective-permute-start.6
  18.2 0.2 collective-permute-start.7
  18.4 0.5 %pack.1.refs_13_ = f32[2,32,128]{2,1,0:T(8,128)S(1)} custom-call(f32[32,32,128]{2,1,0:T(8,128)S(1)} %get-tuple-element.62.wy_ref), custom_call_target="tpu_custom_call" | custom-call | flops 1114112 | bytes 557056 | tf_op jit(solution)/shard_map/pack/pallas_call | solution.py:724
  18.9 2.5 %collective-permute-done.5.refs_1_ = f32[2,32,128]{2,1,0:T(8,128)S(1)} collective-permute-done((f32[2,32,128]{2,1,0:T(8,128)S(1)}, f32[2,32,128]{2,1,0:T(8,128)S(1)}, u32[]{:S(2)}, u32[]{:S(2)}) %collective-permute-start.5) | collective-permute-done | bytes 32800 | tf_op jit(solution)/shard_map/ppermute | solution.py:743
  21.4 1.3 %finish.1 = (f32[32,32,128]{2,1,0:T(8,128)S(1)}, f32[32,32,128]{2,1,0:T(8,128)S(1)}, f32[32,8,128]{2,1,0:T(8,128)S(1)}, f32[1,32,128]{2,1,0:T(8,128)S(1)}, f32[2...) custom-call(f32[4,32,128]{2,1,0:T(8,128)S(1)} %collective-permute-done.4.refs_0_.refs_7_, ...), custom_call_target="tpu_custom_call" | custom-call | flops 8814592 | bytes 4407296 | tf_op jit(solution)/shard_map/finish/pallas_call | solution.py:724
  22.7 0.6 %collective-permute-start.8 = (f32[32,8,128]{2,1,0:T(8,128)S(1)}, f32[32,8,128]{2,1,0:T(8,128)S(1)}, u32[]{:S(2)}, u32[]{:S(2)}) collective-permute-start(f32[32,8,128]{2,1,0:T(8,128)S(1)} %get-tuple-element.69.rows_ref), channel_id=1, source_target_pairs={{0,16},{16,0},{1,17},{17,1},{2,18},{18,2},{3,19},{19,3},{4,20},{20... | collective-permute-start | bytes 393224 | tf_op jit(solution)/shard_map/ppermute | solution.py:743
  23.3 2.4 %collective-permute-start.10 = (f32[2,32,128]{2,1,0:T(8,128)S(1)}, f32[2,32,128]{2,1,0:T(8,128)S(1)}, u32[]{:S(2)}, u32[]{:S(2)}) collective-permute-start(f32[2,32,128]{2,1,0:T(8,128)S(1)} %get-tuple-element.71.outer_ref), channel_id=1, source_target_pairs={{0,12},{4,8},{8,4},{12,0},{1,13},{5,9},{9,5},{13,1},{2,14},{6,10},... | collective-permute-start | bytes 98312 | tf_op jit(solution)/shard_map/ppermute | solution.py:743
  25.7 1.4 %interior.3 = (f32[32,32,128]{2,1,0:T(8,128)S(1)}, f32[32,32,128]{2,1,0:T(8,128)S(1)}, f32[32,32,128]{2,1,0:T(8,128)S(1)}) custom-call(f32[32,32,128]{2,1,0:T(8,128)S(1)} %get-tuple-element.63.p_ref, f32[32,32,128]{2,1,0:T(8,128)S(1)} %get-tuple-element.61.refs_12_.wx_ref, f32[32,32,128]{2,1,0:T(8,128)S(1)} %get-tuple-element.62.wy_ref, f32[32,128]{1,0:T(8,128)S(1)} %copy-done.3), custom_call_target="tpu_custom_call" | custom-call | flops 6324224 | bytes 3162112 | tf_op jit(solution)/shard_map/interior/pallas_call | solution.py:724
  27.1 2.3 %collective-permute-done.9.got_inner_ref = f32[1,32,128]{2,1,0:T(8,128)S(1)} collective-permute-done((f32[1,32,128]{2,1,0:T(8,128)S(1)}, f32[1,32,128]{2,1,0:T(8,128)S(1)}, u32[]{:S(2)}, u32[]{:S(2)}) %collective-permute-start.9) | collective-permute-done | bytes 16416 | tf_op jit(solution)/shard_map/ppermute | solution.py:743
  29.4 1.9 %sweep.3 = (f32[32,32,128]{2,1,0:T(8,128)S(1)}, f32[32,32,128]{2,1,0:T(8,128)S(1)}, f32[32,32,128]{2,1,0:T(8,128)S(1)}, f32[32,32,128]{2,1,0:T(8,128)S(1)}, f32[...) custom-call(f32[32,32,128]{2,1,0:T(8,128)S(1)} %get-tuple-element.63.p, ...), custom_call_target="tpu_custom_call" | custom-call | flops 14991360 | bytes 7495680 | tf_op jit(solution)/shard_map/sweep/pallas_call | solution.py:724
  31.4 0.8 %collective-permute-start.12 = (f32[2,32,128]{2,1,0:T(8,128)S(1)}, f32[2,32,128]{2,1,0:T(8,128)S(1)}, u32[]{:S(2)}, u32[]{:S(2)}) collective-permute-start(f32[2,32,128]{2,1,0:T(8,128)S(1)} %get-tuple-element.75), channel_id=1, source_target_pairs={{0,2},{1,3},{2,0},{3,1},{4,6},{5,7},{6,4},{7,5},{8,10},{9,11},{10,... | collective-permute-start | bytes 98312 | tf_op jit(solution)/shard_map/ppermute | solution.py:743
  32.2 1.1 %collective-permute-start.13 = (f32[2,32,128]{2,1,0:T(8,128)S(1)}, f32[2,32,128]{2,1,0:T(8,128)S(1)}, u32[]{:S(2)}, u32[]{:S(2)}) collective-permute-start(f32[2,32,128]{2,1,0:T(8,128)S(1)} %get-tuple-element.76.refs_4_), channel_id=1, source_target_pairs={{0,1},{1,0},{2,3},{3,2},{4,5},{5,4},{6,7},{7,6},{8,9},{9,8},{10,11... | collective-permute-start | bytes 98312 | tf_op jit(solution)/shard_map/ppermute | solution.py:743
  33.3 0.8 %copy.12 = f32[32,32,128]{2,1,0:T(8,128)} copy(f32[32,32,128]{2,1,0:T(8,128)S(1)} %get-tuple-element.82) | data formatting | bytes 1048576
  34.1 0.8 %copy.13 = f32[32,32,128]{2,1,0:T(8,128)} copy(f32[32,32,128]{2,1,0:T(8,128)S(1)} %get-tuple-element.83) | data formatting | bytes 1048576
  34.9 0.8 %collective-permute-done.12.refs_1_ = f32[2,32,128]{2,1,0:T(8,128)S(1)} collective-permute-done((f32[2,32,128]{2,1,0:T(8,128)S(1)}, f32[2,32,128]{2,1,0:T(8,128)S(1)}, u32[]{:S(2)}, u32[]{:S(2)}) %collective-permute-start.12) | collective-permute-done | bytes 32800 | tf_op jit(solution)/shard_map/ppermute | solution.py:743
  35.7 1.1 %last.1 = (f32[32,32,128]{2,1,0:T(8,128)}, f32[32,32,128]{2,1,0:T(8,128)}) custom-call(f32[3,32,128]{2,1,0:T(8,128)S(1)} %collective-permute-done.11.refs_0_, f32[2,32,128]{2,1,0:T(8,128)S(1)} %collective-permute-done.12.refs_1_, f32[2,32,128]{2,1,0:T(8,128)S(1)} %collective-permute-done.13.refs_2_, f32[2,32,128]{2,1,0:T(8,128)S(1)} %collective-permute-done.14.refs_3_, ...), custom_call_target="tpu_custom_call" | custom-call | flops 7208960 | bytes 3604480 | tf_op jit(solution)/shard_map/last/pallas_call | solution.py:724
  (31 shorter events, 0.2 us)
Async XLA Ops:
  0.6 9.7 %copy-start = (f32[32,32,128]{2,1,0:T(8,128)S(1)}, f32[32,32,128]{2,1,0:T(8,128)}, u32[]{:S(2)}) copy-start(f32[32,32,128]{2,1,0:T(8,128)} %p_ref.3) | copy-start | bytes 1572868
  0.6 9.7 %copy-start.2 = (f32[32,32,128]{2,1,0:T(8,128)S(1)}, f32[32,32,128]{2,1,0:T(8,128)}, u32[]{:S(2)}) copy-start(f32[32,32,128]{2,1,0:T(8,128)} %wy_hbm.1) | copy-start | bytes 1572868
  0.7 9.7 %copy-start.1 = (f32[32,32,128]{2,1,0:T(8,128)S(1)}, f32[32,32,128]{2,1,0:T(8,128)}, u32[]{:S(2)}) copy-start(f32[32,32,128]{2,1,0:T(8,128)} %wx_hbm.1) | copy-start | bytes 1572868
  0.7 9.7 %copy-start.3 = (f32[32,128]{1,0:T(8,128)S(1)}, f32[32,128]{1,0:T(8,128)}, u32[]{:S(2)}) copy-start(f32[32,128]{1,0:T(8,128)} %jac_ref.7) | copy-start | bytes 49156
  3.7 10.6 %collective-permute-start = (f32[33,8,128]{2,1,0:T(8,128)S(1)}, f32[33,8,128]{2,1,0:T(8,128)S(1)}, u32[]{:S(2)}, u32[]{:S(2)}) collective-permute-start(f32[33,8,128]{2,1,0:T(8,128)S(1)} %get-tuple-element.50.rows_ref.srows_ref), channel_id=1, source_target_pairs={{0,16},{16,0},{1,17},{17,1},{2,18},{18,2},{3,19},{19,3},{4,20},{20... | collective-permute-start | bytes 405512 | tf_op jit(solution)/shard_map/ppermute | solution.py:743
  6.7 5.1 %collective-permute-start.3 = (f32[5,32,128]{2,1,0:T(8,128)S(1)}, f32[5,32,128]{2,1,0:T(8,128)S(1)}, u32[]{:S(2)}, u32[]{:S(2)}) collective-permute-start(f32[5,32,128]{2,1,0:T(8,128)S(1)} %get-tuple-element.53.stat_ref), channel_id=1, source_target_pairs={{0,1},{1,0},{2,3},{3,2},{4,5},{5,4},{6,7},{7,6},{8,9},{9,8},{10,11... | collective-permute-start | bytes 245768 | tf_op jit(solution)/shard_map/ppermute | solution.py:743
  6.7 7.5 %collective-permute-start.2 = (f32[3,32,128]{2,1,0:T(8,128)S(1)}, f32[3,32,128]{2,1,0:T(8,128)S(1)}, u32[]{:S(2)}, u32[]{:S(2)}) collective-permute-start(f32[3,32,128]{2,1,0:T(8,128)S(1)} %get-tuple-element.52.outer_ref.souter_ref), channel_id=1, source_target_pairs={{0,12},{4,8},{8,4},{12,0},{1,13},{5,9},{9,5},{13,1},{2,14},{6,10},... | collective-permute-start | bytes 147464 | tf_op jit(solution)/shard_map/ppermute | solution.py:743
  10.3 3.9 %collective-permute-start.1 = (f32[2,32,128]{2,1,0:T(8,128)S(1)}, f32[2,32,128]{2,1,0:T(8,128)S(1)}, u32[]{:S(2)}, u32[]{:S(2)}) collective-permute-start(f32[2,32,128]{2,1,0:T(8,128)S(1)} %get-tuple-element.51.inner_ref.sinner_ref), channel_id=1, source_target_pairs={{0,4},{4,0},{8,12},{12,8},{1,5},{5,1},{9,13},{13,9},{2,6},{6,2},{1... | collective-permute-start | bytes 98312 | tf_op jit(solution)/shard_map/ppermute | solution.py:743
  10.4 3.9 %copy-start.4 = (f32[32,32,128]{2,1,0:T(8,128)S(1)}, f32[32,32,128]{2,1,0:T(8,128)}, u32[]{:S(2)}) copy-start(f32[32,32,128]{2,1,0:T(8,128)} %wz_ref.1) | copy-start | bytes 1572868
  11.8 2.5 %copy-start.5 = (f32[32,128]{1,0:T(8,128)S(1)}, f32[32,128]{1,0:T(8,128)}, u32[]{:S(2)}) copy-start(f32[32,128]{1,0:T(8,128)} %sx_ref.3) | copy-start | bytes 49156
  11.8 2.4 %copy-start.6 = (f32[32,128]{1,0:T(8,128)S(1)}, f32[32,128]{1,0:T(8,128)}, u32[]{:S(2)}) copy-start(f32[32,128]{1,0:T(8,128)} %sy_ref.3) | copy-start | bytes 49156
  16.3 5.2 %collective-permute-start.4 = (f32[4,32,128]{2,1,0:T(8,128)S(1)}, f32[4,32,128]{2,1,0:T(8,128)S(1)}, u32[]{:S(2)}, u32[]{:S(2)}) collective-permute-start(f32[4,32,128]{2,1,0:T(8,128)S(1)} %get-tuple-element.54), channel_id=1, source_target_pairs={{0,3},{1,2},{2,1},{3,0},{4,7},{5,6},{6,5},{7,4},{8,11},{9,10},{10,... | collective-permute-start | bytes 196616 | tf_op jit(solution)/shard_map/ppermute | solution.py:743
  16.5 4.9 %collective-permute-start.5 = (f32[2,32,128]{2,1,0:T(8,128)S(1)}, f32[2,32,128]{2,1,0:T(8,128)S(1)}, u32[]{:S(2)}, u32[]{:S(2)}) collective-permute-start(f32[2,32,128]{2,1,0:T(8,128)S(1)} %get-tuple-element.55), channel_id=1, source_target_pairs={{0,2},{1,3},{2,0},{3,1},{4,6},{5,7},{6,4},{7,5},{8,10},{9,11},{10,... | collective-permute-start | bytes 98312 | tf_op jit(solution)/shard_map/ppermute | solution.py:743
  17.9 3.5 %collective-permute-start.6 = (f32[2,32,128]{2,1,0:T(8,128)S(1)}, f32[2,32,128]{2,1,0:T(8,128)S(1)}, u32[]{:S(2)}, u32[]{:S(2)}) collective-permute-start(f32[2,32,128]{2,1,0:T(8,128)S(1)} %get-tuple-element.56.refs_4_), channel_id=1, source_target_pairs={{0,1},{1,0},{2,3},{3,2},{4,5},{5,4},{6,7},{7,6},{8,9},{9,8},{10,11... | collective-permute-start | bytes 98312 | tf_op jit(solution)/shard_map/ppermute | solution.py:743
  18.2 3.2 %collective-permute-start.7 = (f32[2,32,128]{2,1,0:T(8,128)S(1)}, f32[2,32,128]{2,1,0:T(8,128)S(1)}, u32[]{:S(2)}, u32[]{:S(2)}) collective-permute-start(f32[2,32,128]{2,1,0:T(8,128)S(1)} %get-tuple-element.57.refs_5_), channel_id=1, source_target_pairs={{0,1},{1,0},{2,3},{3,2},{4,5},{5,4},{6,7},{7,6},{8,9},{9,8},{10,11... | collective-permute-start | bytes 98312 | tf_op jit(solution)/shard_map/ppermute | solution.py:743
  22.7 6.7 %collective-permute-start.8 = (f32[32,8,128]{2,1,0:T(8,128)S(1)}, f32[32,8,128]{2,1,0:T(8,128)S(1)}, u32[]{:S(2)}, u32[]{:S(2)}) collective-permute-start(f32[32,8,128]{2,1,0:T(8,128)S(1)} %get-tuple-element.69.rows_ref), channel_id=1, source_target_pairs={{0,16},{16,0},{1,17},{17,1},{2,18},{18,2},{3,19},{19,3},{4,20},{20... | collective-permute-start | bytes 393224 | tf_op jit(solution)/shard_map/ppermute | solution.py:743
  23.3 6.1 %collective-permute-start.10 = (f32[2,32,128]{2,1,0:T(8,128)S(1)}, f32[2,32,128]{2,1,0:T(8,128)S(1)}, u32[]{:S(2)}, u32[]{:S(2)}) collective-permute-start(f32[2,32,128]{2,1,0:T(8,128)S(1)} %get-tuple-element.71.outer_ref), channel_id=1, source_target_pairs={{0,12},{4,8},{8,4},{12,0},{1,13},{5,9},{9,5},{13,1},{2,14},{6,10},... | collective-permute-start | bytes 98312 | tf_op jit(solution)/shard_map/ppermute | solution.py:743
  25.7 3.7 %collective-permute-start.9 = (f32[1,32,128]{2,1,0:T(8,128)S(1)}, f32[1,32,128]{2,1,0:T(8,128)S(1)}, u32[]{:S(2)}, u32[]{:S(2)}) collective-permute-start(f32[1,32,128]{2,1,0:T(8,128)S(1)} %get-tuple-element.70.inner_ref), channel_id=1, source_target_pairs={{0,4},{4,0},{8,12},{12,8},{1,5},{5,1},{9,13},{13,9},{2,6},{6,2},{1... | collective-permute-start | bytes 49160 | tf_op jit(solution)/shard_map/ppermute | solution.py:743
  31.4 4.3 %collective-permute-start.11 = (f32[3,32,128]{2,1,0:T(8,128)S(1)}, f32[3,32,128]{2,1,0:T(8,128)S(1)}, u32[]{:S(2)}, u32[]{:S(2)}) collective-permute-start(f32[3,32,128]{2,1,0:T(8,128)S(1)} %get-tuple-element.74), channel_id=1, source_target_pairs={{0,3},{1,2},{2,1},{3,0},{4,7},{5,6},{6,5},{7,4},{8,11},{9,10},{10,... | collective-permute-start | bytes 147464 | tf_op jit(solution)/shard_map/ppermute | solution.py:743
  31.4 4.2 %collective-permute-start.12 = (f32[2,32,128]{2,1,0:T(8,128)S(1)}, f32[2,32,128]{2,1,0:T(8,128)S(1)}, u32[]{:S(2)}, u32[]{:S(2)}) collective-permute-start(f32[2,32,128]{2,1,0:T(8,128)S(1)} %get-tuple-element.75), channel_id=1, source_target_pairs={{0,2},{1,3},{2,0},{3,1},{4,6},{5,7},{6,4},{7,5},{8,10},{9,11},{10,... | collective-permute-start | bytes 98312 | tf_op jit(solution)/shard_map/ppermute | solution.py:743
  32.2 3.5 %collective-permute-start.13 = (f32[2,32,128]{2,1,0:T(8,128)S(1)}, f32[2,32,128]{2,1,0:T(8,128)S(1)}, u32[]{:S(2)}, u32[]{:S(2)}) collective-permute-start(f32[2,32,128]{2,1,0:T(8,128)S(1)} %get-tuple-element.76.refs_4_), channel_id=1, source_target_pairs={{0,1},{1,0},{2,3},{3,2},{4,5},{5,4},{6,7},{7,6},{8,9},{9,8},{10,11... | collective-permute-start | bytes 98312 | tf_op jit(solution)/shard_map/ppermute | solution.py:743
  33.3 2.4 %collective-permute-start.14 = (f32[2,32,128]{2,1,0:T(8,128)S(1)}, f32[2,32,128]{2,1,0:T(8,128)S(1)}, u32[]{:S(2)}, u32[]{:S(2)}) collective-permute-start(f32[2,32,128]{2,1,0:T(8,128)S(1)} %get-tuple-element.77.refs_5_), channel_id=1, source_target_pairs={{0,1},{1,0},{2,3},{3,2},{4,5},{5,4},{6,7},{7,6},{8,9},{9,8},{10,11... | collective-permute-start | bytes 98312 | tf_op jit(solution)/shard_map/ppermute | solution.py:743

commit v9 on v8

--- a/solution.py
+++ b/solution.py
@@ -219,6 +219,12 @@
         high.payload(p, w, spread_slots(j, False)) for p, w, j in zip(pres[1], wind[1], jac)
     ]
     return down, up
+
+
+def levels_of(chunk, share, body, carry):
+    for k in range(share):
+        carry = body(chunk * share + k, carry)
+    return carry
 
 
 def pack_levels(ref, count, levels):
@@ -261,11 +267,16 @@
         copy.start()
         return copy
 
+    def chunk(index, source, target, c):
+        part = pl.ds(c * share, share)
+        return pltpu.make_async_copy(source.at[part], target.at[part], sems.at[index, c])
+
+    for c in range(CHUNKS):
+        chunk(0, p_hbm, p_ref, c).start()
+        chunk(1, s_hbm, s_ref, c).start()
+    for c in range(CHUNKS):
+        chunk(2, wy_hbm, wy_ref, c).start()
     tail = pl.ds(rows - ROWS, ROWS)
-    parts = [pl.ds(c * share, share) for c in range(CHUNKS)]
-    pres_in = [fetch(p_hbm.at[s], p_ref.at[s], sems.at[0, c]) for c, s in enumerate(parts)]
-    stiff_in = [fetch(s_hbm.at[s], s_ref.at[s], sems.at[1, c]) for c, s in enumerate(parts)]
-    wind_in = [fetch(wy_hbm.at[s], wy_ref.at[s], sems.at[2, c]) for c, s in enumerate(parts)]
     ends_in = [
         fetch(jac_hbm, jac_ref, sems.at[3, 0]),
         fetch(wx_hbm.at[:, pl.ds(0, ROWS)], wx_ref.at[:, pl.ds(0, ROWS)], sems.at[3, 1]),
@@ -274,7 +285,7 @@
     packer = Packer(count)
 
     def down(level, carry):
-        state, excess, prod = carry
+        state, excess, prod = carry[0], list(carry[1]), list(carry[2])
         for t in range(count):
             part = slice(ROWS * t, ROWS * (t + 1))
             rate = 1.0 / s_ref[level, part, :]
@@ -288,7 +299,7 @@
         return packer.add(level, tiles_of(p_ref, level, count), state), excess, prod
 
     def up(step, carry):
-        state, value = carry
+        state, value = carry[0], list(carry[1])
         level = levels - 1 - step
         for t in range(count):
             part = slice(ROWS * t, ROWS * (t + 1))
@@ -297,16 +308,20 @@
         return packer.add(step, tiles_of(wy_ref, step, count), state), value
 
     ones = [jnp.ones((ROWS, 128), jnp.float32)] * count
-    carry = packer.start, list(ones), list(ones)
-    for c in range(CHUNKS):
-        pres_in[c].wait()
-        stiff_in[c].wait()
-        carry = lax.fori_loop(c * share, (c + 1) * share, down, carry, unroll=UNROLL)
+
+    def down_chunk(c, carry):
+        chunk(0, p_hbm, p_ref, c).wait()
+        chunk(1, s_hbm, s_ref, c).wait()
+        return levels_of(c, share, down, carry)
+
+    def up_chunk(c, carry):
+        chunk(2, wy_hbm, wy_ref, c).wait()
+        return levels_of(c, share, up, carry)
+
+    carry = lax.fori_loop(0, CHUNKS, down_chunk, (packer.start, ones, ones))
     pres = packer.done(carry[0])
-    carry = packer.start, [jnp.zeros_like(one) for one in ones]
-    for c in range(CHUNKS):
-        wind_in[c].wait()
-        carry = lax.fori_loop(c * share, (c + 1) * share, up, carry, unroll=UNROLL)
+    zeros = [jnp.zeros_like(one) for one in ones]
+    carry = lax.fori_loop(0, CHUNKS, up_chunk, (packer.start, zeros))
     wind = packer.done(carry[0])
     put_tiles(stat_ref, 0, carry[1])
     stat_ref[1] = q_ref[levels - 1]
@@ -326,7 +341,7 @@
         )
         return state
 
-    lax.fori_loop(0, levels, step, 0, unroll=2 * UNROLL)
+    lax.fori_loop(0, levels, step, 0, unroll=UNROLL)
     rows_ref[levels] = ends
     down_out, up_out = lane_payload(pres, wind, jac)
     put_pair(inner_ref, outer_ref, 0, down_out, up_out)
@@ -485,23 +500,28 @@
             y_ref[level, part, :] = values[k]
         return values, firsts
 
-    for which in (tuple(range(count)),):
-        zeros = [jnp.zeros((ROWS, 128), jnp.float32)] * len(which)
-        bottom, force = star(0, which)
-
-        def step(level, carry, which=which):
-            below, here, force, value, first = carry
-            above, force_next = star(level, which)
-            value, first = sweep(level - 1, which, below, above, force, value, first)
-            return here, above, force_next, value, first
-
-        below, here, force, value, first = lax.fori_loop(
-            1, levels, step, (zeros, bottom, force, zeros, zeros), unroll=2 * UNROLL
-        )
-        value, first = sweep(levels - 1, which, below, zeros, force, value, first)
-        interface(
-            which, first, value, bottom, here, coef_ref, next_ref, cross_ref, mate_ref, share_ref
-        )
+    which = tuple(range(count))
+    put_tiles(y_ref, 0, [jnp.zeros((ROWS, 128), jnp.float32)] * count)
+    zeros = tiles_of(y_ref, 0, count)
+
+    def step(level, carry):
+        below, here, force, value, first = carry
+        above, force_next = star(level, which)
+        before = jnp.maximum(level - 1, 0)
+        new_value, new_first = sweep(before, which, below, above, force, value, first)
+        started = jnp.where(level > 0, 1.0, 0.0)
+        value = [started * n for n in new_value]
+        first = [started * n for n in new_first]
+        return here, above, force_next, value, first
+
+    below, here, force, value, first = lax.fori_loop(
+        0, levels, step, (zeros, zeros, zeros, zeros, zeros), unroll=UNROLL // 2
+    )
+    value, first = sweep(levels - 1, which, below, zeros, force, value, first)
+    bottom = tiles_of(ps_ref, 0, count)
+    interface(
+        which, first, value, bottom, here, coef_ref, next_ref, cross_ref, mate_ref, share_ref
+    )
 
 
 PAIR_COEFS = ("own", "other", "den", "den_end", "den_link", "outer", "total", "facing", "centre", "first", "last")
@@ -634,22 +654,20 @@
 
     def step(index, carry):
         above, here = carry
-        level = levels - 2 - index
+        level = levels - 1 - index
         below = solved(level, here)
-        pressed(level + 1, above, below)
-        return here, below
-
-    carry = over, solved(levels - 1, upper)
-    if ready is None:
-        carry = lax.fori_loop(0, levels - 1, step, carry, unroll=UNROLL)
-    else:
-        done, share = 0, levels // CHUNKS
-        for c in range(CHUNKS - 1, -1, -1):
-            goal = levels - 1 - c * share
-            carry = lax.fori_loop(done, goal, step, carry, unroll=UNROLL)
-            done = goal
+        pressed(jnp.minimum(level + 1, levels - 1), above, below)
+        return [jnp.where(index == 0, o, h) for o, h in zip(over, here)], below
+
+    share = levels // CHUNKS
+
+    def chunk(c, carry):
+        carry = levels_of(c, share, step, carry)
+        if ready is not None:
             ready(c)
-    above, here = carry
+        return carry
+
+    above, here = lax.fori_loop(0, CHUNKS, chunk, (over, upper))
     pressed(0, above, under)
 
 
@@ -671,7 +689,7 @@
         )
         return state
 
-    lax.fori_loop(0, levels, step, 0, unroll=2 * UNROLL)
+    lax.fori_loop(0, levels, step, 0, unroll=UNROLL)
     pres = pack_levels(p_ref, count, levels)
     wind = tiles_of(pw_ref, 0, count), tiles_of(pw_ref, 1, count)
     down, up = lane_payload(pres, wind, planes_of(jac_ref, count))
@@ -686,18 +704,18 @@
     x_hbm, p_hbm, x_ref, p_ref, sems = refs[COLUMN + 4 :]
     levels, rows, _ = y_ref.shape
     share = levels // CHUNKS
-    copies = []
-
-    def send(index, source, target, c):
+
+    def copy(index, source, target, c):
         part = pl.ds(c * share, share)
-        copy = pltpu.make_async_copy(source.at[part], target.at[part], sems.at[index, c])
-        copy.start()
-        copies.append(copy)
-
-    def ready(c):
-        send(0, x_ref, x_hbm, c)
-        if c < CHUNKS - 1:
-            send(1, p_ref, p_hbm, c + 1)
+        return pltpu.make_async_copy(source.at[part], target.at[part], sems.at[index, c])
+
+    def ready(step):
+        c = CHUNKS - 1 - step
+        copy(0, x_ref, x_hbm, c).start()
+
+        @pl.when(step > 0)
+        def _():
+            copy(1, p_ref, p_hbm, c + 1).start()
 
     finish(
         rows // ROWS,
@@ -711,9 +729,10 @@
         column_refs,
         ready,
     )
-    send(1, p_ref, p_hbm, 0)
-    for copy in copies:
-        copy.wait()
+    copy(1, p_ref, p_hbm, 0).start()
+    for c in range(CHUNKS):
+        copy(0, x_ref, x_hbm, c).wait()
+        copy(1, p_ref, p_hbm, c).wait()
 
 
 def call(kernel, name, shapes, *args, far_in=(), far_out=False, scratch=(), keep=()):

time: 37 us -> 35.6 us (0.962)
  Pallas kernels: 12.7 us -> 11.4 us
    pallas_call x9, Pallas kernels: 12.7 us -> 11.4 us  [call(): pl.pallas_call(kernel, out_shape=[pltpu.VMEM(s, jnp.float32) if k in keep...]
where the time goes in v9:
time: 35.6 us; the launch traced here: 35.5 us
  starting transfers between devices  13.6 us (38%)
  Pallas kernels  11.4 us (32%)
  waiting for transfers between devices  8.02 us (23%)
  local copies, waits for them, and re-layouts  1.62 us (5%)
  between operations  0.81 us (2%)
    ppermute x15, starting transfers between devices, swap(): return lax.ppermute(value, axis, [(i, partner(i)) for i in range(count)])  13.6 us
    pallas_call x9, Pallas kernels, call(): pl.pallas_call(kernel, out_shape=[pltpu.VMEM(s, jnp.float32) if k in keep...  11.4 us
    ppermute x15, waiting for transfers between devices, swap(): return lax.ppermute(value, axis, [(i, partner(i)) for i in range(count)])  8.02 us
    unnamed x16, local copies, waits for them, and re-layouts  1.62 us
  transfers between devices with their start and end apart: 15, of which 4 were waited for; matrix products, arithmetic and copies ran while one was open for 4% of the time, Pallas kernels for 9%

profile of v9, /device:TPU:0, one launch (start us, length us, event | category | flops | bytes accessed | tf_op | source)
XLA Modules:
  0.0 35.5 jit_solution(16936586777205094909)
XLA Ops:
  0.7 2.9 %start.1 = (f32[33,8,128]{2,1,0:T(8,128)S(1)}, f32[2,32,128]{2,1,0:T(8,128)S(1)}, f32[3,32,128]{2,1,0:T(8,128)S(1)}, f32[2,32,128]{2,1,0:T(8,128)S(1)}, f32[32,3...) custom-call(f32[32,32,128]{2,1,0:T(8,128)} %p_ref.3, ...), custom_call_target="tpu_custom_call" | custom-call | flops 9084928 | bytes 4542464 | tf_op jit(solution)/shard_map/start/pallas_call | solution.py:743
  3.6 3.0 %collective-permute-start = (f32[33,8,128]{2,1,0:T(8,128)S(1)}, f32[33,8,128]{2,1,0:T(8,128)S(1)}, u32[]{:S(2)}, u32[]{:S(2)}) collective-permute-start(f32[33,8,128]{2,1,0:T(8,128)S(1)} %get-tuple-element.50.rows_ref.srows_ref), channel_id=1, source_target_pairs={{0,16},{16,0},{1,17},{17,1},{2,18},{18,2},{3,19},{19,3},{4,20},{20... | collective-permute-start | bytes 405512 | tf_op jit(solution)/shard_map/ppermute | solution.py:762
  6.6 3.6 %collective-permute-start.2 = (f32[3,32,128]{2,1,0:T(8,128)S(1)}, f32[3,32,128]{2,1,0:T(8,128)S(1)}, u32[]{:S(2)}, u32[]{:S(2)}) collective-permute-start(f32[3,32,128]{2,1,0:T(8,128)S(1)} %get-tuple-element.52.outer_ref.souter_ref), channel_id=1, source_target_pairs={{0,12},{4,8},{8,4},{12,0},{1,13},{5,9},{9,5},{13,1},{2,14},{6,10},... | collective-permute-start | bytes 147464 | tf_op jit(solution)/shard_map/ppermute | solution.py:762
  10.3 1.4 %interior.2 = (f32[32,32,128]{2,1,0:T(8,128)S(1)}, f32[32,32,128]{2,1,0:T(8,128)S(1)}, f32[32,32,128]{2,1,0:T(8,128)S(1)}) custom-call(f32[32,32,128]{2,1,0:T(8,128)S(1)} %copy-done, f32[32,32,128]{2,1,0:T(8,128)S(1)} %copy-done.1, f32[32,32,128]{2,1,0:T(8,128)S(1)} %copy-done.2, f32[32,128]{1,0:T(8,128)S(1)} %copy-done.3), custom_call_target="tpu_custom_call" | custom-call | flops 6324224 | bytes 3162112 | tf_op jit(solution)/shard_map/interior/pallas_call | solution.py:743
  11.8 2.4 %collective-permute-done.1.got_inner_ref.got_sinner_ref = f32[2,32,128]{2,1,0:T(8,128)S(1)} collective-permute-done((f32[2,32,128]{2,1,0:T(8,128)S(1)}, f32[2,32,128]{2,1,0:T(8,128)S(1)}, u32[]{:S(2)}, u32[]{:S(2)}) %collective-permute-start.1) | collective-permute-done | bytes 32800 | tf_op jit(solution)/shard_map/ppermute | solution.py:762
  14.2 1.4 %sweep.2 = (f32[32,32,128]{2,1,0:T(8,128)S(1)}, f32[32,32,128]{2,1,0:T(8,128)S(1)}, f32[32,32,128]{2,1,0:T(8,128)S(1)}, f32[32,32,128]{2,1,0:T(8,128)S(1)}, f32[...) custom-call(f32[32,32,128]{2,1,0:T(8,128)S(1)} %copy-done, ...), custom_call_target="tpu_custom_call" | custom-call | flops 15171584 | bytes 7585792 | tf_op jit(solution)/shard_map/sweep/pallas_call | solution.py:743
  15.6 0.2 collective-permute-start.4
  15.8 1.4 %collective-permute-start.5 = (f32[2,32,128]{2,1,0:T(8,128)S(1)}, f32[2,32,128]{2,1,0:T(8,128)S(1)}, u32[]{:S(2)}, u32[]{:S(2)}) collective-permute-start(f32[2,32,128]{2,1,0:T(8,128)S(1)} %get-tuple-element.55), channel_id=1, source_target_pairs={{0,2},{1,3},{2,0},{3,1},{4,6},{5,7},{6,4},{7,5},{8,10},{9,11},{10,... | collective-permute-start | bytes 98312 | tf_op jit(solution)/shard_map/ppermute | solution.py:762
  17.2 0.3 collective-permute-start.6
  17.5 0.2 collective-permute-start.7
  17.7 0.5 %pack.1.refs_13_ = f32[2,32,128]{2,1,0:T(8,128)S(1)} custom-call(f32[32,32,128]{2,1,0:T(8,128)S(1)} %get-tuple-element.62.wy_ref), custom_call_target="tpu_custom_call" | custom-call | flops 1114112 | bytes 557056 | tf_op jit(solution)/shard_map/pack/pallas_call | solution.py:743
  18.2 2.5 %collective-permute-done.5.refs_1_ = f32[2,32,128]{2,1,0:T(8,128)S(1)} collective-permute-done((f32[2,32,128]{2,1,0:T(8,128)S(1)}, f32[2,32,128]{2,1,0:T(8,128)S(1)}, u32[]{:S(2)}, u32[]{:S(2)}) %collective-permute-start.5) | collective-permute-done | bytes 32800 | tf_op jit(solution)/shard_map/ppermute | solution.py:762
  20.7 1.3 %finish.1 = (f32[32,32,128]{2,1,0:T(8,128)S(1)}, f32[32,32,128]{2,1,0:T(8,128)S(1)}, f32[32,8,128]{2,1,0:T(8,128)S(1)}, f32[1,32,128]{2,1,0:T(8,128)S(1)}, f32[2...) custom-call(f32[4,32,128]{2,1,0:T(8,128)S(1)} %collective-permute-done.4.refs_0_.refs_7_, ...), custom_call_target="tpu_custom_call" | custom-call | flops 8814592 | bytes 4407296 | tf_op jit(solution)/shard_map/finish/pallas_call | solution.py:743
  22.0 0.6 %collective-permute-start.8 = (f32[32,8,128]{2,1,0:T(8,128)S(1)}, f32[32,8,128]{2,1,0:T(8,128)S(1)}, u32[]{:S(2)}, u32[]{:S(2)}) collective-permute-start(f32[32,8,128]{2,1,0:T(8,128)S(1)} %get-tuple-element.69.rows_ref), channel_id=1, source_target_pairs={{0,16},{16,0},{1,17},{17,1},{2,18},{18,2},{3,19},{19,3},{4,20},{20... | collective-permute-start | bytes 393224 | tf_op jit(solution)/shard_map/ppermute | solution.py:762
  22.6 2.4 %collective-permute-start.10 = (f32[2,32,128]{2,1,0:T(8,128)S(1)}, f32[2,32,128]{2,1,0:T(8,128)S(1)}, u32[]{:S(2)}, u32[]{:S(2)}) collective-permute-start(f32[2,32,128]{2,1,0:T(8,128)S(1)} %get-tuple-element.71.outer_ref), channel_id=1, source_target_pairs={{0,12},{4,8},{8,4},{12,0},{1,13},{5,9},{9,5},{13,1},{2,14},{6,10},... | collective-permute-start | bytes 98312 | tf_op jit(solution)/shard_map/ppermute | solution.py:762
  24.9 1.4 %interior.3 = (f32[32,32,128]{2,1,0:T(8,128)S(1)}, f32[32,32,128]{2,1,0:T(8,128)S(1)}, f32[32,32,128]{2,1,0:T(8,128)S(1)}) custom-call(f32[32,32,128]{2,1,0:T(8,128)S(1)} %get-tuple-element.63.p_ref, f32[32,32,128]{2,1,0:T(8,128)S(1)} %get-tuple-element.61.refs_12_.wx_ref, f32[32,32,128]{2,1,0:T(8,128)S(1)} %get-tuple-element.62.wy_ref, f32[32,128]{1,0:T(8,128)S(1)} %copy-done.3), custom_call_target="tpu_custom_call" | custom-call | flops 6324224 | bytes 3162112 | tf_op jit(solution)/shard_map/interior/pallas_call | solution.py:743
  26.4 2.3 %collective-permute-done.9.got_inner_ref = f32[1,32,128]{2,1,0:T(8,128)S(1)} collective-permute-done((f32[1,32,128]{2,1,0:T(8,128)S(1)}, f32[1,32,128]{2,1,0:T(8,128)S(1)}, u32[]{:S(2)}, u32[]{:S(2)}) %collective-permute-start.9) | collective-permute-done | bytes 16416 | tf_op jit(solution)/shard_map/ppermute | solution.py:762
  28.7 1.4 %sweep.3 = (f32[32,32,128]{2,1,0:T(8,128)S(1)}, f32[32,32,128]{2,1,0:T(8,128)S(1)}, f32[32,32,128]{2,1,0:T(8,128)S(1)}, f32[32,32,128]{2,1,0:T(8,128)S(1)}, f32[...) custom-call(f32[32,32,128]{2,1,0:T(8,128)S(1)} %get-tuple-element.63.p, ...), custom_call_target="tpu_custom_call" | custom-call | flops 14991360 | bytes 7495680 | tf_op jit(solution)/shard_map/sweep/pallas_call | solution.py:743
  30.1 0.8 %collective-permute-start.12 = (f32[2,32,128]{2,1,0:T(8,128)S(1)}, f32[2,32,128]{2,1,0:T(8,128)S(1)}, u32[]{:S(2)}, u32[]{:S(2)}) collective-permute-start(f32[2,32,128]{2,1,0:T(8,128)S(1)} %get-tuple-element.75), channel_id=1, source_target_pairs={{0,2},{1,3},{2,0},{3,1},{4,6},{5,7},{6,4},{7,5},{8,10},{9,11},{10,... | collective-permute-start | bytes 98312 | tf_op jit(solution)/shard_map/ppermute | solution.py:762
  30.9 1.1 %collective-permute-start.13 = (f32[2,32,128]{2,1,0:T(8,128)S(1)}, f32[2,32,128]{2,1,0:T(8,128)S(1)}, u32[]{:S(2)}, u32[]{:S(2)}) collective-permute-start(f32[2,32,128]{2,1,0:T(8,128)S(1)} %get-tuple-element.76.refs_4_), channel_id=1, source_target_pairs={{0,1},{1,0},{2,3},{3,2},{4,5},{5,4},{6,7},{7,6},{8,9},{9,8},{10,11... | collective-permute-start | bytes 98312 | tf_op jit(solution)/shard_map/ppermute | solution.py:762
  32.0 0.8 %copy.12 = f32[32,32,128]{2,1,0:T(8,128)} copy(f32[32,32,128]{2,1,0:T(8,128)S(1)} %get-tuple-element.82) | data formatting | bytes 1048576
  32.8 0.8 %copy.13 = f32[32,32,128]{2,1,0:T(8,128)} copy(f32[32,32,128]{2,1,0:T(8,128)S(1)} %get-tuple-element.83) | data formatting | bytes 1048576
  33.6 0.8 %collective-permute-done.12.refs_1_ = f32[2,32,128]{2,1,0:T(8,128)S(1)} collective-permute-done((f32[2,32,128]{2,1,0:T(8,128)S(1)}, f32[2,32,128]{2,1,0:T(8,128)S(1)}, u32[]{:S(2)}, u32[]{:S(2)}) %collective-permute-start.12) | collective-permute-done | bytes 32800 | tf_op jit(solution)/shard_map/ppermute | solution.py:762
  34.3 1.1 %last.1 = (f32[32,32,128]{2,1,0:T(8,128)}, f32[32,32,128]{2,1,0:T(8,128)}) custom-call(f32[3,32,128]{2,1,0:T(8,128)S(1)} %collective-permute-done.11.refs_0_, f32[2,32,128]{2,1,0:T(8,128)S(1)} %collective-permute-done.12.refs_1_, f32[2,32,128]{2,1,0:T(8,128)S(1)} %collective-permute-done.13.refs_2_, f32[2,32,128]{2,1,0:T(8,128)S(1)} %collective-permute-done.14.refs_3_, ...), custom_call_target="tpu_custom_call" | custom-call | flops 7208960 | bytes 3604480 | tf_op jit(solution)/shard_map/last/pallas_call | solution.py:743
  (31 shorter events, 0.2 us)
Async XLA Ops:
  0.6 9.6 %copy-start = (f32[32,32,128]{2,1,0:T(8,128)S(1)}, f32[32,32,128]{2,1,0:T(8,128)}, u32[]{:S(2)}) copy-start(f32[32,32,128]{2,1,0:T(8,128)} %p_ref.3) | copy-start | bytes 1572868
  0.6 9.6 %copy-start.2 = (f32[32,32,128]{2,1,0:T(8,128)S(1)}, f32[32,32,128]{2,1,0:T(8,128)}, u32[]{:S(2)}) copy-start(f32[32,32,128]{2,1,0:T(8,128)} %wy_hbm.1) | copy-start | bytes 1572868
  0.7 9.6 %copy-start.1 = (f32[32,32,128]{2,1,0:T(8,128)S(1)}, f32[32,32,128]{2,1,0:T(8,128)}, u32[]{:S(2)}) copy-start(f32[32,32,128]{2,1,0:T(8,128)} %wx_hbm.1) | copy-start | bytes 1572868
  0.7 9.6 %copy-start.3 = (f32[32,128]{1,0:T(8,128)S(1)}, f32[32,128]{1,0:T(8,128)}, u32[]{:S(2)}) copy-start(f32[32,128]{1,0:T(8,128)} %jac_ref.7) | copy-start | bytes 49156
  3.6 10.6 %collective-permute-start = (f32[33,8,128]{2,1,0:T(8,128)S(1)}, f32[33,8,128]{2,1,0:T(8,128)S(1)}, u32[]{:S(2)}, u32[]{:S(2)}) collective-permute-start(f32[33,8,128]{2,1,0:T(8,128)S(1)} %get-tuple-element.50.rows_ref.srows_ref), channel_id=1, source_target_pairs={{0,16},{16,0},{1,17},{17,1},{2,18},{18,2},{3,19},{19,3},{4,20},{20... | collective-permute-start | bytes 405512 | tf_op jit(solution)/shard_map/ppermute | solution.py:762
  6.6 5.1 %collective-permute-start.3 = (f32[5,32,128]{2,1,0:T(8,128)S(1)}, f32[5,32,128]{2,1,0:T(8,128)S(1)}, u32[]{:S(2)}, u32[]{:S(2)}) collective-permute-start(f32[5,32,128]{2,1,0:T(8,128)S(1)} %get-tuple-element.53.stat_ref), channel_id=1, source_target_pairs={{0,1},{1,0},{2,3},{3,2},{4,5},{5,4},{6,7},{7,6},{8,9},{9,8},{10,11... | collective-permute-start | bytes 245768 | tf_op jit(solution)/shard_map/ppermute | solution.py:762
  6.6 7.5 %collective-permute-start.2 = (f32[3,32,128]{2,1,0:T(8,128)S(1)}, f32[3,32,128]{2,1,0:T(8,128)S(1)}, u32[]{:S(2)}, u32[]{:S(2)}) collective-permute-start(f32[3,32,128]{2,1,0:T(8,128)S(1)} %get-tuple-element.52.outer_ref.souter_ref), channel_id=1, source_target_pairs={{0,12},{4,8},{8,4},{12,0},{1,13},{5,9},{9,5},{13,1},{2,14},{6,10},... | collective-permute-start | bytes 147464 | tf_op jit(solution)/shard_map/ppermute | solution.py:762
  10.2 3.9 %collective-permute-start.1 = (f32[2,32,128]{2,1,0:T(8,128)S(1)}, f32[2,32,128]{2,1,0:T(8,128)S(1)}, u32[]{:S(2)}, u32[]{:S(2)}) collective-permute-start(f32[2,32,128]{2,1,0:T(8,128)S(1)} %get-tuple-element.51.inner_ref.sinner_ref), channel_id=1, source_target_pairs={{0,4},{4,0},{8,12},{12,8},{1,5},{5,1},{9,13},{13,9},{2,6},{6,2},{1... | collective-permute-start | bytes 98312 | tf_op jit(solution)/shard_map/ppermute | solution.py:762
  10.2 3.9 %copy-start.4 = (f32[32,32,128]{2,1,0:T(8,128)S(1)}, f32[32,32,128]{2,1,0:T(8,128)}, u32[]{:S(2)}) copy-start(f32[32,32,128]{2,1,0:T(8,128)} %wz_ref.1) | copy-start | bytes 1572868
  11.7 2.5 %copy-start.5 = (f32[32,128]{1,0:T(8,128)S(1)}, f32[32,128]{1,0:T(8,128)}, u32[]{:S(2)}) copy-start(f32[32,128]{1,0:T(8,128)} %sx_ref.3) | copy-start | bytes 49156
  11.7 2.4 %copy-start.6 = (f32[32,128]{1,0:T(8,128)S(1)}, f32[32,128]{1,0:T(8,128)}, u32[]{:S(2)}) copy-start(f32[32,128]{1,0:T(8,128)} %sy_ref.3) | copy-start | bytes 49156
  15.6 5.2 %collective-permute-start.4 = (f32[4,32,128]{2,1,0:T(8,128)S(1)}, f32[4,32,128]{2,1,0:T(8,128)S(1)}, u32[]{:S(2)}, u32[]{:S(2)}) collective-permute-start(f32[4,32,128]{2,1,0:T(8,128)S(1)} %get-tuple-element.54), channel_id=1, source_target_pairs={{0,3},{1,2},{2,1},{3,0},{4,7},{5,6},{6,5},{7,4},{8,11},{9,10},{10,... | collective-permute-start | bytes 196616 | tf_op jit(solution)/shard_map/ppermute | solution.py:762
  15.8 4.9 %collective-permute-start.5 = (f32[2,32,128]{2,1,0:T(8,128)S(1)}, f32[2,32,128]{2,1,0:T(8,128)S(1)}, u32[]{:S(2)}, u32[]{:S(2)}) collective-permute-start(f32[2,32,128]{2,1,0:T(8,128)S(1)} %get-tuple-element.55), channel_id=1, source_target_pairs={{0,2},{1,3},{2,0},{3,1},{4,6},{5,7},{6,4},{7,5},{8,10},{9,11},{10,... | collective-permute-start | bytes 98312 | tf_op jit(solution)/shard_map/ppermute | solution.py:762
  17.2 3.5 %collective-permute-start.6 = (f32[2,32,128]{2,1,0:T(8,128)S(1)}, f32[2,32,128]{2,1,0:T(8,128)S(1)}, u32[]{:S(2)}, u32[]{:S(2)}) collective-permute-start(f32[2,32,128]{2,1,0:T(8,128)S(1)} %get-tuple-element.56.refs_4_), channel_id=1, source_target_pairs={{0,1},{1,0},{2,3},{3,2},{4,5},{5,4},{6,7},{7,6},{8,9},{9,8},{10,11... | collective-permute-start | bytes 98312 | tf_op jit(solution)/shard_map/ppermute | solution.py:762
  17.5 3.2 %collective-permute-start.7 = (f32[2,32,128]{2,1,0:T(8,128)S(1)}, f32[2,32,128]{2,1,0:T(8,128)S(1)}, u32[]{:S(2)}, u32[]{:S(2)}) collective-permute-start(f32[2,32,128]{2,1,0:T(8,128)S(1)} %get-tuple-element.57.refs_5_), channel_id=1, source_target_pairs={{0,1},{1,0},{2,3},{3,2},{4,5},{5,4},{6,7},{7,6},{8,9},{9,8},{10,11... | collective-permute-start | bytes 98312 | tf_op jit(solution)/shard_map/ppermute | solution.py:762
  22.0 6.7 %collective-permute-start.8 = (f32[32,8,128]{2,1,0:T(8,128)S(1)}, f32[32,8,128]{2,1,0:T(8,128)S(1)}, u32[]{:S(2)}, u32[]{:S(2)}) collective-permute-start(f32[32,8,128]{2,1,0:T(8,128)S(1)} %get-tuple-element.69.rows_ref), channel_id=1, source_target_pairs={{0,16},{16,0},{1,17},{17,1},{2,18},{18,2},{3,19},{19,3},{4,20},{20... | collective-permute-start | bytes 393224 | tf_op jit(solution)/shard_map/ppermute | solution.py:762
  22.6 6.1 %collective-permute-start.10 = (f32[2,32,128]{2,1,0:T(8,128)S(1)}, f32[2,32,128]{2,1,0:T(8,128)S(1)}, u32[]{:S(2)}, u32[]{:S(2)}) collective-permute-start(f32[2,32,128]{2,1,0:T(8,128)S(1)} %get-tuple-element.71.outer_ref), channel_id=1, source_target_pairs={{0,12},{4,8},{8,4},{12,0},{1,13},{5,9},{9,5},{13,1},{2,14},{6,10},... | collective-permute-start | bytes 98312 | tf_op jit(solution)/shard_map/ppermute | solution.py:762
  24.9 3.7 %collective-permute-start.9 = (f32[1,32,128]{2,1,0:T(8,128)S(1)}, f32[1,32,128]{2,1,0:T(8,128)S(1)}, u32[]{:S(2)}, u32[]{:S(2)}) collective-permute-start(f32[1,32,128]{2,1,0:T(8,128)S(1)} %get-tuple-element.70.inner_ref), channel_id=1, source_target_pairs={{0,4},{4,0},{8,12},{12,8},{1,5},{5,1},{9,13},{13,9},{2,6},{6,2},{1... | collective-permute-start | bytes 49160 | tf_op jit(solution)/shard_map/ppermute | solution.py:762
  30.0 4.3 %collective-permute-start.11 = (f32[3,32,128]{2,1,0:T(8,128)S(1)}, f32[3,32,128]{2,1,0:T(8,128)S(1)}, u32[]{:S(2)}, u32[]{:S(2)}) collective-permute-start(f32[3,32,128]{2,1,0:T(8,128)S(1)} %get-tuple-element.74), channel_id=1, source_target_pairs={{0,3},{1,2},{2,1},{3,0},{4,7},{5,6},{6,5},{7,4},{8,11},{9,10},{10,... | collective-permute-start | bytes 147464 | tf_op jit(solution)/shard_map/ppermute | solution.py:762
  30.1 4.2 %collective-permute-start.12 = (f32[2,32,128]{2,1,0:T(8,128)S(1)}, f32[2,32,128]{2,1,0:T(8,128)S(1)}, u32[]{:S(2)}, u32[]{:S(2)}) collective-permute-start(f32[2,32,128]{2,1,0:T(8,128)S(1)} %get-tuple-element.75), channel_id=1, source_target_pairs={{0,2},{1,3},{2,0},{3,1},{4,6},{5,7},{6,4},{7,5},{8,10},{9,11},{10,... | collective-permute-start | bytes 98312 | tf_op jit(solution)/shard_map/ppermute | solution.py:762
  30.9 3.5 %collective-permute-start.13 = (f32[2,32,128]{2,1,0:T(8,128)S(1)}, f32[2,32,128]{2,1,0:T(8,128)S(1)}, u32[]{:S(2)}, u32[]{:S(2)}) collective-permute-start(f32[2,32,128]{2,1,0:T(8,128)S(1)} %get-tuple-element.76.refs_4_), channel_id=1, source_target_pairs={{0,1},{1,0},{2,3},{3,2},{4,5},{5,4},{6,7},{7,6},{8,9},{9,8},{10,11... | collective-permute-start | bytes 98312 | tf_op jit(solution)/shard_map/ppermute | solution.py:762
  32.0 2.4 %collective-permute-start.14 = (f32[2,32,128]{2,1,0:T(8,128)S(1)}, f32[2,32,128]{2,1,0:T(8,128)S(1)}, u32[]{:S(2)}, u32[]{:S(2)}) collective-permute-start(f32[2,32,128]{2,1,0:T(8,128)S(1)} %get-tuple-element.77.refs_5_), channel_id=1, source_target_pairs={{0,1},{1,0},{2,3},{3,2},{4,5},{5,4},{6,7},{7,6},{8,9},{9,8},{10,11... | collective-permute-start | bytes 98312 | tf_op jit(solution)/shard_map/ppermute | solution.py:762

commit v10 on v9

--- a/solution.py
+++ b/solution.py
@@ -19,7 +19,7 @@
 SLOT = 4
 UNROLL = 8
 CHUNKS = 4
-COLUMN = 8
+COLUMN = 9
 STATS = 5
 
 
@@ -276,11 +276,9 @@
         chunk(1, s_hbm, s_ref, c).start()
     for c in range(CHUNKS):
         chunk(2, wy_hbm, wy_ref, c).start()
-    tail = pl.ds(rows - ROWS, ROWS)
     ends_in = [
         fetch(jac_hbm, jac_ref, sems.at[3, 0]),
-        fetch(wx_hbm.at[:, pl.ds(0, ROWS)], wx_ref.at[:, pl.ds(0, ROWS)], sems.at[3, 1]),
-        fetch(wx_hbm.at[:, tail], wx_ref.at[:, pl.ds(ROWS, ROWS)], sems.at[3, 2]),
+        fetch(wx_hbm, wx_ref, sems.at[3, 1]),
     ]
     packer = Packer(count)
 
@@ -337,7 +335,9 @@
 
     def step(level, state):
         rows_ref[level] = edge.payload(
-            both_ends(tiles_of(p_ref, level, count)), both_ends(tiles_of(wx_ref, level, 2)), ends
+            both_ends(tiles_of(p_ref, level, count)),
+            both_ends(tiles_of(wx_ref, level, count)),
+            ends,
         )
         return state
 
@@ -417,14 +417,12 @@
     got_sinner_ref,
     got_souter_ref,
     coef_ref,
+    far_ref,
     nx_ref,
     ny_ref,
     ps_ref,
     y_ref,
-    next_ref,
-    cross_ref,
-    mate_ref,
-    share_ref,
+    *outs,
 ):
     levels, rows, _ = p_ref.shape
     count = rows // ROWS
@@ -519,12 +517,10 @@
     )
     value, first = sweep(levels - 1, which, below, zeros, force, value, first)
     bottom = tiles_of(ps_ref, 0, count)
-    interface(
-        which, first, value, bottom, here, coef_ref, next_ref, cross_ref, mate_ref, share_ref
-    )
-
-
-PAIR_COEFS = ("own", "other", "den", "den_end", "den_link", "outer", "total", "facing", "centre", "first", "last")
+    interface(first, value, bottom, here, coef_ref, far_ref, outs)
+
+
+PAIR_COEFS = ("own", "other", "den", "den_end", "den_link", "outer", "total", "facing", "first", "last")
 
 
 def place_in_column():
@@ -532,7 +528,7 @@
     return (mine == 0) | (mine == 3), mine < 2, lax.rem(mine, 2) == 0
 
 
-def kernel_s(stat_ref, mate_ref, coef_ref):
+def kernel_s(stat_ref, mate_ref, coef_ref, send_ref):
     outermost, lower, even = place_in_column()
     for t in range(coef_ref.shape[1] // ROWS):
         part = slice(ROWS * t, ROWS * (t + 1))
@@ -557,65 +553,57 @@
             outer=outer_end,
             total=centre + weight * link,
             facing=vert_coef * jnp.where(even, mate[3], mate[4]),
-            centre=vert_coef * jnp.where(lower, inner[4], inner[3]),
             first=vert_coef * mine[3],
             last=vert_coef * mine[4],
         )
         for k, name in enumerate(PAIR_COEFS):
             coef_ref[k, part, :] = coefs[name]
-
-
-def interface(
-    which, first, value, star_first, star_last, coef_ref, next_ref, cross_ref, mate_ref, share_ref
-):
+        send_ref[0, part, :] = coefs["total"]
+        send_ref[1, part, :] = vert_coef * jnp.where(lower, inner[4], inner[3])
+
+
+def interface(first, value, star_first, star_last, coef_ref, far_ref, outs):
+    next_ref, cross_ref, own_ref, star_ref, share_ref = outs
     outermost, lower, even = place_in_column()
-    for t, tile in enumerate(which):
-        part = slice(ROWS * tile, ROWS * (tile + 1))
+    for t in range(len(first)):
+        part = slice(ROWS * t, ROWS * (t + 1))
         coef = {name: coef_ref[k, part, :] for k, name in enumerate(PAIR_COEFS)}
         sign = jnp.where(lower, 1.0, -1.0)
         star_centre = jnp.where(lower, star_last[t], star_first[t])
         star_outer = jnp.where(lower, star_first[t], star_last[t])
-        facing = jnp.where(outermost, coef["facing"], 0.0)
+        facing = jnp.where(outermost, coef["facing"], far_ref[1, part, :])
         centre = jnp.where(lower, value[t], first[t]) + sign * facing * star_centre
         outer = jnp.where(lower, first[t], value[t]) - sign * coef["facing"] * star_outer
         total = coef["own"] * centre + coef["other"] * outer
-        for ref in (next_ref, cross_ref, share_ref):
-            ref[0, part, :] = total
-            ref[1, part, :] = star_centre
-        if next_ref.shape[0] > 3:
-            next_ref[2, part, :] = coef["total"]
-            next_ref[3, part, :] = coef["centre"]
-        mate_ref[0, part, :] = jnp.where(outermost, centre, outer)
-        mate_ref[1, part, :] = jnp.where(even, star_last[t], star_first[t])
+        next_ref[0, part, :] = total
+        next_ref[1, part, :] = star_centre
+        cross_ref[part, :] = total
+        own_ref[part, :] = jnp.where(outermost, centre, outer)
+        star_ref[part, :] = jnp.where(even, star_last[t], star_first[t])
+        share_ref[part, :] = total
 
 
 def boundary(
     count,
     got_next_ref,
     got_cross_ref,
-    got_mate_ref,
+    got_own_ref,
+    got_star_ref,
     got_share_ref,
-    mate_ref,
+    own_ref,
     share_ref,
     coef_ref,
     far_ref,
 ):
     outermost, lower, _ = place_in_column()
-    sign = jnp.where(lower, 1.0, -1.0)
     parts = []
     for t in range(count):
         part = slice(ROWS * t, ROWS * (t + 1))
         coef = {name: coef_ref[k, part, :] for k, name in enumerate(PAIR_COEFS)}
-        far_total, far_facing = far_ref[2, part, :], far_ref[3, part, :]
-        own, got = mate_ref[0, part, :], got_mate_ref[0, part, :]
-        this_star = jnp.where(outermost, got_share_ref[1, part, :], share_ref[1, part, :])
-        next_star = jnp.where(outermost, got_cross_ref[1, part, :], got_next_ref[1, part, :])
-        this = share_ref[0, part, :] + got_share_ref[0, part, :] + sign * far_facing * this_star
-        that = (
-            got_cross_ref[0, part, :]
-            + got_next_ref[0, part, :]
-            - sign * coef["centre"] * next_star
-        )
+        far_total = far_ref[0, part, :]
+        own, got = own_ref[part, :], got_own_ref[part, :]
+        this = share_ref[part, :] + got_share_ref[part, :]
+        that = got_cross_ref[part, :] + got_next_ref[0, part, :]
         middle = (that + far_total * this) / (1.0 - coef["total"] * far_total)
         from_outer = jnp.where(outermost, own, got)
         from_inner = jnp.where(outermost, got, own)
@@ -625,8 +613,8 @@
         zero = jnp.zeros_like(own)
         centre = jnp.where(outermost, between, middle)
         outer = jnp.where(outermost, zero, from_outer + coef["outer"] * between)
-        mate_star = got_mate_ref[1, part, :]
-        star_centre = jnp.where(outermost, mate_star, next_star)
+        mate_star = got_star_ref[part, :]
+        star_centre = jnp.where(outermost, mate_star, got_next_ref[1, part, :])
         star_outer = jnp.where(outermost, zero, mate_star)
         below, above = jnp.where(lower, outer, centre), jnp.where(lower, centre, outer)
         star_below = jnp.where(lower, star_outer, star_centre)
@@ -778,12 +766,11 @@
     return got_inner, got_outer
 
 
-def exchange_column(following, cross, mate, share):
+def exchange_column(following, cross, own, star, share):
     got_cross = swap(cross, "lev", lambda i: i ^ 2)
     got_next = swap(following, "lev", lambda i: i ^ 3)
-    got_mate = swap(mate, "lev", lambda i: i ^ 1)
-    got_share = swap(share, "lev", lambda i: i ^ 1)
-    return got_next, got_cross, got_mate, got_share, mate, share
+    mates = [swap(value, "lev", lambda i: i ^ 1) for value in (own, star, share)]
+    return [got_next, got_cross, *mates, own, share]
 
 
 def local(wind_x, wind_y, wind_z, pressure, jacobian, slope_x, slope_y, stiffness):
@@ -794,27 +781,30 @@
     assert lanes == 128 and levels * SLOT == 128 and rows % ROWS == 0
     assert lax.axis_size("lev") == 4 and lax.axis_size("gy") % 2 == 0
 
-    edge, inner, outer, ends, rate, inv, prod, gain, stat = call(
+    edge, inner, outer, ends, rate, inv, prod, gain, stat, *fields = call(
         kernel_a,
         "start",
-        [(levels + 1, ROWS, lanes), pair, (3,) + plane, pair] + [field] * 4 + [(STATS,) + plane],
+        [(levels + 1, ROWS, lanes), pair, (3,) + plane, pair]
+        + [field] * 4
+        + [(STATS,) + plane]
+        + [field] * 3,
         pressure,
         wind_x,
         wind_y,
         jacobian,
         stiffness,
         far_in=(0, 1, 2, 3, 4),
+        keep=(9, 10, 11),
         scratch=[
-            pltpu.VMEM(field, jnp.float32),
-            pltpu.VMEM((levels, 2 * ROWS, lanes), jnp.float32),
-            pltpu.VMEM(field, jnp.float32),
             pltpu.VMEM(plane, jnp.float32),
             pltpu.VMEM(field, jnp.float32),
             pltpu.SemaphoreType.DMA((4, CHUNKS)),
         ],
     )
+    pressure, wind_x, wind_y = fields
     mate = swap(stat, "lev", lambda i: i ^ 1)
-    (coef,) = call(kernel_s, "pairs", [(len(PAIR_COEFS),) + plane], stat, mate)
+    coef, send = call(kernel_s, "pairs", [(len(PAIR_COEFS),) + plane, pair], stat, mate)
+    far = swap(send, "lev", lambda i: i ^ 2)
     sent = (edge, inner, outer)
     got = (exchange_rows(edge),) + exchange_lanes(inner, outer)
     static_edges = sent + got
@@ -825,7 +815,7 @@
         wind_x, wind_y, star, value, *faces = call(
             kernel_b,
             "sweep",
-            [field, field, field, field, (3 if substep else 4,) + plane, pair, pair, pair],
+            [field] * 4 + [pair] + [plane] * 4,
             pressure,
             *closed,
             wind_z,
@@ -840,12 +830,10 @@
             *got,
             *static_edges,
             coef,
-            keep=tuple(range(8)),
-        )
-        column = exchange_column(*faces)
-        if not substep:
-            far = column[0]
-        column += (coef, far)
+            far,
+            keep=tuple(range(9)),
+        )
+        column = exchange_column(*faces) + [coef, far]
         if substep < SUBSTEPS - 1:
             (packed,) = call(kernel_n, "pack", [pair], wind_y)
             wind_z, pressure, edge, inner, outer, ends = call(

time: 35.6 us -> 34.4 us (0.966)
  waiting for transfers between devices: 8.02 us -> 4.4 us
  starting transfers between devices: 13.6 us -> 16.2 us
    ppermute x15 -> x18, waiting for transfers between devices: 8.02 us -> 4.4 us  [swap(): return lax.ppermute(value, axis, [(i, partner(i)) for i in range(count)])]
    ppermute x15 -> x18, starting transfers between devices: 13.6 us -> 16.2 us  [swap(): return lax.ppermute(value, axis, [(i, partner(i)) for i in range(count)])]
    unnamed x16 -> x10, local copies, waits for them, and re-layouts: 1.62 us -> 1.6 us
  transfers between devices with their start and end apart: 15 -> 18, of which waited for: 4 -> 4; matrix products, arithmetic and copies ran while one was open for 4% -> 5% of each run, Pallas kernels for 9% -> 10%
where the time goes in v10:
time: 34.4 us; the launch traced here: 34.2 us
  starting transfers between devices  16.2 us (47%)
  Pallas kernels  11.3 us (33%)
  waiting for transfers between devices  4.4 us (13%)
  local copies, waits for them, and re-layouts  1.6 us (5%)
  between operations  0.75 us (2%)
    ppermute x18, starting transfers between devices, swap(): return lax.ppermute(value, axis, [(i, partner(i)) for i in range(count)])  16.2 us
    pallas_call x9, Pallas kernels, call(): pl.pallas_call(kernel, out_shape=[pltpu.VMEM(s, jnp.float32) if k in keep...  11.3 us
    ppermute x18, waiting for transfers between devices, swap(): return lax.ppermute(value, axis, [(i, partner(i)) for i in range(count)])  4.4 us
    unnamed x10, local copies, waits for them, and re-layouts  1.6 us
  transfers between devices with their start and end apart: 18, of which 4 were waited for; matrix products, arithmetic and copies ran while one was open for 5% of the time, Pallas kernels for 10%

profile of v10, /device:TPU:0, one launch (start us, length us, event | category | flops | bytes accessed | tf_op | source)
XLA Modules:
  0.0 34.2 jit_solution(15292483542302168526)
XLA Ops:
  0.6 2.8 %start.1 = (f32[33,8,128]{2,1,0:T(8,128)S(1)}, f32[2,32,128]{2,1,0:T(8,128)S(1)}, f32[3,32,128]{2,1,0:T(8,128)S(1)}, f32[2,32,128]{2,1,0:T(8,128)S(1)}, f32[32,3...) custom-call(f32[32,32,128]{2,1,0:T(8,128)} %p_hbm.1, ...), custom_call_target="tpu_custom_call" | custom-call | flops 12230656 | bytes 6115328 | tf_op jit(solution)/shard_map/start/pallas_call | solution.py:731
  3.4 3.0 %collective-permute-start = (f32[33,8,128]{2,1,0:T(8,128)S(1)}, f32[33,8,128]{2,1,0:T(8,128)S(1)}, u32[]{:S(2)}, u32[]{:S(2)}) collective-permute-start(f32[33,8,128]{2,1,0:T(8,128)S(1)} %get-tuple-element.60.rows_ref.srows_ref), channel_id=1, source_target_pairs={{0,16},{16,0},{1,17},{17,1},{2,18},{18,2},{3,19},{19,3},{4,20},{20... | collective-permute-start | bytes 405512 | tf_op jit(solution)/shard_map/ppermute | solution.py:750
  6.5 3.6 %collective-permute-start.2 = (f32[3,32,128]{2,1,0:T(8,128)S(1)}, f32[3,32,128]{2,1,0:T(8,128)S(1)}, u32[]{:S(2)}, u32[]{:S(2)}) collective-permute-start(f32[3,32,128]{2,1,0:T(8,128)S(1)} %get-tuple-element.62.outer_ref.souter_ref), channel_id=1, source_target_pairs={{0,12},{4,8},{8,4},{12,0},{1,13},{5,9},{9,5},{13,1},{2,14},{6,10},... | collective-permute-start | bytes 147464 | tf_op jit(solution)/shard_map/ppermute | solution.py:750
  10.1 1.6 %collective-permute-start.4 = (f32[2,32,128]{2,1,0:T(8,128)S(1)}, f32[2,32,128]{2,1,0:T(8,128)S(1)}, u32[]{:S(2)}, u32[]{:S(2)}) collective-permute-start(f32[2,32,128]{2,1,0:T(8,128)S(1)} %get-tuple-element.65), channel_id=1, source_target_pairs={{0,2},{1,3},{2,0},{3,1},{4,6},{5,7},{6,4},{7,5},{8,10},{9,11},{10,... | collective-permute-start | bytes 98312 | tf_op jit(solution)/shard_map/ppermute | solution.py:750
  11.7 1.4 %interior.2 = (f32[32,32,128]{2,1,0:T(8,128)S(1)}, f32[32,32,128]{2,1,0:T(8,128)S(1)}, f32[32,32,128]{2,1,0:T(8,128)S(1)}) custom-call(f32[32,32,128]{2,1,0:T(8,128)S(1)} %get-tuple-element.50.p_ref, f32[32,32,128]{2,1,0:T(8,128)S(1)} %get-tuple-element.51.wx_ref, f32[32,32,128]{2,1,0:T(8,128)S(1)} %get-tuple-element.52.wy_ref, f32[32,128]{1,0:T(8,128)S(1)} %copy-done), custom_call_target="tpu_custom_call" | custom-call | flops 6324224 | bytes 3162112 | tf_op jit(solution)/shard_map/interior/pallas_call | solution.py:731
  13.1 0.9 %collective-permute-done.1.got_inner_ref.got_sinner_ref = f32[2,32,128]{2,1,0:T(8,128)S(1)} collective-permute-done((f32[2,32,128]{2,1,0:T(8,128)S(1)}, f32[2,32,128]{2,1,0:T(8,128)S(1)}, u32[]{:S(2)}, u32[]{:S(2)}) %collective-permute-start.1) | collective-permute-done | bytes 32800 | tf_op jit(solution)/shard_map/ppermute | solution.py:750
  14.1 1.4 %sweep.2 = (f32[32,32,128]{2,1,0:T(8,128)S(1)}, f32[32,32,128]{2,1,0:T(8,128)S(1)}, f32[32,32,128]{2,1,0:T(8,128)S(1)}, f32[32,32,128]{2,1,0:T(8,128)S(1)}, f32[...) custom-call(f32[32,32,128]{2,1,0:T(8,128)S(1)} %get-tuple-element.50, ...), custom_call_target="tpu_custom_call" | custom-call | flops 15073280 | bytes 7536640 | tf_op jit(solution)/shard_map/sweep/pallas_call | solution.py:731
  15.7 1.4 %collective-permute-start.6 = (f32[32,128]{1,0:T(8,128)S(1)}, f32[32,128]{1,0:T(8,128)S(1)}, u32[]{:S(2)}, u32[]{:S(2)}) collective-permute-start(f32[32,128]{1,0:T(8,128)S(1)} %get-tuple-element.67), channel_id=1, source_target_pairs={{0,2},{1,3},{2,0},{3,1},{4,6},{5,7},{6,4},{7,5},{8,10},{9,11},{10,... | collective-permute-start | bytes 49160 | tf_op jit(solution)/shard_map/ppermute | solution.py:750
  17.1 0.3 collective-permute-start.8
  17.7 0.3 collective-permute-start.9
  17.9 0.5 %pack.1.refs_14_ = f32[2,32,128]{2,1,0:T(8,128)S(1)} custom-call(f32[32,32,128]{2,1,0:T(8,128)S(1)} %get-tuple-element.75.wy_ref), custom_call_target="tpu_custom_call" | custom-call | flops 1114112 | bytes 557056 | tf_op jit(solution)/shard_map/pack/pallas_call | solution.py:731
  18.4 1.1 %collective-permute-done.6.refs_1_ = f32[32,128]{1,0:T(8,128)S(1)} collective-permute-done((f32[32,128]{1,0:T(8,128)S(1)}, f32[32,128]{1,0:T(8,128)S(1)}, u32[]{:S(2)}, u32[]{:S(2)}) %collective-permute-start.6) | collective-permute-done | bytes 16416 | tf_op jit(solution)/shard_map/ppermute | solution.py:750
  19.5 1.3 %finish.1 = (f32[32,32,128]{2,1,0:T(8,128)S(1)}, f32[32,32,128]{2,1,0:T(8,128)S(1)}, f32[32,8,128]{2,1,0:T(8,128)S(1)}, f32[1,32,128]{2,1,0:T(8,128)S(1)}, f32[2...) custom-call(f32[2,32,128]{2,1,0:T(8,128)S(1)} %collective-permute-done.5.refs_0_, ...), custom_call_target="tpu_custom_call" | custom-call | flops 8519680 | bytes 4259840 | tf_op jit(solution)/shard_map/finish/pallas_call | solution.py:731
  20.8 0.6 %collective-permute-start.10 = (f32[32,8,128]{2,1,0:T(8,128)S(1)}, f32[32,8,128]{2,1,0:T(8,128)S(1)}, u32[]{:S(2)}, u32[]{:S(2)}) collective-permute-start(f32[32,8,128]{2,1,0:T(8,128)S(1)} %get-tuple-element.82.rows_ref), channel_id=1, source_target_pairs={{0,16},{16,0},{1,17},{17,1},{2,18},{18,2},{3,19},{19,3},{4,20},{20... | collective-permute-start | bytes 393224 | tf_op jit(solution)/shard_map/ppermute | solution.py:750
  21.3 2.6 %collective-permute-start.12 = (f32[2,32,128]{2,1,0:T(8,128)S(1)}, f32[2,32,128]{2,1,0:T(8,128)S(1)}, u32[]{:S(2)}, u32[]{:S(2)}) collective-permute-start(f32[2,32,128]{2,1,0:T(8,128)S(1)} %get-tuple-element.84.outer_ref), channel_id=1, source_target_pairs={{0,12},{4,8},{8,4},{12,0},{1,13},{5,9},{9,5},{13,1},{2,14},{6,10},... | collective-permute-start | bytes 98312 | tf_op jit(solution)/shard_map/ppermute | solution.py:750
  23.9 1.4 %interior.3 = (f32[32,32,128]{2,1,0:T(8,128)S(1)}, f32[32,32,128]{2,1,0:T(8,128)S(1)}, f32[32,32,128]{2,1,0:T(8,128)S(1)}) custom-call(f32[32,32,128]{2,1,0:T(8,128)S(1)} %get-tuple-element.76.p_ref, f32[32,32,128]{2,1,0:T(8,128)S(1)} %get-tuple-element.74.refs_13_.wx_ref, f32[32,32,128]{2,1,0:T(8,128)S(1)} %get-tuple-element.75.wy_ref, f32[32,128]{1,0:T(8,128)S(1)} %copy-done), custom_call_target="tpu_custom_call" | custom-call | flops 6324224 | bytes 3162112 | tf_op jit(solution)/shard_map/interior/pallas_call | solution.py:731
  25.4 2.3 %collective-permute-done.11.got_inner_ref = f32[1,32,128]{2,1,0:T(8,128)S(1)} collective-permute-done((f32[1,32,128]{2,1,0:T(8,128)S(1)}, f32[1,32,128]{2,1,0:T(8,128)S(1)}, u32[]{:S(2)}, u32[]{:S(2)}) %collective-permute-start.11) | collective-permute-done | bytes 16416 | tf_op jit(solution)/shard_map/ppermute | solution.py:750
  27.7 1.4 %sweep.3 = (f32[32,32,128]{2,1,0:T(8,128)S(1)}, f32[32,32,128]{2,1,0:T(8,128)S(1)}, f32[32,32,128]{2,1,0:T(8,128)S(1)}, f32[32,32,128]{2,1,0:T(8,128)S(1)}, f32[...) custom-call(f32[32,32,128]{2,1,0:T(8,128)S(1)} %get-tuple-element.76, ...), custom_call_target="tpu_custom_call" | custom-call | flops 14925824 | bytes 7462912 | tf_op jit(solution)/shard_map/sweep/pallas_call | solution.py:731
  29.1 1.2 %collective-permute-start.14 = (f32[32,128]{1,0:T(8,128)S(1)}, f32[32,128]{1,0:T(8,128)S(1)}, u32[]{:S(2)}, u32[]{:S(2)}) collective-permute-start(f32[32,128]{1,0:T(8,128)S(1)} %get-tuple-element.88), channel_id=1, source_target_pairs={{0,2},{1,3},{2,0},{3,1},{4,6},{5,7},{6,4},{7,5},{8,10},{9,11},{10,... | collective-permute-start | bytes 49160 | tf_op jit(solution)/shard_map/ppermute | solution.py:750
  30.3 0.7 %collective-permute-start.16 = (f32[32,128]{1,0:T(8,128)S(1)}, f32[32,128]{1,0:T(8,128)S(1)}, u32[]{:S(2)}, u32[]{:S(2)}) collective-permute-start(f32[32,128]{1,0:T(8,128)S(1)} %get-tuple-element.90), channel_id=1, source_target_pairs={{0,1},{1,0},{2,3},{3,2},{4,5},{5,4},{6,7},{7,6},{8,9},{9,8},{10,11... | collective-permute-start | bytes 49160 | tf_op jit(solution)/shard_map/ppermute | solution.py:750
  31.0 0.5 %collective-permute-start.17 = (f32[32,128]{1,0:T(8,128)S(1)}, f32[32,128]{1,0:T(8,128)S(1)}, u32[]{:S(2)}, u32[]{:S(2)}) collective-permute-start(f32[32,128]{1,0:T(8,128)S(1)} %get-tuple-element.91.refs_6_), channel_id=1, source_target_pairs={{0,1},{1,0},{2,3},{3,2},{4,5},{5,4},{6,7},{7,6},{8,9},{9,8},{10,11... | collective-permute-start | bytes 49160 | tf_op jit(solution)/shard_map/ppermute | solution.py:750
  31.5 0.8 %copy.12 = f32[32,32,128]{2,1,0:T(8,128)} copy(f32[32,32,128]{2,1,0:T(8,128)S(1)} %get-tuple-element.96) | data formatting | bytes 1048576
  32.3 0.8 %copy.13 = f32[32,32,128]{2,1,0:T(8,128)} copy(f32[32,32,128]{2,1,0:T(8,128)S(1)} %get-tuple-element.97) | data formatting | bytes 1048576
  33.1 1.1 %last.1 = (f32[32,32,128]{2,1,0:T(8,128)}, f32[32,32,128]{2,1,0:T(8,128)}) custom-call(f32[2,32,128]{2,1,0:T(8,128)S(1)} %collective-permute-done.13.refs_0_, f32[32,128]{1,0:T(8,128)S(1)} %collective-permute-done.14.refs_1_, f32[32,128]{1,0:T(8,128)S(1)} %collective-permute-done.15.refs_2_, f32[32,128]{1,0:T(8,128)S(1)} %collective-permute-done.16.refs_3_, ...), custom_call_target="tpu_custom_call" | custom-call | flops 6946816 | bytes 3473408 | tf_op jit(solution)/shard_map/last/pallas_call | solution.py:731
  (31 shorter events, 0.7 us)
Async XLA Ops:
  3.4 10.7 %collective-permute-start = (f32[33,8,128]{2,1,0:T(8,128)S(1)}, f32[33,8,128]{2,1,0:T(8,128)S(1)}, u32[]{:S(2)}, u32[]{:S(2)}) collective-permute-start(f32[33,8,128]{2,1,0:T(8,128)S(1)} %get-tuple-element.60.rows_ref.srows_ref), channel_id=1, source_target_pairs={{0,16},{16,0},{1,17},{17,1},{2,18},{18,2},{3,19},{19,3},{4,20},{20... | collective-permute-start | bytes 405512 | tf_op jit(solution)/shard_map/ppermute | solution.py:750
  6.5 3.6 %collective-permute-start.3 = (f32[5,32,128]{2,1,0:T(8,128)S(1)}, f32[5,32,128]{2,1,0:T(8,128)S(1)}, u32[]{:S(2)}, u32[]{:S(2)}) collective-permute-start(f32[5,32,128]{2,1,0:T(8,128)S(1)} %get-tuple-element.63.stat_ref), channel_id=1, source_target_pairs={{0,1},{1,0},{2,3},{3,2},{4,5},{5,4},{6,7},{7,6},{8,9},{9,8},{10,11... | collective-permute-start | bytes 245768 | tf_op jit(solution)/shard_map/ppermute | solution.py:750
  6.5 7.5 %collective-permute-start.2 = (f32[3,32,128]{2,1,0:T(8,128)S(1)}, f32[3,32,128]{2,1,0:T(8,128)S(1)}, u32[]{:S(2)}, u32[]{:S(2)}) collective-permute-start(f32[3,32,128]{2,1,0:T(8,128)S(1)} %get-tuple-element.62.outer_ref.souter_ref), channel_id=1, source_target_pairs={{0,12},{4,8},{8,4},{12,0},{1,13},{5,9},{9,5},{13,1},{2,14},{6,10},... | collective-permute-start | bytes 147464 | tf_op jit(solution)/shard_map/ppermute | solution.py:750
  10.1 3.9 %collective-permute-start.1 = (f32[2,32,128]{2,1,0:T(8,128)S(1)}, f32[2,32,128]{2,1,0:T(8,128)S(1)}, u32[]{:S(2)}, u32[]{:S(2)}) collective-permute-start(f32[2,32,128]{2,1,0:T(8,128)S(1)} %get-tuple-element.61.inner_ref.sinner_ref), channel_id=1, source_target_pairs={{0,4},{4,0},{8,12},{12,8},{1,5},{5,1},{9,13},{13,9},{2,6},{6,2},{1... | collective-permute-start | bytes 98312 | tf_op jit(solution)/shard_map/ppermute | solution.py:750
  10.1 1.6 %copy-start = (f32[32,128]{1,0:T(8,128)S(1)}, f32[32,128]{1,0:T(8,128)}, u32[]{:S(2)}) copy-start(f32[32,128]{1,0:T(8,128)} %jac_ref.7) | copy-start | bytes 49156
  10.1 4.0 %collective-permute-start.4 = (f32[2,32,128]{2,1,0:T(8,128)S(1)}, f32[2,32,128]{2,1,0:T(8,128)S(1)}, u32[]{:S(2)}, u32[]{:S(2)}) collective-permute-start(f32[2,32,128]{2,1,0:T(8,128)S(1)} %get-tuple-element.65), channel_id=1, source_target_pairs={{0,2},{1,3},{2,0},{3,1},{4,6},{5,7},{6,4},{7,5},{8,10},{9,11},{10,... | collective-permute-start | bytes 98312 | tf_op jit(solution)/shard_map/ppermute | solution.py:750
  11.7 2.4 %copy-start.1 = (f32[32,32,128]{2,1,0:T(8,128)S(1)}, f32[32,32,128]{2,1,0:T(8,128)}, u32[]{:S(2)}) copy-start(f32[32,32,128]{2,1,0:T(8,128)} %wz_ref.1) | copy-start | bytes 1572868
  11.7 2.4 %copy-start.2 = (f32[32,128]{1,0:T(8,128)S(1)}, f32[32,128]{1,0:T(8,128)}, u32[]{:S(2)}) copy-start(f32[32,128]{1,0:T(8,128)} %sx_ref.3) | copy-start | bytes 49156
  11.7 2.4 %copy-start.3 = (f32[32,128]{1,0:T(8,128)S(1)}, f32[32,128]{1,0:T(8,128)}, u32[]{:S(2)}) copy-start(f32[32,128]{1,0:T(8,128)} %sy_ref.3) | copy-start | bytes 49156
  15.5 4.0 %collective-permute-start.5 = (f32[2,32,128]{2,1,0:T(8,128)S(1)}, f32[2,32,128]{2,1,0:T(8,128)S(1)}, u32[]{:S(2)}, u32[]{:S(2)}) collective-permute-start(f32[2,32,128]{2,1,0:T(8,128)S(1)} %get-tuple-element.66), channel_id=1, source_target_pairs={{0,3},{1,2},{2,1},{3,0},{4,7},{5,6},{6,5},{7,4},{8,11},{9,10},{10,... | collective-permute-start | bytes 98312 | tf_op jit(solution)/shard_map/ppermute | solution.py:750
  15.7 3.7 %collective-permute-start.6 = (f32[32,128]{1,0:T(8,128)S(1)}, f32[32,128]{1,0:T(8,128)S(1)}, u32[]{:S(2)}, u32[]{:S(2)}) collective-permute-start(f32[32,128]{1,0:T(8,128)S(1)} %get-tuple-element.67), channel_id=1, source_target_pairs={{0,2},{1,3},{2,0},{3,1},{4,6},{5,7},{6,4},{7,5},{8,10},{9,11},{10,... | collective-permute-start | bytes 49160 | tf_op jit(solution)/shard_map/ppermute | solution.py:750
  17.1 2.3 %collective-permute-start.8 = (f32[32,128]{1,0:T(8,128)S(1)}, f32[32,128]{1,0:T(8,128)S(1)}, u32[]{:S(2)}, u32[]{:S(2)}) collective-permute-start(f32[32,128]{1,0:T(8,128)S(1)} %get-tuple-element.69), channel_id=1, source_target_pairs={{0,1},{1,0},{2,3},{3,2},{4,5},{5,4},{6,7},{7,6},{8,9},{9,8},{10,11... | collective-permute-start | bytes 49160 | tf_op jit(solution)/shard_map/ppermute | solution.py:750
  17.4 2.1 %collective-permute-start.7 = (f32[32,128]{1,0:T(8,128)S(1)}, f32[32,128]{1,0:T(8,128)S(1)}, u32[]{:S(2)}, u32[]{:S(2)}) collective-permute-start(f32[32,128]{1,0:T(8,128)S(1)} %get-tuple-element.68.refs_5_), channel_id=1, source_target_pairs={{0,1},{1,0},{2,3},{3,2},{4,5},{5,4},{6,7},{7,6},{8,9},{9,8},{10,11... | collective-permute-start | bytes 49160 | tf_op jit(solution)/shard_map/ppermute | solution.py:750
  17.7 1.8 %collective-permute-start.9 = (f32[32,128]{1,0:T(8,128)S(1)}, f32[32,128]{1,0:T(8,128)S(1)}, u32[]{:S(2)}, u32[]{:S(2)}) collective-permute-start(f32[32,128]{1,0:T(8,128)S(1)} %get-tuple-element.70.refs_6_), channel_id=1, source_target_pairs={{0,1},{1,0},{2,3},{3,2},{4,5},{5,4},{6,7},{7,6},{8,9},{9,8},{10,11... | collective-permute-start | bytes 49160 | tf_op jit(solution)/shard_map/ppermute | solution.py:750
  20.8 6.9 %collective-permute-start.10 = (f32[32,8,128]{2,1,0:T(8,128)S(1)}, f32[32,8,128]{2,1,0:T(8,128)S(1)}, u32[]{:S(2)}, u32[]{:S(2)}) collective-permute-start(f32[32,8,128]{2,1,0:T(8,128)S(1)} %get-tuple-element.82.rows_ref), channel_id=1, source_target_pairs={{0,16},{16,0},{1,17},{17,1},{2,18},{18,2},{3,19},{19,3},{4,20},{20... | collective-permute-start | bytes 393224 | tf_op jit(solution)/shard_map/ppermute | solution.py:750
  21.3 6.3 %collective-permute-start.12 = (f32[2,32,128]{2,1,0:T(8,128)S(1)}, f32[2,32,128]{2,1,0:T(8,128)S(1)}, u32[]{:S(2)}, u32[]{:S(2)}) collective-permute-start(f32[2,32,128]{2,1,0:T(8,128)S(1)} %get-tuple-element.84.outer_ref), channel_id=1, source_target_pairs={{0,12},{4,8},{8,4},{12,0},{1,13},{5,9},{9,5},{13,1},{2,14},{6,10},... | collective-permute-start | bytes 98312 | tf_op jit(solution)/shard_map/ppermute | solution.py:750
  23.9 3.7 %collective-permute-start.11 = (f32[1,32,128]{2,1,0:T(8,128)S(1)}, f32[1,32,128]{2,1,0:T(8,128)S(1)}, u32[]{:S(2)}, u32[]{:S(2)}) collective-permute-start(f32[1,32,128]{2,1,0:T(8,128)S(1)} %get-tuple-element.83.inner_ref), channel_id=1, source_target_pairs={{0,4},{4,0},{8,12},{12,8},{1,5},{5,1},{9,13},{13,9},{2,6},{6,2},{1... | collective-permute-start | bytes 49160 | tf_op jit(solution)/shard_map/ppermute | solution.py:750
  29.0 4.1 %collective-permute-start.13 = (f32[2,32,128]{2,1,0:T(8,128)S(1)}, f32[2,32,128]{2,1,0:T(8,128)S(1)}, u32[]{:S(2)}, u32[]{:S(2)}) collective-permute-start(f32[2,32,128]{2,1,0:T(8,128)S(1)} %get-tuple-element.87), channel_id=1, source_target_pairs={{0,3},{1,2},{2,1},{3,0},{4,7},{5,6},{6,5},{7,4},{8,11},{9,10},{10,... | collective-permute-start | bytes 98312 | tf_op jit(solution)/shard_map/ppermute | solution.py:750
  29.1 3.9 %collective-permute-start.14 = (f32[32,128]{1,0:T(8,128)S(1)}, f32[32,128]{1,0:T(8,128)S(1)}, u32[]{:S(2)}, u32[]{:S(2)}) collective-permute-start(f32[32,128]{1,0:T(8,128)S(1)} %get-tuple-element.88), channel_id=1, source_target_pairs={{0,2},{1,3},{2,0},{3,1},{4,6},{5,7},{6,4},{7,5},{8,10},{9,11},{10,... | collective-permute-start | bytes 49160 | tf_op jit(solution)/shard_map/ppermute | solution.py:750
  30.3 2.8 %collective-permute-start.16 = (f32[32,128]{1,0:T(8,128)S(1)}, f32[32,128]{1,0:T(8,128)S(1)}, u32[]{:S(2)}, u32[]{:S(2)}) collective-permute-start(f32[32,128]{1,0:T(8,128)S(1)} %get-tuple-element.90), channel_id=1, source_target_pairs={{0,1},{1,0},{2,3},{3,2},{4,5},{5,4},{6,7},{7,6},{8,9},{9,8},{10,11... | collective-permute-start | bytes 49160 | tf_op jit(solution)/shard_map/ppermute | solution.py:750
  31.0 2.1 %collective-permute-start.15 = (f32[32,128]{1,0:T(8,128)S(1)}, f32[32,128]{1,0:T(8,128)S(1)}, u32[]{:S(2)}, u32[]{:S(2)}) collective-permute-start(f32[32,128]{1,0:T(8,128)S(1)} %get-tuple-element.89.refs_5_), channel_id=1, source_target_pairs={{0,1},{1,0},{2,3},{3,2},{4,5},{5,4},{6,7},{7,6},{8,9},{9,8},{10,11... | collective-permute-start | bytes 49160 | tf_op jit(solution)/shard_map/ppermute | solution.py:750
  31.0 2.1 %collective-permute-start.17 = (f32[32,128]{1,0:T(8,128)S(1)}, f32[32,128]{1,0:T(8,128)S(1)}, u32[]{:S(2)}, u32[]{:S(2)}) collective-permute-start(f32[32,128]{1,0:T(8,128)S(1)} %get-tuple-element.91.refs_6_), channel_id=1, source_target_pairs={{0,1},{1,0},{2,3},{3,2},{4,5},{5,4},{6,7},{7,6},{8,9},{9,8},{10,11... | collective-permute-start | bytes 49160 | tf_op jit(solution)/shard_map/ppermute | solution.py:750

commit v11 on v10

--- a/solution.py
+++ b/solution.py
@@ -144,11 +144,11 @@
         out = jnp.where(lane < SLOT, tile, 0.0)
     else:
         out = pltpu.roll(jnp.where(lane >= 128 - SLOT, tile, 0.0), SLOT, 1)
-    by = SLOT
-    while by < 128:
-        out = out + pltpu.roll(out, by, 1)
-        by *= 2
-    return out
+    for by in (SLOT, 4 * SLOT):
+        out = (out + pltpu.roll(out, by, 1)) + (
+            pltpu.roll(out, 2 * by, 1) + pltpu.roll(out, 3 * by, 1)
+        )
+    return out + pltpu.roll(out, 64, 1)
 
 
 class Packer:
@@ -212,12 +212,8 @@
 
 def lane_payload(pres, wind, jac):
     low, high = lane_edge(LOW), lane_edge(HIGH)
-    down = [
-        low.payload(p, w, spread_slots(j, True)) for p, w, j in zip(pres[0], wind[0], jac)
-    ]
-    up = [
-        high.payload(p, w, spread_slots(j, False)) for p, w, j in zip(pres[1], wind[1], jac)
-    ]
+    down = [low.payload(p, w, j) for p, w, j in zip(pres[0], wind[0], jac[0])]
+    up = [high.payload(p, w, j) for p, w, j in zip(pres[1], wind[1], jac[1])]
     return down, up
 
 
@@ -343,15 +339,10 @@
 
     lax.fori_loop(0, levels, step, 0, unroll=UNROLL)
     rows_ref[levels] = ends
-    down_out, up_out = lane_payload(pres, wind, jac)
+    slots = [[spread_slots(j, low) for j in jac] for low in (True, False)]
+    put_pair(inner_ref, outer_ref, 1, *slots)
+    down_out, up_out = lane_payload(pres, wind, slots)
     put_pair(inner_ref, outer_ref, 0, down_out, up_out)
-    put_pair(
-        inner_ref,
-        outer_ref,
-        1,
-        [spread_slots(j, True) for j in jac],
-        [spread_slots(j, False) for j in jac],
-    )
     put_tiles(pp_ref, 0, pres[0])
     put_tiles(pp_ref, 1, pres[1])
 
@@ -661,12 +652,14 @@
 
 def kernel_c(*refs):
     column_refs = refs[:COLUMN]
-    y_ref, q_ref, i_ref, ps_ref, wx_ref, pw_ref, jac_ref = refs[COLUMN : COLUMN + 7]
-    x_ref, p_ref, rows_ref, inner_ref, outer_ref, pp_ref = refs[COLUMN + 7 :]
+    y_ref, q_ref, i_ref, ps_ref, wx_ref, pw_ref, srows_ref, sinner_ref, souter_ref = refs[
+        COLUMN : COLUMN + 9
+    ]
+    x_ref, p_ref, rows_ref, inner_ref, outer_ref, pp_ref = refs[COLUMN + 9 :]
     levels, rows, _ = y_ref.shape
     count = rows // ROWS
     edge = row_edge()
-    ends = both_ends(planes_of(jac_ref, count))
+    ends = srows_ref[levels]
     finish(count, levels, y_ref, q_ref, i_ref, ps_ref, x_ref, p_ref, column_refs)
 
     def step(level, state):
@@ -680,7 +673,13 @@
     lax.fori_loop(0, levels, step, 0, unroll=UNROLL)
     pres = pack_levels(p_ref, count, levels)
     wind = tiles_of(pw_ref, 0, count), tiles_of(pw_ref, 1, count)
-    down, up = lane_payload(pres, wind, planes_of(jac_ref, count))
+    slots = zip(
+        *(
+            get_pair(sinner_ref, souter_ref, 1, slice(ROWS * t, ROWS * (t + 1)))
+            for t in range(count)
+        )
+    )
+    down, up = lane_payload(pres, wind, list(slots))
     put_pair(inner_ref, outer_ref, 0, down, up)
     put_tiles(pp_ref, 0, pres[0])
     put_tiles(pp_ref, 1, pres[1])
@@ -688,10 +687,17 @@
 
 def kernel_d(*refs):
     column_refs = refs[:COLUMN]
-    y_ref, q_ref, i_ref, ps_ref = refs[COLUMN : COLUMN + 4]
-    x_hbm, p_hbm, x_ref, p_ref, sems = refs[COLUMN + 4 :]
+    y_ref, q_ref, i_ref, ps_ref, nx_ref, ny_ref = refs[COLUMN : COLUMN + 6]
+    nx_hbm, ny_hbm, x_hbm, p_hbm, x_ref, p_ref, sems = refs[COLUMN + 6 :]
     levels, rows, _ = y_ref.shape
     share = levels // CHUNKS
+
+    winds = [
+        pltpu.make_async_copy(source, target, sems.at[2, k])
+        for k, (source, target) in enumerate(((nx_ref, nx_hbm), (ny_ref, ny_hbm)))
+    ]
+    for wind in winds:
+        wind.start()
 
     def copy(index, source, target, c):
         part = pl.ds(c * share, share)
@@ -721,6 +727,8 @@
     for c in range(CHUNKS):
         copy(0, x_ref, x_hbm, c).wait()
         copy(1, p_ref, p_hbm, c).wait()
+    for wind in winds:
+        wind.wait()
 
 
 def call(kernel, name, shapes, *args, far_in=(), far_out=False, scratch=(), keep=()):
@@ -847,25 +855,27 @@
                 star,
                 wind_x,
                 packed,
-                jacobian,
+                *static_edges[:3],
             )
             sent = (edge, inner, outer)
             got = (exchange_rows(edge),) + exchange_lanes(inner, outer)
         else:
-            wind_z, pressure = call(
+            wind_x, wind_y, wind_z, pressure = call(
                 kernel_d,
                 "last",
-                [field, field],
+                [field] * 4,
                 *column,
                 value,
                 prod,
                 inv,
                 star,
+                wind_x,
+                wind_y,
                 far_out=True,
                 scratch=[
                     pltpu.VMEM(field, jnp.float32),
                     pltpu.VMEM(field, jnp.float32),
-                    pltpu.SemaphoreType.DMA((2, CHUNKS)),
+                    pltpu.SemaphoreType.DMA((3, CHUNKS)),
                 ],
             )
     return wind_x, wind_y, wind_z, pressure

time: 34.4 us -> 34.2 us (level)
  local copies, waits for them, and re-layouts: 1.6 us -> 0.01 us
  waiting for transfers between devices: 4.4 us -> 5.85 us
    unnamed x10 -> x8, local copies, waits for them, and re-layouts: 1.6 us -> 0.01 us
    ppermute x18, waiting for transfers between devices: 4.4 us -> 5.85 us  [swap(): return lax.ppermute(value, axis, [(i, partner(i)) for i in range(count)])]
  transfers between devices with their start and end apart: 18 -> 18, of which waited for: 4 -> 5; matrix products, arithmetic and copies ran while one was open for 5% -> 0% of each run, Pallas kernels for 10% -> 10%
where the time goes in v11:
time: 34.2 us; the launch traced here: 34 us
  starting transfers between devices  16.2 us (47%)
  Pallas kernels  11.2 us (33%)
  waiting for transfers between devices  5.85 us (17%)
  between operations  0.74 us (2%)
    ppermute x18, starting transfers between devices, swap(): return lax.ppermute(value, axis, [(i, partner(i)) for i in range(count)])  16.2 us
    pallas_call x9, Pallas kernels, call(): pl.pallas_call(kernel, out_shape=[pltpu.VMEM(s, jnp.float32) if k in keep...  11.2 us
    ppermute x18, waiting for transfers between devices, swap(): return lax.ppermute(value, axis, [(i, partner(i)) for i in range(count)])  5.85 us
  transfers between devices with their start and end apart: 18, of which 5 were waited for; matrix products, arithmetic and copies ran while one was open for 0% of the time, Pallas kernels for 10%

profile of v11, /device:TPU:0, one launch (start us, length us, event | category | flops | bytes accessed | tf_op | source)
XLA Modules:
  0.0 34.0 jit_solution(1301814065734096740)
XLA Ops:
  0.6 2.7 %start.1 = (f32[33,8,128]{2,1,0:T(8,128)S(1)}, f32[2,32,128]{2,1,0:T(8,128)S(1)}, f32[3,32,128]{2,1,0:T(8,128)S(1)}, f32[2,32,128]{2,1,0:T(8,128)S(1)}, f32[32,3...) custom-call(f32[32,32,128]{2,1,0:T(8,128)} %p_hbm.1, ...), custom_call_target="tpu_custom_call" | custom-call | flops 12230656 | bytes 6115328 | tf_op jit(solution)/shard_map/start/pallas_call | solution.py:739
  3.3 3.0 %collective-permute-start = (f32[33,8,128]{2,1,0:T(8,128)S(1)}, f32[33,8,128]{2,1,0:T(8,128)S(1)}, u32[]{:S(2)}, u32[]{:S(2)}) collective-permute-start(f32[33,8,128]{2,1,0:T(8,128)S(1)} %get-tuple-element.58.rows_ref.srows_ref.refs_15_), channel_id=1, source_target_pairs={{0,16},{16,0},{1,17},{17,1},{2,18},{18,2},{3,19},{19,3},{4,20},{20... | collective-permute-start | bytes 405512 | tf_op jit(solution)/shard_map/ppermute | solution.py:758
  6.4 3.6 %collective-permute-start.2 = (f32[3,32,128]{2,1,0:T(8,128)S(1)}, f32[3,32,128]{2,1,0:T(8,128)S(1)}, u32[]{:S(2)}, u32[]{:S(2)}) collective-permute-start(f32[3,32,128]{2,1,0:T(8,128)S(1)} %get-tuple-element.60.outer_ref.souter_ref.refs_17_), channel_id=1, source_target_pairs={{0,12},{4,8},{8,4},{12,0},{1,13},{5,9},{9,5},{13,1},{2,14},{6,10},... | collective-permute-start | bytes 147464 | tf_op jit(solution)/shard_map/ppermute | solution.py:758
  10.0 1.6 %collective-permute-start.4 = (f32[2,32,128]{2,1,0:T(8,128)S(1)}, f32[2,32,128]{2,1,0:T(8,128)S(1)}, u32[]{:S(2)}, u32[]{:S(2)}) collective-permute-start(f32[2,32,128]{2,1,0:T(8,128)S(1)} %get-tuple-element.63), channel_id=1, source_target_pairs={{0,2},{1,3},{2,0},{3,1},{4,6},{5,7},{6,4},{7,5},{8,10},{9,11},{10,... | collective-permute-start | bytes 98312 | tf_op jit(solution)/shard_map/ppermute | solution.py:758
  11.6 1.4 %interior.2 = (f32[32,32,128]{2,1,0:T(8,128)S(1)}, f32[32,32,128]{2,1,0:T(8,128)S(1)}, f32[32,32,128]{2,1,0:T(8,128)S(1)}) custom-call(f32[32,32,128]{2,1,0:T(8,128)S(1)} %get-tuple-element.48.p_ref, f32[32,32,128]{2,1,0:T(8,128)S(1)} %get-tuple-element.49.wx_ref, f32[32,32,128]{2,1,0:T(8,128)S(1)} %get-tuple-element.50.wy_ref, f32[32,128]{1,0:T(8,128)S(1)} %copy-done.1), custom_call_target="tpu_custom_call" | custom-call | flops 6324224 | bytes 3162112 | tf_op jit(solution)/shard_map/interior/pallas_call | solution.py:739
  13.0 0.9 %collective-permute-done.1.got_inner_ref.got_sinner_ref = f32[2,32,128]{2,1,0:T(8,128)S(1)} collective-permute-done((f32[2,32,128]{2,1,0:T(8,128)S(1)}, f32[2,32,128]{2,1,0:T(8,128)S(1)}, u32[]{:S(2)}, u32[]{:S(2)}) %collective-permute-start.1) | collective-permute-done | bytes 32800 | tf_op jit(solution)/shard_map/ppermute | solution.py:758
  14.0 1.4 %sweep.2 = (f32[32,32,128]{2,1,0:T(8,128)S(1)}, f32[32,32,128]{2,1,0:T(8,128)S(1)}, f32[32,32,128]{2,1,0:T(8,128)S(1)}, f32[32,32,128]{2,1,0:T(8,128)S(1)}, f32[...) custom-call(f32[32,32,128]{2,1,0:T(8,128)S(1)} %get-tuple-element.48, ...), custom_call_target="tpu_custom_call" | custom-call | flops 15073280 | bytes 7536640 | tf_op jit(solution)/shard_map/sweep/pallas_call | solution.py:739
  15.4 0.2 collective-permute-start.5
  15.6 1.4 %collective-permute-start.6 = (f32[32,128]{1,0:T(8,128)S(1)}, f32[32,128]{1,0:T(8,128)S(1)}, u32[]{:S(2)}, u32[]{:S(2)}) collective-permute-start(f32[32,128]{1,0:T(8,128)S(1)} %get-tuple-element.65), channel_id=1, source_target_pairs={{0,2},{1,3},{2,0},{3,1},{4,6},{5,7},{6,4},{7,5},{8,10},{9,11},{10,... | collective-permute-start | bytes 49160 | tf_op jit(solution)/shard_map/ppermute | solution.py:758
  17.0 0.3 collective-permute-start.8
  17.5 0.3 collective-permute-start.9
  17.8 0.5 %pack.1.refs_14_ = f32[2,32,128]{2,1,0:T(8,128)S(1)} custom-call(f32[32,32,128]{2,1,0:T(8,128)S(1)} %get-tuple-element.73.wy_ref), custom_call_target="tpu_custom_call" | custom-call | flops 1114112 | bytes 557056 | tf_op jit(solution)/shard_map/pack/pallas_call | solution.py:739
  18.3 1.1 %collective-permute-done.6.refs_1_ = f32[32,128]{1,0:T(8,128)S(1)} collective-permute-done((f32[32,128]{1,0:T(8,128)S(1)}, f32[32,128]{1,0:T(8,128)S(1)}, u32[]{:S(2)}, u32[]{:S(2)}) %collective-permute-start.6) | collective-permute-done | bytes 16416 | tf_op jit(solution)/shard_map/ppermute | solution.py:758
  19.4 1.0 %finish.1 = (f32[32,32,128]{2,1,0:T(8,128)S(1)}, f32[32,32,128]{2,1,0:T(8,128)S(1)}, f32[32,8,128]{2,1,0:T(8,128)S(1)}, f32[1,32,128]{2,1,0:T(8,128)S(1)}, f32[2...) custom-call(f32[2,32,128]{2,1,0:T(8,128)S(1)} %collective-permute-done.5.refs_0_, ...), custom_call_target="tpu_custom_call" | custom-call | flops 8921088 | bytes 4460544 | tf_op jit(solution)/shard_map/finish/pallas_call | solution.py:739
  20.4 0.5 %collective-permute-start.10 = (f32[32,8,128]{2,1,0:T(8,128)S(1)}, f32[32,8,128]{2,1,0:T(8,128)S(1)}, u32[]{:S(2)}, u32[]{:S(2)}) collective-permute-start(f32[32,8,128]{2,1,0:T(8,128)S(1)} %get-tuple-element.80.rows_ref), channel_id=1, source_target_pairs={{0,16},{16,0},{1,17},{17,1},{2,18},{18,2},{3,19},{19,3},{4,20},{20... | collective-permute-start | bytes 393224 | tf_op jit(solution)/shard_map/ppermute | solution.py:758
  20.9 2.6 %collective-permute-start.12 = (f32[2,32,128]{2,1,0:T(8,128)S(1)}, f32[2,32,128]{2,1,0:T(8,128)S(1)}, u32[]{:S(2)}, u32[]{:S(2)}) collective-permute-start(f32[2,32,128]{2,1,0:T(8,128)S(1)} %get-tuple-element.82.outer_ref), channel_id=1, source_target_pairs={{0,12},{4,8},{8,4},{12,0},{1,13},{5,9},{9,5},{13,1},{2,14},{6,10},... | collective-permute-start | bytes 98312 | tf_op jit(solution)/shard_map/ppermute | solution.py:758
  23.5 1.4 %interior.3 = (f32[32,32,128]{2,1,0:T(8,128)S(1)}, f32[32,32,128]{2,1,0:T(8,128)S(1)}, f32[32,32,128]{2,1,0:T(8,128)S(1)}) custom-call(f32[32,32,128]{2,1,0:T(8,128)S(1)} %get-tuple-element.74.p_ref, f32[32,32,128]{2,1,0:T(8,128)S(1)} %get-tuple-element.72.refs_13_.wx_ref, f32[32,32,128]{2,1,0:T(8,128)S(1)} %get-tuple-element.73.wy_ref, f32[32,128]{1,0:T(8,128)S(1)} %copy-done.1), custom_call_target="tpu_custom_call" | custom-call | flops 6324224 | bytes 3162112 | tf_op jit(solution)/shard_map/interior/pallas_call | solution.py:739
  25.0 2.3 %collective-permute-done.11.got_inner_ref = f32[1,32,128]{2,1,0:T(8,128)S(1)} collective-permute-done((f32[1,32,128]{2,1,0:T(8,128)S(1)}, f32[1,32,128]{2,1,0:T(8,128)S(1)}, u32[]{:S(2)}, u32[]{:S(2)}) %collective-permute-start.11) | collective-permute-done | bytes 16416 | tf_op jit(solution)/shard_map/ppermute | solution.py:758
  27.3 1.4 %sweep.3 = (f32[32,32,128]{2,1,0:T(8,128)S(1)}, f32[32,32,128]{2,1,0:T(8,128)S(1)}, f32[32,32,128]{2,1,0:T(8,128)S(1)}, f32[32,32,128]{2,1,0:T(8,128)S(1)}, f32[...) custom-call(f32[32,32,128]{2,1,0:T(8,128)S(1)} %get-tuple-element.74, ...), custom_call_target="tpu_custom_call" | custom-call | flops 14925824 | bytes 7462912 | tf_op jit(solution)/shard_map/sweep/pallas_call | solution.py:739
  28.7 1.2 %collective-permute-start.14 = (f32[32,128]{1,0:T(8,128)S(1)}, f32[32,128]{1,0:T(8,128)S(1)}, u32[]{:S(2)}, u32[]{:S(2)}) collective-permute-start(f32[32,128]{1,0:T(8,128)S(1)} %get-tuple-element.84), channel_id=1, source_target_pairs={{0,2},{1,3},{2,0},{3,1},{4,6},{5,7},{6,4},{7,5},{8,10},{9,11},{10,... | collective-permute-start | bytes 49160 | tf_op jit(solution)/shard_map/ppermute | solution.py:758
  29.9 0.7 %collective-permute-start.16 = (f32[32,128]{1,0:T(8,128)S(1)}, f32[32,128]{1,0:T(8,128)S(1)}, u32[]{:S(2)}, u32[]{:S(2)}) collective-permute-start(f32[32,128]{1,0:T(8,128)S(1)} %get-tuple-element.86), channel_id=1, source_target_pairs={{0,1},{1,0},{2,3},{3,2},{4,5},{5,4},{6,7},{7,6},{8,9},{9,8},{10,11... | collective-permute-start | bytes 49160 | tf_op jit(solution)/shard_map/ppermute | solution.py:758
  30.6 0.5 %collective-permute-start.17 = (f32[32,128]{1,0:T(8,128)S(1)}, f32[32,128]{1,0:T(8,128)S(1)}, u32[]{:S(2)}, u32[]{:S(2)}) collective-permute-start(f32[32,128]{1,0:T(8,128)S(1)} %get-tuple-element.87.refs_6_), channel_id=1, source_target_pairs={{0,1},{1,0},{2,3},{3,2},{4,5},{5,4},{6,7},{7,6},{8,9},{9,8},{10,11... | collective-permute-start | bytes 49160 | tf_op jit(solution)/shard_map/ppermute | solution.py:758
  31.1 1.5 %collective-permute-done.14.refs_1_ = f32[32,128]{1,0:T(8,128)S(1)} collective-permute-done((f32[32,128]{1,0:T(8,128)S(1)}, f32[32,128]{1,0:T(8,128)S(1)}, u32[]{:S(2)}, u32[]{:S(2)}) %collective-permute-start.14) | collective-permute-done | bytes 16416 | tf_op jit(solution)/shard_map/ppermute | solution.py:758
  32.6 1.4 %last.1 = (f32[32,32,128]{2,1,0:T(8,128)}, f32[32,32,128]{2,1,0:T(8,128)}, f32[32,32,128]{2,1,0:T(8,128)}, f32[32,32,128]{2,1,0:T(8,128)}) custom-call(f32[2,32,128]{2,1,0:T(8,128)S(1)} %collective-permute-done.13.refs_0_, f32[32,128]{1,0:T(8,128)S(1)} %collective-permute-done.14.refs_1_, f32[32,128]{1,0:T(8,128)S(1)} %collective-permute-done.15.refs_2_, ...), custom_call_target="tpu_custom_call" | custom-call | flops 11141120 | bytes 5570560 | tf_op jit(solution)/shard_map/last/pallas_call | solution.py:739
  (29 shorter events, 0.5 us)
Async XLA Ops:
  3.3 10.7 %collective-permute-start = (f32[33,8,128]{2,1,0:T(8,128)S(1)}, f32[33,8,128]{2,1,0:T(8,128)S(1)}, u32[]{:S(2)}, u32[]{:S(2)}) collective-permute-start(f32[33,8,128]{2,1,0:T(8,128)S(1)} %get-tuple-element.58.rows_ref.srows_ref.refs_15_), channel_id=1, source_target_pairs={{0,16},{16,0},{1,17},{17,1},{2,18},{18,2},{3,19},{19,3},{4,20},{20... | collective-permute-start | bytes 405512 | tf_op jit(solution)/shard_map/ppermute | solution.py:758
  6.3 3.6 %collective-permute-start.3 = (f32[5,32,128]{2,1,0:T(8,128)S(1)}, f32[5,32,128]{2,1,0:T(8,128)S(1)}, u32[]{:S(2)}, u32[]{:S(2)}) collective-permute-start(f32[5,32,128]{2,1,0:T(8,128)S(1)} %get-tuple-element.61.stat_ref), channel_id=1, source_target_pairs={{0,1},{1,0},{2,3},{3,2},{4,5},{5,4},{6,7},{7,6},{8,9},{9,8},{10,11... | collective-permute-start | bytes 245768 | tf_op jit(solution)/shard_map/ppermute | solution.py:758
  6.4 7.5 %collective-permute-start.2 = (f32[3,32,128]{2,1,0:T(8,128)S(1)}, f32[3,32,128]{2,1,0:T(8,128)S(1)}, u32[]{:S(2)}, u32[]{:S(2)}) collective-permute-start(f32[3,32,128]{2,1,0:T(8,128)S(1)} %get-tuple-element.60.outer_ref.souter_ref.refs_17_), channel_id=1, source_target_pairs={{0,12},{4,8},{8,4},{12,0},{1,13},{5,9},{9,5},{13,1},{2,14},{6,10},... | collective-permute-start | bytes 147464 | tf_op jit(solution)/shard_map/ppermute | solution.py:758
  10.0 3.9 %collective-permute-start.1 = (f32[2,32,128]{2,1,0:T(8,128)S(1)}, f32[2,32,128]{2,1,0:T(8,128)S(1)}, u32[]{:S(2)}, u32[]{:S(2)}) collective-permute-start(f32[2,32,128]{2,1,0:T(8,128)S(1)} %get-tuple-element.59.inner_ref.sinner_ref.refs_16_), channel_id=1, source_target_pairs={{0,4},{4,0},{8,12},{12,8},{1,5},{5,1},{9,13},{13,9},{2,6},{6,2},{1... | collective-permute-start | bytes 98312 | tf_op jit(solution)/shard_map/ppermute | solution.py:758
  10.0 1.6 %copy-start.1 = (f32[32,128]{1,0:T(8,128)S(1)}, f32[32,128]{1,0:T(8,128)}, u32[]{:S(2)}) copy-start(f32[32,128]{1,0:T(8,128)} %jac_ref.7) | copy-start | bytes 49156
  10.0 4.0 %collective-permute-start.4 = (f32[2,32,128]{2,1,0:T(8,128)S(1)}, f32[2,32,128]{2,1,0:T(8,128)S(1)}, u32[]{:S(2)}, u32[]{:S(2)}) collective-permute-start(f32[2,32,128]{2,1,0:T(8,128)S(1)} %get-tuple-element.63), channel_id=1, source_target_pairs={{0,2},{1,3},{2,0},{3,1},{4,6},{5,7},{6,4},{7,5},{8,10},{9,11},{10,... | collective-permute-start | bytes 98312 | tf_op jit(solution)/shard_map/ppermute | solution.py:758
  11.6 2.4 %copy-start = (f32[32,32,128]{2,1,0:T(8,128)S(1)}, f32[32,32,128]{2,1,0:T(8,128)}, u32[]{:S(2)}) copy-start(f32[32,32,128]{2,1,0:T(8,128)} %wz_ref.1) | copy-start | bytes 1572868
  11.6 2.4 %copy-start.2 = (f32[32,128]{1,0:T(8,128)S(1)}, f32[32,128]{1,0:T(8,128)}, u32[]{:S(2)}) copy-start(f32[32,128]{1,0:T(8,128)} %sx_ref.3) | copy-start | bytes 49156
  11.6 2.4 %copy-start.3 = (f32[32,128]{1,0:T(8,128)S(1)}, f32[32,128]{1,0:T(8,128)}, u32[]{:S(2)}) copy-start(f32[32,128]{1,0:T(8,128)} %sy_ref.3) | copy-start | bytes 49156
  15.4 4.0 %collective-permute-start.5 = (f32[2,32,128]{2,1,0:T(8,128)S(1)}, f32[2,32,128]{2,1,0:T(8,128)S(1)}, u32[]{:S(2)}, u32[]{:S(2)}) collective-permute-start(f32[2,32,128]{2,1,0:T(8,128)S(1)} %get-tuple-element.64), channel_id=1, source_target_pairs={{0,3},{1,2},{2,1},{3,0},{4,7},{5,6},{6,5},{7,4},{8,11},{9,10},{10,... | collective-permute-start | bytes 98312 | tf_op jit(solution)/shard_map/ppermute | solution.py:758
  15.6 3.7 %collective-permute-start.6 = (f32[32,128]{1,0:T(8,128)S(1)}, f32[32,128]{1,0:T(8,128)S(1)}, u32[]{:S(2)}, u32[]{:S(2)}) collective-permute-start(f32[32,128]{1,0:T(8,128)S(1)} %get-tuple-element.65), channel_id=1, source_target_pairs={{0,2},{1,3},{2,0},{3,1},{4,6},{5,7},{6,4},{7,5},{8,10},{9,11},{10,... | collective-permute-start | bytes 49160 | tf_op jit(solution)/shard_map/ppermute | solution.py:758
  17.0 2.3 %collective-permute-start.8 = (f32[32,128]{1,0:T(8,128)S(1)}, f32[32,128]{1,0:T(8,128)S(1)}, u32[]{:S(2)}, u32[]{:S(2)}) collective-permute-start(f32[32,128]{1,0:T(8,128)S(1)} %get-tuple-element.67), channel_id=1, source_target_pairs={{0,1},{1,0},{2,3},{3,2},{4,5},{5,4},{6,7},{7,6},{8,9},{9,8},{10,11... | collective-permute-start | bytes 49160 | tf_op jit(solution)/shard_map/ppermute | solution.py:758
  17.3 2.1 %collective-permute-start.7 = (f32[32,128]{1,0:T(8,128)S(1)}, f32[32,128]{1,0:T(8,128)S(1)}, u32[]{:S(2)}, u32[]{:S(2)}) collective-permute-start(f32[32,128]{1,0:T(8,128)S(1)} %get-tuple-element.66.refs_5_), channel_id=1, source_target_pairs={{0,1},{1,0},{2,3},{3,2},{4,5},{5,4},{6,7},{7,6},{8,9},{9,8},{10,11... | collective-permute-start | bytes 49160 | tf_op jit(solution)/shard_map/ppermute | solution.py:758
  17.5 1.8 %collective-permute-start.9 = (f32[32,128]{1,0:T(8,128)S(1)}, f32[32,128]{1,0:T(8,128)S(1)}, u32[]{:S(2)}, u32[]{:S(2)}) collective-permute-start(f32[32,128]{1,0:T(8,128)S(1)} %get-tuple-element.68.refs_6_), channel_id=1, source_target_pairs={{0,1},{1,0},{2,3},{3,2},{4,5},{5,4},{6,7},{7,6},{8,9},{9,8},{10,11... | collective-permute-start | bytes 49160 | tf_op jit(solution)/shard_map/ppermute | solution.py:758
  20.4 6.9 %collective-permute-start.10 = (f32[32,8,128]{2,1,0:T(8,128)S(1)}, f32[32,8,128]{2,1,0:T(8,128)S(1)}, u32[]{:S(2)}, u32[]{:S(2)}) collective-permute-start(f32[32,8,128]{2,1,0:T(8,128)S(1)} %get-tuple-element.80.rows_ref), channel_id=1, source_target_pairs={{0,16},{16,0},{1,17},{17,1},{2,18},{18,2},{3,19},{19,3},{4,20},{20... | collective-permute-start | bytes 393224 | tf_op jit(solution)/shard_map/ppermute | solution.py:758
  20.9 6.3 %collective-permute-start.12 = (f32[2,32,128]{2,1,0:T(8,128)S(1)}, f32[2,32,128]{2,1,0:T(8,128)S(1)}, u32[]{:S(2)}, u32[]{:S(2)}) collective-permute-start(f32[2,32,128]{2,1,0:T(8,128)S(1)} %get-tuple-element.82.outer_ref), channel_id=1, source_target_pairs={{0,12},{4,8},{8,4},{12,0},{1,13},{5,9},{9,5},{13,1},{2,14},{6,10},... | collective-permute-start | bytes 98312 | tf_op jit(solution)/shard_map/ppermute | solution.py:758
  23.5 3.7 %collective-permute-start.11 = (f32[1,32,128]{2,1,0:T(8,128)S(1)}, f32[1,32,128]{2,1,0:T(8,128)S(1)}, u32[]{:S(2)}, u32[]{:S(2)}) collective-permute-start(f32[1,32,128]{2,1,0:T(8,128)S(1)} %get-tuple-element.81.inner_ref), channel_id=1, source_target_pairs={{0,4},{4,0},{8,12},{12,8},{1,5},{5,1},{9,13},{13,9},{2,6},{6,2},{1... | collective-permute-start | bytes 49160 | tf_op jit(solution)/shard_map/ppermute | solution.py:758
  28.6 3.9 %collective-permute-start.13 = (f32[2,32,128]{2,1,0:T(8,128)S(1)}, f32[2,32,128]{2,1,0:T(8,128)S(1)}, u32[]{:S(2)}, u32[]{:S(2)}) collective-permute-start(f32[2,32,128]{2,1,0:T(8,128)S(1)} %get-tuple-element.83), channel_id=1, source_target_pairs={{0,3},{1,2},{2,1},{3,0},{4,7},{5,6},{6,5},{7,4},{8,11},{9,10},{10,... | collective-permute-start | bytes 98312 | tf_op jit(solution)/shard_map/ppermute | solution.py:758
  28.7 3.8 %collective-permute-start.14 = (f32[32,128]{1,0:T(8,128)S(1)}, f32[32,128]{1,0:T(8,128)S(1)}, u32[]{:S(2)}, u32[]{:S(2)}) collective-permute-start(f32[32,128]{1,0:T(8,128)S(1)} %get-tuple-element.84), channel_id=1, source_target_pairs={{0,2},{1,3},{2,0},{3,1},{4,6},{5,7},{6,4},{7,5},{8,10},{9,11},{10,... | collective-permute-start | bytes 49160 | tf_op jit(solution)/shard_map/ppermute | solution.py:758
  29.9 2.7 %collective-permute-start.16 = (f32[32,128]{1,0:T(8,128)S(1)}, f32[32,128]{1,0:T(8,128)S(1)}, u32[]{:S(2)}, u32[]{:S(2)}) collective-permute-start(f32[32,128]{1,0:T(8,128)S(1)} %get-tuple-element.86), channel_id=1, source_target_pairs={{0,1},{1,0},{2,3},{3,2},{4,5},{5,4},{6,7},{7,6},{8,9},{9,8},{10,11... | collective-permute-start | bytes 49160 | tf_op jit(solution)/shard_map/ppermute | solution.py:758
  30.6 2.0 %collective-permute-start.15 = (f32[32,128]{1,0:T(8,128)S(1)}, f32[32,128]{1,0:T(8,128)S(1)}, u32[]{:S(2)}, u32[]{:S(2)}) collective-permute-start(f32[32,128]{1,0:T(8,128)S(1)} %get-tuple-element.85.refs_5_), channel_id=1, source_target_pairs={{0,1},{1,0},{2,3},{3,2},{4,5},{5,4},{6,7},{7,6},{8,9},{9,8},{10,11... | collective-permute-start | bytes 49160 | tf_op jit(solution)/shard_map/ppermute | solution.py:758
  30.6 2.0 %collective-permute-start.17 = (f32[32,128]{1,0:T(8,128)S(1)}, f32[32,128]{1,0:T(8,128)S(1)}, u32[]{:S(2)}, u32[]{:S(2)}) collective-permute-start(f32[32,128]{1,0:T(8,128)S(1)} %get-tuple-element.87.refs_6_), channel_id=1, source_target_pairs={{0,1},{1,0},{2,3},{3,2},{4,5},{5,4},{6,7},{7,6},{8,9},{9,8},{10,11... | collective-permute-start | bytes 49160 | tf_op jit(solution)/shard_map/ppermute | solution.py:758

commit v12 on v11

--- a/solution.py
+++ b/solution.py
@@ -687,17 +687,10 @@
 
 def kernel_d(*refs):
     column_refs = refs[:COLUMN]
-    y_ref, q_ref, i_ref, ps_ref, nx_ref, ny_ref = refs[COLUMN : COLUMN + 6]
-    nx_hbm, ny_hbm, x_hbm, p_hbm, x_ref, p_ref, sems = refs[COLUMN + 6 :]
+    y_ref, q_ref, i_ref, ps_ref = refs[COLUMN : COLUMN + 4]
+    x_hbm, p_hbm, x_ref, p_ref, sems = refs[COLUMN + 4 :]
     levels, rows, _ = y_ref.shape
     share = levels // CHUNKS
-
-    winds = [
-        pltpu.make_async_copy(source, target, sems.at[2, k])
-        for k, (source, target) in enumerate(((nx_ref, nx_hbm), (ny_ref, ny_hbm)))
-    ]
-    for wind in winds:
-        wind.start()
 
     def copy(index, source, target, c):
         part = pl.ds(c * share, share)
@@ -727,8 +720,6 @@
     for c in range(CHUNKS):
         copy(0, x_ref, x_hbm, c).wait()
         copy(1, p_ref, p_hbm, c).wait()
-    for wind in winds:
-        wind.wait()
 
 
 def call(kernel, name, shapes, *args, far_in=(), far_out=False, scratch=(), keep=()):
@@ -860,22 +851,20 @@
             sent = (edge, inner, outer)
             got = (exchange_rows(edge),) + exchange_lanes(inner, outer)
         else:
-            wind_x, wind_y, wind_z, pressure = call(
+            wind_z, pressure = call(
                 kernel_d,
                 "last",
-                [field] * 4,
+                [field] * 2,
                 *column,
                 value,
                 prod,
                 inv,
                 star,
-                wind_x,
-                wind_y,
                 far_out=True,
                 scratch=[
                     pltpu.VMEM(field, jnp.float32),
                     pltpu.VMEM(field, jnp.float32),
-                    pltpu.SemaphoreType.DMA((3, CHUNKS)),
+                    pltpu.SemaphoreType.DMA((2, CHUNKS)),
                 ],
             )
     return wind_x, wind_y, wind_z, pressure

time: 34.2 us -> 34 us (level)
  local copies, waits for them, and re-layouts: 0.01 us -> 1.6 us
  waiting for transfers between devices: 5.85 us -> 4.4 us
    unnamed x8 -> x10, local copies, waits for them, and re-layouts: 0.01 us -> 1.6 us
    ppermute x18, waiting for transfers between devices: 5.85 us -> 4.4 us  [swap(): return lax.ppermute(value, axis, [(i, partner(i)) for i in range(count)])]
  transfers between devices with their start and end apart: 18 -> 18, of which waited for: 5 -> 4; matrix products, arithmetic and copies ran while one was open for 0% -> 5% of each run, Pallas kernels for 10% -> 10%
where the time goes in v12:
time: 34 us; the launch traced here: 33.8 us
  starting transfers between devices  16.2 us (48%)
  Pallas kernels  10.9 us (32%)
  waiting for transfers between devices  4.4 us (13%)
  local copies, waits for them, and re-layouts  1.6 us (5%)
  between operations  0.75 us (2%)
    ppermute x18, starting transfers between devices, swap(): return lax.ppermute(value, axis, [(i, partner(i)) for i in range(count)])  16.2 us
    pallas_call x9, Pallas kernels, call(): pl.pallas_call(kernel, out_shape=[pltpu.VMEM(s, jnp.float32) if k in keep...  10.9 us
    ppermute x18, waiting for transfers between devices, swap(): return lax.ppermute(value, axis, [(i, partner(i)) for i in range(count)])  4.4 us
    unnamed x10, local copies, waits for them, and re-layouts  1.6 us
  transfers between devices with their start and end apart: 18, of which 4 were waited for; matrix products, arithmetic and copies ran while one was open for 5% of the time, Pallas kernels for 10%

profile of v12, /device:TPU:0, one launch (start us, length us, event | category | flops | bytes accessed | tf_op | source)
XLA Modules:
  0.0 33.8 jit_solution(4691142131675396182)
XLA Ops:
  0.6 2.7 %start.1 = (f32[33,8,128]{2,1,0:T(8,128)S(1)}, f32[2,32,128]{2,1,0:T(8,128)S(1)}, f32[3,32,128]{2,1,0:T(8,128)S(1)}, f32[2,32,128]{2,1,0:T(8,128)S(1)}, f32[32,3...) custom-call(f32[32,32,128]{2,1,0:T(8,128)} %p_hbm.1, ...), custom_call_target="tpu_custom_call" | custom-call | flops 12230656 | bytes 6115328 | tf_op jit(solution)/shard_map/start/pallas_call | solution.py:730
  3.3 3.0 %collective-permute-start = (f32[33,8,128]{2,1,0:T(8,128)S(1)}, f32[33,8,128]{2,1,0:T(8,128)S(1)}, u32[]{:S(2)}, u32[]{:S(2)}) collective-permute-start(f32[33,8,128]{2,1,0:T(8,128)S(1)} %get-tuple-element.60.rows_ref.srows_ref.refs_15_), channel_id=1, source_target_pairs={{0,16},{16,0},{1,17},{17,1},{2,18},{18,2},{3,19},{19,3},{4,20},{20... | collective-permute-start | bytes 405512 | tf_op jit(solution)/shard_map/ppermute | solution.py:749
  6.4 3.6 %collective-permute-start.2 = (f32[3,32,128]{2,1,0:T(8,128)S(1)}, f32[3,32,128]{2,1,0:T(8,128)S(1)}, u32[]{:S(2)}, u32[]{:S(2)}) collective-permute-start(f32[3,32,128]{2,1,0:T(8,128)S(1)} %get-tuple-element.62.outer_ref.souter_ref.refs_17_), channel_id=1, source_target_pairs={{0,12},{4,8},{8,4},{12,0},{1,13},{5,9},{9,5},{13,1},{2,14},{6,10},... | collective-permute-start | bytes 147464 | tf_op jit(solution)/shard_map/ppermute | solution.py:749
  10.0 1.6 %collective-permute-start.4 = (f32[2,32,128]{2,1,0:T(8,128)S(1)}, f32[2,32,128]{2,1,0:T(8,128)S(1)}, u32[]{:S(2)}, u32[]{:S(2)}) collective-permute-start(f32[2,32,128]{2,1,0:T(8,128)S(1)} %get-tuple-element.65), channel_id=1, source_target_pairs={{0,2},{1,3},{2,0},{3,1},{4,6},{5,7},{6,4},{7,5},{8,10},{9,11},{10,... | collective-permute-start | bytes 98312 | tf_op jit(solution)/shard_map/ppermute | solution.py:749
  11.6 1.4 %interior.2 = (f32[32,32,128]{2,1,0:T(8,128)S(1)}, f32[32,32,128]{2,1,0:T(8,128)S(1)}, f32[32,32,128]{2,1,0:T(8,128)S(1)}) custom-call(f32[32,32,128]{2,1,0:T(8,128)S(1)} %get-tuple-element.50.p_ref, f32[32,32,128]{2,1,0:T(8,128)S(1)} %get-tuple-element.51.wx_ref, f32[32,32,128]{2,1,0:T(8,128)S(1)} %get-tuple-element.52.wy_ref, f32[32,128]{1,0:T(8,128)S(1)} %copy-done.1), custom_call_target="tpu_custom_call" | custom-call | flops 6324224 | bytes 3162112 | tf_op jit(solution)/shard_map/interior/pallas_call | solution.py:730
  13.0 0.9 %collective-permute-done.1.got_inner_ref.got_sinner_ref = f32[2,32,128]{2,1,0:T(8,128)S(1)} collective-permute-done((f32[2,32,128]{2,1,0:T(8,128)S(1)}, f32[2,32,128]{2,1,0:T(8,128)S(1)}, u32[]{:S(2)}, u32[]{:S(2)}) %collective-permute-start.1) | collective-permute-done | bytes 32800 | tf_op jit(solution)/shard_map/ppermute | solution.py:749
  14.0 1.4 %sweep.2 = (f32[32,32,128]{2,1,0:T(8,128)S(1)}, f32[32,32,128]{2,1,0:T(8,128)S(1)}, f32[32,32,128]{2,1,0:T(8,128)S(1)}, f32[32,32,128]{2,1,0:T(8,128)S(1)}, f32[...) custom-call(f32[32,32,128]{2,1,0:T(8,128)S(1)} %get-tuple-element.50, ...), custom_call_target="tpu_custom_call" | custom-call | flops 15073280 | bytes 7536640 | tf_op jit(solution)/shard_map/sweep/pallas_call | solution.py:730
  15.6 1.4 %collective-permute-start.6 = (f32[32,128]{1,0:T(8,128)S(1)}, f32[32,128]{1,0:T(8,128)S(1)}, u32[]{:S(2)}, u32[]{:S(2)}) collective-permute-start(f32[32,128]{1,0:T(8,128)S(1)} %get-tuple-element.67), channel_id=1, source_target_pairs={{0,2},{1,3},{2,0},{3,1},{4,6},{5,7},{6,4},{7,5},{8,10},{9,11},{10,... | collective-permute-start | bytes 49160 | tf_op jit(solution)/shard_map/ppermute | solution.py:749
  17.0 0.3 collective-permute-start.8
  17.5 0.3 collective-permute-start.9
  17.8 0.5 %pack.1.refs_14_ = f32[2,32,128]{2,1,0:T(8,128)S(1)} custom-call(f32[32,32,128]{2,1,0:T(8,128)S(1)} %get-tuple-element.75.wy_ref), custom_call_target="tpu_custom_call" | custom-call | flops 1114112 | bytes 557056 | tf_op jit(solution)/shard_map/pack/pallas_call | solution.py:730
  18.3 1.1 %collective-permute-done.6.refs_1_ = f32[32,128]{1,0:T(8,128)S(1)} collective-permute-done((f32[32,128]{1,0:T(8,128)S(1)}, f32[32,128]{1,0:T(8,128)S(1)}, u32[]{:S(2)}, u32[]{:S(2)}) %collective-permute-start.6) | collective-permute-done | bytes 16416 | tf_op jit(solution)/shard_map/ppermute | solution.py:749
  19.4 1.0 %finish.1 = (f32[32,32,128]{2,1,0:T(8,128)S(1)}, f32[32,32,128]{2,1,0:T(8,128)S(1)}, f32[32,8,128]{2,1,0:T(8,128)S(1)}, f32[1,32,128]{2,1,0:T(8,128)S(1)}, f32[2...) custom-call(f32[2,32,128]{2,1,0:T(8,128)S(1)} %collective-permute-done.5.refs_0_, ...), custom_call_target="tpu_custom_call" | custom-call | flops 8921088 | bytes 4460544 | tf_op jit(solution)/shard_map/finish/pallas_call | solution.py:730
  20.4 0.5 %collective-permute-start.10 = (f32[32,8,128]{2,1,0:T(8,128)S(1)}, f32[32,8,128]{2,1,0:T(8,128)S(1)}, u32[]{:S(2)}, u32[]{:S(2)}) collective-permute-start(f32[32,8,128]{2,1,0:T(8,128)S(1)} %get-tuple-element.82.rows_ref), channel_id=1, source_target_pairs={{0,16},{16,0},{1,17},{17,1},{2,18},{18,2},{3,19},{19,3},{4,20},{20... | collective-permute-start | bytes 393224 | tf_op jit(solution)/shard_map/ppermute | solution.py:749
  20.9 2.6 %collective-permute-start.12 = (f32[2,32,128]{2,1,0:T(8,128)S(1)}, f32[2,32,128]{2,1,0:T(8,128)S(1)}, u32[]{:S(2)}, u32[]{:S(2)}) collective-permute-start(f32[2,32,128]{2,1,0:T(8,128)S(1)} %get-tuple-element.84.outer_ref), channel_id=1, source_target_pairs={{0,12},{4,8},{8,4},{12,0},{1,13},{5,9},{9,5},{13,1},{2,14},{6,10},... | collective-permute-start | bytes 98312 | tf_op jit(solution)/shard_map/ppermute | solution.py:749
  23.5 1.4 %interior.3 = (f32[32,32,128]{2,1,0:T(8,128)S(1)}, f32[32,32,128]{2,1,0:T(8,128)S(1)}, f32[32,32,128]{2,1,0:T(8,128)S(1)}) custom-call(f32[32,32,128]{2,1,0:T(8,128)S(1)} %get-tuple-element.76.p_ref, f32[32,32,128]{2,1,0:T(8,128)S(1)} %get-tuple-element.74.refs_13_.wx_ref, f32[32,32,128]{2,1,0:T(8,128)S(1)} %get-tuple-element.75.wy_ref, f32[32,128]{1,0:T(8,128)S(1)} %copy-done.1), custom_call_target="tpu_custom_call" | custom-call | flops 6324224 | bytes 3162112 | tf_op jit(solution)/shard_map/interior/pallas_call | solution.py:730
  25.0 2.3 %collective-permute-done.11.got_inner_ref = f32[1,32,128]{2,1,0:T(8,128)S(1)} collective-permute-done((f32[1,32,128]{2,1,0:T(8,128)S(1)}, f32[1,32,128]{2,1,0:T(8,128)S(1)}, u32[]{:S(2)}, u32[]{:S(2)}) %collective-permute-start.11) | collective-permute-done | bytes 16416 | tf_op jit(solution)/shard_map/ppermute | solution.py:749
  27.3 1.4 %sweep.3 = (f32[32,32,128]{2,1,0:T(8,128)S(1)}, f32[32,32,128]{2,1,0:T(8,128)S(1)}, f32[32,32,128]{2,1,0:T(8,128)S(1)}, f32[32,32,128]{2,1,0:T(8,128)S(1)}, f32[...) custom-call(f32[32,32,128]{2,1,0:T(8,128)S(1)} %get-tuple-element.76, ...), custom_call_target="tpu_custom_call" | custom-call | flops 14925824 | bytes 7462912 | tf_op jit(solution)/shard_map/sweep/pallas_call | solution.py:730
  28.7 1.2 %collective-permute-start.14 = (f32[32,128]{1,0:T(8,128)S(1)}, f32[32,128]{1,0:T(8,128)S(1)}, u32[]{:S(2)}, u32[]{:S(2)}) collective-permute-start(f32[32,128]{1,0:T(8,128)S(1)} %get-tuple-element.88), channel_id=1, source_target_pairs={{0,2},{1,3},{2,0},{3,1},{4,6},{5,7},{6,4},{7,5},{8,10},{9,11},{10,... | collective-permute-start | bytes 49160 | tf_op jit(solution)/shard_map/ppermute | solution.py:749
  29.9 0.7 %collective-permute-start.16 = (f32[32,128]{1,0:T(8,128)S(1)}, f32[32,128]{1,0:T(8,128)S(1)}, u32[]{:S(2)}, u32[]{:S(2)}) collective-permute-start(f32[32,128]{1,0:T(8,128)S(1)} %get-tuple-element.90), channel_id=1, source_target_pairs={{0,1},{1,0},{2,3},{3,2},{4,5},{5,4},{6,7},{7,6},{8,9},{9,8},{10,11... | collective-permute-start | bytes 49160 | tf_op jit(solution)/shard_map/ppermute | solution.py:749
  30.6 0.5 %collective-permute-start.17 = (f32[32,128]{1,0:T(8,128)S(1)}, f32[32,128]{1,0:T(8,128)S(1)}, u32[]{:S(2)}, u32[]{:S(2)}) collective-permute-start(f32[32,128]{1,0:T(8,128)S(1)} %get-tuple-element.91.refs_6_), channel_id=1, source_target_pairs={{0,1},{1,0},{2,3},{3,2},{4,5},{5,4},{6,7},{7,6},{8,9},{9,8},{10,11... | collective-permute-start | bytes 49160 | tf_op jit(solution)/shard_map/ppermute | solution.py:749
  31.1 0.8 %copy.12 = f32[32,32,128]{2,1,0:T(8,128)} copy(f32[32,32,128]{2,1,0:T(8,128)S(1)} %get-tuple-element.96) | data formatting | bytes 1048576
  31.9 0.8 %copy.13 = f32[32,32,128]{2,1,0:T(8,128)} copy(f32[32,32,128]{2,1,0:T(8,128)S(1)} %get-tuple-element.97) | data formatting | bytes 1048576
  32.7 1.1 %last.1 = (f32[32,32,128]{2,1,0:T(8,128)}, f32[32,32,128]{2,1,0:T(8,128)}) custom-call(f32[2,32,128]{2,1,0:T(8,128)S(1)} %collective-permute-done.13.refs_0_, f32[32,128]{1,0:T(8,128)S(1)} %collective-permute-done.14.refs_1_, f32[32,128]{1,0:T(8,128)S(1)} %collective-permute-done.15.refs_2_, f32[32,128]{1,0:T(8,128)S(1)} %collective-permute-done.16.refs_3_, ...), custom_call_target="tpu_custom_call" | custom-call | flops 6946816 | bytes 3473408 | tf_op jit(solution)/shard_map/last/pallas_call | solution.py:730
  (31 shorter events, 0.7 us)
Async XLA Ops:
  3.3 10.7 %collective-permute-start = (f32[33,8,128]{2,1,0:T(8,128)S(1)}, f32[33,8,128]{2,1,0:T(8,128)S(1)}, u32[]{:S(2)}, u32[]{:S(2)}) collective-permute-start(f32[33,8,128]{2,1,0:T(8,128)S(1)} %get-tuple-element.60.rows_ref.srows_ref.refs_15_), channel_id=1, source_target_pairs={{0,16},{16,0},{1,17},{17,1},{2,18},{18,2},{3,19},{19,3},{4,20},{20... | collective-permute-start | bytes 405512 | tf_op jit(solution)/shard_map/ppermute | solution.py:749
  6.3 3.6 %collective-permute-start.3 = (f32[5,32,128]{2,1,0:T(8,128)S(1)}, f32[5,32,128]{2,1,0:T(8,128)S(1)}, u32[]{:S(2)}, u32[]{:S(2)}) collective-permute-start(f32[5,32,128]{2,1,0:T(8,128)S(1)} %get-tuple-element.63.stat_ref), channel_id=1, source_target_pairs={{0,1},{1,0},{2,3},{3,2},{4,5},{5,4},{6,7},{7,6},{8,9},{9,8},{10,11... | collective-permute-start | bytes 245768 | tf_op jit(solution)/shard_map/ppermute | solution.py:749
  6.4 7.5 %collective-permute-start.2 = (f32[3,32,128]{2,1,0:T(8,128)S(1)}, f32[3,32,128]{2,1,0:T(8,128)S(1)}, u32[]{:S(2)}, u32[]{:S(2)}) collective-permute-start(f32[3,32,128]{2,1,0:T(8,128)S(1)} %get-tuple-element.62.outer_ref.souter_ref.refs_17_), channel_id=1, source_target_pairs={{0,12},{4,8},{8,4},{12,0},{1,13},{5,9},{9,5},{13,1},{2,14},{6,10},... | collective-permute-start | bytes 147464 | tf_op jit(solution)/shard_map/ppermute | solution.py:749
  10.0 3.9 %collective-permute-start.1 = (f32[2,32,128]{2,1,0:T(8,128)S(1)}, f32[2,32,128]{2,1,0:T(8,128)S(1)}, u32[]{:S(2)}, u32[]{:S(2)}) collective-permute-start(f32[2,32,128]{2,1,0:T(8,128)S(1)} %get-tuple-element.61.inner_ref.sinner_ref.refs_16_), channel_id=1, source_target_pairs={{0,4},{4,0},{8,12},{12,8},{1,5},{5,1},{9,13},{13,9},{2,6},{6,2},{1... | collective-permute-start | bytes 98312 | tf_op jit(solution)/shard_map/ppermute | solution.py:749
  10.0 1.6 %copy-start.1 = (f32[32,128]{1,0:T(8,128)S(1)}, f32[32,128]{1,0:T(8,128)}, u32[]{:S(2)}) copy-start(f32[32,128]{1,0:T(8,128)} %jac_ref.7) | copy-start | bytes 49156
  10.0 4.0 %collective-permute-start.4 = (f32[2,32,128]{2,1,0:T(8,128)S(1)}, f32[2,32,128]{2,1,0:T(8,128)S(1)}, u32[]{:S(2)}, u32[]{:S(2)}) collective-permute-start(f32[2,32,128]{2,1,0:T(8,128)S(1)} %get-tuple-element.65), channel_id=1, source_target_pairs={{0,2},{1,3},{2,0},{3,1},{4,6},{5,7},{6,4},{7,5},{8,10},{9,11},{10,... | collective-permute-start | bytes 98312 | tf_op jit(solution)/shard_map/ppermute | solution.py:749
  11.6 2.4 %copy-start = (f32[32,32,128]{2,1,0:T(8,128)S(1)}, f32[32,32,128]{2,1,0:T(8,128)}, u32[]{:S(2)}) copy-start(f32[32,32,128]{2,1,0:T(8,128)} %wz_ref.1) | copy-start | bytes 1572868
  11.6 2.4 %copy-start.2 = (f32[32,128]{1,0:T(8,128)S(1)}, f32[32,128]{1,0:T(8,128)}, u32[]{:S(2)}) copy-start(f32[32,128]{1,0:T(8,128)} %sx_ref.3) | copy-start | bytes 49156
  11.6 2.4 %copy-start.3 = (f32[32,128]{1,0:T(8,128)S(1)}, f32[32,128]{1,0:T(8,128)}, u32[]{:S(2)}) copy-start(f32[32,128]{1,0:T(8,128)} %sy_ref.3) | copy-start | bytes 49156
  15.4 4.0 %collective-permute-start.5 = (f32[2,32,128]{2,1,0:T(8,128)S(1)}, f32[2,32,128]{2,1,0:T(8,128)S(1)}, u32[]{:S(2)}, u32[]{:S(2)}) collective-permute-start(f32[2,32,128]{2,1,0:T(8,128)S(1)} %get-tuple-element.66), channel_id=1, source_target_pairs={{0,3},{1,2},{2,1},{3,0},{4,7},{5,6},{6,5},{7,4},{8,11},{9,10},{10,... | collective-permute-start | bytes 98312 | tf_op jit(solution)/shard_map/ppermute | solution.py:749
  15.6 3.7 %collective-permute-start.6 = (f32[32,128]{1,0:T(8,128)S(1)}, f32[32,128]{1,0:T(8,128)S(1)}, u32[]{:S(2)}, u32[]{:S(2)}) collective-permute-start(f32[32,128]{1,0:T(8,128)S(1)} %get-tuple-element.67), channel_id=1, source_target_pairs={{0,2},{1,3},{2,0},{3,1},{4,6},{5,7},{6,4},{7,5},{8,10},{9,11},{10,... | collective-permute-start | bytes 49160 | tf_op jit(solution)/shard_map/ppermute | solution.py:749
  17.0 2.3 %collective-permute-start.8 = (f32[32,128]{1,0:T(8,128)S(1)}, f32[32,128]{1,0:T(8,128)S(1)}, u32[]{:S(2)}, u32[]{:S(2)}) collective-permute-start(f32[32,128]{1,0:T(8,128)S(1)} %get-tuple-element.69), channel_id=1, source_target_pairs={{0,1},{1,0},{2,3},{3,2},{4,5},{5,4},{6,7},{7,6},{8,9},{9,8},{10,11... | collective-permute-start | bytes 49160 | tf_op jit(solution)/shard_map/ppermute | solution.py:749
  17.3 2.1 %collective-permute-start.7 = (f32[32,128]{1,0:T(8,128)S(1)}, f32[32,128]{1,0:T(8,128)S(1)}, u32[]{:S(2)}, u32[]{:S(2)}) collective-permute-start(f32[32,128]{1,0:T(8,128)S(1)} %get-tuple-element.68.refs_5_), channel_id=1, source_target_pairs={{0,1},{1,0},{2,3},{3,2},{4,5},{5,4},{6,7},{7,6},{8,9},{9,8},{10,11... | collective-permute-start | bytes 49160 | tf_op jit(solution)/shard_map/ppermute | solution.py:749
  17.5 1.8 %collective-permute-start.9 = (f32[32,128]{1,0:T(8,128)S(1)}, f32[32,128]{1,0:T(8,128)S(1)}, u32[]{:S(2)}, u32[]{:S(2)}) collective-permute-start(f32[32,128]{1,0:T(8,128)S(1)} %get-tuple-element.70.refs_6_), channel_id=1, source_target_pairs={{0,1},{1,0},{2,3},{3,2},{4,5},{5,4},{6,7},{7,6},{8,9},{9,8},{10,11... | collective-permute-start | bytes 49160 | tf_op jit(solution)/shard_map/ppermute | solution.py:749
  20.4 6.9 %collective-permute-start.10 = (f32[32,8,128]{2,1,0:T(8,128)S(1)}, f32[32,8,128]{2,1,0:T(8,128)S(1)}, u32[]{:S(2)}, u32[]{:S(2)}) collective-permute-start(f32[32,8,128]{2,1,0:T(8,128)S(1)} %get-tuple-element.82.rows_ref), channel_id=1, source_target_pairs={{0,16},{16,0},{1,17},{17,1},{2,18},{18,2},{3,19},{19,3},{4,20},{20... | collective-permute-start | bytes 393224 | tf_op jit(solution)/shard_map/ppermute | solution.py:749
  20.9 6.3 %collective-permute-start.12 = (f32[2,32,128]{2,1,0:T(8,128)S(1)}, f32[2,32,128]{2,1,0:T(8,128)S(1)}, u32[]{:S(2)}, u32[]{:S(2)}) collective-permute-start(f32[2,32,128]{2,1,0:T(8,128)S(1)} %get-tuple-element.84.outer_ref), channel_id=1, source_target_pairs={{0,12},{4,8},{8,4},{12,0},{1,13},{5,9},{9,5},{13,1},{2,14},{6,10},... | collective-permute-start | bytes 98312 | tf_op jit(solution)/shard_map/ppermute | solution.py:749
  23.5 3.7 %collective-permute-start.11 = (f32[1,32,128]{2,1,0:T(8,128)S(1)}, f32[1,32,128]{2,1,0:T(8,128)S(1)}, u32[]{:S(2)}, u32[]{:S(2)}) collective-permute-start(f32[1,32,128]{2,1,0:T(8,128)S(1)} %get-tuple-element.83.inner_ref), channel_id=1, source_target_pairs={{0,4},{4,0},{8,12},{12,8},{1,5},{5,1},{9,13},{13,9},{2,6},{6,2},{1... | collective-permute-start | bytes 49160 | tf_op jit(solution)/shard_map/ppermute | solution.py:749
  28.7 4.1 %collective-permute-start.13 = (f32[2,32,128]{2,1,0:T(8,128)S(1)}, f32[2,32,128]{2,1,0:T(8,128)S(1)}, u32[]{:S(2)}, u32[]{:S(2)}) collective-permute-start(f32[2,32,128]{2,1,0:T(8,128)S(1)} %get-tuple-element.87), channel_id=1, source_target_pairs={{0,3},{1,2},{2,1},{3,0},{4,7},{5,6},{6,5},{7,4},{8,11},{9,10},{10,... | collective-permute-start | bytes 98312 | tf_op jit(solution)/shard_map/ppermute | solution.py:749
  28.7 3.9 %collective-permute-start.14 = (f32[32,128]{1,0:T(8,128)S(1)}, f32[32,128]{1,0:T(8,128)S(1)}, u32[]{:S(2)}, u32[]{:S(2)}) collective-permute-start(f32[32,128]{1,0:T(8,128)S(1)} %get-tuple-element.88), channel_id=1, source_target_pairs={{0,2},{1,3},{2,0},{3,1},{4,6},{5,7},{6,4},{7,5},{8,10},{9,11},{10,... | collective-permute-start | bytes 49160 | tf_op jit(solution)/shard_map/ppermute | solution.py:749
  29.9 2.8 %collective-permute-start.16 = (f32[32,128]{1,0:T(8,128)S(1)}, f32[32,128]{1,0:T(8,128)S(1)}, u32[]{:S(2)}, u32[]{:S(2)}) collective-permute-start(f32[32,128]{1,0:T(8,128)S(1)} %get-tuple-element.90), channel_id=1, source_target_pairs={{0,1},{1,0},{2,3},{3,2},{4,5},{5,4},{6,7},{7,6},{8,9},{9,8},{10,11... | collective-permute-start | bytes 49160 | tf_op jit(solution)/shard_map/ppermute | solution.py:749
  30.6 2.1 %collective-permute-start.15 = (f32[32,128]{1,0:T(8,128)S(1)}, f32[32,128]{1,0:T(8,128)S(1)}, u32[]{:S(2)}, u32[]{:S(2)}) collective-permute-start(f32[32,128]{1,0:T(8,128)S(1)} %get-tuple-element.89.refs_5_), channel_id=1, source_target_pairs={{0,1},{1,0},{2,3},{3,2},{4,5},{5,4},{6,7},{7,6},{8,9},{9,8},{10,11... | collective-permute-start | bytes 49160 | tf_op jit(solution)/shard_map/ppermute | solution.py:749
  30.6 2.1 %collective-permute-start.17 = (f32[32,128]{1,0:T(8,128)S(1)}, f32[32,128]{1,0:T(8,128)S(1)}, u32[]{:S(2)}, u32[]{:S(2)}) collective-permute-start(f32[32,128]{1,0:T(8,128)S(1)} %get-tuple-element.91.refs_6_), channel_id=1, source_target_pairs={{0,1},{1,0},{2,3},{3,2},{4,5},{5,4},{6,7},{7,6},{8,9},{9,8},{10,11... | collective-permute-start | bytes 49160 | tf_op jit(solution)/shard_map/ppermute | solution.py:749

commit v13 on v12

--- a/solution.py
+++ b/solution.py
@@ -504,7 +504,7 @@
         return here, above, force_next, value, first
 
     below, here, force, value, first = lax.fori_loop(
-        0, levels, step, (zeros, zeros, zeros, zeros, zeros), unroll=UNROLL // 2
+        0, levels, step, (zeros, zeros, zeros, zeros, zeros), unroll=UNROLL
     )
     value, first = sweep(levels - 1, which, below, zeros, force, value, first)
     bottom = tiles_of(ps_ref, 0, count)

time: 34 us -> 33.4 us (0.982)
  Pallas kernels: 10.9 us -> 10.3 us
    pallas_call x9, Pallas kernels: 10.9 us -> 10.3 us  [call(): pl.pallas_call(kernel, out_shape=[pltpu.VMEM(s, jnp.float32) if k in keep...]
where the time goes in v13:
time: 33.4 us; the launch traced here: 33.3 us
  starting transfers between devices  16.2 us (49%)
  Pallas kernels  10.3 us (31%)
  waiting for transfers between devices  4.4 us (13%)
  local copies, waits for them, and re-layouts  1.6 us (5%)
  between operations  0.75 us (2%)
    ppermute x18, starting transfers between devices, swap(): return lax.ppermute(value, axis, [(i, partner(i)) for i in range(count)])  16.2 us
    pallas_call x9, Pallas kernels, call(): pl.pallas_call(kernel, out_shape=[pltpu.VMEM(s, jnp.float32) if k in keep...  10.3 us
    ppermute x18, waiting for transfers between devices, swap(): return lax.ppermute(value, axis, [(i, partner(i)) for i in range(count)])  4.4 us
    unnamed x10, local copies, waits for them, and re-layouts  1.6 us
  transfers between devices with their start and end apart: 18, of which 4 were waited for; matrix products, arithmetic and copies ran while one was open for 5% of the time, Pallas kernels for 10%

profile of v13, /device:TPU:0, one launch (start us, length us, event | category | flops | bytes accessed | tf_op | source)
XLA Modules:
  0.0 33.3 jit_solution(5703330974424276401)
XLA Ops:
  0.6 2.7 %start.1 = (f32[33,8,128]{2,1,0:T(8,128)S(1)}, f32[2,32,128]{2,1,0:T(8,128)S(1)}, f32[3,32,128]{2,1,0:T(8,128)S(1)}, f32[2,32,128]{2,1,0:T(8,128)S(1)}, f32[32,3...) custom-call(f32[32,32,128]{2,1,0:T(8,128)} %p_hbm.1, ...), custom_call_target="tpu_custom_call" | custom-call | flops 12230656 | bytes 6115328 | tf_op jit(solution)/shard_map/start/pallas_call | solution.py:730
  3.3 3.0 %collective-permute-start = (f32[33,8,128]{2,1,0:T(8,128)S(1)}, f32[33,8,128]{2,1,0:T(8,128)S(1)}, u32[]{:S(2)}, u32[]{:S(2)}) collective-permute-start(f32[33,8,128]{2,1,0:T(8,128)S(1)} %get-tuple-element.60.rows_ref.srows_ref.refs_15_), channel_id=1, source_target_pairs={{0,16},{16,0},{1,17},{17,1},{2,18},{18,2},{3,19},{19,3},{4,20},{20... | collective-permute-start | bytes 405512 | tf_op jit(solution)/shard_map/ppermute | solution.py:749
  6.4 3.6 %collective-permute-start.2 = (f32[3,32,128]{2,1,0:T(8,128)S(1)}, f32[3,32,128]{2,1,0:T(8,128)S(1)}, u32[]{:S(2)}, u32[]{:S(2)}) collective-permute-start(f32[3,32,128]{2,1,0:T(8,128)S(1)} %get-tuple-element.62.outer_ref.souter_ref.refs_17_), channel_id=1, source_target_pairs={{0,12},{4,8},{8,4},{12,0},{1,13},{5,9},{9,5},{13,1},{2,14},{6,10},... | collective-permute-start | bytes 147464 | tf_op jit(solution)/shard_map/ppermute | solution.py:749
  10.0 1.6 %collective-permute-start.4 = (f32[2,32,128]{2,1,0:T(8,128)S(1)}, f32[2,32,128]{2,1,0:T(8,128)S(1)}, u32[]{:S(2)}, u32[]{:S(2)}) collective-permute-start(f32[2,32,128]{2,1,0:T(8,128)S(1)} %get-tuple-element.65), channel_id=1, source_target_pairs={{0,2},{1,3},{2,0},{3,1},{4,6},{5,7},{6,4},{7,5},{8,10},{9,11},{10,... | collective-permute-start | bytes 98312 | tf_op jit(solution)/shard_map/ppermute | solution.py:749
  11.6 1.4 %interior.2 = (f32[32,32,128]{2,1,0:T(8,128)S(1)}, f32[32,32,128]{2,1,0:T(8,128)S(1)}, f32[32,32,128]{2,1,0:T(8,128)S(1)}) custom-call(f32[32,32,128]{2,1,0:T(8,128)S(1)} %get-tuple-element.50.p_ref, f32[32,32,128]{2,1,0:T(8,128)S(1)} %get-tuple-element.51.wx_ref, f32[32,32,128]{2,1,0:T(8,128)S(1)} %get-tuple-element.52.wy_ref, f32[32,128]{1,0:T(8,128)S(1)} %copy-done.1), custom_call_target="tpu_custom_call" | custom-call | flops 6324224 | bytes 3162112 | tf_op jit(solution)/shard_map/interior/pallas_call | solution.py:730
  13.0 0.9 %collective-permute-done.1.got_inner_ref.got_sinner_ref = f32[2,32,128]{2,1,0:T(8,128)S(1)} collective-permute-done((f32[2,32,128]{2,1,0:T(8,128)S(1)}, f32[2,32,128]{2,1,0:T(8,128)S(1)}, u32[]{:S(2)}, u32[]{:S(2)}) %collective-permute-start.1) | collective-permute-done | bytes 32800 | tf_op jit(solution)/shard_map/ppermute | solution.py:749
  14.0 1.1 %sweep.2 = (f32[32,32,128]{2,1,0:T(8,128)S(1)}, f32[32,32,128]{2,1,0:T(8,128)S(1)}, f32[32,32,128]{2,1,0:T(8,128)S(1)}, f32[32,32,128]{2,1,0:T(8,128)S(1)}, f32[...) custom-call(f32[32,32,128]{2,1,0:T(8,128)S(1)} %get-tuple-element.50, ...), custom_call_target="tpu_custom_call" | custom-call | flops 15073280 | bytes 7536640 | tf_op jit(solution)/shard_map/sweep/pallas_call | solution.py:730
  15.4 1.4 %collective-permute-start.6 = (f32[32,128]{1,0:T(8,128)S(1)}, f32[32,128]{1,0:T(8,128)S(1)}, u32[]{:S(2)}, u32[]{:S(2)}) collective-permute-start(f32[32,128]{1,0:T(8,128)S(1)} %get-tuple-element.67), channel_id=1, source_target_pairs={{0,2},{1,3},{2,0},{3,1},{4,6},{5,7},{6,4},{7,5},{8,10},{9,11},{10,... | collective-permute-start | bytes 49160 | tf_op jit(solution)/shard_map/ppermute | solution.py:749
  16.8 0.3 collective-permute-start.8
  17.3 0.3 collective-permute-start.9
  17.6 0.5 %pack.1.refs_14_ = f32[2,32,128]{2,1,0:T(8,128)S(1)} custom-call(f32[32,32,128]{2,1,0:T(8,128)S(1)} %get-tuple-element.75.wy_ref), custom_call_target="tpu_custom_call" | custom-call | flops 1114112 | bytes 557056 | tf_op jit(solution)/shard_map/pack/pallas_call | solution.py:730
  18.0 1.1 %collective-permute-done.6.refs_1_ = f32[32,128]{1,0:T(8,128)S(1)} collective-permute-done((f32[32,128]{1,0:T(8,128)S(1)}, f32[32,128]{1,0:T(8,128)S(1)}, u32[]{:S(2)}, u32[]{:S(2)}) %collective-permute-start.6) | collective-permute-done | bytes 16416 | tf_op jit(solution)/shard_map/ppermute | solution.py:749
  19.1 1.0 %finish.1 = (f32[32,32,128]{2,1,0:T(8,128)S(1)}, f32[32,32,128]{2,1,0:T(8,128)S(1)}, f32[32,8,128]{2,1,0:T(8,128)S(1)}, f32[1,32,128]{2,1,0:T(8,128)S(1)}, f32[2...) custom-call(f32[2,32,128]{2,1,0:T(8,128)S(1)} %collective-permute-done.5.refs_0_, ...), custom_call_target="tpu_custom_call" | custom-call | flops 8921088 | bytes 4460544 | tf_op jit(solution)/shard_map/finish/pallas_call | solution.py:730
  20.1 0.5 %collective-permute-start.10 = (f32[32,8,128]{2,1,0:T(8,128)S(1)}, f32[32,8,128]{2,1,0:T(8,128)S(1)}, u32[]{:S(2)}, u32[]{:S(2)}) collective-permute-start(f32[32,8,128]{2,1,0:T(8,128)S(1)} %get-tuple-element.82.rows_ref), channel_id=1, source_target_pairs={{0,16},{16,0},{1,17},{17,1},{2,18},{18,2},{3,19},{19,3},{4,20},{20... | collective-permute-start | bytes 393224 | tf_op jit(solution)/shard_map/ppermute | solution.py:749
  20.7 2.6 %collective-permute-start.12 = (f32[2,32,128]{2,1,0:T(8,128)S(1)}, f32[2,32,128]{2,1,0:T(8,128)S(1)}, u32[]{:S(2)}, u32[]{:S(2)}) collective-permute-start(f32[2,32,128]{2,1,0:T(8,128)S(1)} %get-tuple-element.84.outer_ref), channel_id=1, source_target_pairs={{0,12},{4,8},{8,4},{12,0},{1,13},{5,9},{9,5},{13,1},{2,14},{6,10},... | collective-permute-start | bytes 98312 | tf_op jit(solution)/shard_map/ppermute | solution.py:749
  23.3 1.4 %interior.3 = (f32[32,32,128]{2,1,0:T(8,128)S(1)}, f32[32,32,128]{2,1,0:T(8,128)S(1)}, f32[32,32,128]{2,1,0:T(8,128)S(1)}) custom-call(f32[32,32,128]{2,1,0:T(8,128)S(1)} %get-tuple-element.76.p_ref, f32[32,32,128]{2,1,0:T(8,128)S(1)} %get-tuple-element.74.refs_13_.wx_ref, f32[32,32,128]{2,1,0:T(8,128)S(1)} %get-tuple-element.75.wy_ref, f32[32,128]{1,0:T(8,128)S(1)} %copy-done.1), custom_call_target="tpu_custom_call" | custom-call | flops 6324224 | bytes 3162112 | tf_op jit(solution)/shard_map/interior/pallas_call | solution.py:730
  24.7 2.3 %collective-permute-done.11.got_inner_ref = f32[1,32,128]{2,1,0:T(8,128)S(1)} collective-permute-done((f32[1,32,128]{2,1,0:T(8,128)S(1)}, f32[1,32,128]{2,1,0:T(8,128)S(1)}, u32[]{:S(2)}, u32[]{:S(2)}) %collective-permute-start.11) | collective-permute-done | bytes 16416 | tf_op jit(solution)/shard_map/ppermute | solution.py:749
  27.0 1.1 %sweep.3 = (f32[32,32,128]{2,1,0:T(8,128)S(1)}, f32[32,32,128]{2,1,0:T(8,128)S(1)}, f32[32,32,128]{2,1,0:T(8,128)S(1)}, f32[32,32,128]{2,1,0:T(8,128)S(1)}, f32[...) custom-call(f32[32,32,128]{2,1,0:T(8,128)S(1)} %get-tuple-element.76, ...), custom_call_target="tpu_custom_call" | custom-call | flops 14925824 | bytes 7462912 | tf_op jit(solution)/shard_map/sweep/pallas_call | solution.py:730
  28.1 1.2 %collective-permute-start.14 = (f32[32,128]{1,0:T(8,128)S(1)}, f32[32,128]{1,0:T(8,128)S(1)}, u32[]{:S(2)}, u32[]{:S(2)}) collective-permute-start(f32[32,128]{1,0:T(8,128)S(1)} %get-tuple-element.88), channel_id=1, source_target_pairs={{0,2},{1,3},{2,0},{3,1},{4,6},{5,7},{6,4},{7,5},{8,10},{9,11},{10,... | collective-permute-start | bytes 49160 | tf_op jit(solution)/shard_map/ppermute | solution.py:749
  29.3 0.7 %collective-permute-start.16 = (f32[32,128]{1,0:T(8,128)S(1)}, f32[32,128]{1,0:T(8,128)S(1)}, u32[]{:S(2)}, u32[]{:S(2)}) collective-permute-start(f32[32,128]{1,0:T(8,128)S(1)} %get-tuple-element.90), channel_id=1, source_target_pairs={{0,1},{1,0},{2,3},{3,2},{4,5},{5,4},{6,7},{7,6},{8,9},{9,8},{10,11... | collective-permute-start | bytes 49160 | tf_op jit(solution)/shard_map/ppermute | solution.py:749
  30.0 0.5 %collective-permute-start.17 = (f32[32,128]{1,0:T(8,128)S(1)}, f32[32,128]{1,0:T(8,128)S(1)}, u32[]{:S(2)}, u32[]{:S(2)}) collective-permute-start(f32[32,128]{1,0:T(8,128)S(1)} %get-tuple-element.91.refs_6_), channel_id=1, source_target_pairs={{0,1},{1,0},{2,3},{3,2},{4,5},{5,4},{6,7},{7,6},{8,9},{9,8},{10,11... | collective-permute-start | bytes 49160 | tf_op jit(solution)/shard_map/ppermute | solution.py:749
  30.5 0.8 %copy.12 = f32[32,32,128]{2,1,0:T(8,128)} copy(f32[32,32,128]{2,1,0:T(8,128)S(1)} %get-tuple-element.96) | data formatting | bytes 1048576
  31.3 0.8 %copy.13 = f32[32,32,128]{2,1,0:T(8,128)} copy(f32[32,32,128]{2,1,0:T(8,128)S(1)} %get-tuple-element.97) | data formatting | bytes 1048576
  32.1 1.1 %last.1 = (f32[32,32,128]{2,1,0:T(8,128)}, f32[32,32,128]{2,1,0:T(8,128)}) custom-call(f32[2,32,128]{2,1,0:T(8,128)S(1)} %collective-permute-done.13.refs_0_, f32[32,128]{1,0:T(8,128)S(1)} %collective-permute-done.14.refs_1_, f32[32,128]{1,0:T(8,128)S(1)} %collective-permute-done.15.refs_2_, f32[32,128]{1,0:T(8,128)S(1)} %collective-permute-done.16.refs_3_, ...), custom_call_target="tpu_custom_call" | custom-call | flops 6946816 | bytes 3473408 | tf_op jit(solution)/shard_map/last/pallas_call | solution.py:730
  (31 shorter events, 0.7 us)
Async XLA Ops:
  3.3 10.7 %collective-permute-start = (f32[33,8,128]{2,1,0:T(8,128)S(1)}, f32[33,8,128]{2,1,0:T(8,128)S(1)}, u32[]{:S(2)}, u32[]{:S(2)}) collective-permute-start(f32[33,8,128]{2,1,0:T(8,128)S(1)} %get-tuple-element.60.rows_ref.srows_ref.refs_15_), channel_id=1, source_target_pairs={{0,16},{16,0},{1,17},{17,1},{2,18},{18,2},{3,19},{19,3},{4,20},{20... | collective-permute-start | bytes 405512 | tf_op jit(solution)/shard_map/ppermute | solution.py:749
  6.3 3.6 %collective-permute-start.3 = (f32[5,32,128]{2,1,0:T(8,128)S(1)}, f32[5,32,128]{2,1,0:T(8,128)S(1)}, u32[]{:S(2)}, u32[]{:S(2)}) collective-permute-start(f32[5,32,128]{2,1,0:T(8,128)S(1)} %get-tuple-element.63.stat_ref), channel_id=1, source_target_pairs={{0,1},{1,0},{2,3},{3,2},{4,5},{5,4},{6,7},{7,6},{8,9},{9,8},{10,11... | collective-permute-start | bytes 245768 | tf_op jit(solution)/shard_map/ppermute | solution.py:749
  6.4 7.5 %collective-permute-start.2 = (f32[3,32,128]{2,1,0:T(8,128)S(1)}, f32[3,32,128]{2,1,0:T(8,128)S(1)}, u32[]{:S(2)}, u32[]{:S(2)}) collective-permute-start(f32[3,32,128]{2,1,0:T(8,128)S(1)} %get-tuple-element.62.outer_ref.souter_ref.refs_17_), channel_id=1, source_target_pairs={{0,12},{4,8},{8,4},{12,0},{1,13},{5,9},{9,5},{13,1},{2,14},{6,10},... | collective-permute-start | bytes 147464 | tf_op jit(solution)/shard_map/ppermute | solution.py:749
  10.0 3.9 %collective-permute-start.1 = (f32[2,32,128]{2,1,0:T(8,128)S(1)}, f32[2,32,128]{2,1,0:T(8,128)S(1)}, u32[]{:S(2)}, u32[]{:S(2)}) collective-permute-start(f32[2,32,128]{2,1,0:T(8,128)S(1)} %get-tuple-element.61.inner_ref.sinner_ref.refs_16_), channel_id=1, source_target_pairs={{0,4},{4,0},{8,12},{12,8},{1,5},{5,1},{9,13},{13,9},{2,6},{6,2},{1... | collective-permute-start | bytes 98312 | tf_op jit(solution)/shard_map/ppermute | solution.py:749
  10.0 1.6 %copy-start.1 = (f32[32,128]{1,0:T(8,128)S(1)}, f32[32,128]{1,0:T(8,128)}, u32[]{:S(2)}) copy-start(f32[32,128]{1,0:T(8,128)} %jac_ref.7) | copy-start | bytes 49156
  10.0 4.0 %collective-permute-start.4 = (f32[2,32,128]{2,1,0:T(8,128)S(1)}, f32[2,32,128]{2,1,0:T(8,128)S(1)}, u32[]{:S(2)}, u32[]{:S(2)}) collective-permute-start(f32[2,32,128]{2,1,0:T(8,128)S(1)} %get-tuple-element.65), channel_id=1, source_target_pairs={{0,2},{1,3},{2,0},{3,1},{4,6},{5,7},{6,4},{7,5},{8,10},{9,11},{10,... | collective-permute-start | bytes 98312 | tf_op jit(solution)/shard_map/ppermute | solution.py:749
  11.6 2.4 %copy-start = (f32[32,32,128]{2,1,0:T(8,128)S(1)}, f32[32,32,128]{2,1,0:T(8,128)}, u32[]{:S(2)}) copy-start(f32[32,32,128]{2,1,0:T(8,128)} %wz_ref.1) | copy-start | bytes 1572868
  11.6 2.4 %copy-start.2 = (f32[32,128]{1,0:T(8,128)S(1)}, f32[32,128]{1,0:T(8,128)}, u32[]{:S(2)}) copy-start(f32[32,128]{1,0:T(8,128)} %sx_ref.3) | copy-start | bytes 49156
  11.6 2.4 %copy-start.3 = (f32[32,128]{1,0:T(8,128)S(1)}, f32[32,128]{1,0:T(8,128)}, u32[]{:S(2)}) copy-start(f32[32,128]{1,0:T(8,128)} %sy_ref.3) | copy-start | bytes 49156
  15.1 4.0 %collective-permute-start.5 = (f32[2,32,128]{2,1,0:T(8,128)S(1)}, f32[2,32,128]{2,1,0:T(8,128)S(1)}, u32[]{:S(2)}, u32[]{:S(2)}) collective-permute-start(f32[2,32,128]{2,1,0:T(8,128)S(1)} %get-tuple-element.66), channel_id=1, source_target_pairs={{0,3},{1,2},{2,1},{3,0},{4,7},{5,6},{6,5},{7,4},{8,11},{9,10},{10,... | collective-permute-start | bytes 98312 | tf_op jit(solution)/shard_map/ppermute | solution.py:749
  15.4 3.7 %collective-permute-start.6 = (f32[32,128]{1,0:T(8,128)S(1)}, f32[32,128]{1,0:T(8,128)S(1)}, u32[]{:S(2)}, u32[]{:S(2)}) collective-permute-start(f32[32,128]{1,0:T(8,128)S(1)} %get-tuple-element.67), channel_id=1, source_target_pairs={{0,2},{1,3},{2,0},{3,1},{4,6},{5,7},{6,4},{7,5},{8,10},{9,11},{10,... | collective-permute-start | bytes 49160 | tf_op jit(solution)/shard_map/ppermute | solution.py:749
  16.8 2.3 %collective-permute-start.8 = (f32[32,128]{1,0:T(8,128)S(1)}, f32[32,128]{1,0:T(8,128)S(1)}, u32[]{:S(2)}, u32[]{:S(2)}) collective-permute-start(f32[32,128]{1,0:T(8,128)S(1)} %get-tuple-element.69), channel_id=1, source_target_pairs={{0,1},{1,0},{2,3},{3,2},{4,5},{5,4},{6,7},{7,6},{8,9},{9,8},{10,11... | collective-permute-start | bytes 49160 | tf_op jit(solution)/shard_map/ppermute | solution.py:749
  17.0 2.1 %collective-permute-start.7 = (f32[32,128]{1,0:T(8,128)S(1)}, f32[32,128]{1,0:T(8,128)S(1)}, u32[]{:S(2)}, u32[]{:S(2)}) collective-permute-start(f32[32,128]{1,0:T(8,128)S(1)} %get-tuple-element.68.refs_5_), channel_id=1, source_target_pairs={{0,1},{1,0},{2,3},{3,2},{4,5},{5,4},{6,7},{7,6},{8,9},{9,8},{10,11... | collective-permute-start | bytes 49160 | tf_op jit(solution)/shard_map/ppermute | solution.py:749
  17.3 1.8 %collective-permute-start.9 = (f32[32,128]{1,0:T(8,128)S(1)}, f32[32,128]{1,0:T(8,128)S(1)}, u32[]{:S(2)}, u32[]{:S(2)}) collective-permute-start(f32[32,128]{1,0:T(8,128)S(1)} %get-tuple-element.70.refs_6_), channel_id=1, source_target_pairs={{0,1},{1,0},{2,3},{3,2},{4,5},{5,4},{6,7},{7,6},{8,9},{9,8},{10,11... | collective-permute-start | bytes 49160 | tf_op jit(solution)/shard_map/ppermute | solution.py:749
  20.1 6.9 %collective-permute-start.10 = (f32[32,8,128]{2,1,0:T(8,128)S(1)}, f32[32,8,128]{2,1,0:T(8,128)S(1)}, u32[]{:S(2)}, u32[]{:S(2)}) collective-permute-start(f32[32,8,128]{2,1,0:T(8,128)S(1)} %get-tuple-element.82.rows_ref), channel_id=1, source_target_pairs={{0,16},{16,0},{1,17},{17,1},{2,18},{18,2},{3,19},{19,3},{4,20},{20... | collective-permute-start | bytes 393224 | tf_op jit(solution)/shard_map/ppermute | solution.py:749
  20.7 6.3 %collective-permute-start.12 = (f32[2,32,128]{2,1,0:T(8,128)S(1)}, f32[2,32,128]{2,1,0:T(8,128)S(1)}, u32[]{:S(2)}, u32[]{:S(2)}) collective-permute-start(f32[2,32,128]{2,1,0:T(8,128)S(1)} %get-tuple-element.84.outer_ref), channel_id=1, source_target_pairs={{0,12},{4,8},{8,4},{12,0},{1,13},{5,9},{9,5},{13,1},{2,14},{6,10},... | collective-permute-start | bytes 98312 | tf_op jit(solution)/shard_map/ppermute | solution.py:749
  23.3 3.7 %collective-permute-start.11 = (f32[1,32,128]{2,1,0:T(8,128)S(1)}, f32[1,32,128]{2,1,0:T(8,128)S(1)}, u32[]{:S(2)}, u32[]{:S(2)}) collective-permute-start(f32[1,32,128]{2,1,0:T(8,128)S(1)} %get-tuple-element.83.inner_ref), channel_id=1, source_target_pairs={{0,4},{4,0},{8,12},{12,8},{1,5},{5,1},{9,13},{13,9},{2,6},{6,2},{1... | collective-permute-start | bytes 49160 | tf_op jit(solution)/shard_map/ppermute | solution.py:749
  28.1 4.1 %collective-permute-start.13 = (f32[2,32,128]{2,1,0:T(8,128)S(1)}, f32[2,32,128]{2,1,0:T(8,128)S(1)}, u32[]{:S(2)}, u32[]{:S(2)}) collective-permute-start(f32[2,32,128]{2,1,0:T(8,128)S(1)} %get-tuple-element.87), channel_id=1, source_target_pairs={{0,3},{1,2},{2,1},{3,0},{4,7},{5,6},{6,5},{7,4},{8,11},{9,10},{10,... | collective-permute-start | bytes 98312 | tf_op jit(solution)/shard_map/ppermute | solution.py:749
  28.1 3.9 %collective-permute-start.14 = (f32[32,128]{1,0:T(8,128)S(1)}, f32[32,128]{1,0:T(8,128)S(1)}, u32[]{:S(2)}, u32[]{:S(2)}) collective-permute-start(f32[32,128]{1,0:T(8,128)S(1)} %get-tuple-element.88), channel_id=1, source_target_pairs={{0,2},{1,3},{2,0},{3,1},{4,6},{5,7},{6,4},{7,5},{8,10},{9,11},{10,... | collective-permute-start | bytes 49160 | tf_op jit(solution)/shard_map/ppermute | solution.py:749
  29.3 2.8 %collective-permute-start.16 = (f32[32,128]{1,0:T(8,128)S(1)}, f32[32,128]{1,0:T(8,128)S(1)}, u32[]{:S(2)}, u32[]{:S(2)}) collective-permute-start(f32[32,128]{1,0:T(8,128)S(1)} %get-tuple-element.90), channel_id=1, source_target_pairs={{0,1},{1,0},{2,3},{3,2},{4,5},{5,4},{6,7},{7,6},{8,9},{9,8},{10,11... | collective-permute-start | bytes 49160 | tf_op jit(solution)/shard_map/ppermute | solution.py:749
  30.0 2.1 %collective-permute-start.15 = (f32[32,128]{1,0:T(8,128)S(1)}, f32[32,128]{1,0:T(8,128)S(1)}, u32[]{:S(2)}, u32[]{:S(2)}) collective-permute-start(f32[32,128]{1,0:T(8,128)S(1)} %get-tuple-element.89.refs_5_), channel_id=1, source_target_pairs={{0,1},{1,0},{2,3},{3,2},{4,5},{5,4},{6,7},{7,6},{8,9},{9,8},{10,11... | collective-permute-start | bytes 49160 | tf_op jit(solution)/shard_map/ppermute | solution.py:749
  30.0 2.1 %collective-permute-start.17 = (f32[32,128]{1,0:T(8,128)S(1)}, f32[32,128]{1,0:T(8,128)S(1)}, u32[]{:S(2)}, u32[]{:S(2)}) collective-permute-start(f32[32,128]{1,0:T(8,128)S(1)} %get-tuple-element.91.refs_6_), channel_id=1, source_target_pairs={{0,1},{1,0},{2,3},{3,2},{4,5},{5,4},{6,7},{7,6},{8,9},{9,8},{10,11... | collective-permute-start | bytes 49160 | tf_op jit(solution)/shard_map/ppermute | solution.py:749

commit v14 on v13

--- a/solution.py
+++ b/solution.py
@@ -504,7 +504,7 @@
         return here, above, force_next, value, first
 
     below, here, force, value, first = lax.fori_loop(
-        0, levels, step, (zeros, zeros, zeros, zeros, zeros), unroll=UNROLL
+        0, levels, step, (zeros, zeros, zeros, zeros, zeros), unroll=2 * UNROLL
     )
     value, first = sweep(levels - 1, which, below, zeros, force, value, first)
     bottom = tiles_of(ps_ref, 0, count)

time: 33.4 us -> 33.4 us (level)
  no operation moved by 1% of the time
where the time goes in v14:
time: 33.4 us; the launch traced here: 33.2 us
  starting transfers between devices  16.2 us (49%)
  Pallas kernels  10.3 us (31%)
  waiting for transfers between devices  4.4 us (13%)
  local copies, waits for them, and re-layouts  1.6 us (5%)
  between operations  0.75 us (2%)
    ppermute x18, starting transfers between devices, swap(): return lax.ppermute(value, axis, [(i, partner(i)) for i in range(count)])  16.2 us
    pallas_call x9, Pallas kernels, call(): pl.pallas_call(kernel, out_shape=[pltpu.VMEM(s, jnp.float32) if k in keep...  10.3 us
    ppermute x18, waiting for transfers between devices, swap(): return lax.ppermute(value, axis, [(i, partner(i)) for i in range(count)])  4.4 us
    unnamed x10, local copies, waits for them, and re-layouts  1.6 us
  transfers between devices with their start and end apart: 18, of which 4 were waited for; matrix products, arithmetic and copies ran while one was open for 5% of the time, Pallas kernels for 10%

profile of v14, /device:TPU:0, one launch (start us, length us, event | category | flops | bytes accessed | tf_op | source)
XLA Modules:
  0.0 33.2 jit_solution(17191417379430598144)
XLA Ops:
  0.6 2.7 %start.1 = (f32[33,8,128]{2,1,0:T(8,128)S(1)}, f32[2,32,128]{2,1,0:T(8,128)S(1)}, f32[3,32,128]{2,1,0:T(8,128)S(1)}, f32[2,32,128]{2,1,0:T(8,128)S(1)}, f32[32,3...) custom-call(f32[32,32,128]{2,1,0:T(8,128)} %p_hbm.1, ...), custom_call_target="tpu_custom_call" | custom-call | flops 12230656 | bytes 6115328 | tf_op jit(solution)/shard_map/start/pallas_call | solution.py:730
  3.3 3.0 %collective-permute-start = (f32[33,8,128]{2,1,0:T(8,128)S(1)}, f32[33,8,128]{2,1,0:T(8,128)S(1)}, u32[]{:S(2)}, u32[]{:S(2)}) collective-permute-start(f32[33,8,128]{2,1,0:T(8,128)S(1)} %get-tuple-element.60.rows_ref.srows_ref.refs_15_), channel_id=1, source_target_pairs={{0,16},{16,0},{1,17},{17,1},{2,18},{18,2},{3,19},{19,3},{4,20},{20... | collective-permute-start | bytes 405512 | tf_op jit(solution)/shard_map/ppermute | solution.py:749
  6.4 3.6 %collective-permute-start.2 = (f32[3,32,128]{2,1,0:T(8,128)S(1)}, f32[3,32,128]{2,1,0:T(8,128)S(1)}, u32[]{:S(2)}, u32[]{:S(2)}) collective-permute-start(f32[3,32,128]{2,1,0:T(8,128)S(1)} %get-tuple-element.62.outer_ref.souter_ref.refs_17_), channel_id=1, source_target_pairs={{0,12},{4,8},{8,4},{12,0},{1,13},{5,9},{9,5},{13,1},{2,14},{6,10},... | collective-permute-start | bytes 147464 | tf_op jit(solution)/shard_map/ppermute | solution.py:749
  10.0 1.6 %collective-permute-start.4 = (f32[2,32,128]{2,1,0:T(8,128)S(1)}, f32[2,32,128]{2,1,0:T(8,128)S(1)}, u32[]{:S(2)}, u32[]{:S(2)}) collective-permute-start(f32[2,32,128]{2,1,0:T(8,128)S(1)} %get-tuple-element.65), channel_id=1, source_target_pairs={{0,2},{1,3},{2,0},{3,1},{4,6},{5,7},{6,4},{7,5},{8,10},{9,11},{10,... | collective-permute-start | bytes 98312 | tf_op jit(solution)/shard_map/ppermute | solution.py:749
  11.6 1.4 %interior.2 = (f32[32,32,128]{2,1,0:T(8,128)S(1)}, f32[32,32,128]{2,1,0:T(8,128)S(1)}, f32[32,32,128]{2,1,0:T(8,128)S(1)}) custom-call(f32[32,32,128]{2,1,0:T(8,128)S(1)} %get-tuple-element.50.p_ref, f32[32,32,128]{2,1,0:T(8,128)S(1)} %get-tuple-element.51.wx_ref, f32[32,32,128]{2,1,0:T(8,128)S(1)} %get-tuple-element.52.wy_ref, f32[32,128]{1,0:T(8,128)S(1)} %copy-done.1), custom_call_target="tpu_custom_call" | custom-call | flops 6324224 | bytes 3162112 | tf_op jit(solution)/shard_map/interior/pallas_call | solution.py:730
  13.0 0.9 %collective-permute-done.1.got_inner_ref.got_sinner_ref = f32[2,32,128]{2,1,0:T(8,128)S(1)} collective-permute-done((f32[2,32,128]{2,1,0:T(8,128)S(1)}, f32[2,32,128]{2,1,0:T(8,128)S(1)}, u32[]{:S(2)}, u32[]{:S(2)}) %collective-permute-start.1) | collective-permute-done | bytes 32800 | tf_op jit(solution)/shard_map/ppermute | solution.py:749
  14.0 1.1 %sweep.2 = (f32[32,32,128]{2,1,0:T(8,128)S(1)}, f32[32,32,128]{2,1,0:T(8,128)S(1)}, f32[32,32,128]{2,1,0:T(8,128)S(1)}, f32[32,32,128]{2,1,0:T(8,128)S(1)}, f32[...) custom-call(f32[32,32,128]{2,1,0:T(8,128)S(1)} %get-tuple-element.50, ...), custom_call_target="tpu_custom_call" | custom-call | flops 15073280 | bytes 7536640 | tf_op jit(solution)/shard_map/sweep/pallas_call | solution.py:730
  15.3 1.4 %collective-permute-start.6 = (f32[32,128]{1,0:T(8,128)S(1)}, f32[32,128]{1,0:T(8,128)S(1)}, u32[]{:S(2)}, u32[]{:S(2)}) collective-permute-start(f32[32,128]{1,0:T(8,128)S(1)} %get-tuple-element.67), channel_id=1, source_target_pairs={{0,2},{1,3},{2,0},{3,1},{4,6},{5,7},{6,4},{7,5},{8,10},{9,11},{10,... | collective-permute-start | bytes 49160 | tf_op jit(solution)/shard_map/ppermute | solution.py:749
  16.7 0.3 collective-permute-start.8
  17.2 0.3 collective-permute-start.9
  17.5 0.5 %pack.1.refs_14_ = f32[2,32,128]{2,1,0:T(8,128)S(1)} custom-call(f32[32,32,128]{2,1,0:T(8,128)S(1)} %get-tuple-element.75.wy_ref), custom_call_target="tpu_custom_call" | custom-call | flops 1114112 | bytes 557056 | tf_op jit(solution)/shard_map/pack/pallas_call | solution.py:730
  18.0 1.1 %collective-permute-done.6.refs_1_ = f32[32,128]{1,0:T(8,128)S(1)} collective-permute-done((f32[32,128]{1,0:T(8,128)S(1)}, f32[32,128]{1,0:T(8,128)S(1)}, u32[]{:S(2)}, u32[]{:S(2)}) %collective-permute-start.6) | collective-permute-done | bytes 16416 | tf_op jit(solution)/shard_map/ppermute | solution.py:749
  19.1 1.0 %finish.1 = (f32[32,32,128]{2,1,0:T(8,128)S(1)}, f32[32,32,128]{2,1,0:T(8,128)S(1)}, f32[32,8,128]{2,1,0:T(8,128)S(1)}, f32[1,32,128]{2,1,0:T(8,128)S(1)}, f32[2...) custom-call(f32[2,32,128]{2,1,0:T(8,128)S(1)} %collective-permute-done.5.refs_0_, ...), custom_call_target="tpu_custom_call" | custom-call | flops 8921088 | bytes 4460544 | tf_op jit(solution)/shard_map/finish/pallas_call | solution.py:730
  20.1 0.5 %collective-permute-start.10 = (f32[32,8,128]{2,1,0:T(8,128)S(1)}, f32[32,8,128]{2,1,0:T(8,128)S(1)}, u32[]{:S(2)}, u32[]{:S(2)}) collective-permute-start(f32[32,8,128]{2,1,0:T(8,128)S(1)} %get-tuple-element.82.rows_ref), channel_id=1, source_target_pairs={{0,16},{16,0},{1,17},{17,1},{2,18},{18,2},{3,19},{19,3},{4,20},{20... | collective-permute-start | bytes 393224 | tf_op jit(solution)/shard_map/ppermute | solution.py:749
  20.6 2.6 %collective-permute-start.12 = (f32[2,32,128]{2,1,0:T(8,128)S(1)}, f32[2,32,128]{2,1,0:T(8,128)S(1)}, u32[]{:S(2)}, u32[]{:S(2)}) collective-permute-start(f32[2,32,128]{2,1,0:T(8,128)S(1)} %get-tuple-element.84.outer_ref), channel_id=1, source_target_pairs={{0,12},{4,8},{8,4},{12,0},{1,13},{5,9},{9,5},{13,1},{2,14},{6,10},... | collective-permute-start | bytes 98312 | tf_op jit(solution)/shard_map/ppermute | solution.py:749
  23.2 1.4 %interior.3 = (f32[32,32,128]{2,1,0:T(8,128)S(1)}, f32[32,32,128]{2,1,0:T(8,128)S(1)}, f32[32,32,128]{2,1,0:T(8,128)S(1)}) custom-call(f32[32,32,128]{2,1,0:T(8,128)S(1)} %get-tuple-element.76.p_ref, f32[32,32,128]{2,1,0:T(8,128)S(1)} %get-tuple-element.74.refs_13_.wx_ref, f32[32,32,128]{2,1,0:T(8,128)S(1)} %get-tuple-element.75.wy_ref, f32[32,128]{1,0:T(8,128)S(1)} %copy-done.1), custom_call_target="tpu_custom_call" | custom-call | flops 6324224 | bytes 3162112 | tf_op jit(solution)/shard_map/interior/pallas_call | solution.py:730
  24.6 2.3 %collective-permute-done.11.got_inner_ref = f32[1,32,128]{2,1,0:T(8,128)S(1)} collective-permute-done((f32[1,32,128]{2,1,0:T(8,128)S(1)}, f32[1,32,128]{2,1,0:T(8,128)S(1)}, u32[]{:S(2)}, u32[]{:S(2)}) %collective-permute-start.11) | collective-permute-done | bytes 16416 | tf_op jit(solution)/shard_map/ppermute | solution.py:749
  27.0 1.0 %sweep.3 = (f32[32,32,128]{2,1,0:T(8,128)S(1)}, f32[32,32,128]{2,1,0:T(8,128)S(1)}, f32[32,32,128]{2,1,0:T(8,128)S(1)}, f32[32,32,128]{2,1,0:T(8,128)S(1)}, f32[...) custom-call(f32[32,32,128]{2,1,0:T(8,128)S(1)} %get-tuple-element.76, ...), custom_call_target="tpu_custom_call" | custom-call | flops 14925824 | bytes 7462912 | tf_op jit(solution)/shard_map/sweep/pallas_call | solution.py:730
  28.1 1.2 %collective-permute-start.14 = (f32[32,128]{1,0:T(8,128)S(1)}, f32[32,128]{1,0:T(8,128)S(1)}, u32[]{:S(2)}, u32[]{:S(2)}) collective-permute-start(f32[32,128]{1,0:T(8,128)S(1)} %get-tuple-element.88), channel_id=1, source_target_pairs={{0,2},{1,3},{2,0},{3,1},{4,6},{5,7},{6,4},{7,5},{8,10},{9,11},{10,... | collective-permute-start | bytes 49160 | tf_op jit(solution)/shard_map/ppermute | solution.py:749
  29.2 0.7 %collective-permute-start.16 = (f32[32,128]{1,0:T(8,128)S(1)}, f32[32,128]{1,0:T(8,128)S(1)}, u32[]{:S(2)}, u32[]{:S(2)}) collective-permute-start(f32[32,128]{1,0:T(8,128)S(1)} %get-tuple-element.90), channel_id=1, source_target_pairs={{0,1},{1,0},{2,3},{3,2},{4,5},{5,4},{6,7},{7,6},{8,9},{9,8},{10,11... | collective-permute-start | bytes 49160 | tf_op jit(solution)/shard_map/ppermute | solution.py:749
  29.9 0.5 %collective-permute-start.17 = (f32[32,128]{1,0:T(8,128)S(1)}, f32[32,128]{1,0:T(8,128)S(1)}, u32[]{:S(2)}, u32[]{:S(2)}) collective-permute-start(f32[32,128]{1,0:T(8,128)S(1)} %get-tuple-element.91.refs_6_), channel_id=1, source_target_pairs={{0,1},{1,0},{2,3},{3,2},{4,5},{5,4},{6,7},{7,6},{8,9},{9,8},{10,11... | collective-permute-start | bytes 49160 | tf_op jit(solution)/shard_map/ppermute | solution.py:749
  30.4 0.8 %copy.12 = f32[32,32,128]{2,1,0:T(8,128)} copy(f32[32,32,128]{2,1,0:T(8,128)S(1)} %get-tuple-element.96) | data formatting | bytes 1048576
  31.2 0.8 %copy.13 = f32[32,32,128]{2,1,0:T(8,128)} copy(f32[32,32,128]{2,1,0:T(8,128)S(1)} %get-tuple-element.97) | data formatting | bytes 1048576
  32.0 1.1 %last.1 = (f32[32,32,128]{2,1,0:T(8,128)}, f32[32,32,128]{2,1,0:T(8,128)}) custom-call(f32[2,32,128]{2,1,0:T(8,128)S(1)} %collective-permute-done.13.refs_0_, f32[32,128]{1,0:T(8,128)S(1)} %collective-permute-done.14.refs_1_, f32[32,128]{1,0:T(8,128)S(1)} %collective-permute-done.15.refs_2_, f32[32,128]{1,0:T(8,128)S(1)} %collective-permute-done.16.refs_3_, ...), custom_call_target="tpu_custom_call" | custom-call | flops 6946816 | bytes 3473408 | tf_op jit(solution)/shard_map/last/pallas_call | solution.py:730
  (31 shorter events, 0.7 us)
Async XLA Ops:
  3.3 10.7 %collective-permute-start = (f32[33,8,128]{2,1,0:T(8,128)S(1)}, f32[33,8,128]{2,1,0:T(8,128)S(1)}, u32[]{:S(2)}, u32[]{:S(2)}) collective-permute-start(f32[33,8,128]{2,1,0:T(8,128)S(1)} %get-tuple-element.60.rows_ref.srows_ref.refs_15_), channel_id=1, source_target_pairs={{0,16},{16,0},{1,17},{17,1},{2,18},{18,2},{3,19},{19,3},{4,20},{20... | collective-permute-start | bytes 405512 | tf_op jit(solution)/shard_map/ppermute | solution.py:749
  6.3 3.6 %collective-permute-start.3 = (f32[5,32,128]{2,1,0:T(8,128)S(1)}, f32[5,32,128]{2,1,0:T(8,128)S(1)}, u32[]{:S(2)}, u32[]{:S(2)}) collective-permute-start(f32[5,32,128]{2,1,0:T(8,128)S(1)} %get-tuple-element.63.stat_ref), channel_id=1, source_target_pairs={{0,1},{1,0},{2,3},{3,2},{4,5},{5,4},{6,7},{7,6},{8,9},{9,8},{10,11... | collective-permute-start | bytes 245768 | tf_op jit(solution)/shard_map/ppermute | solution.py:749
  6.4 7.5 %collective-permute-start.2 = (f32[3,32,128]{2,1,0:T(8,128)S(1)}, f32[3,32,128]{2,1,0:T(8,128)S(1)}, u32[]{:S(2)}, u32[]{:S(2)}) collective-permute-start(f32[3,32,128]{2,1,0:T(8,128)S(1)} %get-tuple-element.62.outer_ref.souter_ref.refs_17_), channel_id=1, source_target_pairs={{0,12},{4,8},{8,4},{12,0},{1,13},{5,9},{9,5},{13,1},{2,14},{6,10},... | collective-permute-start | bytes 147464 | tf_op jit(solution)/shard_map/ppermute | solution.py:749
  10.0 3.9 %collective-permute-start.1 = (f32[2,32,128]{2,1,0:T(8,128)S(1)}, f32[2,32,128]{2,1,0:T(8,128)S(1)}, u32[]{:S(2)}, u32[]{:S(2)}) collective-permute-start(f32[2,32,128]{2,1,0:T(8,128)S(1)} %get-tuple-element.61.inner_ref.sinner_ref.refs_16_), channel_id=1, source_target_pairs={{0,4},{4,0},{8,12},{12,8},{1,5},{5,1},{9,13},{13,9},{2,6},{6,2},{1... | collective-permute-start | bytes 98312 | tf_op jit(solution)/shard_map/ppermute | solution.py:749
  10.0 1.6 %copy-start.1 = (f32[32,128]{1,0:T(8,128)S(1)}, f32[32,128]{1,0:T(8,128)}, u32[]{:S(2)}) copy-start(f32[32,128]{1,0:T(8,128)} %jac_ref.7) | copy-start | bytes 49156
  10.0 4.0 %collective-permute-start.4 = (f32[2,32,128]{2,1,0:T(8,128)S(1)}, f32[2,32,128]{2,1,0:T(8,128)S(1)}, u32[]{:S(2)}, u32[]{:S(2)}) collective-permute-start(f32[2,32,128]{2,1,0:T(8,128)S(1)} %get-tuple-element.65), channel_id=1, source_target_pairs={{0,2},{1,3},{2,0},{3,1},{4,6},{5,7},{6,4},{7,5},{8,10},{9,11},{10,... | collective-permute-start | bytes 98312 | tf_op jit(solution)/shard_map/ppermute | solution.py:749
  11.6 2.4 %copy-start = (f32[32,32,128]{2,1,0:T(8,128)S(1)}, f32[32,32,128]{2,1,0:T(8,128)}, u32[]{:S(2)}) copy-start(f32[32,32,128]{2,1,0:T(8,128)} %wz_ref.1) | copy-start | bytes 1572868
  11.6 2.4 %copy-start.2 = (f32[32,128]{1,0:T(8,128)S(1)}, f32[32,128]{1,0:T(8,128)}, u32[]{:S(2)}) copy-start(f32[32,128]{1,0:T(8,128)} %sx_ref.3) | copy-start | bytes 49156
  11.6 2.4 %copy-start.3 = (f32[32,128]{1,0:T(8,128)S(1)}, f32[32,128]{1,0:T(8,128)}, u32[]{:S(2)}) copy-start(f32[32,128]{1,0:T(8,128)} %sy_ref.3) | copy-start | bytes 49156
  15.1 4.0 %collective-permute-start.5 = (f32[2,32,128]{2,1,0:T(8,128)S(1)}, f32[2,32,128]{2,1,0:T(8,128)S(1)}, u32[]{:S(2)}, u32[]{:S(2)}) collective-permute-start(f32[2,32,128]{2,1,0:T(8,128)S(1)} %get-tuple-element.66), channel_id=1, source_target_pairs={{0,3},{1,2},{2,1},{3,0},{4,7},{5,6},{6,5},{7,4},{8,11},{9,10},{10,... | collective-permute-start | bytes 98312 | tf_op jit(solution)/shard_map/ppermute | solution.py:749
  15.3 3.7 %collective-permute-start.6 = (f32[32,128]{1,0:T(8,128)S(1)}, f32[32,128]{1,0:T(8,128)S(1)}, u32[]{:S(2)}, u32[]{:S(2)}) collective-permute-start(f32[32,128]{1,0:T(8,128)S(1)} %get-tuple-element.67), channel_id=1, source_target_pairs={{0,2},{1,3},{2,0},{3,1},{4,6},{5,7},{6,4},{7,5},{8,10},{9,11},{10,... | collective-permute-start | bytes 49160 | tf_op jit(solution)/shard_map/ppermute | solution.py:749
  16.7 2.3 %collective-permute-start.8 = (f32[32,128]{1,0:T(8,128)S(1)}, f32[32,128]{1,0:T(8,128)S(1)}, u32[]{:S(2)}, u32[]{:S(2)}) collective-permute-start(f32[32,128]{1,0:T(8,128)S(1)} %get-tuple-element.69), channel_id=1, source_target_pairs={{0,1},{1,0},{2,3},{3,2},{4,5},{5,4},{6,7},{7,6},{8,9},{9,8},{10,11... | collective-permute-start | bytes 49160 | tf_op jit(solution)/shard_map/ppermute | solution.py:749
  17.0 2.1 %collective-permute-start.7 = (f32[32,128]{1,0:T(8,128)S(1)}, f32[32,128]{1,0:T(8,128)S(1)}, u32[]{:S(2)}, u32[]{:S(2)}) collective-permute-start(f32[32,128]{1,0:T(8,128)S(1)} %get-tuple-element.68.refs_5_), channel_id=1, source_target_pairs={{0,1},{1,0},{2,3},{3,2},{4,5},{5,4},{6,7},{7,6},{8,9},{9,8},{10,11... | collective-permute-start | bytes 49160 | tf_op jit(solution)/shard_map/ppermute | solution.py:749
  17.2 1.8 %collective-permute-start.9 = (f32[32,128]{1,0:T(8,128)S(1)}, f32[32,128]{1,0:T(8,128)S(1)}, u32[]{:S(2)}, u32[]{:S(2)}) collective-permute-start(f32[32,128]{1,0:T(8,128)S(1)} %get-tuple-element.70.refs_6_), channel_id=1, source_target_pairs={{0,1},{1,0},{2,3},{3,2},{4,5},{5,4},{6,7},{7,6},{8,9},{9,8},{10,11... | collective-permute-start | bytes 49160 | tf_op jit(solution)/shard_map/ppermute | solution.py:749
  20.1 6.9 %collective-permute-start.10 = (f32[32,8,128]{2,1,0:T(8,128)S(1)}, f32[32,8,128]{2,1,0:T(8,128)S(1)}, u32[]{:S(2)}, u32[]{:S(2)}) collective-permute-start(f32[32,8,128]{2,1,0:T(8,128)S(1)} %get-tuple-element.82.rows_ref), channel_id=1, source_target_pairs={{0,16},{16,0},{1,17},{17,1},{2,18},{18,2},{3,19},{19,3},{4,20},{20... | collective-permute-start | bytes 393224 | tf_op jit(solution)/shard_map/ppermute | solution.py:749
  20.6 6.3 %collective-permute-start.12 = (f32[2,32,128]{2,1,0:T(8,128)S(1)}, f32[2,32,128]{2,1,0:T(8,128)S(1)}, u32[]{:S(2)}, u32[]{:S(2)}) collective-permute-start(f32[2,32,128]{2,1,0:T(8,128)S(1)} %get-tuple-element.84.outer_ref), channel_id=1, source_target_pairs={{0,12},{4,8},{8,4},{12,0},{1,13},{5,9},{9,5},{13,1},{2,14},{6,10},... | collective-permute-start | bytes 98312 | tf_op jit(solution)/shard_map/ppermute | solution.py:749
  23.2 3.7 %collective-permute-start.11 = (f32[1,32,128]{2,1,0:T(8,128)S(1)}, f32[1,32,128]{2,1,0:T(8,128)S(1)}, u32[]{:S(2)}, u32[]{:S(2)}) collective-permute-start(f32[1,32,128]{2,1,0:T(8,128)S(1)} %get-tuple-element.83.inner_ref), channel_id=1, source_target_pairs={{0,4},{4,0},{8,12},{12,8},{1,5},{5,1},{9,13},{13,9},{2,6},{6,2},{1... | collective-permute-start | bytes 49160 | tf_op jit(solution)/shard_map/ppermute | solution.py:749
  28.0 4.1 %collective-permute-start.13 = (f32[2,32,128]{2,1,0:T(8,128)S(1)}, f32[2,32,128]{2,1,0:T(8,128)S(1)}, u32[]{:S(2)}, u32[]{:S(2)}) collective-permute-start(f32[2,32,128]{2,1,0:T(8,128)S(1)} %get-tuple-element.87), channel_id=1, source_target_pairs={{0,3},{1,2},{2,1},{3,0},{4,7},{5,6},{6,5},{7,4},{8,11},{9,10},{10,... | collective-permute-start | bytes 98312 | tf_op jit(solution)/shard_map/ppermute | solution.py:749
  28.1 3.9 %collective-permute-start.14 = (f32[32,128]{1,0:T(8,128)S(1)}, f32[32,128]{1,0:T(8,128)S(1)}, u32[]{:S(2)}, u32[]{:S(2)}) collective-permute-start(f32[32,128]{1,0:T(8,128)S(1)} %get-tuple-element.88), channel_id=1, source_target_pairs={{0,2},{1,3},{2,0},{3,1},{4,6},{5,7},{6,4},{7,5},{8,10},{9,11},{10,... | collective-permute-start | bytes 49160 | tf_op jit(solution)/shard_map/ppermute | solution.py:749
  29.2 2.8 %collective-permute-start.16 = (f32[32,128]{1,0:T(8,128)S(1)}, f32[32,128]{1,0:T(8,128)S(1)}, u32[]{:S(2)}, u32[]{:S(2)}) collective-permute-start(f32[32,128]{1,0:T(8,128)S(1)} %get-tuple-element.90), channel_id=1, source_target_pairs={{0,1},{1,0},{2,3},{3,2},{4,5},{5,4},{6,7},{7,6},{8,9},{9,8},{10,11... | collective-permute-start | bytes 49160 | tf_op jit(solution)/shard_map/ppermute | solution.py:749
  29.9 2.1 %collective-permute-start.15 = (f32[32,128]{1,0:T(8,128)S(1)}, f32[32,128]{1,0:T(8,128)S(1)}, u32[]{:S(2)}, u32[]{:S(2)}) collective-permute-start(f32[32,128]{1,0:T(8,128)S(1)} %get-tuple-element.89.refs_5_), channel_id=1, source_target_pairs={{0,1},{1,0},{2,3},{3,2},{4,5},{5,4},{6,7},{7,6},{8,9},{9,8},{10,11... | collective-permute-start | bytes 49160 | tf_op jit(solution)/shard_map/ppermute | solution.py:749
  29.9 2.1 %collective-permute-start.17 = (f32[32,128]{1,0:T(8,128)S(1)}, f32[32,128]{1,0:T(8,128)S(1)}, u32[]{:S(2)}, u32[]{:S(2)}) collective-permute-start(f32[32,128]{1,0:T(8,128)S(1)} %get-tuple-element.91.refs_6_), channel_id=1, source_target_pairs={{0,1},{1,0},{2,3},{3,2},{4,5},{5,4},{6,7},{7,6},{8,9},{9,8},{10,11... | collective-permute-start | bytes 49160 | tf_op jit(solution)/shard_map/ppermute | solution.py:749
